TPU v7x, 32 devices: a whole 2x2x4 slice. The times are simulated.
32 devices in a mesh: wide: 16 (over z, y, core), narrow: 2 (over x).
Axes of the slice: x: 2, y: 2, z: 4, core: 2. Of those that a mesh axis runs over, the one named last changes fastest.
Arguments:
- features: bfloat16 [16, 256, 2, 256], P(None, 'wide', None, 'narrow'), may hold values from -6 to 6
- cotangent: bfloat16 [16, 256, 2, 256], P(None, 'wide', None, 'narrow'), may hold values from -6 to 6
- coarse_weight: bfloat16 [32, 16, 3, 3, 3], replicated, may hold values from -0.3125 to 0.3125
- fine_weight: bfloat16 [16, 48, 3, 3, 3], replicated, may hold values from -0.15625 to 0.15625
Outputs:
- output: bfloat16 [16, 256, 2, 256], P(None, 'wide', None, 'narrow')
- grad_features: bfloat16 [16, 256, 2, 256], P(None, 'wide', None, 'narrow')
- grad_fine: float32 [16, 48, 3, 3, 3], replicated
- grad_coarse: float32 [32, 16, 3, 3, 3], replicated
All inputs are finite; a program needn't handle non-finite values.
Results may differ from a plain program's by a relative error of at most 0.012.
Values may be sent and summed in bfloat16 or wider, within the bound.
No kernel may reach another device: no remote copies, remote signals or barrier semaphores. Data moves between devices by JAX's collectives and lax.ppermute only.
A program may use at most 64 MiB of HBM per device.

v0:
```python
import math

import jax
import jax.numpy as jnp
from jax import lax
from jax.sharding import PartitionSpec as P


def extended_2(array, sides, width):
    for axis, dim in sides:
        count, length = (lax.axis_size(axis), array.shape[dim])
        up = [(i, (i + 1) % count) for i in range(count - 1)]
        down = [(j, i) for i, j in up]
        last = lax.slice_in_dim(array, length - width, length, axis=dim)
        first = lax.slice_in_dim(array, 0, width, axis=dim)
        before = lax.ppermute(last, axis, up)
        after = lax.ppermute(first, axis, down)
        array = jnp.concatenate([before, array, after], axis=dim)
    return array


def shortened(array):
    return jax.tree.map(lambda a: a.astype(jnp.bfloat16) if a.dtype == jnp.float32 else a, array)


def correlate(padded, kernel):
    result = lax.conv_general_dilated(
        padded[None],
        kernel,
        (1, 1, 1),
        "VALID",
        dimension_numbers=("NCHWD", "OIHWD", "NCHWD"),
        preferred_element_type=jnp.float32,
    )
    return result[0]


def weight_grad(padded, grad):
    result = lax.conv_general_dilated(
        padded[:, None],
        grad[:, None],
        (1, 1, 1),
        "VALID",
        dimension_numbers=("NCHWD", "OIHWD", "NCHWD"),
        preferred_element_type=jnp.float32,
    )
    return jnp.transpose(result, (1, 0, 2, 3, 4))


def flipped(kernel):
    return jnp.transpose(kernel[:, :, ::-1, ::-1, ::-1], (1, 0, 2, 3, 4))


def pool_sum(field):
    chans, rows, planes, cols = field.shape
    return field.reshape(chans, rows // 2, 2, planes // 2, 2, cols // 2, 2).sum(axis=(2, 4, 6))


def upsample(field):
    chans, rows, planes, cols = field.shape
    spread = jnp.broadcast_to(
        field[:, :, None, :, None, :, None], (chans, rows, 2, planes, 2, cols, 2)
    )
    return spread.reshape(chans, 2 * rows, 2 * planes, 2 * cols)


def silu_slope(value):
    sig = jax.nn.sigmoid(value)
    return sig * (1.0 + value * (1.0 - sig))


def fine_padded(field):
    extended = extended_2(field, (("wide", 1), ("narrow", 3)), 1)
    return jnp.pad(extended, ((0, 0), (0, 0), (1, 1), (0, 0)))


def coarse_padded(field):
    extended = extended_2(field, ((("wide", "narrow"), 1),), 1)
    return jnp.pad(extended, ((0, 0), (0, 0), (1, 1), (1, 1)))


def into_coarse(field):
    return jax.tree.map(
        lambda part, own: part.astype(own.dtype),
        lax.all_to_all(shortened(field), "narrow", split_axis=1, concat_axis=3, tiled=True),
        field,
    )


def into_fine(field):
    return jax.tree.map(
        lambda part, own: part.astype(own.dtype),
        lax.all_to_all(shortened(field), "narrow", split_axis=3, concat_axis=1, tiled=True),
        field,
    )


def shards(features, cotangent, coarse_weight, fine_weight):
    channels = features.shape[0]
    pooled = (pool_sum(features.astype(jnp.float32)) / 8.0).astype(jnp.bfloat16)
    coarse_ext = coarse_padded(into_coarse(pooled))
    coarse_pre = correlate(coarse_ext, coarse_weight)
    coarse_act = jax.nn.silu(coarse_pre).astype(jnp.bfloat16)
    upsampled = upsample(into_fine(coarse_act))
    joined_ext = fine_padded(jnp.concatenate([features, upsampled], 0))
    cotangent_ext = fine_padded(cotangent)
    output = correlate(joined_ext, fine_weight).astype(jnp.bfloat16)
    local_fine = weight_grad(joined_ext, cotangent)
    grad_joined = correlate(cotangent_ext, flipped(fine_weight))
    grad_act = into_coarse(pool_sum(grad_joined[channels:]).astype(jnp.bfloat16))
    grad_pre = (grad_act.astype(jnp.float32) * silu_slope(coarse_pre)).astype(jnp.bfloat16)
    local_coarse = weight_grad(coarse_ext, grad_pre)
    grad_pooled = correlate(coarse_padded(grad_pre), flipped(coarse_weight)).astype(jnp.bfloat16)
    grad_features = (
        grad_joined[:channels] + upsample(into_fine(grad_pooled)).astype(jnp.float32) / 8.0
    ).astype(jnp.bfloat16)
    fine_total, coarse_total = lax.psum((local_fine, local_coarse), ("wide", "narrow"))
    all_cells = (
        features.shape[1]
        * features.shape[2]
        * features.shape[3]
        * lax.axis_size("wide")
        * lax.axis_size("narrow")
    )
    return (
        output,
        grad_features,
        fine_total / math.sqrt(all_cells),
        coarse_total / math.sqrt(all_cells // 8),
    )


def solution(mesh):
    placed = (P(None, "wide", None, "narrow"), P(None, "wide", None, "narrow"), P(), P())
    return jax.shard_map(
        shards,
        mesh=mesh,
        in_specs=placed,
        out_specs=(P(None, "wide", None, "narrow"), P(None, "wide", None, "narrow"), P(), P()),
        check_vma=False,
    )
```

profile of v0, /device:TPU:0, one launch (start us, length us, event | category | flops | bytes accessed | tf_op | source)
XLA Modules:
  0.0 354.5 jit_solution(3009151019038733010)
XLA Ops:
  8.0 2.4 collective-permute-start.6
  15.0 3.6 %all-to-all-start = ((bf16[2,2,2048]{2,1,0:T(2,128)(2,1)}), bf16[2,2,2048]{2,1,0:T(2,128)(2,1)S(1)}, u32[]{:S(2)}, u32[]{:S(2)}) async-start(bf16[2,2,2048]{2,1,0:T(2,128)(2,1)} %reshape.285), calls=%async_computation | async-start | bytes 32768 | tf_op jit(solution)/shard_map/all_to_all | solution.py:85
  18.7 3.7 %copy.238 = bf16[16,1,16,2,128]{0,1,4,3,2:T(2,128)(2,1)} copy(bf16[16,1,16,2,128]{4,3,2,0,1:T(2,128)(2,1)S(1)} %bitcast.184) | data formatting | bytes 262144 | tf_op jit(solution)/shard_map/broadcast_in_dim | solution.py:41
  24.1 4.6 %collective-permute-start.8 = (bf16[16,18,2,1]{3,2,1,0:T(2,128)(2,1)S(1)}, bf16[16,18,2,1]{3,2,1,0:T(2,128)(2,1)S(1)}, u32[]{:S(2)}, u32[]{:S(2)}) collective-permute-start(bf16[16,18,2,1]{3,2,1,0:T(2,128)(2,1)S(1)} %get-tuple-element.32), channel_id=1, source_target_pairs={{0,1},{2,3},{4,5},{6,7},{8,9},{10,11},{12,13},{14,15},{16,17},{18,... | collective-permute-start | bytes 3464 | tf_op jit(solution)/shard_map/ppermute | solution.py:16
  30.2 5.0 %collective-permute-start = (bf16[16,1,1,128]{3,0,1,2:T(8,128)(2,1)S(1)}, bf16[16,1,1,128]{3,0,1,2:T(8,128)(2,1)S(1)}, u32[]{:S(2)}, u32[]{:S(2)}) collective-permute-start(bf16[16,1,1,128]{3,0,1,2:T(8,128)(2,1)S(1)} %get-tuple-element.40), channel_id=1, source_target_pairs={{0,1},{1,2},{2,3},{3,4},{4,5},{5,6},{6,7},{7,8},{8,9},{9,10},{10,1... | collective-permute-start | bytes 12296 | tf_op jit(solution)/shard_map/ppermute | solution.py:16
  38.7 5.0 %copy.222 = bf16[16,18,4,1,8,17]{0,4,5,2,1,3:T(8,128)(2,1)} copy(bf16[16,18,4,1,8,17]{5,4,2,1,0,3:T(8,128)(2,1)S(1)} %reshape.284) | data formatting | bytes 626688 | tf_op jit(solution)/shard_map/conv_general_dilated | solution.py:27
  44.8 5.0 %fusion.24 = f32[16,2,8,17,48]{4,2,3,1,0:T(8,128)S(1)} fusion(bf16[16,48,3,3,3]{1,0,4,3,2:T(8,128)(2,1)S(1)} %copy-done, bf16[16,18,4,1,7,2]{0,4,5,2,1,3:T(8,128)(2,1)S(1)} %slice.82, bf16[16,18,4,1,8,17]{0,4,5,2,1,3:T(8,128)(2,1)} %copy.222, pred[8,17]{0,1:T(8,128)(4,1)S(1)} %copy-done.8), kind=kOutput, calls=%fused_computation.32 | convolution fusion | flops 181745664 | bytes 1222792 | tf_op jit(solution)/shard_map/conv_general_dilated | solution.py:27
  54.9 3.4 all-to-all-start.2
  58.3 2.8 copy.223
  61.1 2.1 reshape.245
  69.1 3.3 all-to-all-start.1
  73.7 4.5 %collective-permute-start.10 = (bf16[32,1,1,128]{3,0,2,1:T(8,128)(2,1)S(1)}, bf16[32,1,1,128]{3,0,2,1:T(8,128)(2,1)S(1)}, u32[]{:S(2)}, u32[]{:S(2)}) collective-permute-start(bf16[32,1,1,128]{3,0,2,1:T(8,128)(2,1)S(1)} %get-tuple-element.38), channel_id=1, source_target_pairs={{0,1},{1,2},{2,3},{3,4},{4,5},{5,6},{6,7},{7,8},{8,9},{9,10},{10,1... | collective-permute-start | bytes 24584 | tf_op jit(solution)/shard_map/ppermute | solution.py:16
  78.5 4.4 %fusion.97 = f32[32,16,3,3,3]{0,1,4,3,2:T(8,128)S(1)} fusion(bf16[16,1,6,3,130]{0,1,4,3,2:T(2,128)(2,1)S(1)} %copy.245, bf16[32,1,4,1,128]{0,1,4,3,2:T(2,128)(2,1)S(1)} %copy.246), kind=kOutput, calls=%fused_computation.143 | convolution fusion | flops 14155776 | bytes 162944 | tf_op jit(solution)/shard_map/transpose | solution.py:47
  82.9 47.9 %psum.15 = f32[32,16,3,3,3]{0,1,4,3,2:T(8,128)S(1)} all-reduce(f32[32,16,3,3,3]{0,1,4,3,2:T(8,128)S(1)} %fusion.97), channel_id=1, replica_groups=mesh['wide'=16,'narrow'=2] {'wide','narrow'}, use_global_device_ids=true, to_apply=%region_5.6 | all-reduce | flops 13824 | bytes 110592 | tf_op jit(solution)/shard_map/psum | solution.py:117
  136.1 3.2 all-to-all-start.3
  142.1 3.0 collective-permute-start.2
  147.9 4.6 %collective-permute-start.4 = (bf16[48,18,2,1]{3,0,2,1:T(8,128)(2,1)S(1)}, bf16[48,18,2,1]{3,0,2,1:T(8,128)(2,1)S(1)}, u32[]{:S(2)}, u32[]{:S(2)}) collective-permute-start(bf16[48,18,2,1]{3,0,2,1:T(8,128)(2,1)S(1)} %get-tuple-element.28), channel_id=1, source_target_pairs={{0,1},{2,3},{4,5},{6,7},{8,9},{10,11},{12,13},{14,15},{16,17},{18,... | collective-permute-start | bytes 10376 | tf_op jit(solution)/shard_map/ppermute | solution.py:16
  153.4 7.3 %collective-permute-done.5 = bf16[48,18,2,1]{3,0,2,1:T(8,128)(2,1)S(1)} collective-permute-done((bf16[48,18,2,1]{3,0,2,1:T(8,128)(2,1)S(1)}, bf16[48,18,2,1]{3,0,2,1:T(8,128)(2,1)S(1)}, u32[]{:S(2)}, u32[]{:S(2)}) %collective-permute-start.5) | collective-permute-done | bytes 3488 | tf_op jit(solution)/shard_map/ppermute | solution.py:17
  162.6 2.0 fusion.107
  164.6 4.9 %copy.259 = bf16[48,18,4,1,130]{0,2,4,1,3:T(4,128)(2,1)S(1)} copy(bf16[48,18,4,1,130]{4,0,2,1,3:T(8,128)(2,1)} %fusion.107) | data formatting | bytes 1797120
  171.2 5.5 %fusion.9 = bf16[16,2,8,17,16]{4,2,3,1,0:T(8,128)(2,1)S(1)} fusion(bf16[16,48,3,3,3]{1,0,4,3,2:T(8,128)(2,1)S(1)} %copy-done, bf16[48,18,4,1,7,2]{0,4,5,2,1,3:T(8,128)(2,1)S(1)} %slice.78, bf16[48,18,4,1,8,17]{0,4,5,2,1,3:T(8,128)(2,1)S(1)} %copy.216), kind=kOutput, calls=%fused_computation.12 | convolution fusion | flops 183638016 | bytes 1217536 | tf_op jit(solution)/shard_map/conv_general_dilated | solution.py:27
  181.5 8.8 %copy.237 = bf16[48,1,18,4,130]{0,1,4,3,2:T(2,128)(2,1)} copy(bf16[48,1,18,4,130]{4,0,3,2,1:T(8,128)(2,1)S(1)} %fusion.106) | data formatting | bytes 1797120 | tf_op jit(solution)/shard_map/broadcast_in_dim | solution.py:40
  190.4 31.3 %fusion.96 = f32[16,48,3,3,3]{1,0,4,3,2:T(8,128)} fusion(bf16[48,1,18,4,130]{0,1,4,3,2:T(2,128)(2,1)} %copy.237, bf16[16,1,16,2,128]{0,1,4,3,2:T(2,128)(2,1)} %copy.238), kind=kOutput, calls=%fused_computation.142 | convolution fusion | flops 169869312 | bytes 1112576 | tf_op jit(solution)/shard_map/transpose | solution.py:47
  222.5 123.4 %all-reduce.6.cloned.1.call-done = f32[16,48,3,3,3]{1,0,4,3,2:T(8,128)} async-done(((f32[16,48,3,3,3]{1,0,4,3,2:T(8,128)}), f32[16,48,3,3,3]{1,0,4,3,2:T(8,128)}) %all-reduce.6.cloned.1.call-update) | async-done | bytes 82960 | tf_op jit(solution)/shard_map/psum | solution.py:117
  (132 shorter events, 47.8 us)
Async XLA Ops:
  7.2 37.6 %copy-start = (bf16[16,48,3,3,3]{1,0,4,3,2:T(8,128)(2,1)S(1)}, bf16[16,48,3,3,3]{1,0,4,3,2:T(8,128)(2,1)}, u32[]{:S(2)}) copy-start(bf16[16,48,3,3,3]{1,0,4,3,2:T(8,128)(2,1)} %param.7) | copy-start | bytes 124420
  7.2 11.5 %copy-start.3 = (bf16[16,16,2,128]{3,2,1,0:T(2,128)(2,1)S(1)}, bf16[16,16,2,128]{3,2,1,0:T(2,128)(2,1)}, u32[]{:S(2)}) copy-start(bf16[16,16,2,128]{3,2,1,0:T(2,128)(2,1)} %param.5) | copy-start | bytes 393220
  7.2 11.4 %copy-start.5 = (bf16[16,16,2,128]{3,2,1,0:T(2,128)(2,1)S(1)}, bf16[16,16,2,128]{3,2,1,0:T(2,128)(2,1)}, u32[]{:S(2)}) copy-start(bf16[16,16,2,128]{3,2,1,0:T(2,128)(2,1)} %param.4) | copy-start | bytes 393220
  8.0 14.4 %collective-permute-start.6 = (bf16[16,1,2,128]{3,2,1,0:T(2,128)(2,1)S(1)}, bf16[16,1,2,128]{3,2,1,0:T(2,128)(2,1)S(1)}, u32[]{:S(2)}, u32[]{:S(2)}) collective-permute-start(bf16[16,1,2,128]{3,2,1,0:T(2,128)(2,1)S(1)} %get-tuple-element.35), channel_id=1, source_target_pairs={{0,2},{2,4},{4,6},{6,8},{8,10},{10,12},{12,14},{14,16},{16,18},{18... | collective-permute-start | bytes 24584 | tf_op jit(solution)/shard_map/ppermute | solution.py:16
  10.4 12.2 %collective-permute-start.7 = (bf16[16,1,2,128]{3,2,1,0:T(2,128)(2,1)S(1)}, bf16[16,1,2,128]{3,2,1,0:T(2,128)(2,1)S(1)}, u32[]{:S(2)}, u32[]{:S(2)}) collective-permute-start(bf16[16,1,2,128]{3,2,1,0:T(2,128)(2,1)S(1)} %get-tuple-element.34), channel_id=1, source_target_pairs={{2,0},{4,2},{6,4},{8,6},{10,8},{12,10},{14,12},{16,14},{18,16},{20... | collective-permute-start | bytes 24584 | tf_op jit(solution)/shard_map/ppermute | solution.py:17
  15.0 13.7 %all-to-all-start = ((bf16[2,2,2048]{2,1,0:T(2,128)(2,1)}), bf16[2,2,2048]{2,1,0:T(2,128)(2,1)S(1)}, u32[]{:S(2)}, u32[]{:S(2)}) async-start(bf16[2,2,2048]{2,1,0:T(2,128)(2,1)} %reshape.285), calls=%async_computation | async-start | bytes 32768 | tf_op jit(solution)/shard_map/all_to_all | solution.py:85
  22.8 12.4 %collective-permute-start.9 = (bf16[16,18,2,1]{3,2,1,0:T(2,128)(2,1)S(1)}, bf16[16,18,2,1]{3,2,1,0:T(2,128)(2,1)S(1)}, u32[]{:S(2)}, u32[]{:S(2)}) collective-permute-start(bf16[16,18,2,1]{3,2,1,0:T(2,128)(2,1)S(1)} %get-tuple-element.33), channel_id=1, source_target_pairs={{1,0},{3,2},{5,4},{7,6},{9,8},{11,10},{13,12},{15,14},{17,16},{19,... | collective-permute-start | bytes 3464 | tf_op jit(solution)/shard_map/ppermute | solution.py:17
  24.1 11.2 %collective-permute-start.8 = (bf16[16,18,2,1]{3,2,1,0:T(2,128)(2,1)S(1)}, bf16[16,18,2,1]{3,2,1,0:T(2,128)(2,1)S(1)}, u32[]{:S(2)}, u32[]{:S(2)}) collective-permute-start(bf16[16,18,2,1]{3,2,1,0:T(2,128)(2,1)S(1)} %get-tuple-element.32), channel_id=1, source_target_pairs={{0,1},{2,3},{4,5},{6,7},{8,9},{10,11},{12,13},{14,15},{16,17},{18,... | collective-permute-start | bytes 3464 | tf_op jit(solution)/shard_map/ppermute | solution.py:16
  28.9 34.3 %collective-permute-start.1 = (bf16[16,1,1,128]{3,0,1,2:T(8,128)(2,1)S(1)}, bf16[16,1,1,128]{3,0,1,2:T(8,128)(2,1)S(1)}, u32[]{:S(2)}, u32[]{:S(2)}) collective-permute-start(bf16[16,1,1,128]{3,0,1,2:T(8,128)(2,1)S(1)} %get-tuple-element.41), channel_id=1, source_target_pairs={{1,0},{2,1},{3,2},{4,3},{5,4},{6,5},{7,6},{8,7},{9,8},{10,9},{11,1... | collective-permute-start | bytes 12296 | tf_op jit(solution)/shard_map/ppermute | solution.py:17
  30.2 33.0 %collective-permute-start = (bf16[16,1,1,128]{3,0,1,2:T(8,128)(2,1)S(1)}, bf16[16,1,1,128]{3,0,1,2:T(8,128)(2,1)S(1)}, u32[]{:S(2)}, u32[]{:S(2)}) collective-permute-start(bf16[16,1,1,128]{3,0,1,2:T(8,128)(2,1)S(1)} %get-tuple-element.40), channel_id=1, source_target_pairs={{0,1},{1,2},{2,3},{3,4},{4,5},{5,6},{6,7},{7,8},{8,9},{9,10},{10,1... | collective-permute-start | bytes 12296 | tf_op jit(solution)/shard_map/ppermute | solution.py:16
  38.7 6.1 %copy-start.8 = (pred[8,17]{0,1:T(8,128)(4,1)S(1)}, pred[8,17]{0,1:T(8,128)(4,1)}, u32[]{:S(2)}) copy-start(pred[8,17]{0,1:T(8,128)(4,1)} %constant.48) | copy-start | bytes 412
  54.9 12.7 %all-to-all-start.2 = ((bf16[2,2,4096]{2,1,0:T(2,128)(2,1)}), bf16[2,2,4096]{2,1,0:T(2,128)(2,1)S(1)}, u32[]{:S(2)}, u32[]{:S(2)}) async-start(bf16[2,2,4096]{2,1,0:T(2,128)(2,1)} %reshape.289), calls=%async_computation.2 | async-start | bytes 65536 | tf_op jit(solution)/shard_map/all_to_all | solution.py:85
  61.1 3.8 %copy-start.7 = (bf16[32,16,3,3,3]{0,1,4,3,2:T(8,128)(2,1)S(1)}, bf16[32,16,3,3,3]{0,1,4,3,2:T(8,128)(2,1)}, u32[]{:S(2)}) copy-start(bf16[32,16,3,3,3]{0,1,4,3,2:T(8,128)(2,1)} %param.6) | copy-start | bytes 82948
  69.1 66.9 %all-to-all-start.1 = ((bf16[2,2,4096]{2,1,0:T(2,128)(2,1)}), bf16[2,2,4096]{2,1,0:T(2,128)(2,1)S(1)}, u32[]{:S(2)}, u32[]{:S(2)}) async-start(bf16[2,2,4096]{2,1,0:T(2,128)(2,1)} %reshape.287), calls=%async_computation.1 | async-start | bytes 65536 | tf_op jit(solution)/shard_map/all_to_all | solution.py:93
  72.4 59.1 %collective-permute-start.11 = (bf16[32,1,1,128]{3,0,2,1:T(8,128)(2,1)S(1)}, bf16[32,1,1,128]{3,0,2,1:T(8,128)(2,1)S(1)}, u32[]{:S(2)}, u32[]{:S(2)}) collective-permute-start(bf16[32,1,1,128]{3,0,2,1:T(8,128)(2,1)S(1)} %get-tuple-element.39), channel_id=1, source_target_pairs={{1,0},{2,1},{3,2},{4,3},{5,4},{6,5},{7,6},{8,7},{9,8},{10,9},{11,1... | collective-permute-start | bytes 24584 | tf_op jit(solution)/shard_map/ppermute | solution.py:17
  73.7 57.8 %collective-permute-start.10 = (bf16[32,1,1,128]{3,0,2,1:T(8,128)(2,1)S(1)}, bf16[32,1,1,128]{3,0,2,1:T(8,128)(2,1)S(1)}, u32[]{:S(2)}, u32[]{:S(2)}) collective-permute-start(bf16[32,1,1,128]{3,0,2,1:T(8,128)(2,1)S(1)} %get-tuple-element.38), channel_id=1, source_target_pairs={{0,1},{1,2},{2,3},{3,4},{4,5},{5,6},{6,7},{7,8},{8,9},{9,10},{10,1... | collective-permute-start | bytes 24584 | tf_op jit(solution)/shard_map/ppermute | solution.py:16
  136.1 9.1 %all-to-all-start.3 = ((bf16[2,2,2048]{2,1,0:T(2,128)(2,1)}), bf16[2,2,2048]{2,1,0:T(2,128)(2,1)S(1)}, u32[]{:S(2)}, u32[]{:S(2)}) async-start(bf16[2,2,2048]{2,1,0:T(2,128)(2,1)} %reshape.291), calls=%async_computation.3 | async-start | bytes 32768 | tf_op jit(solution)/shard_map/all_to_all | solution.py:93
  139.3 206.5 %all-reduce.6.cloned.1.call-start = ((), (), s32[]{:S(2)}) async-start(), calls=%async_computation.4 | async-start | bytes 442368 | tf_op jit(solution)/shard_map/psum | solution.py:117
  140.8 5.6 %collective-permute-start.3 = (bf16[48,1,2,128]{3,0,2,1:T(8,128)(2,1)S(1)}, bf16[48,1,2,128]{3,0,2,1:T(8,128)(2,1)S(1)}, u32[]{:S(2)}, u32[]{:S(2)}) collective-permute-start(bf16[48,1,2,128]{3,0,2,1:T(8,128)(2,1)S(1)} %get-tuple-element.31), channel_id=1, source_target_pairs={{2,0},{4,2},{6,4},{8,6},{10,8},{12,10},{14,12},{16,14},{18,16},{20... | collective-permute-start | bytes 73736 | tf_op jit(solution)/shard_map/ppermute | solution.py:17
  142.1 4.3 %collective-permute-start.2 = (bf16[48,1,2,128]{3,0,2,1:T(8,128)(2,1)S(1)}, bf16[48,1,2,128]{3,0,2,1:T(8,128)(2,1)S(1)}, u32[]{:S(2)}, u32[]{:S(2)}) collective-permute-start(bf16[48,1,2,128]{3,0,2,1:T(8,128)(2,1)S(1)} %get-tuple-element.30), channel_id=1, source_target_pairs={{0,2},{2,4},{4,6},{6,8},{8,10},{10,12},{12,14},{14,16},{16,18},{18... | collective-permute-start | bytes 73736 | tf_op jit(solution)/shard_map/ppermute | solution.py:16
  146.7 14.0 %collective-permute-start.5 = (bf16[48,18,2,1]{3,0,2,1:T(8,128)(2,1)S(1)}, bf16[48,18,2,1]{3,0,2,1:T(8,128)(2,1)S(1)}, u32[]{:S(2)}, u32[]{:S(2)}) collective-permute-start(bf16[48,18,2,1]{3,0,2,1:T(8,128)(2,1)S(1)} %get-tuple-element.29), channel_id=1, source_target_pairs={{1,0},{3,2},{5,4},{7,6},{9,8},{11,10},{13,12},{15,14},{17,16},{19,... | collective-permute-start | bytes 10376 | tf_op jit(solution)/shard_map/ppermute | solution.py:17
  147.9 13.9 %collective-permute-start.4 = (bf16[48,18,2,1]{3,0,2,1:T(8,128)(2,1)S(1)}, bf16[48,18,2,1]{3,0,2,1:T(8,128)(2,1)S(1)}, u32[]{:S(2)}, u32[]{:S(2)}) collective-permute-start(bf16[48,18,2,1]{3,0,2,1:T(8,128)(2,1)S(1)} %get-tuple-element.28), channel_id=1, source_target_pairs={{0,1},{2,3},{4,5},{6,7},{8,9},{10,11},{12,13},{14,15},{16,17},{18,... | collective-permute-start | bytes 10376 | tf_op jit(solution)/shard_map/ppermute | solution.py:16
  178.8 1.7 copy-start.2
  190.4 31.3 %copy-start.4 = (bf16[16,2,1,136,16]{3,4,1,0,2:T(8,128)(2,1)S(1)}, bf16[16,2,1,136,16]{3,4,1,0,2:T(8,128)(2,1)}, u32[]{:S(2)}) copy-start(bf16[16,2,1,136,16]{3,4,1,0,2:T(8,128)(2,1)} %reshape.238) | copy-start | bytes 417796
  (2 other events, 2.0 us)
Sparse Core Ops, SparseCore 0:
  221.8 124.0 all-reduce.5
where the time goes:
time: 359 us; the launch traced here: 355 us
  waiting for transfers between devices  132 us (37%)
  local copies, waits for them, and re-layouts  54.3 us (15%)
  matrix products  48.1 us (13%)
  blocking collectives  47.9 us (13%)
  starting transfers between devices  45.8 us (13%)
  between operations  15 us (4%)
  other arithmetic  11.6 us (3%)
    psum x1, waiting for transfers between devices, shards(): lax.psum((local_fine, local_coarse), ('wide', 'narrow'))  123 us
    psum x1, blocking collectives, shards(): lax.psum((local_fine, local_coarse), ('wide', 'narrow'))  47.9 us
    transpose x2, matrix products, weight_grad(): return jnp.transpose(result, (1, 0, 2, 3, 4))  35.7 us
    ppermute x6, starting transfers between devices, extended_2(): before = lax.ppermute(last, axis, up)  24.1 us
    conv_general_dilated x19, local copies, waits for them, and re-layouts, correlate(): lax.conv_general_dilated(padded[None], kernel, (1, 1, 1), 'VALID', dimens...  20.2 us
    conv_general_dilated x4, matrix products, correlate(): lax.conv_general_dilated(padded[None], kernel, (1, 1, 1), 'VALID', dimens...  12.4 us
    unnamed x33, local copies, waits for them, and re-layouts  11 us
    broadcast_in_dim x2, local copies, waits for them, and re-layouts, weight_grad(): padded[:, None]  10.2 us
  transfers between devices with their start and end apart: 17, of which 3 were waited for; matrix products, arithmetic and copies ran while one was open for 14% of the time, Pallas kernels for 0%

commit v1 on v0

v1 whole, which is shorter than its diff:
```python
import functools
import math

import jax
import jax.numpy as jnp
from jax import lax
from jax.experimental import pallas as pl
from jax.experimental.pallas import tpu as pltpu
from jax.sharding import PartitionSpec as P

C1, C2 = 16, 32
ROWS, COLS = 16, 128
HALO = 4
EXT = ROWS + 2 * HALO
BF, F32 = jnp.bfloat16, jnp.float32
VMEM_LIMIT = 48 * 1024 * 1024


def lanes_of(shape):
    return lax.broadcasted_iota(jnp.int32, shape, len(shape) - 1)


def row(index, count=1):
    return slice(index * COLS, (index + count) * COLS)


def pack_kernel(sides, f_ref, g_ref, s_ref, up_ref, down_ref, strip_ref, wide_ref):
    lane = lanes_of((C1, COLS))
    place = lax.axis_index("narrow")
    for a, ref in enumerate((f_ref, g_ref)):
        wide_ref[...] = ref[...].astype(F32)
        for z in range(2):
            chans = slice(a * 32 + z * 16, a * 32 + z * 16 + 16)
            strips = [jnp.zeros((C1, COLS), F32) for _ in range(sides)]
            for y in range(ROWS):
                value = wide_ref[pl.ds(2 * y + z, C1, stride=2 * ROWS), :]
                s_ref[chans, row(y)] = value.astype(BF)
                start = HALO * (y + HALO)
                inside = (lane >= start) & (lane < start + HALO)
                for side in range(sides):
                    if sides == 2:
                        shift = start + HALO * side
                    else:
                        shift = start + HALO * (1 - place)
                    strips[side] = jnp.where(inside, pltpu.roll(value, shift, 1), strips[side])
            for side in range(sides):
                strip_ref[chans, row(side)] = strips[side].astype(BF)
                turned = pltpu.roll(strips[side], 64, 1)
                up_ref[chans, row(HALO + side)] = jnp.where(lane < 16, turned, 0.0).astype(BF)
                down_ref[chans, row(HALO + side)] = jnp.where(
                    (lane >= 80) & (lane < 96), turned, 0.0
                ).astype(BF)
    up_ref[:, row(0, HALO)] = s_ref[:, row(ROWS - HALO, HALO)]
    down_ref[:, row(0, HALO)] = s_ref[:, row(0, HALO)]


def pack(features, cotangent, sides):
    flat = lambda a: a.reshape(C1 * ROWS * 2, COLS)
    message = jax.ShapeDtypeStruct((64, (HALO + sides) * COLS), BF)
    return pl.pallas_call(
        functools.partial(pack_kernel, sides),
        out_shape=(
            jax.ShapeDtypeStruct((64, ROWS * COLS), BF),
            message,
            message,
            jax.ShapeDtypeStruct((64, sides * COLS), BF),
        ),
        scratch_shapes=[pltpu.VMEM((C1 * ROWS * 2, COLS), F32)],
        compiler_params=pltpu.CompilerParams(vmem_limit_bytes=VMEM_LIMIT),
        cost_estimate=pl.CostEstimate(flops=10**6, bytes_accessed=10**6, transcendentals=0),
        name="pack",
    )(flat(features), flat(cotangent))


def turn(main, side, by):
    lane = lanes_of(main.shape)
    a, b = pltpu.roll(main, (-by) % COLS, 1), pltpu.roll(side, (-by) % COLS, 1)
    crossed = lane >= COLS - by if by > 0 else lane < -by
    return jnp.where(crossed, b, a), jnp.where(crossed, a, b)


def pair_sum(value):
    lane = lanes_of(value.shape)
    other = jnp.where(lane % 2 == 0, pltpu.roll(value, COLS - 1, 1), pltpu.roll(value, 1, 1))
    return value + other


def dot(a, b):
    return jnp.dot(a, b, preferred_element_type=F32)


def dot_nt(a, b):
    return lax.dot_general(a, b, (((1,), (1,)), ((), ())), preferred_element_type=F32)


def block_kernel(
    counts,
    s_ref, up_ref, down_ref, left_ref, right_ref, wo_ref, wg_ref, wc_ref, wq_ref,
    out_ref, gf_ref, gw_ref,
    ext_ref, side_ref, jst_ref, gst_ref, gsb_ref, pst_ref, psb_ref, qst_ref,
    pre_ref, prb_ref, ro_ref, rg_ref, rgb_ref, rq_ref, gp_ref, flat_ref, fa_ref, fb_ref, fc_ref,
):
    w, n = lax.axis_index("wide"), lax.axis_index("narrow")
    lane32 = lanes_of((C2, COLS))
    lane64 = lanes_of((64, COLS))
    flag = lambda is_there: jnp.where(is_there, 1.0, 0.0)
    has_left, has_right = flag(n > 0), flag(n < counts[1] - 1)
    has_above, has_below = flag(w > 0), flag(w < counts[0] - 1)

    ext_ref[:, row(0, HALO)] = up_ref[:, row(0, HALO)]
    ext_ref[:, row(HALO, ROWS)] = s_ref[...]
    ext_ref[:, row(HALO + ROWS, HALO)] = down_ref[:, row(0, HALO)]

    left = left_ref[...].astype(F32) * has_left
    right = right_ref[...].astype(F32) * has_right
    for r in range(EXT):
        at_right = pltpu.roll(right, (-HALO * r) % COLS, 1)
        at_left = pltpu.roll(left, (COLS - HALO - HALO * r) % COLS, 1)
        side_ref[:, row(r)] = jnp.where(
            lane64 < HALO, at_right, jnp.where(lane64 >= COLS - HALO, at_left, 0.0)
        ).astype(BF)

    half = [None, None]
    for r in range(EXT):
        both = [ref[0:32, row(r)].astype(F32) for ref in (ext_ref, side_ref)]
        if r % 2 == 0:
            half = both
        else:
            mean = []
            for first, second in zip(half, both):
                total = first + second
                mean.append((pair_sum(total[0:16] + total[16:32]) * 0.125).astype(BF).astype(F32))
            for d in range(3):
                a, b = mean if d == 1 else turn(mean[0], mean[1], 2 * (d - 1))
                pst_ref[d * 16 : d * 16 + 16, row(r // 2)] = a.astype(BF)
                psb_ref[d * 16 : d * 16 + 16, row(r // 2)] = b.astype(BF)
        if HALO - 1 <= r <= HALO + ROWS:
            at = r - HALO + 1
            for d in range(3):
                a = both[0] if d == 1 else turn(both[0], both[1], d - 1)[0]
                jst_ref[d * 64 : d * 64 + 32, row(at)] = a.astype(BF)

    pre_ref[...] = dot(wc_ref[...], pst_ref[...])
    prb_ref[...] = dot(wc_ref[...], psb_ref[...])

    for at in range(22):
        a0 = ext_ref[32:64, row(at + 1)].astype(F32)
        b0 = side_ref[32:64, row(at + 1)].astype(F32)
        for d in range(3):
            a, b = (a0, b0) if d == 1 else turn(a0, b0, d - 1)
            gst_ref[d * 32 : d * 32 + 32, row(at)] = a.astype(BF)
            gsb_ref[d * 32 : d * 32 + 32, row(at)] = b.astype(BF)
    rg_ref[...] = dot(wg_ref[...], gst_ref[...])
    for d in range(3):
        rgb_ref[d * 32 : d * 32 + 32, :] = dot(
            wg_ref[d * 64 + 32 : d * 64 + 64, :], gsb_ref[...]
        )

    for at in range(10):
        keep = has_above if at == 0 else has_below if at == 9 else 1.0
        keep_side = keep * jnp.where(lane32 < 64, has_right, has_left)
        act, grad = [], []
        for ref, joined_ref, base, size, kept in (
            (pre_ref, rg_ref, 32, 64, keep),
            (prb_ref, rgb_ref, 0, 32, keep_side),
        ):
            value = (
                ref[0:32, row(at)] + ref[32:64, row(at + 1)] + ref[64:96, row(at + 2)]
            )
            sig = 1.0 / (1.0 + jnp.exp(-value))
            act.append((value * sig * kept).astype(BF).astype(F32))
            total = jnp.zeros((C2, COLS), F32)
            for r in (2 * at, 2 * at + 1):
                for d in range(3):
                    lo = d * size + base
                    total = total + joined_ref[lo : lo + 32, row(r + d)]
            grad_act = pair_sum(total).astype(BF).astype(F32)
            grad_pre = grad_act * (sig * (1.0 + value * (1.0 - sig)))
            grad.append((grad_pre * kept).astype(BF).astype(F32))
        for d in range(3):
            a = act[0] if d == 1 else turn(act[0], act[1], d - 1)[0]
            a = a.astype(BF)
            for r in (2 * at - 1, 2 * at):
                if 0 <= r < 18:
                    jst_ref[d * 64 + 32 : d * 64 + 64, row(r)] = a
            q = grad[0] if d == 1 else turn(grad[0], grad[1], 2 * (d - 1))[0]
            qst_ref[d * 32 : d * 32 + 32, row(at)] = q.astype(BF)

    ro_ref[...] = dot(wo_ref[...], jst_ref[...])
    for y in range(ROWS):
        value = ro_ref[0:32, row(y)] + ro_ref[32:64, row(y + 1)] + ro_ref[64:96, row(y + 2)]
        for z in range(2):
            flat_ref[pl.ds(2 * y + z, C1, stride=2 * ROWS), :] = value[z * 16 : z * 16 + 16]
    out_ref[...] = flat_ref[...].astype(BF)

    rq_ref[...] = dot(wq_ref[...], qst_ref[...])
    for at in range(ROWS // 2):
        pooled = rq_ref[0:16, row(at)] + rq_ref[16:32, row(at + 1)] + rq_ref[32:48, row(at + 2)]
        pooled = pooled.astype(BF).astype(F32) * 0.125
        for y in (2 * at, 2 * at + 1):
            for z in range(2):
                total = pooled
                for d in range(3):
                    lo = d * 64 + z * 16
                    total = total + rg_ref[lo : lo + 16, row(y + 2 + d)]
                flat_ref[pl.ds(2 * y + z, C1, stride=2 * ROWS), :] = total
    gf_ref[...] = flat_ref[...].astype(BF)

    own = row(1, ROWS)
    fa_ref[0:16, :] = jst_ref[64:80, own]
    fa_ref[16:48, :] = jst_ref[96:128, own]
    fa_ref[48:64, :] = jst_ref[64:80, own]
    fa_ref[64:96, :] = jst_ref[96:128, own]
    fa_ref[96:128, :] = jnp.zeros((32, ROWS * COLS), BF)
    fb_ref[0:48, :] = jst_ref[80:128, own]
    fb_ref[48:96, :] = jst_ref[80:128, own]
    fb_ref[96:128, :] = jnp.zeros((32, ROWS * COLS), BF)
    fc_ref[0:96, :] = jnp.zeros((96, 8 * COLS), BF)
    fc_ref[96:128, :] = qst_ref[32:64, row(1, 8)]
    fine, coarse = {}, {}
    for ky in range(3):
        shifted = gst_ref[:, row(4 - ky, ROWS)]
        ra, rb = dot_nt(shifted, fa_ref[...]), dot_nt(shifted, fb_ref[...])
        rc = dot_nt(pst_ref[:, row(1 + ky, 8)], fc_ref[...])
        for kx in range(3):
            lo = (2 - kx) * 32
            fine[ky, 0, kx] = ra[lo + 16 : lo + 32]
            fine[ky, 1, kx] = ra[lo : lo + 16] + rb[lo + 16 : lo + 32]
            fine[ky, 2, kx] = rb[lo : lo + 16]
            coarse[ky, kx] = rc[kx * 16 : kx * 16 + 16] * 0.5
    lane16 = lanes_of((16, COLS))
    order = [(ky, kz, kx) for ky in range(3) for kz in range(3) for kx in range(3)]
    for i in range(16):
        value = jnp.zeros((16, COLS), F32)
        if i < 14:
            value = jnp.where(lane16 < 48, fine[order[i]], value)
        if i < 13:
            value = jnp.where((lane16 >= 48) & (lane16 < 96), fine[order[14 + i]], value)
        if i < 9:
            value = jnp.where(lane16 >= 96, coarse[i // 3, i % 3], value)
        gw_ref[i * 16 : i * 16 + 16, :] = value


def block(counts, operands):
    cells = (C1 * ROWS * 2, COLS)
    v = lambda rows_, lanes_, kind: pltpu.VMEM((rows_, lanes_ * COLS), kind)
    return pl.pallas_call(
        functools.partial(block_kernel, counts),
        out_shape=(
            jax.ShapeDtypeStruct(cells, BF),
            jax.ShapeDtypeStruct(cells, BF),
            jax.ShapeDtypeStruct((256, COLS), F32),
        ),
        scratch_shapes=[
            v(64, EXT, BF), v(64, EXT, BF),
            v(192, 18, BF),
            v(96, 22, BF), v(96, 22, BF),
            v(48, 12, BF), v(48, 12, BF),
            v(96, 10, BF),
            v(96, 12, F32), v(96, 12, F32),
            v(96, 18, F32),
            v(192, 22, F32), v(96, 22, F32),
            v(48, 10, F32),
            v(32, 8, BF),
            pltpu.VMEM(cells, F32),
            v(128, ROWS, BF), v(128, ROWS, BF), v(128, 8, BF),
        ],
        compiler_params=pltpu.CompilerParams(vmem_limit_bytes=VMEM_LIMIT),
        cost_estimate=pl.CostEstimate(flops=10**9, bytes_accessed=4 * 10**6, transcendentals=10**5),
        name="block",
    )(*operands)


def spread_kernel(fine_scale, coarse_scale, sum_ref, fine_ref, coarse_ref):
    for i in range(27):
        if i < 14:
            value = sum_ref[i * 16 : i * 16 + 16, :]
        else:
            value = pltpu.roll(sum_ref[(i - 14) * 16 : (i - 14) * 16 + 16, :], 80, 1)
        fine_ref[i * 16 : i * 16 + 16, :] = value[:, 0:48] * fine_scale
        ky, kz, kx = i // 9, i // 3 % 3, i % 3
        if kz == 1:
            at = (ky * 3 + kx) * 16
            value = pltpu.roll(sum_ref[at : at + 16, :], 32, 1)[:, 0:32] * coarse_scale
        else:
            value = jnp.zeros((16, 32), F32)
        coarse_ref[i * 16 : i * 16 + 16, :] = value


def spread(total, fine_scale, coarse_scale):
    return pl.pallas_call(
        functools.partial(spread_kernel, fine_scale, coarse_scale),
        out_shape=(
            jax.ShapeDtypeStruct((432, 48), F32),
            jax.ShapeDtypeStruct((432, 32), F32),
        ),
        compiler_params=pltpu.CompilerParams(vmem_limit_bytes=VMEM_LIMIT),
        name="spread",
    )(total)


def weight_matrices(coarse_weight, fine_weight):
    fine = jnp.transpose(fine_weight, (2, 3, 4, 0, 1))
    planes = []
    for zo in range(2):
        first, second = fine[:, 1 - zo], fine[:, 2 - zo]
        both = (first[..., C1:].astype(F32) + second[..., C1:].astype(F32)).astype(BF)
        planes.append(jnp.concatenate([first[..., :C1], second[..., :C1], both], -1))
    stacked = jnp.stack(planes, 1)
    wo = jnp.transpose(stacked, (0, 1, 3, 2, 4)).reshape(96, 192)
    wg = jnp.transpose(stacked[::-1, :, ::-1], (0, 4, 2, 1, 3)).reshape(192, 96)
    middle = coarse_weight[:, :, :, 1, :]
    wc = jnp.transpose(middle, (2, 0, 3, 1)).reshape(96, 48)
    wq = jnp.transpose(middle[:, :, ::-1, ::-1], (2, 1, 3, 0)).reshape(48, 96)
    return wo, wg, wc, wq


def shards(features, cotangent, coarse_weight, fine_weight):
    wide, narrow = lax.axis_size("wide"), lax.axis_size("narrow")
    matrices = weight_matrices(coarse_weight, fine_weight)
    sides = 1 if narrow == 2 else 2
    own, up, down, strip = pack(features, cotangent, sides)
    above = lax.ppermute(up, "wide", [(i, i + 1) for i in range(wide - 1)])
    below = lax.ppermute(down, "wide", [(i + 1, i) for i in range(wide - 1)])
    strip = strip + above[:, HALO * COLS :] + below[:, HALO * COLS :]
    if sides == 1:
        left = right = lax.ppermute(strip, "narrow", [(0, 1), (1, 0)])
    else:
        right = lax.ppermute(strip[:, :COLS], "narrow", [(i + 1, i) for i in range(narrow - 1)])
        left = lax.ppermute(strip[:, COLS:], "narrow", [(i, i + 1) for i in range(narrow - 1)])
    output, grad_features, grads = block(
        (wide, narrow), (own, above, below, left, right) + matrices
    )
    devices = wide * narrow
    share = -(-256 // devices)
    grads = jnp.pad(grads, ((0, share * devices - 256), (0, 0))).reshape(devices, share, COLS)
    both = ("wide", "narrow")
    parts = lax.all_to_all(grads, both, 0, 0, tiled=True)
    total = jnp.broadcast_to(jnp.sum(parts, 0, keepdims=True), parts.shape)
    total = lax.all_to_all(total, both, 0, 0, tiled=True)
    total = total.reshape(share * devices, COLS)[:256]
    all_cells = features.shape[1] * features.shape[2] * features.shape[3] * devices
    grad_fine, grad_coarse = spread(
        total, 1.0 / math.sqrt(all_cells), 1.0 / math.sqrt(all_cells // 8)
    )
    grad_fine = jnp.transpose(grad_fine.reshape(3, 3, 3, C1, C1 + C2), (3, 4, 0, 1, 2))
    grad_coarse = jnp.transpose(grad_coarse.reshape(3, 3, 3, C1, C2), (4, 3, 0, 1, 2))
    return (
        output.reshape(features.shape),
        grad_features.reshape(features.shape),
        grad_fine,
        grad_coarse,
    )


def solution(mesh):
    placed = P(None, "wide", None, "narrow")
    return jax.shard_map(
        shards,
        mesh=mesh,
        in_specs=(placed, placed, P(), P()),
        out_specs=(placed, placed, P(), P()),
        check_vma=False,
    )
```

time: 359 us -> 45.7 us (0.13); the launches traced: 355 us -> 45.4 us
  waiting for transfers between devices: 132 us -> 4.33 us
  local copies, waits for them, and re-layouts: 54.3 us -> 3.41 us
  matrix products: 48.1 us -> 0 us
  starting transfers between devices: 45.8 us -> 5.28 us
  blocking collectives: 47.9 us -> 26 us
  between operations: 15 us -> 0.76 us
  other arithmetic: 11.6 us -> 0.28 us
  Pallas kernels: 0 us -> 5.28 us
    psum x1 -> x0, waiting for transfers between devices: 123 us -> none  [shards(): lax.psum((local_fine, local_coarse), ('wide', 'narrow'))]
    psum x1 -> x0, blocking collectives: 47.9 us -> none  [shards(): lax.psum((local_fine, local_coarse), ('wide', 'narrow'))]
    transpose x2 -> x0, matrix products: 35.7 us -> none  [weight_grad(): return jnp.transpose(result, (1, 0, 2, 3, 4))]
    ppermute x12 -> x3, starting transfers between devices: 31.9 us -> 5.28 us  [the longest x1 2.49 us: shards(): above = lax.ppermute(up, 'wide', [(i, i + 1) for i in range(wide - 1)])]
    all_to_all x0 -> x2, blocking collectives: none -> 26 us  [the longest x1 15.7 us: shards(): parts = lax.all_to_all(grads, both, 0, 0, tiled=True)]
    conv_general_dilated x19 -> x0, local copies, waits for them, and re-layouts: 20.2 us -> none  [correlate(): lax.conv_general_dilated(padded[None], kernel, (1, 1, 1), 'VALID', dimens...]
    broadcast_in_dim x12 -> x1, local copies, waits for them, and re-layouts: 16.8 us -> 0.01 us  [shards(): total = jnp.broadcast_to(jnp.sum(parts, 0, keepdims=True), parts.shape)]
    all_to_all x4 -> x0, starting transfers between devices: 13.5 us -> none  [the longest x2 7.02 us: into_coarse(): lax.all_to_all(shortened(field), 'narrow', split_axis=1, concat_axis=3, t...]
  transfers between devices with their start and end apart: 17 -> 3, of which waited for: 3 -> 2; matrix products, arithmetic and copies ran while one was open for 14% -> 4% of each run, Pallas kernels for 0% -> 0%
where the time goes in v1:
time: 45.7 us; the launch traced here: 45.4 us
  blocking collectives  26 us (57%)
  Pallas kernels  5.28 us (12%)
  starting transfers between devices  5.28 us (12%)
  waiting for transfers between devices  4.33 us (9%)
  local copies, waits for them, and re-layouts  3.41 us (7%)
  between operations  0.76 us (2%)
    all_to_all x1, blocking collectives, shards(): parts = lax.all_to_all(grads, both, 0, 0, tiled=True)  15.7 us
    all_to_all x1, blocking collectives, shards(): total = lax.all_to_all(total, both, 0, 0, tiled=True)  10.3 us
    pallas_call x1, Pallas kernels, block(): pl.pallas_call(functools.partial(block_kernel, counts), out_shape=(jax.Sh...  3.91 us
    ppermute x1, waiting for transfers between devices, shards(): below = lax.ppermute(down, 'wide', [(i + 1, i) for i in range(wide - 1)])  2.9 us
    ppermute x1, starting transfers between devices, shards(): above = lax.ppermute(up, 'wide', [(i, i + 1) for i in range(wide - 1)])  2.49 us
    unnamed x6, local copies, waits for them, and re-layouts  1.8 us
    ppermute x1, starting transfers between devices, shards(): left = right = lax.ppermute(strip, 'narrow', [(0, 1), (1, 0)])  1.49 us
    ppermute x1, waiting for transfers between devices, shards(): left = right = lax.ppermute(strip, 'narrow', [(0, 1), (1, 0)])  1.43 us
  transfers between devices with their start and end apart: 3, of which 2 were waited for; matrix products, arithmetic and copies ran while one was open for 4% of the time, Pallas kernels for 0%

profile of v1, /device:TPU:0, one launch (start us, length us, event | category | flops | bytes accessed | tf_op | source)
XLA Modules:
  0.0 45.4 jit_solution(12024173048723634669)
XLA Ops:
  0.6 0.0 copy-start
  0.6 0.9 %copy-done = bf16[16,16,2,128]{3,2,1,0:T(2,128)(2,1)S(1)} copy-done((bf16[16,16,2,128]{3,2,1,0:T(2,128)(2,1)S(1)}, bf16[16,16,2,128]{3,2,1,0:T(2,128)(2,1)}, u32[]{:S(2)}) %copy-start) | copy-done | bytes 131096
  1.5 0.9 %copy-done.1 = bf16[16,16,2,128]{3,2,1,0:T(2,128)(2,1)S(1)} copy-done((bf16[16,16,2,128]{3,2,1,0:T(2,128)(2,1)S(1)}, bf16[16,16,2,128]{3,2,1,0:T(2,128)(2,1)}, u32[]{:S(2)}) %copy-start.1) | copy-done | bytes 131096
  2.4 0.5 %pack.1 = (bf16[64,2048]{1,0:T(8,128)(2,1)S(1)}, bf16[64,640]{1,0:T(8,128)(2,1)S(1)}, bf16[64,640]{1,0:T(8,128)(2,1)S(1)}, bf16[64,128]{1,0:T(8,128)(2,1)S(1)}) custom-call(bf16[512,128]{1,0:T(8,128)(2,1)S(1)} %bitcast.46, bf16[512,128]{1,0:T(8,128)(2,1)S(1)} %bitcast.47), custom_call_target="tpu_custom_call" | custom-call | flops 1000000 | bytes 1000000 | tf_op jit(solution)/shard_map/pack/pallas_call | solution.py:60
  3.0 2.5 %collective-permute-start = (bf16[64,640]{1,0:T(8,128)(2,1)S(1)}, bf16[64,640]{1,0:T(8,128)(2,1)S(1)}, u32[]{:S(2)}, u32[]{:S(2)}) collective-permute-start(bf16[64,640]{1,0:T(8,128)(2,1)S(1)} %get-tuple-element.14), channel_id=1, source_target_pairs={{0,2},{2,4},{4,6},{6,8},{8,10},{10,12},{12,14},{14,16},{16,18},{18... | collective-permute-start | bytes 245768 | tf_op jit(solution)/shard_map/ppermute | solution.py:323
  5.5 1.3 %collective-permute-start.1 = (bf16[64,640]{1,0:T(8,128)(2,1)S(1)}, bf16[64,640]{1,0:T(8,128)(2,1)S(1)}, u32[]{:S(2)}, u32[]{:S(2)}) collective-permute-start(bf16[64,640]{1,0:T(8,128)(2,1)S(1)} %get-tuple-element.15), channel_id=1, source_target_pairs={{2,0},{4,2},{6,4},{8,6},{10,8},{12,10},{14,12},{16,14},{18,16},{20... | collective-permute-start | bytes 245768 | tf_op jit(solution)/shard_map/ppermute | solution.py:324
  6.8 0.8 %slice_bitcast_fusion.4 = (bf16[32,16,3,3]{0,1,3,2:T(8,128)(2,1)S(1)}, bf16[3,32,3,16]{1,3,2,0:T(8,128)(2,1)S(1)}) fusion(bf16[32,16,3,3,3]{0,1,4,3,2:T(8,128)(2,1)} %param.6), kind=kLoop, calls=%fused_computation.13 | loop fusion | bytes 27648 | tf_op jit(solution)/shard_map/squeeze | solution.py:312
  7.5 0.0 copy-done.2
  7.6 0.1 fusion
  7.7 0.1 maximum_bitcast_fusion
  7.8 0.0 collective-permute-done.up_ref
  7.9 2.9 %collective-permute-done.1.down_ref = bf16[64,640]{1,0:T(8,128)(2,1)S(1)} collective-permute-done((bf16[64,640]{1,0:T(8,128)(2,1)S(1)}, bf16[64,640]{1,0:T(8,128)(2,1)S(1)}, u32[]{:S(2)}, u32[]{:S(2)}) %collective-permute-start.1) | collective-permute-done | bytes 81952 | tf_op jit(solution)/shard_map/ppermute | solution.py:324
  10.8 1.5 %collective-permute-start.2 = (bf16[64,128]{1,0:T(8,128)(2,1)S(1)}, bf16[64,128]{1,0:T(8,128)(2,1)S(1)}, u32[]{:S(2)}, u32[]{:S(2)}) collective-permute-start(bf16[64,128]{1,0:T(8,128)(2,1)S(1)} %slice_add_fusion), channel_id=1, source_target_pairs={{0,1},{1,0},{2,3},{3,2},{4,5},{5,4},{6,7},{7,6},{8,9},{9,8},{10,11... | collective-permute-start | bytes 49160 | tf_op jit(solution)/shard_map/ppermute | solution.py:327
  12.3 0.1 reshape.50.wq_ref
  12.4 0.1 reshape.49
  12.5 0.1 copy.21.wc_ref
  12.7 0.1 reshape.48
  12.8 0.1 copy.20.wg_ref
  13.0 0.1 reshape.47.wo_ref
  13.1 1.4 %collective-permute-done.2.left_ref.right_ref = bf16[64,128]{1,0:T(8,128)(2,1)S(1)} collective-permute-done((bf16[64,128]{1,0:T(8,128)(2,1)S(1)}, bf16[64,128]{1,0:T(8,128)(2,1)S(1)}, u32[]{:S(2)}, u32[]{:S(2)}) %collective-permute-start.2) | collective-permute-done | bytes 16416 | tf_op jit(solution)/shard_map/ppermute | solution.py:327
  14.5 3.9 %block.1 = (bf16[512,128]{1,0:T(8,128)(2,1)}, bf16[512,128]{1,0:T(8,128)(2,1)}, f32[256,128]{1,0:T(8,128)S(1)}) custom-call(bf16[64,2048]{1,0:T(8,128)(2,1)S(1)} %get-tuple-element.13.s_ref, bf16[64,640]{1,0:T(8,128)(2,1)S(1)} %collective-permute-done.up_ref, bf16[64,640]{1,0:T(8,128)(2,1)S(1)} %collective-permute-done.1.down_ref, ...), custom_call_target="tpu_custom_call" | custom-call | flops 1000000000 | bytes 4000000 | tf_op jit(solution)/shard_map/block/pallas_call | solution.py:247
  18.4 15.7 %all_to_all.10 = f32[32,8,128]{2,1,0:T(8,128)S(1)} all-to-all(f32[32,8,128]{2,1,0:T(8,128)S(1)} %bitcast.48), channel_id=1, replica_groups=mesh['wide'=16,'narrow'=2] {'wide','narrow'}, dimensions={0} | all-to-all | bytes 262144 | tf_op jit(solution)/shard_map/all_to_all | solution.py:338
  34.2 10.3 %all_to_all.11 = f32[32,8,128]{2,1,0:T(8,128)S(1)} all-to-all(f32[32,8,128]{2,1,0:T(8,128)S(1)} %broadcast_in_dim.2), channel_id=1, replica_groups=mesh['wide'=16,'narrow'=2] {'wide','narrow'}, dimensions={0} | all-to-all | bytes 262144 | tf_op jit(solution)/shard_map/all_to_all | solution.py:340
  44.5 0.9 %spread.1 = (f32[432,48]{1,0:T(8,128)}, f32[432,32]{1,0:T(8,128)}) custom-call(f32[256,128]{1,0:T(8,128)S(1)} %bitcast.45), custom_call_target="tpu_custom_call" | custom-call | tf_op jit(solution)/shard_map/spread/pallas_call | solution.py:291
  (13 shorter events, 0.2 us)
Async XLA Ops:
  0.6 0.9 %copy-start = (bf16[16,16,2,128]{3,2,1,0:T(2,128)(2,1)S(1)}, bf16[16,16,2,128]{3,2,1,0:T(2,128)(2,1)}, u32[]{:S(2)}) copy-start(bf16[16,16,2,128]{3,2,1,0:T(2,128)(2,1)} %param.4) | copy-start | bytes 393220
  1.5 0.9 %copy-start.1 = (bf16[16,16,2,128]{3,2,1,0:T(2,128)(2,1)S(1)}, bf16[16,16,2,128]{3,2,1,0:T(2,128)(2,1)}, u32[]{:S(2)}) copy-start(bf16[16,16,2,128]{3,2,1,0:T(2,128)(2,1)} %param.5) | copy-start | bytes 393220
  3.0 4.6 %copy-start.2 = (bf16[16,48,3,3,3]{1,0,4,3,2:T(8,128)(2,1)S(1)}, bf16[16,48,3,3,3]{1,0,4,3,2:T(8,128)(2,1)}, u32[]{:S(2)}) copy-start(bf16[16,48,3,3,3]{1,0,4,3,2:T(8,128)(2,1)} %param.7) | copy-start | bytes 124420
  3.0 4.9 %collective-permute-start = (bf16[64,640]{1,0:T(8,128)(2,1)S(1)}, bf16[64,640]{1,0:T(8,128)(2,1)S(1)}, u32[]{:S(2)}, u32[]{:S(2)}) collective-permute-start(bf16[64,640]{1,0:T(8,128)(2,1)S(1)} %get-tuple-element.14), channel_id=1, source_target_pairs={{0,2},{2,4},{4,6},{6,8},{8,10},{10,12},{12,14},{14,16},{16,18},{18... | collective-permute-start | bytes 245768 | tf_op jit(solution)/shard_map/ppermute | solution.py:323
  5.5 5.3 %collective-permute-start.1 = (bf16[64,640]{1,0:T(8,128)(2,1)S(1)}, bf16[64,640]{1,0:T(8,128)(2,1)S(1)}, u32[]{:S(2)}, u32[]{:S(2)}) collective-permute-start(bf16[64,640]{1,0:T(8,128)(2,1)S(1)} %get-tuple-element.15), channel_id=1, source_target_pairs={{2,0},{4,2},{6,4},{8,6},{10,8},{12,10},{14,12},{16,14},{18,16},{20... | collective-permute-start | bytes 245768 | tf_op jit(solution)/shard_map/ppermute | solution.py:324
  10.8 3.7 %collective-permute-start.2 = (bf16[64,128]{1,0:T(8,128)(2,1)S(1)}, bf16[64,128]{1,0:T(8,128)(2,1)S(1)}, u32[]{:S(2)}, u32[]{:S(2)}) collective-permute-start(bf16[64,128]{1,0:T(8,128)(2,1)S(1)} %slice_add_fusion), channel_id=1, source_target_pairs={{0,1},{1,0},{2,3},{3,2},{4,5},{5,4},{6,7},{7,6},{8,9},{9,8},{10,11... | collective-permute-start | bytes 49160 | tf_op jit(solution)/shard_map/ppermute | solution.py:327

commit v2 on v1

--- a/solution.py
+++ b/solution.py
@@ -13,6 +13,7 @@
 HALO = 4
 EXT = ROWS + 2 * HALO
 BF, F32 = jnp.bfloat16, jnp.float32
+WIDE = ("far", "near")
 VMEM_LIMIT = 48 * 1024 * 1024
 
 
@@ -100,7 +101,7 @@
     ext_ref, side_ref, jst_ref, gst_ref, gsb_ref, pst_ref, psb_ref, qst_ref,
     pre_ref, prb_ref, ro_ref, rg_ref, rgb_ref, rq_ref, gp_ref, flat_ref, fa_ref, fb_ref, fc_ref,
 ):
-    w, n = lax.axis_index("wide"), lax.axis_index("narrow")
+    w, n = lax.axis_index(WIDE), lax.axis_index("narrow")
     lane32 = lanes_of((C2, COLS))
     lane64 = lanes_of((64, COLS))
     flag = lambda is_there: jnp.where(is_there, 1.0, 0.0)
@@ -315,13 +316,27 @@
     return wo, wg, wc, wq
 
 
+def summed(grads):
+    group, others = "far", ("near", "narrow")
+    count = lax.axis_size(group)
+    length = grads.shape[0]
+    share = -(-length // count)
+    grads = jnp.pad(grads, ((0, share * count - length), (0, 0))).reshape(count, share, COLS)
+    part = jnp.sum(lax.all_to_all(grads, group, 0, 0, tiled=True), 0)
+    copies = jnp.broadcast_to(part, (lax.axis_size(others),) + part.shape)
+    part = jnp.sum(lax.all_to_all(copies, others, 0, 0, tiled=True), 0)
+    copies = jnp.broadcast_to(part, (count,) + part.shape)
+    total = lax.all_to_all(copies, group, 0, 0, tiled=True)
+    return total.reshape(share * count, COLS)[:length]
+
+
 def shards(features, cotangent, coarse_weight, fine_weight):
-    wide, narrow = lax.axis_size("wide"), lax.axis_size("narrow")
+    wide, narrow = lax.axis_size(WIDE), lax.axis_size("narrow")
     matrices = weight_matrices(coarse_weight, fine_weight)
     sides = 1 if narrow == 2 else 2
     own, up, down, strip = pack(features, cotangent, sides)
-    above = lax.ppermute(up, "wide", [(i, i + 1) for i in range(wide - 1)])
-    below = lax.ppermute(down, "wide", [(i + 1, i) for i in range(wide - 1)])
+    above = lax.ppermute(up, WIDE, [(i, i + 1) for i in range(wide - 1)])
+    below = lax.ppermute(down, WIDE, [(i + 1, i) for i in range(wide - 1)])
     strip = strip + above[:, HALO * COLS :] + below[:, HALO * COLS :]
     if sides == 1:
         left = right = lax.ppermute(strip, "narrow", [(0, 1), (1, 0)])
@@ -331,14 +346,8 @@
     output, grad_features, grads = block(
         (wide, narrow), (own, above, below, left, right) + matrices
     )
+    total = summed(grads)
     devices = wide * narrow
-    share = -(-256 // devices)
-    grads = jnp.pad(grads, ((0, share * devices - 256), (0, 0))).reshape(devices, share, COLS)
-    both = ("wide", "narrow")
-    parts = lax.all_to_all(grads, both, 0, 0, tiled=True)
-    total = jnp.broadcast_to(jnp.sum(parts, 0, keepdims=True), parts.shape)
-    total = lax.all_to_all(total, both, 0, 0, tiled=True)
-    total = total.reshape(share * devices, COLS)[:256]
     all_cells = features.shape[1] * features.shape[2] * features.shape[3] * devices
     grad_fine, grad_coarse = spread(
         total, 1.0 / math.sqrt(all_cells), 1.0 / math.sqrt(all_cells // 8)
@@ -354,10 +363,12 @@
 
 
 def solution(mesh):
-    placed = P(None, "wide", None, "narrow")
+    wide, narrow = mesh.shape["wide"], mesh.shape["narrow"]
+    finer = jax.sharding.Mesh(mesh.devices.reshape(wide // 2, 2, narrow), WIDE + ("narrow",))
+    placed = P(None, WIDE, None, "narrow")
     return jax.shard_map(
         shards,
-        mesh=mesh,
+        mesh=finer,
         in_specs=(placed, placed, P(), P()),
         out_specs=(placed, placed, P(), P()),
         check_vma=False,

time: 45.7 us -> 50.9 us (1.11)
  blocking collectives: 26 us -> 31.1 us
    all_to_all x2 -> x3, blocking collectives: 26 us -> 31.1 us  [the longest x1 14.6 us: summed(): part = jnp.sum(lax.all_to_all(grads, group, 0, 0, tiled=True), 0)]
where the time goes in v2:
time: 50.9 us; the launch traced here: 50.5 us
  blocking collectives  31.1 us (61%)
  Pallas kernels  5.28 us (10%)
  starting transfers between devices  5.28 us (10%)
  waiting for transfers between devices  4.33 us (9%)
  local copies, waits for them, and re-layouts  3.41 us (7%)
  between operations  0.78 us (2%)
    all_to_all x1, blocking collectives, summed(): part = jnp.sum(lax.all_to_all(grads, group, 0, 0, tiled=True), 0)  14.6 us
    all_to_all x1, blocking collectives, summed(): total = lax.all_to_all(copies, group, 0, 0, tiled=True)  9.85 us
    all_to_all x1, blocking collectives, summed(): part = jnp.sum(lax.all_to_all(copies, others, 0, 0, tiled=True), 0)  6.68 us
    pallas_call x1, Pallas kernels, block(): pl.pallas_call(functools.partial(block_kernel, counts), out_shape=(jax.Sh...  3.91 us
    ppermute x1, waiting for transfers between devices, shards(): below = lax.ppermute(down, WIDE, [(i + 1, i) for i in range(wide - 1)])  2.9 us
    ppermute x1, starting transfers between devices, shards(): above = lax.ppermute(up, WIDE, [(i, i + 1) for i in range(wide - 1)])  2.49 us
    unnamed x6, local copies, waits for them, and re-layouts  1.8 us
    ppermute x1, starting transfers between devices, shards(): left = right = lax.ppermute(strip, 'narrow', [(0, 1), (1, 0)])  1.49 us
  transfers between devices with their start and end apart: 3, of which 2 were waited for; matrix products, arithmetic and copies ran while one was open for 4% of the time, Pallas kernels for 0%

profile of v2, /device:TPU:0, one launch (start us, length us, event | category | flops | bytes accessed | tf_op | source)
XLA Modules:
  0.0 50.5 jit_solution(16872537610272153354)
XLA Ops:
  0.6 0.9 %copy-done = bf16[16,16,2,128]{3,2,1,0:T(2,128)(2,1)S(1)} copy-done((bf16[16,16,2,128]{3,2,1,0:T(2,128)(2,1)S(1)}, bf16[16,16,2,128]{3,2,1,0:T(2,128)(2,1)}, u32[]{:S(2)}) %copy-start) | copy-done | bytes 131096
  1.5 0.9 %copy-done.1 = bf16[16,16,2,128]{3,2,1,0:T(2,128)(2,1)S(1)} copy-done((bf16[16,16,2,128]{3,2,1,0:T(2,128)(2,1)S(1)}, bf16[16,16,2,128]{3,2,1,0:T(2,128)(2,1)}, u32[]{:S(2)}) %copy-start.1) | copy-done | bytes 131096
  2.4 0.5 %pack.1 = (bf16[64,2048]{1,0:T(8,128)(2,1)S(1)}, bf16[64,640]{1,0:T(8,128)(2,1)S(1)}, bf16[64,640]{1,0:T(8,128)(2,1)S(1)}, bf16[64,128]{1,0:T(8,128)(2,1)S(1)}) custom-call(bf16[512,128]{1,0:T(8,128)(2,1)S(1)} %bitcast.46, bf16[512,128]{1,0:T(8,128)(2,1)S(1)} %bitcast.47), custom_call_target="tpu_custom_call" | custom-call | flops 1000000 | bytes 1000000 | tf_op jit(solution)/shard_map/pack/pallas_call | solution.py:61
  3.0 2.5 %collective-permute-start = (bf16[64,640]{1,0:T(8,128)(2,1)S(1)}, bf16[64,640]{1,0:T(8,128)(2,1)S(1)}, u32[]{:S(2)}, u32[]{:S(2)}) collective-permute-start(bf16[64,640]{1,0:T(8,128)(2,1)S(1)} %get-tuple-element.14), channel_id=1, source_target_pairs={{0,2},{2,4},{4,6},{6,8},{8,10},{10,12},{12,14},{14,16},{16,18},{18... | collective-permute-start | bytes 245768 | tf_op jit(solution)/shard_map/ppermute | solution.py:338
  5.5 1.3 %collective-permute-start.1 = (bf16[64,640]{1,0:T(8,128)(2,1)S(1)}, bf16[64,640]{1,0:T(8,128)(2,1)S(1)}, u32[]{:S(2)}, u32[]{:S(2)}) collective-permute-start(bf16[64,640]{1,0:T(8,128)(2,1)S(1)} %get-tuple-element.15), channel_id=1, source_target_pairs={{2,0},{4,2},{6,4},{8,6},{10,8},{12,10},{14,12},{16,14},{18,16},{20... | collective-permute-start | bytes 245768 | tf_op jit(solution)/shard_map/ppermute | solution.py:339
  6.8 0.8 %slice_bitcast_fusion.4 = (bf16[32,16,3,3]{0,1,3,2:T(8,128)(2,1)S(1)}, bf16[3,32,3,16]{1,3,2,0:T(8,128)(2,1)S(1)}) fusion(bf16[32,16,3,3,3]{0,1,4,3,2:T(8,128)(2,1)} %param.6), kind=kLoop, calls=%fused_computation.13 | loop fusion | bytes 27648 | tf_op jit(solution)/shard_map/squeeze | solution.py:313
  7.5 0.0 copy-done.2
  7.6 0.1 fusion
  7.7 0.1 maximum_bitcast_fusion
  7.8 0.0 collective-permute-done.up_ref
  7.9 2.9 %collective-permute-done.1.down_ref = bf16[64,640]{1,0:T(8,128)(2,1)S(1)} collective-permute-done((bf16[64,640]{1,0:T(8,128)(2,1)S(1)}, bf16[64,640]{1,0:T(8,128)(2,1)S(1)}, u32[]{:S(2)}, u32[]{:S(2)}) %collective-permute-start.1) | collective-permute-done | bytes 81952 | tf_op jit(solution)/shard_map/ppermute | solution.py:339
  10.8 1.5 %collective-permute-start.2 = (bf16[64,128]{1,0:T(8,128)(2,1)S(1)}, bf16[64,128]{1,0:T(8,128)(2,1)S(1)}, u32[]{:S(2)}, u32[]{:S(2)}) collective-permute-start(bf16[64,128]{1,0:T(8,128)(2,1)S(1)} %slice_add_fusion), channel_id=1, source_target_pairs={{0,1},{1,0},{2,3},{3,2},{4,5},{5,4},{6,7},{7,6},{8,9},{9,8},{10,11... | collective-permute-start | bytes 49160 | tf_op jit(solution)/shard_map/ppermute | solution.py:342
  12.3 0.1 reshape.49.wq_ref
  12.4 0.1 reshape.48
  12.5 0.1 copy.29.wc_ref
  12.7 0.1 reshape.47
  12.8 0.1 copy.28.wg_ref
  13.0 0.1 reshape.46.wo_ref
  13.1 1.4 %collective-permute-done.2.left_ref.right_ref = bf16[64,128]{1,0:T(8,128)(2,1)S(1)} collective-permute-done((bf16[64,128]{1,0:T(8,128)(2,1)S(1)}, bf16[64,128]{1,0:T(8,128)(2,1)S(1)}, u32[]{:S(2)}, u32[]{:S(2)}) %collective-permute-start.2) | collective-permute-done | bytes 16416 | tf_op jit(solution)/shard_map/ppermute | solution.py:342
  14.5 3.9 %block.1 = (bf16[512,128]{1,0:T(8,128)(2,1)}, bf16[512,128]{1,0:T(8,128)(2,1)}, f32[256,128]{1,0:T(8,128)S(1)}) custom-call(bf16[64,2048]{1,0:T(8,128)(2,1)S(1)} %get-tuple-element.13.s_ref, bf16[64,640]{1,0:T(8,128)(2,1)S(1)} %collective-permute-done.up_ref, bf16[64,640]{1,0:T(8,128)(2,1)S(1)} %collective-permute-done.1.down_ref, ...), custom_call_target="tpu_custom_call" | custom-call | flops 1000000000 | bytes 4000000 | tf_op jit(solution)/shard_map/block/pallas_call | solution.py:248
  18.4 14.6 %all_to_all.15 = f32[8,32,128]{2,1,0:T(8,128)S(1)} all-to-all(f32[8,32,128]{2,1,0:T(8,128)S(1)} %bitcast.48), channel_id=1, replica_groups=mesh['far'=8,'near'=2,'narrow'=2] {'far'}, dimensions={0} | all-to-all | bytes 262144 | tf_op jit(solution)/shard_map/all_to_all | solution.py:325
  33.0 6.7 %all_to_all.16 = f32[4,32,128]{2,1,0:T(8,128)S(1)} all-to-all(f32[4,32,128]{2,1,0:T(8,128)S(1)} %broadcast_in_dim.6), channel_id=1, replica_groups=mesh['far'=8,'near'=2,'narrow'=2] {'near','narrow'}, dimensions={0} | all-to-all | bytes 131072 | tf_op jit(solution)/shard_map/all_to_all | solution.py:327
  39.8 9.9 %all_to_all.17 = f32[8,32,128]{2,1,0:T(8,128)S(1)} all-to-all(f32[8,32,128]{2,1,0:T(8,128)S(1)} %broadcast_in_dim.7), channel_id=1, replica_groups=mesh['far'=8,'near'=2,'narrow'=2] {'far'}, dimensions={0} | all-to-all | bytes 262144 | tf_op jit(solution)/shard_map/all_to_all | solution.py:329
  49.6 0.9 %spread.1 = (f32[432,48]{1,0:T(8,128)}, f32[432,32]{1,0:T(8,128)}) custom-call(f32[256,128]{1,0:T(8,128)S(1)} %bitcast.45), custom_call_target="tpu_custom_call" | custom-call | tf_op jit(solution)/shard_map/spread/pallas_call | solution.py:292
  (16 shorter events, 0.2 us)
Async XLA Ops:
  0.6 0.9 %copy-start = (bf16[16,16,2,128]{3,2,1,0:T(2,128)(2,1)S(1)}, bf16[16,16,2,128]{3,2,1,0:T(2,128)(2,1)}, u32[]{:S(2)}) copy-start(bf16[16,16,2,128]{3,2,1,0:T(2,128)(2,1)} %param.4) | copy-start | bytes 393220
  1.5 0.9 %copy-start.1 = (bf16[16,16,2,128]{3,2,1,0:T(2,128)(2,1)S(1)}, bf16[16,16,2,128]{3,2,1,0:T(2,128)(2,1)}, u32[]{:S(2)}) copy-start(bf16[16,16,2,128]{3,2,1,0:T(2,128)(2,1)} %param.5) | copy-start | bytes 393220
  3.0 4.6 %copy-start.2 = (bf16[16,48,3,3,3]{1,0,4,3,2:T(8,128)(2,1)S(1)}, bf16[16,48,3,3,3]{1,0,4,3,2:T(8,128)(2,1)}, u32[]{:S(2)}) copy-start(bf16[16,48,3,3,3]{1,0,4,3,2:T(8,128)(2,1)} %param.7) | copy-start | bytes 124420
  3.0 4.9 %collective-permute-start = (bf16[64,640]{1,0:T(8,128)(2,1)S(1)}, bf16[64,640]{1,0:T(8,128)(2,1)S(1)}, u32[]{:S(2)}, u32[]{:S(2)}) collective-permute-start(bf16[64,640]{1,0:T(8,128)(2,1)S(1)} %get-tuple-element.14), channel_id=1, source_target_pairs={{0,2},{2,4},{4,6},{6,8},{8,10},{10,12},{12,14},{14,16},{16,18},{18... | collective-permute-start | bytes 245768 | tf_op jit(solution)/shard_map/ppermute | solution.py:338
  5.5 5.3 %collective-permute-start.1 = (bf16[64,640]{1,0:T(8,128)(2,1)S(1)}, bf16[64,640]{1,0:T(8,128)(2,1)S(1)}, u32[]{:S(2)}, u32[]{:S(2)}) collective-permute-start(bf16[64,640]{1,0:T(8,128)(2,1)S(1)} %get-tuple-element.15), channel_id=1, source_target_pairs={{2,0},{4,2},{6,4},{8,6},{10,8},{12,10},{14,12},{16,14},{18,16},{20... | collective-permute-start | bytes 245768 | tf_op jit(solution)/shard_map/ppermute | solution.py:339
  10.8 3.7 %collective-permute-start.2 = (bf16[64,128]{1,0:T(8,128)(2,1)S(1)}, bf16[64,128]{1,0:T(8,128)(2,1)S(1)}, u32[]{:S(2)}, u32[]{:S(2)}) collective-permute-start(bf16[64,128]{1,0:T(8,128)(2,1)S(1)} %slice_add_fusion), channel_id=1, source_target_pairs={{0,1},{1,0},{2,3},{3,2},{4,5},{5,4},{6,7},{7,6},{8,9},{9,8},{10,11... | collective-permute-start | bytes 49160 | tf_op jit(solution)/shard_map/ppermute | solution.py:342

commit v3 on v1

--- a/solution.py
+++ b/solution.py
@@ -24,10 +24,18 @@
     return slice(index * COLS, (index + count) * COLS)
 
 
-def pack_kernel(sides, f_ref, g_ref, s_ref, up_ref, down_ref, strip_ref, wide_ref):
+def pack_kernel(sides, f_hbm, g_hbm, s_ref, even_ref, odd_ref, strip_ref, f_ref, g_ref, wide_ref, sems):
+    copies = [
+        pltpu.make_async_copy(hbm, ref, sems.at[a])
+        for a, (hbm, ref) in enumerate(((f_hbm, f_ref), (g_hbm, g_ref)))
+    ]
+    for copy in copies:
+        copy.start()
     lane = lanes_of((C1, COLS))
     place = lax.axis_index("narrow")
+    odd = lax.axis_index("wide") % 2
     for a, ref in enumerate((f_ref, g_ref)):
+        copies[a].wait()
         wide_ref[...] = ref[...].astype(F32)
         for z in range(2):
             chans = slice(a * 32 + z * 16, a * 32 + z * 16 + 16)
@@ -46,12 +54,12 @@
             for side in range(sides):
                 strip_ref[chans, row(side)] = strips[side].astype(BF)
                 turned = pltpu.roll(strips[side], 64, 1)
-                up_ref[chans, row(HALO + side)] = jnp.where(lane < 16, turned, 0.0).astype(BF)
-                down_ref[chans, row(HALO + side)] = jnp.where(
-                    (lane >= 80) & (lane < 96), turned, 0.0
-                ).astype(BF)
-    up_ref[:, row(0, HALO)] = s_ref[:, row(ROWS - HALO, HALO)]
-    down_ref[:, row(0, HALO)] = s_ref[:, row(0, HALO)]
+                for ref, first in ((even_ref, 80 * odd), (odd_ref, 80 - 80 * odd)):
+                    kept = (lane >= first) & (lane < first + 4 * HALO)
+                    ref[chans, row(HALO + side)] = jnp.where(kept, turned, 0.0).astype(BF)
+    last = (ROWS - HALO) * COLS
+    for ref, first in ((even_ref, last - last * odd), (odd_ref, last * odd)):
+        ref[:, row(0, HALO)] = s_ref[:, pl.ds(pl.multiple_of(first, COLS), HALO * COLS)]
 
 
 def pack(features, cotangent, sides):
@@ -65,7 +73,13 @@
             message,
             jax.ShapeDtypeStruct((64, sides * COLS), BF),
         ),
-        scratch_shapes=[pltpu.VMEM((C1 * ROWS * 2, COLS), F32)],
+        in_specs=[pl.BlockSpec(memory_space=pltpu.HBM)] * 2,
+        scratch_shapes=[
+            pltpu.VMEM((C1 * ROWS * 2, COLS), BF),
+            pltpu.VMEM((C1 * ROWS * 2, COLS), BF),
+            pltpu.VMEM((C1 * ROWS * 2, COLS), F32),
+            pltpu.SemaphoreType.DMA((2,)),
+        ],
         compiler_params=pltpu.CompilerParams(vmem_limit_bytes=VMEM_LIMIT),
         cost_estimate=pl.CostEstimate(flops=10**6, bytes_accessed=10**6, transcendentals=0),
         name="pack",
@@ -95,7 +109,7 @@
 
 def block_kernel(
     counts,
-    s_ref, up_ref, down_ref, left_ref, right_ref, wo_ref, wg_ref, wc_ref, wq_ref,
+    s_ref, even_ref, odd_ref, left_ref, right_ref, wo_ref, wg_ref, wc_ref, wq_ref,
     out_ref, gf_ref, gw_ref,
     ext_ref, side_ref, jst_ref, gst_ref, gsb_ref, pst_ref, psb_ref, qst_ref,
     pre_ref, prb_ref, ro_ref, rg_ref, rgb_ref, rq_ref, gp_ref, flat_ref, fa_ref, fb_ref, fc_ref,
@@ -107,9 +121,11 @@
     has_left, has_right = flag(n > 0), flag(n < counts[1] - 1)
     has_above, has_below = flag(w > 0), flag(w < counts[0] - 1)
 
-    ext_ref[:, row(0, HALO)] = up_ref[:, row(0, HALO)]
+    odd = w % 2
+    below = (HALO + ROWS) * COLS
     ext_ref[:, row(HALO, ROWS)] = s_ref[...]
-    ext_ref[:, row(HALO + ROWS, HALO)] = down_ref[:, row(0, HALO)]
+    for ref, first in ((even_ref, below - below * odd), (odd_ref, below * odd)):
+        ext_ref[:, pl.ds(pl.multiple_of(first, COLS), HALO * COLS)] = ref[:, row(0, HALO)]
 
     left = left_ref[...].astype(F32) * has_left
     right = right_ref[...].astype(F32) * has_right
@@ -319,17 +335,20 @@
     wide, narrow = lax.axis_size("wide"), lax.axis_size("narrow")
     matrices = weight_matrices(coarse_weight, fine_weight)
     sides = 1 if narrow == 2 else 2
-    own, up, down, strip = pack(features, cotangent, sides)
-    above = lax.ppermute(up, "wide", [(i, i + 1) for i in range(wide - 1)])
-    below = lax.ppermute(down, "wide", [(i + 1, i) for i in range(wide - 1)])
-    strip = strip + above[:, HALO * COLS :] + below[:, HALO * COLS :]
+    own, to_even, to_odd, strip = pack(features, cotangent, sides)
+    swaps = lambda start: [
+        pair for i in range(start, wide - 1, 2) for pair in ((i, i + 1), (i + 1, i))
+    ]
+    even = lax.ppermute(to_even, "wide", swaps(0))
+    odd = lax.ppermute(to_odd, "wide", swaps(1))
+    strip = strip + even[:, HALO * COLS :] + odd[:, HALO * COLS :]
     if sides == 1:
         left = right = lax.ppermute(strip, "narrow", [(0, 1), (1, 0)])
     else:
         right = lax.ppermute(strip[:, :COLS], "narrow", [(i + 1, i) for i in range(narrow - 1)])
         left = lax.ppermute(strip[:, COLS:], "narrow", [(i, i + 1) for i in range(narrow - 1)])
     output, grad_features, grads = block(
-        (wide, narrow), (own, above, below, left, right) + matrices
+        (wide, narrow), (own, even, odd, left, right) + matrices
     )
     devices = wide * narrow
     share = -(-256 // devices)

time: 45.7 us -> 44.2 us (0.967)
  waiting for transfers between devices: 4.33 us -> 0.9 us
  blocking collectives: 26 us -> 29.1 us
  starting transfers between devices: 5.28 us -> 3.75 us
    all_to_all x1, blocking collectives: 15.7 us -> 18.8 us  [shards(): parts = lax.all_to_all(grads, both, 0, 0, tiled=True)]
    ppermute x2, waiting for transfers between devices: 2.91 us -> 0.01 us  [the longest x1 0.01 us: shards(): even = lax.ppermute(to_even, 'wide', swaps(0))]
    ppermute x2, starting transfers between devices: 3.78 us -> 1.17 us  [the longest x1 0.65 us: shards(): odd = lax.ppermute(to_odd, 'wide', swaps(1))]
    ppermute x1, starting transfers between devices: 1.49 us -> 2.58 us  [shards(): left = right = lax.ppermute(strip, 'narrow', [(0, 1), (1, 0)])]
    ppermute x1, waiting for transfers between devices: 1.43 us -> 0.9 us  [shards(): left = right = lax.ppermute(strip, 'narrow', [(0, 1), (1, 0)])]
    pallas_call x1, Pallas kernels: 0.51 us -> 0.98 us  [pack(): pl.pallas_call(functools.partial(pack_kernel, sides), out_shape=(jax.Shap...]
  transfers between devices with their start and end apart: 3 -> 3, of which waited for: 2 -> 1; matrix products, arithmetic and copies ran while one was open for 4% -> 4% of each run, Pallas kernels for 0% -> 0%
where the time goes in v3:
time: 44.2 us; the launch traced here: 44 us
  blocking collectives  29.1 us (66%)
  Pallas kernels  5.72 us (13%)
  starting transfers between devices  3.75 us (8%)
  local copies, waits for them, and re-layouts  3.41 us (8%)
  waiting for transfers between devices  0.9 us (2%)
  between operations  0.78 us (2%)
    all_to_all x1, blocking collectives, shards(): parts = lax.all_to_all(grads, both, 0, 0, tiled=True)  18.8 us
    all_to_all x1, blocking collectives, shards(): total = lax.all_to_all(total, both, 0, 0, tiled=True)  10.3 us
    pallas_call x1, Pallas kernels, block(): pl.pallas_call(functools.partial(block_kernel, counts), out_shape=(jax.Sh...  3.88 us
    ppermute x1, starting transfers between devices, shards(): left = right = lax.ppermute(strip, 'narrow', [(0, 1), (1, 0)])  2.58 us
    unnamed x6, local copies, waits for them, and re-layouts  1.81 us
    pallas_call x1, Pallas kernels, pack(): pl.pallas_call(functools.partial(pack_kernel, sides), out_shape=(jax.Shap...  0.98 us
    ppermute x1, waiting for transfers between devices, shards(): left = right = lax.ppermute(strip, 'narrow', [(0, 1), (1, 0)])  0.9 us
  transfers between devices with their start and end apart: 3, of which 1 were waited for; matrix products, arithmetic and copies ran while one was open for 4% of the time, Pallas kernels for 0%

profile of v3, /device:TPU:0, one launch (start us, length us, event | category | flops | bytes accessed | tf_op | source)
XLA Modules:
  0.0 44.0 jit_solution(14423934365360132914)
XLA Ops:
  0.6 0.0 copy-start
  0.6 0.9 %copy-done = bf16[16,16,2,128]{3,2,1,0:T(2,128)(2,1)S(1)} copy-done((bf16[16,16,2,128]{3,2,1,0:T(2,128)(2,1)S(1)}, bf16[16,16,2,128]{3,2,1,0:T(2,128)(2,1)}, u32[]{:S(2)}) %copy-start) | copy-done | bytes 131096
  1.5 0.9 %copy-done.1 = bf16[16,16,2,128]{3,2,1,0:T(2,128)(2,1)S(1)} copy-done((bf16[16,16,2,128]{3,2,1,0:T(2,128)(2,1)S(1)}, bf16[16,16,2,128]{3,2,1,0:T(2,128)(2,1)}, u32[]{:S(2)}) %copy-start.1) | copy-done | bytes 131096
  2.4 1.0 %pack.1 = (bf16[64,2048]{1,0:T(8,128)(2,1)S(1)}, bf16[64,640]{1,0:T(8,128)(2,1)S(1)}, bf16[64,640]{1,0:T(8,128)(2,1)S(1)}, bf16[64,128]{1,0:T(8,128)(2,1)S(1)}) custom-call(bf16[512,128]{1,0:T(8,128)(2,1)S(1)} %bitcast.46, bf16[512,128]{1,0:T(8,128)(2,1)S(1)} %bitcast.47), custom_call_target="tpu_custom_call" | custom-call | flops 1000000 | bytes 1000000 | tf_op jit(solution)/shard_map/pack/pallas_call | solution.py:68
  3.4 0.0 copy-start.2
  3.4 0.5 %collective-permute-start = (bf16[64,640]{1,0:T(8,128)(2,1)S(1)}, bf16[64,640]{1,0:T(8,128)(2,1)S(1)}, u32[]{:S(2)}, u32[]{:S(2)}) collective-permute-start(bf16[64,640]{1,0:T(8,128)(2,1)S(1)} %get-tuple-element.14), channel_id=1, source_target_pairs={{0,2},{2,0},{4,6},{6,4},{8,10},{10,8},{12,14},{14,12},{16,18},{18,... | collective-permute-start | bytes 245768 | tf_op jit(solution)/shard_map/ppermute | solution.py:342
  4.0 0.7 %collective-permute-start.1 = (bf16[64,640]{1,0:T(8,128)(2,1)S(1)}, bf16[64,640]{1,0:T(8,128)(2,1)S(1)}, u32[]{:S(2)}, u32[]{:S(2)}) collective-permute-start(bf16[64,640]{1,0:T(8,128)(2,1)S(1)} %get-tuple-element.15), channel_id=1, source_target_pairs={{2,4},{4,2},{6,8},{8,6},{10,12},{12,10},{14,16},{16,14},{18,20},{2... | collective-permute-start | bytes 245768 | tf_op jit(solution)/shard_map/ppermute | solution.py:343
  4.6 0.8 %slice_bitcast_fusion.4 = (bf16[32,16,3,3]{0,1,3,2:T(8,128)(2,1)S(1)}, bf16[3,32,3,16]{1,3,2,0:T(8,128)(2,1)S(1)}) fusion(bf16[32,16,3,3,3]{0,1,4,3,2:T(8,128)(2,1)} %param.6), kind=kLoop, calls=%fused_computation.13 | loop fusion | bytes 27648 | tf_op jit(solution)/shard_map/squeeze | solution.py:328
  5.4 0.1 fusion
  5.5 0.1 maximum_bitcast_fusion
  5.7 0.0 collective-permute-done.even_ref
  5.7 0.0 collective-permute-done.1.odd_ref
  5.7 2.6 %collective-permute-start.2 = (bf16[64,128]{1,0:T(8,128)(2,1)S(1)}, bf16[64,128]{1,0:T(8,128)(2,1)S(1)}, u32[]{:S(2)}, u32[]{:S(2)}) collective-permute-start(bf16[64,128]{1,0:T(8,128)(2,1)S(1)} %slice_add_fusion), channel_id=1, source_target_pairs={{0,1},{1,0},{2,3},{3,2},{4,5},{5,4},{6,7},{7,6},{8,9},{9,8},{10,11... | collective-permute-start | bytes 49160 | tf_op jit(solution)/shard_map/ppermute | solution.py:346
  8.3 0.1 reshape.50.wq_ref
  8.5 0.1 reshape.49
  8.6 0.1 copy.21.wc_ref
  8.7 0.1 reshape.48
  8.9 0.1 copy.20.wg_ref
  9.0 0.1 reshape.47.wo_ref
  9.1 0.9 %collective-permute-done.2.left_ref.right_ref = bf16[64,128]{1,0:T(8,128)(2,1)S(1)} collective-permute-done((bf16[64,128]{1,0:T(8,128)(2,1)S(1)}, bf16[64,128]{1,0:T(8,128)(2,1)S(1)}, u32[]{:S(2)}, u32[]{:S(2)}) %collective-permute-start.2) | collective-permute-done | bytes 16416 | tf_op jit(solution)/shard_map/ppermute | solution.py:346
  10.0 3.9 %block.1 = (bf16[512,128]{1,0:T(8,128)(2,1)}, bf16[512,128]{1,0:T(8,128)(2,1)}, f32[256,128]{1,0:T(8,128)S(1)}) custom-call(bf16[64,2048]{1,0:T(8,128)(2,1)S(1)} %get-tuple-element.13.s_ref, bf16[64,640]{1,0:T(8,128)(2,1)S(1)} %collective-permute-done.even_ref, bf16[64,640]{1,0:T(8,128)(2,1)S(1)} %collective-permute-done.1.odd_ref, ...), custom_call_target="tpu_custom_call" | custom-call | flops 1000000000 | bytes 4000000 | tf_op jit(solution)/shard_map/block/pallas_call | solution.py:263
  13.9 18.8 %all_to_all.10 = f32[32,8,128]{2,1,0:T(8,128)S(1)} all-to-all(f32[32,8,128]{2,1,0:T(8,128)S(1)} %bitcast.48), channel_id=1, replica_groups=mesh['wide'=16,'narrow'=2] {'wide','narrow'}, dimensions={0} | all-to-all | bytes 262144 | tf_op jit(solution)/shard_map/all_to_all | solution.py:357
  32.8 10.3 %all_to_all.11 = f32[32,8,128]{2,1,0:T(8,128)S(1)} all-to-all(f32[32,8,128]{2,1,0:T(8,128)S(1)} %broadcast_in_dim.2), channel_id=1, replica_groups=mesh['wide'=16,'narrow'=2] {'wide','narrow'}, dimensions={0} | all-to-all | bytes 262144 | tf_op jit(solution)/shard_map/all_to_all | solution.py:359
  43.1 0.9 %spread.1 = (f32[432,48]{1,0:T(8,128)}, f32[432,32]{1,0:T(8,128)}) custom-call(f32[256,128]{1,0:T(8,128)S(1)} %bitcast.45), custom_call_target="tpu_custom_call" | custom-call | tf_op jit(solution)/shard_map/spread/pallas_call | solution.py:307
  (13 shorter events, 0.2 us)
Async XLA Ops:
  0.6 0.9 %copy-start = (bf16[16,16,2,128]{3,2,1,0:T(2,128)(2,1)S(1)}, bf16[16,16,2,128]{3,2,1,0:T(2,128)(2,1)}, u32[]{:S(2)}) copy-start(bf16[16,16,2,128]{3,2,1,0:T(2,128)(2,1)} %param.4) | copy-start | bytes 393220
  1.5 0.9 %copy-start.1 = (bf16[16,16,2,128]{3,2,1,0:T(2,128)(2,1)S(1)}, bf16[16,16,2,128]{3,2,1,0:T(2,128)(2,1)}, u32[]{:S(2)}) copy-start(bf16[16,16,2,128]{3,2,1,0:T(2,128)(2,1)} %param.5) | copy-start | bytes 393220
  3.4 2.0 %copy-start.2 = (bf16[16,48,3,3,3]{1,0,4,3,2:T(8,128)(2,1)S(1)}, bf16[16,48,3,3,3]{1,0,4,3,2:T(8,128)(2,1)}, u32[]{:S(2)}) copy-start(bf16[16,48,3,3,3]{1,0,4,3,2:T(8,128)(2,1)} %param.7) | copy-start | bytes 124420
  3.4 2.3 %collective-permute-start = (bf16[64,640]{1,0:T(8,128)(2,1)S(1)}, bf16[64,640]{1,0:T(8,128)(2,1)S(1)}, u32[]{:S(2)}, u32[]{:S(2)}) collective-permute-start(bf16[64,640]{1,0:T(8,128)(2,1)S(1)} %get-tuple-element.14), channel_id=1, source_target_pairs={{0,2},{2,0},{4,6},{6,4},{8,10},{10,8},{12,14},{14,12},{16,18},{18,... | collective-permute-start | bytes 245768 | tf_op jit(solution)/shard_map/ppermute | solution.py:342
  4.0 1.8 %collective-permute-start.1 = (bf16[64,640]{1,0:T(8,128)(2,1)S(1)}, bf16[64,640]{1,0:T(8,128)(2,1)S(1)}, u32[]{:S(2)}, u32[]{:S(2)}) collective-permute-start(bf16[64,640]{1,0:T(8,128)(2,1)S(1)} %get-tuple-element.15), channel_id=1, source_target_pairs={{2,4},{4,2},{6,8},{8,6},{10,12},{12,10},{14,16},{16,14},{18,20},{2... | collective-permute-start | bytes 245768 | tf_op jit(solution)/shard_map/ppermute | solution.py:343
  5.7 4.3 %collective-permute-start.2 = (bf16[64,128]{1,0:T(8,128)(2,1)S(1)}, bf16[64,128]{1,0:T(8,128)(2,1)S(1)}, u32[]{:S(2)}, u32[]{:S(2)}) collective-permute-start(bf16[64,128]{1,0:T(8,128)(2,1)S(1)} %slice_add_fusion), channel_id=1, source_target_pairs={{0,1},{1,0},{2,3},{3,2},{4,5},{5,4},{6,7},{7,6},{8,9},{9,8},{10,11... | collective-permute-start | bytes 49160 | tf_op jit(solution)/shard_map/ppermute | solution.py:346

commit v4 on v3

--- a/solution.py
+++ b/solution.py
@@ -24,19 +24,12 @@
     return slice(index * COLS, (index + count) * COLS)
 
 
-def pack_kernel(sides, f_hbm, g_hbm, s_ref, even_ref, odd_ref, strip_ref, f_ref, g_ref, wide_ref, sems):
-    copies = [
-        pltpu.make_async_copy(hbm, ref, sems.at[a])
-        for a, (hbm, ref) in enumerate(((f_hbm, f_ref), (g_hbm, g_ref)))
-    ]
-    for copy in copies:
-        copy.start()
+def pack_kernel(sides, in_ref, s_ref, even_ref, odd_ref, strip_ref, wide_ref):
     lane = lanes_of((C1, COLS))
     place = lax.axis_index("narrow")
     odd = lax.axis_index("wide") % 2
-    for a, ref in enumerate((f_ref, g_ref)):
-        copies[a].wait()
-        wide_ref[...] = ref[...].astype(F32)
+    for a in range(2):
+        wide_ref[...] = in_ref[a].astype(F32)
         for z in range(2):
             chans = slice(a * 32 + z * 16, a * 32 + z * 16 + 16)
             strips = [jnp.zeros((C1, COLS), F32) for _ in range(sides)]
@@ -73,17 +66,11 @@
             message,
             jax.ShapeDtypeStruct((64, sides * COLS), BF),
         ),
-        in_specs=[pl.BlockSpec(memory_space=pltpu.HBM)] * 2,
-        scratch_shapes=[
-            pltpu.VMEM((C1 * ROWS * 2, COLS), BF),
-            pltpu.VMEM((C1 * ROWS * 2, COLS), BF),
-            pltpu.VMEM((C1 * ROWS * 2, COLS), F32),
-            pltpu.SemaphoreType.DMA((2,)),
-        ],
+        scratch_shapes=[pltpu.VMEM((C1 * ROWS * 2, COLS), F32)],
         compiler_params=pltpu.CompilerParams(vmem_limit_bytes=VMEM_LIMIT),
         cost_estimate=pl.CostEstimate(flops=10**6, bytes_accessed=10**6, transcendentals=0),
         name="pack",
-    )(flat(features), flat(cotangent))
+    )(jnp.stack([flat(features), flat(cotangent)]))
 
 
 def turn(main, side, by):
@@ -254,7 +241,7 @@
             value = jnp.where((lane16 >= 48) & (lane16 < 96), fine[order[14 + i]], value)
         if i < 9:
             value = jnp.where(lane16 >= 96, coarse[i // 3, i % 3], value)
-        gw_ref[i * 16 : i * 16 + 16, :] = value
+        gw_ref[i * 16 : i * 16 + 16, :] = value.astype(BF)
 
 
 def block(counts, operands):
@@ -265,7 +252,7 @@
         out_shape=(
             jax.ShapeDtypeStruct(cells, BF),
             jax.ShapeDtypeStruct(cells, BF),
-            jax.ShapeDtypeStruct((256, COLS), F32),
+            jax.ShapeDtypeStruct((256, COLS), BF),
         ),
         scratch_shapes=[
             v(64, EXT, BF), v(64, EXT, BF),
@@ -287,17 +274,36 @@
     )(*operands)
 
 
+def add_kernel(parts_ref, copies_ref):
+    total = parts_ref[0].astype(F32)
+    for i in range(1, parts_ref.shape[0]):
+        total = total + parts_ref[i].astype(F32)
+    total = total.astype(BF)
+    for i in range(parts_ref.shape[0]):
+        copies_ref[i] = total
+
+
+def add_up(parts):
+    return pl.pallas_call(
+        add_kernel,
+        out_shape=jax.ShapeDtypeStruct(parts.shape, BF),
+        compiler_params=pltpu.CompilerParams(vmem_limit_bytes=VMEM_LIMIT),
+        name="add_up",
+    )(parts)
+
+
 def spread_kernel(fine_scale, coarse_scale, sum_ref, fine_ref, coarse_ref):
     for i in range(27):
         if i < 14:
-            value = sum_ref[i * 16 : i * 16 + 16, :]
+            value = sum_ref[i * 16 : i * 16 + 16, :].astype(F32)
         else:
-            value = pltpu.roll(sum_ref[(i - 14) * 16 : (i - 14) * 16 + 16, :], 80, 1)
+            at = (i - 14) * 16
+            value = pltpu.roll(sum_ref[at : at + 16, :].astype(F32), 80, 1)
         fine_ref[i * 16 : i * 16 + 16, :] = value[:, 0:48] * fine_scale
         ky, kz, kx = i // 9, i // 3 % 3, i % 3
         if kz == 1:
             at = (ky * 3 + kx) * 16
-            value = pltpu.roll(sum_ref[at : at + 16, :], 32, 1)[:, 0:32] * coarse_scale
+            value = pltpu.roll(sum_ref[at : at + 16, :].astype(F32), 32, 1)[:, 0:32] * coarse_scale
         else:
             value = jnp.zeros((16, 32), F32)
         coarse_ref[i * 16 : i * 16 + 16, :] = value
@@ -355,8 +361,7 @@
     grads = jnp.pad(grads, ((0, share * devices - 256), (0, 0))).reshape(devices, share, COLS)
     both = ("wide", "narrow")
     parts = lax.all_to_all(grads, both, 0, 0, tiled=True)
-    total = jnp.broadcast_to(jnp.sum(parts, 0, keepdims=True), parts.shape)
-    total = lax.all_to_all(total, both, 0, 0, tiled=True)
+    total = lax.all_to_all(add_up(parts), both, 0, 0, tiled=True)
     total = total.reshape(share * devices, COLS)[:256]
     all_cells = features.shape[1] * features.shape[2] * features.shape[3] * devices
     grad_fine, grad_coarse = spread(

time: 44.2 us -> 41.3 us (0.934)
  blocking collectives: 29.1 us -> 27 us
  local copies, waits for them, and re-layouts: 3.41 us -> 1.59 us
  other arithmetic: 0.28 us -> 1.24 us
    unnamed x6 -> x2, local copies, waits for them, and re-layouts: 1.81 us -> 0.01 us
    all_to_all x1, blocking collectives: 18.8 us -> 17.8 us  [shards(): parts = lax.all_to_all(grads, both, 0, 0, tiled=True)]
    all_to_all x1, blocking collectives: 10.3 us -> 9.3 us  [shards(): total = lax.all_to_all(add_up(parts), both, 0, 0, tiled=True)]
    another operation x0 -> x1, other arithmetic: none -> 0.99 us  [pack(): jnp.stack([flat(features), flat(cotangent)])]
    pallas_call x1, Pallas kernels: 0.98 us -> 0.48 us  [pack(): pl.pallas_call(functools.partial(pack_kernel, sides), out_shape=(jax.Shap...]
    pallas_call x1, Pallas kernels: 3.88 us -> 4.36 us  [block(): pl.pallas_call(functools.partial(block_kernel, counts), out_shape=(jax.Sh...]
where the time goes in v4:
time: 41.3 us; the launch traced here: 41 us
  blocking collectives  27 us (65%)
  Pallas kernels  5.73 us (14%)
  starting transfers between devices  3.75 us (9%)
  local copies, waits for them, and re-layouts  1.59 us (4%)
  other arithmetic  1.24 us (3%)
  waiting for transfers between devices  0.9 us (2%)
  between operations  0.75 us (2%)
    all_to_all x1, blocking collectives, shards(): parts = lax.all_to_all(grads, both, 0, 0, tiled=True)  17.8 us
    all_to_all x1, blocking collectives, shards(): total = lax.all_to_all(add_up(parts), both, 0, 0, tiled=True)  9.3 us
    pallas_call x1, Pallas kernels, block(): pl.pallas_call(functools.partial(block_kernel, counts), out_shape=(jax.Sh...  4.36 us
    ppermute x1, starting transfers between devices, shards(): left = right = lax.ppermute(strip, 'narrow', [(0, 1), (1, 0)])  2.58 us
    another operation x1, other arithmetic, pack(): jnp.stack([flat(features), flat(cotangent)])  0.99 us
    ppermute x1, waiting for transfers between devices, shards(): left = right = lax.ppermute(strip, 'narrow', [(0, 1), (1, 0)])  0.9 us
    pallas_call x1, Pallas kernels, spread(): pl.pallas_call(functools.partial(spread_kernel, fine_scale, coarse_scale)...  0.85 us
  transfers between devices with their start and end apart: 3, of which 1 were waited for; matrix products, arithmetic and copies ran while one was open for 4% of the time, Pallas kernels for 0%

profile of v4, /device:TPU:0, one launch (start us, length us, event | category | flops | bytes accessed | tf_op | source)
XLA Modules:
  0.0 41.0 jit_solution(7826161087365050263)
XLA Ops:
  0.6 1.0 %pad_maximum_fusion.in_ref = bf16[2,512,128]{2,1,0:T(8,128)(2,1)S(1)} fusion(bf16[1,512,128]{2,1,0:T(8,128)(2,1)} %bitcast.50, bf16[1,512,128]{2,1,0:T(8,128)(2,1)} %bitcast.51), kind=kLoop, calls=%fused_computation | loop fusion | flops 131072 | bytes 524288 | tf_op jit(solution)/shard_map/stack | solution.py:73
  1.6 0.5 %pack.1 = (bf16[64,2048]{1,0:T(8,128)(2,1)S(1)}, bf16[64,640]{1,0:T(8,128)(2,1)S(1)}, bf16[64,640]{1,0:T(8,128)(2,1)S(1)}, bf16[64,128]{1,0:T(8,128)(2,1)S(1)}) custom-call(bf16[2,512,128]{2,1,0:T(8,128)(2,1)S(1)} %pad_maximum_fusion.in_ref), custom_call_target="tpu_custom_call" | custom-call | flops 1000000 | bytes 1000000 | tf_op jit(solution)/shard_map/pack/pallas_call | solution.py:61
  2.1 0.0 copy-start
  2.1 0.5 %collective-permute-start = (bf16[64,640]{1,0:T(8,128)(2,1)S(1)}, bf16[64,640]{1,0:T(8,128)(2,1)S(1)}, u32[]{:S(2)}, u32[]{:S(2)}) collective-permute-start(bf16[64,640]{1,0:T(8,128)(2,1)S(1)} %get-tuple-element.14), channel_id=1, source_target_pairs={{0,2},{2,0},{4,6},{6,4},{8,10},{10,8},{12,14},{14,12},{16,18},{18,... | collective-permute-start | bytes 245768 | tf_op jit(solution)/shard_map/ppermute | solution.py:348
  2.6 0.7 %collective-permute-start.1 = (bf16[64,640]{1,0:T(8,128)(2,1)S(1)}, bf16[64,640]{1,0:T(8,128)(2,1)S(1)}, u32[]{:S(2)}, u32[]{:S(2)}) collective-permute-start(bf16[64,640]{1,0:T(8,128)(2,1)S(1)} %get-tuple-element.15), channel_id=1, source_target_pairs={{2,4},{4,2},{6,8},{8,6},{10,12},{12,10},{14,16},{16,14},{18,20},{2... | collective-permute-start | bytes 245768 | tf_op jit(solution)/shard_map/ppermute | solution.py:349
  3.3 0.8 %slice_bitcast_fusion.4 = (bf16[32,16,3,3]{0,1,3,2:T(8,128)(2,1)S(1)}, bf16[3,32,3,16]{1,3,2,0:T(8,128)(2,1)S(1)}) fusion(bf16[32,16,3,3,3]{0,1,4,3,2:T(8,128)(2,1)} %param.6), kind=kLoop, calls=%fused_computation.14 | loop fusion | bytes 27648 | tf_op jit(solution)/shard_map/squeeze | solution.py:334
  4.1 0.0 copy-done
  4.1 0.1 fusion
  4.2 0.1 maximum_bitcast_fusion
  4.4 0.0 collective-permute-done.even_ref
  4.4 0.0 collective-permute-done.1.odd_ref
  4.4 2.6 %collective-permute-start.2 = (bf16[64,128]{1,0:T(8,128)(2,1)S(1)}, bf16[64,128]{1,0:T(8,128)(2,1)S(1)}, u32[]{:S(2)}, u32[]{:S(2)}) collective-permute-start(bf16[64,128]{1,0:T(8,128)(2,1)S(1)} %slice_add_fusion), channel_id=1, source_target_pairs={{0,1},{1,0},{2,3},{3,2},{4,5},{5,4},{6,7},{7,6},{8,9},{9,8},{10,11... | collective-permute-start | bytes 49160 | tf_op jit(solution)/shard_map/ppermute | solution.py:352
  7.0 0.1 reshape.41.wq_ref
  7.1 0.1 reshape.40
  7.2 0.1 copy.21.wc_ref
  7.4 0.1 reshape.39
  7.5 0.1 copy.20.wg_ref
  7.7 0.1 reshape.38.wo_ref
  7.8 0.9 %collective-permute-done.2.left_ref.right_ref = bf16[64,128]{1,0:T(8,128)(2,1)S(1)} collective-permute-done((bf16[64,128]{1,0:T(8,128)(2,1)S(1)}, bf16[64,128]{1,0:T(8,128)(2,1)S(1)}, u32[]{:S(2)}, u32[]{:S(2)}) %collective-permute-start.2) | collective-permute-done | bytes 16416 | tf_op jit(solution)/shard_map/ppermute | solution.py:352
  8.7 4.4 %block.1 = (bf16[512,128]{1,0:T(8,128)(2,1)}, bf16[512,128]{1,0:T(8,128)(2,1)}, bf16[256,128]{1,0:T(8,128)(2,1)S(1)}) custom-call(bf16[64,2048]{1,0:T(8,128)(2,1)S(1)} %get-tuple-element.13.s_ref, bf16[64,640]{1,0:T(8,128)(2,1)S(1)} %collective-permute-done.even_ref, bf16[64,640]{1,0:T(8,128)(2,1)S(1)} %collective-permute-done.1.odd_ref, ...), custom_call_target="tpu_custom_call" | custom-call | flops 1000000000 | bytes 4000000 | tf_op jit(solution)/shard_map/block/pallas_call | solution.py:250
  13.1 17.8 %all_to_all.10.parts_ref = bf16[32,8,128]{2,1,0:T(8,128)(2,1)S(1)} all-to-all(bf16[32,8,128]{2,1,0:T(8,128)(2,1)S(1)} %bitcast.46), channel_id=1, replica_groups=mesh['wide'=16,'narrow'=2] {'wide','narrow'}, dimensions={0} | all-to-all | bytes 131072 | tf_op jit(solution)/shard_map/all_to_all | solution.py:363
  30.9 9.3 %all_to_all.11 = bf16[32,8,128]{2,1,0:T(8,128)(2,1)S(1)} all-to-all(bf16[32,8,128]{2,1,0:T(8,128)(2,1)S(1)} %add_up.1), channel_id=1, replica_groups=mesh['wide'=16,'narrow'=2] {'wide','narrow'}, dimensions={0} | all-to-all | bytes 131072 | tf_op jit(solution)/shard_map/all_to_all | solution.py:364
  40.2 0.9 %spread.1 = (f32[432,48]{1,0:T(8,128)}, f32[432,32]{1,0:T(8,128)}) custom-call(bf16[256,128]{1,0:T(8,128)(2,1)S(1)} %bitcast.45), custom_call_target="tpu_custom_call" | custom-call | tf_op jit(solution)/shard_map/spread/pallas_call | solution.py:313
  (10 shorter events, 0.2 us)
Async XLA Ops:
  2.1 2.0 %copy-start = (bf16[16,48,3,3,3]{1,0,4,3,2:T(8,128)(2,1)S(1)}, bf16[16,48,3,3,3]{1,0,4,3,2:T(8,128)(2,1)}, u32[]{:S(2)}) copy-start(bf16[16,48,3,3,3]{1,0,4,3,2:T(8,128)(2,1)} %param.7) | copy-start | bytes 124420
  2.1 2.3 %collective-permute-start = (bf16[64,640]{1,0:T(8,128)(2,1)S(1)}, bf16[64,640]{1,0:T(8,128)(2,1)S(1)}, u32[]{:S(2)}, u32[]{:S(2)}) collective-permute-start(bf16[64,640]{1,0:T(8,128)(2,1)S(1)} %get-tuple-element.14), channel_id=1, source_target_pairs={{0,2},{2,0},{4,6},{6,4},{8,10},{10,8},{12,14},{14,12},{16,18},{18,... | collective-permute-start | bytes 245768 | tf_op jit(solution)/shard_map/ppermute | solution.py:348
  2.6 1.8 %collective-permute-start.1 = (bf16[64,640]{1,0:T(8,128)(2,1)S(1)}, bf16[64,640]{1,0:T(8,128)(2,1)S(1)}, u32[]{:S(2)}, u32[]{:S(2)}) collective-permute-start(bf16[64,640]{1,0:T(8,128)(2,1)S(1)} %get-tuple-element.15), channel_id=1, source_target_pairs={{2,4},{4,2},{6,8},{8,6},{10,12},{12,10},{14,16},{16,14},{18,20},{2... | collective-permute-start | bytes 245768 | tf_op jit(solution)/shard_map/ppermute | solution.py:349
  4.4 4.3 %collective-permute-start.2 = (bf16[64,128]{1,0:T(8,128)(2,1)S(1)}, bf16[64,128]{1,0:T(8,128)(2,1)S(1)}, u32[]{:S(2)}, u32[]{:S(2)}) collective-permute-start(bf16[64,128]{1,0:T(8,128)(2,1)S(1)} %slice_add_fusion), channel_id=1, source_target_pairs={{0,1},{1,0},{2,3},{3,2},{4,5},{5,4},{6,7},{7,6},{8,9},{9,8},{10,11... | collective-permute-start | bytes 49160 | tf_op jit(solution)/shard_map/ppermute | solution.py:352

commit v5 on v4

--- a/solution.py
+++ b/solution.py
@@ -13,6 +13,7 @@
 HALO = 4
 EXT = ROWS + 2 * HALO
 BF, F32 = jnp.bfloat16, jnp.float32
+WIDE = ("far", "near")
 VMEM_LIMIT = 48 * 1024 * 1024
 
 
@@ -27,7 +28,7 @@
 def pack_kernel(sides, in_ref, s_ref, even_ref, odd_ref, strip_ref, wide_ref):
     lane = lanes_of((C1, COLS))
     place = lax.axis_index("narrow")
-    odd = lax.axis_index("wide") % 2
+    odd = lax.axis_index(WIDE) % 2
     for a in range(2):
         wide_ref[...] = in_ref[a].astype(F32)
         for z in range(2):
@@ -101,7 +102,7 @@
     ext_ref, side_ref, jst_ref, gst_ref, gsb_ref, pst_ref, psb_ref, qst_ref,
     pre_ref, prb_ref, ro_ref, rg_ref, rgb_ref, rq_ref, gp_ref, flat_ref, fa_ref, fb_ref, fc_ref,
 ):
-    w, n = lax.axis_index("wide"), lax.axis_index("narrow")
+    w, n = lax.axis_index(WIDE), lax.axis_index("narrow")
     lane32 = lanes_of((C2, COLS))
     lane64 = lanes_of((64, COLS))
     flag = lambda is_there: jnp.where(is_there, 1.0, 0.0)
@@ -279,17 +280,29 @@
     for i in range(1, parts_ref.shape[0]):
         total = total + parts_ref[i].astype(F32)
     total = total.astype(BF)
-    for i in range(parts_ref.shape[0]):
+    for i in range(copies_ref.shape[0]):
         copies_ref[i] = total
 
 
-def add_up(parts):
+def add_up(parts, copies):
     return pl.pallas_call(
         add_kernel,
-        out_shape=jax.ShapeDtypeStruct(parts.shape, BF),
+        out_shape=jax.ShapeDtypeStruct((copies,) + parts.shape[1:], BF),
         compiler_params=pltpu.CompilerParams(vmem_limit_bytes=VMEM_LIMIT),
         name="add_up",
     )(parts)
+
+
+def summed(grads):
+    group, others = "far", ("near", "narrow")
+    count, rest = lax.axis_size(group), lax.axis_size(others)
+    length = grads.shape[0]
+    share = -(-length // count)
+    grads = jnp.pad(grads, ((0, share * count - length), (0, 0))).reshape(count, share, COLS)
+    part = add_up(lax.all_to_all(grads, group, 0, 0, tiled=True), rest)
+    part = add_up(lax.all_to_all(part, others, 0, 0, tiled=True), count)
+    total = lax.all_to_all(part, group, 0, 0, tiled=True)
+    return total.reshape(share * count, COLS)[:length]
 
 
 def spread_kernel(fine_scale, coarse_scale, sum_ref, fine_ref, coarse_ref):
@@ -338,15 +351,15 @@
 
 
 def shards(features, cotangent, coarse_weight, fine_weight):
-    wide, narrow = lax.axis_size("wide"), lax.axis_size("narrow")
+    wide, narrow = lax.axis_size(WIDE), lax.axis_size("narrow")
     matrices = weight_matrices(coarse_weight, fine_weight)
     sides = 1 if narrow == 2 else 2
     own, to_even, to_odd, strip = pack(features, cotangent, sides)
     swaps = lambda start: [
         pair for i in range(start, wide - 1, 2) for pair in ((i, i + 1), (i + 1, i))
     ]
-    even = lax.ppermute(to_even, "wide", swaps(0))
-    odd = lax.ppermute(to_odd, "wide", swaps(1))
+    odd = lax.ppermute(to_odd, WIDE, swaps(1))
+    even = lax.ppermute(to_even, WIDE, swaps(0))
     strip = strip + even[:, HALO * COLS :] + odd[:, HALO * COLS :]
     if sides == 1:
         left = right = lax.ppermute(strip, "narrow", [(0, 1), (1, 0)])
@@ -356,13 +369,8 @@
     output, grad_features, grads = block(
         (wide, narrow), (own, even, odd, left, right) + matrices
     )
+    total = summed(grads)
     devices = wide * narrow
-    share = -(-256 // devices)
-    grads = jnp.pad(grads, ((0, share * devices - 256), (0, 0))).reshape(devices, share, COLS)
-    both = ("wide", "narrow")
-    parts = lax.all_to_all(grads, both, 0, 0, tiled=True)
-    total = lax.all_to_all(add_up(parts), both, 0, 0, tiled=True)
-    total = total.reshape(share * devices, COLS)[:256]
     all_cells = features.shape[1] * features.shape[2] * features.shape[3] * devices
     grad_fine, grad_coarse = spread(
         total, 1.0 / math.sqrt(all_cells), 1.0 / math.sqrt(all_cells // 8)
@@ -378,10 +386,12 @@
 
 
 def solution(mesh):
-    placed = P(None, "wide", None, "narrow")
+    wide, narrow = mesh.shape["wide"], mesh.shape["narrow"]
+    finer = jax.sharding.Mesh(mesh.devices.reshape(wide // 2, 2, narrow), WIDE + ("narrow",))
+    placed = P(None, WIDE, None, "narrow")
     return jax.shard_map(
         shards,
-        mesh=mesh,
+        mesh=finer,
         in_specs=(placed, placed, P(), P()),
         out_specs=(placed, placed, P(), P()),
         check_vma=False,

time: 41.3 us -> 47.1 us (1.14)
  blocking collectives: 27 us -> 32.8 us
    all_to_all x2 -> x3, blocking collectives: 27 us -> 32.8 us  [the longest x1 17 us: summed(): part = add_up(lax.all_to_all(grads, group, 0, 0, tiled=True), rest)]
where the time goes in v5:
time: 47.1 us; the launch traced here: 46.8 us
  blocking collectives  32.8 us (70%)
  Pallas kernels  5.71 us (12%)
  starting transfers between devices  3.75 us (8%)
  local copies, waits for them, and re-layouts  1.59 us (3%)
  other arithmetic  1.24 us (3%)
  waiting for transfers between devices  0.9 us (2%)
  between operations  0.76 us (2%)
    all_to_all x1, blocking collectives, summed(): part = add_up(lax.all_to_all(grads, group, 0, 0, tiled=True), rest)  17 us
    all_to_all x1, blocking collectives, summed(): total = lax.all_to_all(part, group, 0, 0, tiled=True)  9.29 us
    all_to_all x1, blocking collectives, summed(): part = add_up(lax.all_to_all(part, others, 0, 0, tiled=True), count)  6.51 us
    pallas_call x1, Pallas kernels, block(): pl.pallas_call(functools.partial(block_kernel, counts), out_shape=(jax.Sh...  4.36 us
    ppermute x1, starting transfers between devices, shards(): left = right = lax.ppermute(strip, 'narrow', [(0, 1), (1, 0)])  2.58 us
    another operation x1, other arithmetic, pack(): jnp.stack([flat(features), flat(cotangent)])  0.99 us
  transfers between devices with their start and end apart: 3, of which 1 were waited for; matrix products, arithmetic and copies ran while one was open for 4% of the time, Pallas kernels for 0%

profile of v5, /device:TPU:0, one launch (start us, length us, event | category | flops | bytes accessed | tf_op | source)
XLA Modules:
  0.0 46.8 jit_solution(14055714747939774576)
XLA Ops:
  0.6 1.0 %pad_maximum_fusion.in_ref = bf16[2,512,128]{2,1,0:T(8,128)(2,1)S(1)} fusion(bf16[1,512,128]{2,1,0:T(8,128)(2,1)} %bitcast.50, bf16[1,512,128]{2,1,0:T(8,128)(2,1)} %bitcast.51), kind=kLoop, calls=%fused_computation | loop fusion | flops 131072 | bytes 524288 | tf_op jit(solution)/shard_map/stack | solution.py:74
  1.6 0.5 %pack.1 = (bf16[64,2048]{1,0:T(8,128)(2,1)S(1)}, bf16[64,640]{1,0:T(8,128)(2,1)S(1)}, bf16[64,640]{1,0:T(8,128)(2,1)S(1)}, bf16[64,128]{1,0:T(8,128)(2,1)S(1)}) custom-call(bf16[2,512,128]{2,1,0:T(8,128)(2,1)S(1)} %pad_maximum_fusion.in_ref), custom_call_target="tpu_custom_call" | custom-call | flops 1000000 | bytes 1000000 | tf_op jit(solution)/shard_map/pack/pallas_call | solution.py:62
  2.1 0.0 copy-start
  2.1 0.5 %collective-permute-start = (bf16[64,640]{1,0:T(8,128)(2,1)S(1)}, bf16[64,640]{1,0:T(8,128)(2,1)S(1)}, u32[]{:S(2)}, u32[]{:S(2)}) collective-permute-start(bf16[64,640]{1,0:T(8,128)(2,1)S(1)} %get-tuple-element.14), channel_id=1, source_target_pairs={{0,2},{2,0},{4,6},{6,4},{8,10},{10,8},{12,14},{14,12},{16,18},{18,... | collective-permute-start | bytes 245768 | tf_op jit(solution)/shard_map/ppermute | solution.py:362
  2.6 0.7 %collective-permute-start.1 = (bf16[64,640]{1,0:T(8,128)(2,1)S(1)}, bf16[64,640]{1,0:T(8,128)(2,1)S(1)}, u32[]{:S(2)}, u32[]{:S(2)}) collective-permute-start(bf16[64,640]{1,0:T(8,128)(2,1)S(1)} %get-tuple-element.15), channel_id=1, source_target_pairs={{2,4},{4,2},{6,8},{8,6},{10,12},{12,10},{14,16},{16,14},{18,20},{2... | collective-permute-start | bytes 245768 | tf_op jit(solution)/shard_map/ppermute | solution.py:361
  3.3 0.8 %slice_bitcast_fusion.4 = (bf16[32,16,3,3]{0,1,3,2:T(8,128)(2,1)S(1)}, bf16[3,32,3,16]{1,3,2,0:T(8,128)(2,1)S(1)}) fusion(bf16[32,16,3,3,3]{0,1,4,3,2:T(8,128)(2,1)} %param.6), kind=kLoop, calls=%fused_computation.14 | loop fusion | bytes 27648 | tf_op jit(solution)/shard_map/squeeze | solution.py:347
  4.1 0.0 copy-done
  4.1 0.1 fusion
  4.2 0.1 maximum_bitcast_fusion
  4.4 0.0 collective-permute-done.even_ref
  4.4 0.0 collective-permute-done.1.odd_ref
  4.4 2.6 %collective-permute-start.2 = (bf16[64,128]{1,0:T(8,128)(2,1)S(1)}, bf16[64,128]{1,0:T(8,128)(2,1)S(1)}, u32[]{:S(2)}, u32[]{:S(2)}) collective-permute-start(bf16[64,128]{1,0:T(8,128)(2,1)S(1)} %slice_add_fusion), channel_id=1, source_target_pairs={{0,1},{1,0},{2,3},{3,2},{4,5},{5,4},{6,7},{7,6},{8,9},{9,8},{10,11... | collective-permute-start | bytes 49160 | tf_op jit(solution)/shard_map/ppermute | solution.py:365
  7.0 0.1 reshape.41.wq_ref
  7.1 0.1 reshape.40
  7.2 0.1 copy.21.wc_ref
  7.4 0.1 reshape.39
  7.5 0.1 copy.20.wg_ref
  7.7 0.1 reshape.38.wo_ref
  7.8 0.9 %collective-permute-done.2.left_ref.right_ref = bf16[64,128]{1,0:T(8,128)(2,1)S(1)} collective-permute-done((bf16[64,128]{1,0:T(8,128)(2,1)S(1)}, bf16[64,128]{1,0:T(8,128)(2,1)S(1)}, u32[]{:S(2)}, u32[]{:S(2)}) %collective-permute-start.2) | collective-permute-done | bytes 16416 | tf_op jit(solution)/shard_map/ppermute | solution.py:365
  8.7 4.4 %block.1 = (bf16[512,128]{1,0:T(8,128)(2,1)}, bf16[512,128]{1,0:T(8,128)(2,1)}, bf16[256,128]{1,0:T(8,128)(2,1)S(1)}) custom-call(bf16[64,2048]{1,0:T(8,128)(2,1)S(1)} %get-tuple-element.13.s_ref, bf16[64,640]{1,0:T(8,128)(2,1)S(1)} %collective-permute-done.even_ref, bf16[64,640]{1,0:T(8,128)(2,1)S(1)} %collective-permute-done.1.odd_ref, ...), custom_call_target="tpu_custom_call" | custom-call | flops 1000000000 | bytes 4000000 | tf_op jit(solution)/shard_map/block/pallas_call | solution.py:251
  13.1 17.0 %all_to_all.15.parts_ref = bf16[8,32,128]{2,1,0:T(8,128)(2,1)S(1)} all-to-all(bf16[8,32,128]{2,1,0:T(8,128)(2,1)S(1)} %bitcast.46), channel_id=1, replica_groups=mesh['far'=8,'near'=2,'narrow'=2] {'far'}, dimensions={0} | all-to-all | bytes 131072 | tf_op jit(solution)/shard_map/all_to_all | solution.py:302
  30.1 6.5 %all_to_all.16.parts_ref = bf16[4,32,128]{2,1,0:T(8,128)(2,1)S(1)} all-to-all(bf16[4,32,128]{2,1,0:T(8,128)(2,1)S(1)} %add_up.2), channel_id=1, replica_groups=mesh['far'=8,'near'=2,'narrow'=2] {'near','narrow'}, dimensions={0} | all-to-all | bytes 65536 | tf_op jit(solution)/shard_map/all_to_all | solution.py:303
  36.6 9.3 %all_to_all.17 = bf16[8,32,128]{2,1,0:T(8,128)(2,1)S(1)} all-to-all(bf16[8,32,128]{2,1,0:T(8,128)(2,1)S(1)} %add_up.3), channel_id=1, replica_groups=mesh['far'=8,'near'=2,'narrow'=2] {'far'}, dimensions={0} | all-to-all | bytes 131072 | tf_op jit(solution)/shard_map/all_to_all | solution.py:304
  45.9 0.9 %spread.1 = (f32[432,48]{1,0:T(8,128)}, f32[432,32]{1,0:T(8,128)}) custom-call(bf16[256,128]{1,0:T(8,128)(2,1)S(1)} %bitcast.45), custom_call_target="tpu_custom_call" | custom-call | tf_op jit(solution)/shard_map/spread/pallas_call | solution.py:326
  (11 shorter events, 0.2 us)
Async XLA Ops:
  2.1 2.0 %copy-start = (bf16[16,48,3,3,3]{1,0,4,3,2:T(8,128)(2,1)S(1)}, bf16[16,48,3,3,3]{1,0,4,3,2:T(8,128)(2,1)}, u32[]{:S(2)}) copy-start(bf16[16,48,3,3,3]{1,0,4,3,2:T(8,128)(2,1)} %param.7) | copy-start | bytes 124420
  2.1 2.3 %collective-permute-start = (bf16[64,640]{1,0:T(8,128)(2,1)S(1)}, bf16[64,640]{1,0:T(8,128)(2,1)S(1)}, u32[]{:S(2)}, u32[]{:S(2)}) collective-permute-start(bf16[64,640]{1,0:T(8,128)(2,1)S(1)} %get-tuple-element.14), channel_id=1, source_target_pairs={{0,2},{2,0},{4,6},{6,4},{8,10},{10,8},{12,14},{14,12},{16,18},{18,... | collective-permute-start | bytes 245768 | tf_op jit(solution)/shard_map/ppermute | solution.py:362
  2.6 1.8 %collective-permute-start.1 = (bf16[64,640]{1,0:T(8,128)(2,1)S(1)}, bf16[64,640]{1,0:T(8,128)(2,1)S(1)}, u32[]{:S(2)}, u32[]{:S(2)}) collective-permute-start(bf16[64,640]{1,0:T(8,128)(2,1)S(1)} %get-tuple-element.15), channel_id=1, source_target_pairs={{2,4},{4,2},{6,8},{8,6},{10,12},{12,10},{14,16},{16,14},{18,20},{2... | collective-permute-start | bytes 245768 | tf_op jit(solution)/shard_map/ppermute | solution.py:361
  4.4 4.3 %collective-permute-start.2 = (bf16[64,128]{1,0:T(8,128)(2,1)S(1)}, bf16[64,128]{1,0:T(8,128)(2,1)S(1)}, u32[]{:S(2)}, u32[]{:S(2)}) collective-permute-start(bf16[64,128]{1,0:T(8,128)(2,1)S(1)} %slice_add_fusion), channel_id=1, source_target_pairs={{0,1},{1,0},{2,3},{3,2},{4,5},{5,4},{6,7},{7,6},{8,9},{9,8},{10,11... | collective-permute-start | bytes 49160 | tf_op jit(solution)/shard_map/ppermute | solution.py:365

commit v6 on v4

--- a/solution.py
+++ b/solution.py
@@ -342,11 +342,10 @@
     matrices = weight_matrices(coarse_weight, fine_weight)
     sides = 1 if narrow == 2 else 2
     own, to_even, to_odd, strip = pack(features, cotangent, sides)
-    swaps = lambda start: [
-        pair for i in range(start, wide - 1, 2) for pair in ((i, i + 1), (i + 1, i))
-    ]
-    even = lax.ppermute(to_even, "wide", swaps(0))
-    odd = lax.ppermute(to_odd, "wide", swaps(1))
+    swap = [pair for i in range(0, wide - 1, 2) for pair in ((i, i + 1), (i + 1, i))]
+    relay = [pair for i in range(0, wide - 2, 2) for pair in ((i + 2, i), (i + 1, i + 3))]
+    odd = lax.ppermute(lax.ppermute(to_odd, "wide", relay), "wide", swap)
+    even = lax.ppermute(to_even, "wide", swap)
     strip = strip + even[:, HALO * COLS :] + odd[:, HALO * COLS :]
     if sides == 1:
         left = right = lax.ppermute(strip, "narrow", [(0, 1), (1, 0)])

time: 41.3 us -> 43 us (1.041)
  waiting for transfers between devices: 0.9 us -> 6.68 us
  blocking collectives: 27 us -> 23 us
    ppermute x2 -> x3, waiting for transfers between devices: 0.01 us -> 5.75 us  [the longest x2 5.74 us: shards(): odd = lax.ppermute(lax.ppermute(to_odd, 'wide', relay), 'wide', swap)]
    all_to_all x1, blocking collectives: 17.8 us -> 13.7 us  [shards(): parts = lax.all_to_all(grads, both, 0, 0, tiled=True)]
    ppermute x2 -> x3, starting transfers between devices: 1.17 us -> 1.8 us  [the longest x2 1.28 us: shards(): odd = lax.ppermute(lax.ppermute(to_odd, 'wide', relay), 'wide', swap)]
    ppermute x1, starting transfers between devices: 2.58 us -> 1.99 us  [shards(): left = right = lax.ppermute(strip, 'narrow', [(0, 1), (1, 0)])]
  transfers between devices with their start and end apart: 3 -> 4, of which waited for: 1 -> 3; matrix products, arithmetic and copies ran while one was open for 4% -> 4% of each run, Pallas kernels for 0% -> 0%
where the time goes in v6:
time: 43 us; the launch traced here: 42.7 us
  blocking collectives  23 us (53%)
  waiting for transfers between devices  6.68 us (16%)
  Pallas kernels  5.72 us (13%)
  starting transfers between devices  3.79 us (9%)
  local copies, waits for them, and re-layouts  1.59 us (4%)
  other arithmetic  1.24 us (3%)
  between operations  0.74 us (2%)
    all_to_all x1, blocking collectives, shards(): parts = lax.all_to_all(grads, both, 0, 0, tiled=True)  13.7 us
    all_to_all x1, blocking collectives, shards(): total = lax.all_to_all(add_up(parts), both, 0, 0, tiled=True)  9.3 us
    ppermute x2, waiting for transfers between devices, shards(): odd = lax.ppermute(lax.ppermute(to_odd, 'wide', relay), 'wide', swap)  5.74 us
    pallas_call x1, Pallas kernels, block(): pl.pallas_call(functools.partial(block_kernel, counts), out_shape=(jax.Sh...  4.35 us
    ppermute x1, starting transfers between devices, shards(): left = right = lax.ppermute(strip, 'narrow', [(0, 1), (1, 0)])  1.99 us
    ppermute x2, starting transfers between devices, shards(): odd = lax.ppermute(lax.ppermute(to_odd, 'wide', relay), 'wide', swap)  1.28 us
    another operation x1, other arithmetic, pack(): jnp.stack([flat(features), flat(cotangent)])  0.99 us
    ppermute x1, waiting for transfers between devices, shards(): left = right = lax.ppermute(strip, 'narrow', [(0, 1), (1, 0)])  0.93 us
  transfers between devices with their start and end apart: 4, of which 3 were waited for; matrix products, arithmetic and copies ran while one was open for 4% of the time, Pallas kernels for 0%

profile of v6, /device:TPU:0, one launch (start us, length us, event | category | flops | bytes accessed | tf_op | source)
XLA Modules:
  0.0 42.7 jit_solution(2609478863660910551)
XLA Ops:
  0.6 1.0 %pad_maximum_fusion.in_ref = bf16[2,512,128]{2,1,0:T(8,128)(2,1)S(1)} fusion(bf16[1,512,128]{2,1,0:T(8,128)(2,1)} %bitcast.50, bf16[1,512,128]{2,1,0:T(8,128)(2,1)} %bitcast.51), kind=kLoop, calls=%fused_computation | loop fusion | flops 131072 | bytes 524288 | tf_op jit(solution)/shard_map/stack | solution.py:73
  1.6 0.5 %pack.1 = (bf16[64,2048]{1,0:T(8,128)(2,1)S(1)}, bf16[64,640]{1,0:T(8,128)(2,1)S(1)}, bf16[64,640]{1,0:T(8,128)(2,1)S(1)}, bf16[64,128]{1,0:T(8,128)(2,1)S(1)}) custom-call(bf16[2,512,128]{2,1,0:T(8,128)(2,1)S(1)} %pad_maximum_fusion.in_ref), custom_call_target="tpu_custom_call" | custom-call | flops 1000000 | bytes 1000000 | tf_op jit(solution)/shard_map/pack/pallas_call | solution.py:61
  2.1 0.5 %collective-permute-start = (bf16[64,640]{1,0:T(8,128)(2,1)S(1)}, bf16[64,640]{1,0:T(8,128)(2,1)S(1)}, u32[]{:S(2)}, u32[]{:S(2)}) collective-permute-start(bf16[64,640]{1,0:T(8,128)(2,1)S(1)} %get-tuple-element.14), channel_id=1, source_target_pairs={{0,2},{2,0},{4,6},{6,4},{8,10},{10,8},{12,14},{14,12},{16,18},{18,... | collective-permute-start | bytes 245768 | tf_op jit(solution)/shard_map/ppermute | solution.py:348
  2.6 1.3 %collective-permute-start.1 = (bf16[64,640]{1,0:T(8,128)(2,1)S(1)}, bf16[64,640]{1,0:T(8,128)(2,1)S(1)}, u32[]{:S(2)}, u32[]{:S(2)}) collective-permute-start(bf16[64,640]{1,0:T(8,128)(2,1)S(1)} %get-tuple-element.15), channel_id=1, source_target_pairs={{4,0},{2,6},{8,4},{6,10},{12,8},{10,14},{16,12},{14,18},{20,16},{1... | collective-permute-start | bytes 245768 | tf_op jit(solution)/shard_map/ppermute | solution.py:347
  3.9 0.8 %slice_bitcast_fusion.4 = (bf16[32,16,3,3]{0,1,3,2:T(8,128)(2,1)S(1)}, bf16[3,32,3,16]{1,3,2,0:T(8,128)(2,1)S(1)}) fusion(bf16[32,16,3,3,3]{0,1,4,3,2:T(8,128)(2,1)} %param.6), kind=kLoop, calls=%fused_computation.14 | loop fusion | bytes 27648 | tf_op jit(solution)/shard_map/squeeze | solution.py:334
  4.7 0.0 copy-done
  4.7 0.1 fusion
  4.8 0.1 maximum_bitcast_fusion
  5.0 4.5 %collective-permute-done.1 = bf16[64,640]{1,0:T(8,128)(2,1)S(1)} collective-permute-done((bf16[64,640]{1,0:T(8,128)(2,1)S(1)}, bf16[64,640]{1,0:T(8,128)(2,1)S(1)}, u32[]{:S(2)}, u32[]{:S(2)}) %collective-permute-start.1) | collective-permute-done | bytes 81952 | tf_op jit(solution)/shard_map/ppermute | solution.py:347
  9.5 0.0 collective-permute-start.2
  9.5 0.0 collective-permute-done.even_ref
  9.5 1.3 %collective-permute-done.2.odd_ref = bf16[64,640]{1,0:T(8,128)(2,1)S(1)} collective-permute-done((bf16[64,640]{1,0:T(8,128)(2,1)S(1)}, bf16[64,640]{1,0:T(8,128)(2,1)S(1)}, u32[]{:S(2)}, u32[]{:S(2)}) %collective-permute-start.2) | collective-permute-done | bytes 81952 | tf_op jit(solution)/shard_map/ppermute | solution.py:347
  10.8 2.0 %collective-permute-start.3 = (bf16[64,128]{1,0:T(8,128)(2,1)S(1)}, bf16[64,128]{1,0:T(8,128)(2,1)S(1)}, u32[]{:S(2)}, u32[]{:S(2)}) collective-permute-start(bf16[64,128]{1,0:T(8,128)(2,1)S(1)} %slice_add_fusion), channel_id=1, source_target_pairs={{0,1},{1,0},{2,3},{3,2},{4,5},{5,4},{6,7},{7,6},{8,9},{9,8},{10,11... | collective-permute-start | bytes 49160 | tf_op jit(solution)/shard_map/ppermute | solution.py:351
  12.8 0.1 reshape.41.wq_ref
  12.9 0.1 reshape.40
  13.0 0.1 copy.21.wc_ref
  13.2 0.1 reshape.39
  13.3 0.1 copy.20.wg_ref
  13.5 0.1 reshape.38.wo_ref
  13.6 0.9 %collective-permute-done.3.left_ref.right_ref = bf16[64,128]{1,0:T(8,128)(2,1)S(1)} collective-permute-done((bf16[64,128]{1,0:T(8,128)(2,1)S(1)}, bf16[64,128]{1,0:T(8,128)(2,1)S(1)}, u32[]{:S(2)}, u32[]{:S(2)}) %collective-permute-start.3) | collective-permute-done | bytes 16416 | tf_op jit(solution)/shard_map/ppermute | solution.py:351
  14.5 4.3 %block.1 = (bf16[512,128]{1,0:T(8,128)(2,1)}, bf16[512,128]{1,0:T(8,128)(2,1)}, bf16[256,128]{1,0:T(8,128)(2,1)S(1)}) custom-call(bf16[64,2048]{1,0:T(8,128)(2,1)S(1)} %get-tuple-element.13.s_ref, bf16[64,640]{1,0:T(8,128)(2,1)S(1)} %collective-permute-done.even_ref, bf16[64,640]{1,0:T(8,128)(2,1)S(1)} %collective-permute-done.2.odd_ref, ...), custom_call_target="tpu_custom_call" | custom-call | flops 1000000000 | bytes 4000000 | tf_op jit(solution)/shard_map/block/pallas_call | solution.py:250
  18.9 13.7 %all_to_all.10.parts_ref = bf16[32,8,128]{2,1,0:T(8,128)(2,1)S(1)} all-to-all(bf16[32,8,128]{2,1,0:T(8,128)(2,1)S(1)} %bitcast.46), channel_id=1, replica_groups=mesh['wide'=16,'narrow'=2] {'wide','narrow'}, dimensions={0} | all-to-all | bytes 131072 | tf_op jit(solution)/shard_map/all_to_all | solution.py:362
  32.6 9.3 %all_to_all.11 = bf16[32,8,128]{2,1,0:T(8,128)(2,1)S(1)} all-to-all(bf16[32,8,128]{2,1,0:T(8,128)(2,1)S(1)} %add_up.1), channel_id=1, replica_groups=mesh['wide'=16,'narrow'=2] {'wide','narrow'}, dimensions={0} | all-to-all | bytes 131072 | tf_op jit(solution)/shard_map/all_to_all | solution.py:363
  41.9 0.9 %spread.1 = (f32[432,48]{1,0:T(8,128)}, f32[432,32]{1,0:T(8,128)}) custom-call(bf16[256,128]{1,0:T(8,128)(2,1)S(1)} %bitcast.45), custom_call_target="tpu_custom_call" | custom-call | tf_op jit(solution)/shard_map/spread/pallas_call | solution.py:313
  (11 shorter events, 0.2 us)
Async XLA Ops:
  2.1 2.6 %copy-start = (bf16[16,48,3,3,3]{1,0,4,3,2:T(8,128)(2,1)S(1)}, bf16[16,48,3,3,3]{1,0,4,3,2:T(8,128)(2,1)}, u32[]{:S(2)}) copy-start(bf16[16,48,3,3,3]{1,0,4,3,2:T(8,128)(2,1)} %param.7) | copy-start | bytes 124420
  2.1 7.4 %collective-permute-start = (bf16[64,640]{1,0:T(8,128)(2,1)S(1)}, bf16[64,640]{1,0:T(8,128)(2,1)S(1)}, u32[]{:S(2)}, u32[]{:S(2)}) collective-permute-start(bf16[64,640]{1,0:T(8,128)(2,1)S(1)} %get-tuple-element.14), channel_id=1, source_target_pairs={{0,2},{2,0},{4,6},{6,4},{8,10},{10,8},{12,14},{14,12},{16,18},{18,... | collective-permute-start | bytes 245768 | tf_op jit(solution)/shard_map/ppermute | solution.py:348
  2.6 6.8 %collective-permute-start.1 = (bf16[64,640]{1,0:T(8,128)(2,1)S(1)}, bf16[64,640]{1,0:T(8,128)(2,1)S(1)}, u32[]{:S(2)}, u32[]{:S(2)}) collective-permute-start(bf16[64,640]{1,0:T(8,128)(2,1)S(1)} %get-tuple-element.15), channel_id=1, source_target_pairs={{4,0},{2,6},{8,4},{6,10},{12,8},{10,14},{16,12},{14,18},{20,16},{1... | collective-permute-start | bytes 245768 | tf_op jit(solution)/shard_map/ppermute | solution.py:347
  9.5 1.3 %collective-permute-start.2 = (bf16[64,640]{1,0:T(8,128)(2,1)S(1)}, bf16[64,640]{1,0:T(8,128)(2,1)S(1)}, u32[]{:S(2)}, u32[]{:S(2)}) collective-permute-start(bf16[64,640]{1,0:T(8,128)(2,1)S(1)} %collective-permute-done.1), channel_id=1, source_target_pairs={{0,2},{2,0},{4,6},{6,4},{8,10},{10,8},{12,14},{14,12},{16,18},{18,... | collective-permute-start | bytes 245768 | tf_op jit(solution)/shard_map/ppermute | solution.py:347
  10.8 3.7 %collective-permute-start.3 = (bf16[64,128]{1,0:T(8,128)(2,1)S(1)}, bf16[64,128]{1,0:T(8,128)(2,1)S(1)}, u32[]{:S(2)}, u32[]{:S(2)}) collective-permute-start(bf16[64,128]{1,0:T(8,128)(2,1)S(1)} %slice_add_fusion), channel_id=1, source_target_pairs={{0,1},{1,0},{2,3},{3,2},{4,5},{5,4},{6,7},{7,6},{8,9},{9,8},{10,11... | collective-permute-start | bytes 49160 | tf_op jit(solution)/shard_map/ppermute | solution.py:351

commit v7 on v4

--- a/solution.py
+++ b/solution.py
@@ -96,7 +96,7 @@
 
 def block_kernel(
     counts,
-    s_ref, even_ref, odd_ref, left_ref, right_ref, wo_ref, wg_ref, wc_ref, wq_ref,
+    s_ref, odd_ref, even_ref, left_ref, right_ref, wo_ref, wg_ref, wc_ref, wq_ref,
     out_ref, gf_ref, gw_ref,
     ext_ref, side_ref, jst_ref, gst_ref, gsb_ref, pst_ref, psb_ref, qst_ref,
     pre_ref, prb_ref, ro_ref, rg_ref, rgb_ref, rq_ref, gp_ref, flat_ref, fa_ref, fb_ref, fc_ref,
@@ -345,16 +345,16 @@
     swaps = lambda start: [
         pair for i in range(start, wide - 1, 2) for pair in ((i, i + 1), (i + 1, i))
     ]
+    odd = lax.ppermute(to_odd, "wide", swaps(1))
     even = lax.ppermute(to_even, "wide", swaps(0))
-    odd = lax.ppermute(to_odd, "wide", swaps(1))
-    strip = strip + even[:, HALO * COLS :] + odd[:, HALO * COLS :]
+    strip = strip + odd[:, HALO * COLS :] + even[:, HALO * COLS :]
     if sides == 1:
         left = right = lax.ppermute(strip, "narrow", [(0, 1), (1, 0)])
     else:
         right = lax.ppermute(strip[:, :COLS], "narrow", [(i + 1, i) for i in range(narrow - 1)])
         left = lax.ppermute(strip[:, COLS:], "narrow", [(i, i + 1) for i in range(narrow - 1)])
     output, grad_features, grads = block(
-        (wide, narrow), (own, even, odd, left, right) + matrices
+        (wide, narrow), (own, odd, even, left, right) + matrices
     )
     devices = wide * narrow
     share = -(-256 // devices)

time: 41.3 us -> 41.3 us (level)
  blocking collectives: 27 us -> 23.5 us
  starting transfers between devices: 3.75 us -> 6.74 us
  waiting for transfers between devices: 0.9 us -> 1.58 us
    ppermute x1, starting transfers between devices: 0.52 us -> 4.39 us  [shards(): even = lax.ppermute(to_even, 'wide', swaps(0))]
    all_to_all x1, blocking collectives: 17.8 us -> 14.2 us  [shards(): parts = lax.all_to_all(grads, both, 0, 0, tiled=True)]
    ppermute x1, starting transfers between devices: 2.58 us -> 1.56 us  [shards(): left = right = lax.ppermute(strip, 'narrow', [(0, 1), (1, 0)])]
    ppermute x1, waiting for transfers between devices: 0.9 us -> 1.57 us  [shards(): left = right = lax.ppermute(strip, 'narrow', [(0, 1), (1, 0)])]
where the time goes in v7:
time: 41.3 us; the launch traced here: 41.1 us
  blocking collectives  23.5 us (57%)
  starting transfers between devices  6.74 us (16%)
  Pallas kernels  5.72 us (14%)
  local copies, waits for them, and re-layouts  1.59 us (4%)
  waiting for transfers between devices  1.58 us (4%)
  other arithmetic  1.24 us (3%)
  between operations  0.75 us (2%)
    all_to_all x1, blocking collectives, shards(): parts = lax.all_to_all(grads, both, 0, 0, tiled=True)  14.2 us
    all_to_all x1, blocking collectives, shards(): total = lax.all_to_all(add_up(parts), both, 0, 0, tiled=True)  9.3 us
    ppermute x1, starting transfers between devices, shards(): even = lax.ppermute(to_even, 'wide', swaps(0))  4.39 us
    pallas_call x1, Pallas kernels, block(): pl.pallas_call(functools.partial(block_kernel, counts), out_shape=(jax.Sh...  4.35 us
    ppermute x1, waiting for transfers between devices, shards(): left = right = lax.ppermute(strip, 'narrow', [(0, 1), (1, 0)])  1.57 us
    ppermute x1, starting transfers between devices, shards(): left = right = lax.ppermute(strip, 'narrow', [(0, 1), (1, 0)])  1.56 us
    another operation x1, other arithmetic, pack(): jnp.stack([flat(features), flat(cotangent)])  0.99 us
    pallas_call x1, Pallas kernels, spread(): pl.pallas_call(functools.partial(spread_kernel, fine_scale, coarse_scale)...  0.85 us
  transfers between devices with their start and end apart: 3, of which 1 were waited for; matrix products, arithmetic and copies ran while one was open for 4% of the time, Pallas kernels for 0%

profile of v7, /device:TPU:0, one launch (start us, length us, event | category | flops | bytes accessed | tf_op | source)
XLA Modules:
  0.0 41.1 jit_solution(11859537929171535917)
XLA Ops:
  0.6 1.0 %pad_maximum_fusion.in_ref = bf16[2,512,128]{2,1,0:T(8,128)(2,1)S(1)} fusion(bf16[1,512,128]{2,1,0:T(8,128)(2,1)} %bitcast.50, bf16[1,512,128]{2,1,0:T(8,128)(2,1)} %bitcast.51), kind=kLoop, calls=%fused_computation | loop fusion | flops 131072 | bytes 524288 | tf_op jit(solution)/shard_map/stack | solution.py:73
  1.6 0.5 %pack.1 = (bf16[64,2048]{1,0:T(8,128)(2,1)S(1)}, bf16[64,640]{1,0:T(8,128)(2,1)S(1)}, bf16[64,640]{1,0:T(8,128)(2,1)S(1)}, bf16[64,128]{1,0:T(8,128)(2,1)S(1)}) custom-call(bf16[2,512,128]{2,1,0:T(8,128)(2,1)S(1)} %pad_maximum_fusion.in_ref), custom_call_target="tpu_custom_call" | custom-call | flops 1000000 | bytes 1000000 | tf_op jit(solution)/shard_map/pack/pallas_call | solution.py:61
  2.1 0.0 copy-start
  2.1 0.8 %collective-permute-start = (bf16[64,640]{1,0:T(8,128)(2,1)S(1)}, bf16[64,640]{1,0:T(8,128)(2,1)S(1)}, u32[]{:S(2)}, u32[]{:S(2)}) collective-permute-start(bf16[64,640]{1,0:T(8,128)(2,1)S(1)} %get-tuple-element.14), channel_id=1, source_target_pairs={{2,4},{4,2},{6,8},{8,6},{10,12},{12,10},{14,16},{16,14},{18,20},{2... | collective-permute-start | bytes 245768 | tf_op jit(solution)/shard_map/ppermute | solution.py:348
  2.9 4.4 %collective-permute-start.1 = (bf16[64,640]{1,0:T(8,128)(2,1)S(1)}, bf16[64,640]{1,0:T(8,128)(2,1)S(1)}, u32[]{:S(2)}, u32[]{:S(2)}) collective-permute-start(bf16[64,640]{1,0:T(8,128)(2,1)S(1)} %get-tuple-element.15), channel_id=1, source_target_pairs={{0,2},{2,0},{4,6},{6,4},{8,10},{10,8},{12,14},{14,12},{16,18},{18,... | collective-permute-start | bytes 245768 | tf_op jit(solution)/shard_map/ppermute | solution.py:349
  7.3 0.8 %slice_bitcast_fusion.4 = (bf16[32,16,3,3]{0,1,3,2:T(8,128)(2,1)S(1)}, bf16[3,32,3,16]{1,3,2,0:T(8,128)(2,1)S(1)}) fusion(bf16[32,16,3,3,3]{0,1,4,3,2:T(8,128)(2,1)} %param.6), kind=kLoop, calls=%fused_computation.14 | loop fusion | bytes 27648 | tf_op jit(solution)/shard_map/squeeze | solution.py:334
  8.1 0.0 copy-done
  8.1 0.1 fusion
  8.2 0.1 maximum_bitcast_fusion
  8.4 0.0 collective-permute-done.odd_ref
  8.4 0.0 collective-permute-done.1.even_ref
  8.4 1.6 %collective-permute-start.2 = (bf16[64,128]{1,0:T(8,128)(2,1)S(1)}, bf16[64,128]{1,0:T(8,128)(2,1)S(1)}, u32[]{:S(2)}, u32[]{:S(2)}) collective-permute-start(bf16[64,128]{1,0:T(8,128)(2,1)S(1)} %slice_add_fusion), channel_id=1, source_target_pairs={{0,1},{1,0},{2,3},{3,2},{4,5},{5,4},{6,7},{7,6},{8,9},{9,8},{10,11... | collective-permute-start | bytes 49160 | tf_op jit(solution)/shard_map/ppermute | solution.py:352
  10.0 0.1 reshape.41.wq_ref
  10.1 0.1 reshape.40
  10.2 0.1 copy.21.wc_ref
  10.4 0.1 reshape.39
  10.5 0.1 copy.20.wg_ref
  10.7 0.1 reshape.38.wo_ref
  10.8 1.6 %collective-permute-done.2.left_ref.right_ref = bf16[64,128]{1,0:T(8,128)(2,1)S(1)} collective-permute-done((bf16[64,128]{1,0:T(8,128)(2,1)S(1)}, bf16[64,128]{1,0:T(8,128)(2,1)S(1)}, u32[]{:S(2)}, u32[]{:S(2)}) %collective-permute-start.2) | collective-permute-done | bytes 16416 | tf_op jit(solution)/shard_map/ppermute | solution.py:352
  12.4 4.3 %block.1 = (bf16[512,128]{1,0:T(8,128)(2,1)}, bf16[512,128]{1,0:T(8,128)(2,1)}, bf16[256,128]{1,0:T(8,128)(2,1)S(1)}) custom-call(bf16[64,2048]{1,0:T(8,128)(2,1)S(1)} %get-tuple-element.13.s_ref, bf16[64,640]{1,0:T(8,128)(2,1)S(1)} %collective-permute-done.odd_ref, bf16[64,640]{1,0:T(8,128)(2,1)S(1)} %collective-permute-done.1.even_ref, ...), custom_call_target="tpu_custom_call" | custom-call | flops 1000000000 | bytes 4000000 | tf_op jit(solution)/shard_map/block/pallas_call | solution.py:250
  16.7 14.2 %all_to_all.10.parts_ref = bf16[32,8,128]{2,1,0:T(8,128)(2,1)S(1)} all-to-all(bf16[32,8,128]{2,1,0:T(8,128)(2,1)S(1)} %bitcast.46), channel_id=1, replica_groups=mesh['wide'=16,'narrow'=2] {'wide','narrow'}, dimensions={0} | all-to-all | bytes 131072 | tf_op jit(solution)/shard_map/all_to_all | solution.py:363
  30.9 9.3 %all_to_all.11 = bf16[32,8,128]{2,1,0:T(8,128)(2,1)S(1)} all-to-all(bf16[32,8,128]{2,1,0:T(8,128)(2,1)S(1)} %add_up.1), channel_id=1, replica_groups=mesh['wide'=16,'narrow'=2] {'wide','narrow'}, dimensions={0} | all-to-all | bytes 131072 | tf_op jit(solution)/shard_map/all_to_all | solution.py:364
  40.2 0.9 %spread.1 = (f32[432,48]{1,0:T(8,128)}, f32[432,32]{1,0:T(8,128)}) custom-call(bf16[256,128]{1,0:T(8,128)(2,1)S(1)} %bitcast.45), custom_call_target="tpu_custom_call" | custom-call | tf_op jit(solution)/shard_map/spread/pallas_call | solution.py:313
  (10 shorter events, 0.2 us)
Async XLA Ops:
  2.1 6.0 %copy-start = (bf16[16,48,3,3,3]{1,0,4,3,2:T(8,128)(2,1)S(1)}, bf16[16,48,3,3,3]{1,0,4,3,2:T(8,128)(2,1)}, u32[]{:S(2)}) copy-start(bf16[16,48,3,3,3]{1,0,4,3,2:T(8,128)(2,1)} %param.7) | copy-start | bytes 124420
  2.1 6.3 %collective-permute-start = (bf16[64,640]{1,0:T(8,128)(2,1)S(1)}, bf16[64,640]{1,0:T(8,128)(2,1)S(1)}, u32[]{:S(2)}, u32[]{:S(2)}) collective-permute-start(bf16[64,640]{1,0:T(8,128)(2,1)S(1)} %get-tuple-element.14), channel_id=1, source_target_pairs={{2,4},{4,2},{6,8},{8,6},{10,12},{12,10},{14,16},{16,14},{18,20},{2... | collective-permute-start | bytes 245768 | tf_op jit(solution)/shard_map/ppermute | solution.py:348
  2.9 5.5 %collective-permute-start.1 = (bf16[64,640]{1,0:T(8,128)(2,1)S(1)}, bf16[64,640]{1,0:T(8,128)(2,1)S(1)}, u32[]{:S(2)}, u32[]{:S(2)}) collective-permute-start(bf16[64,640]{1,0:T(8,128)(2,1)S(1)} %get-tuple-element.15), channel_id=1, source_target_pairs={{0,2},{2,0},{4,6},{6,4},{8,10},{10,8},{12,14},{14,12},{16,18},{18,... | collective-permute-start | bytes 245768 | tf_op jit(solution)/shard_map/ppermute | solution.py:349
  8.4 4.0 %collective-permute-start.2 = (bf16[64,128]{1,0:T(8,128)(2,1)S(1)}, bf16[64,128]{1,0:T(8,128)(2,1)S(1)}, u32[]{:S(2)}, u32[]{:S(2)}) collective-permute-start(bf16[64,128]{1,0:T(8,128)(2,1)S(1)} %slice_add_fusion), channel_id=1, source_target_pairs={{0,1},{1,0},{2,3},{3,2},{4,5},{5,4},{6,7},{7,6},{8,9},{9,8},{10,11... | collective-permute-start | bytes 49160 | tf_op jit(solution)/shard_map/ppermute | solution.py:352

commit v8 on v6

v8 whole, which is shorter than its diff:
```python
import functools
import math

import jax
import jax.numpy as jnp
from jax import lax
from jax.experimental import pallas as pl
from jax.experimental.pallas import tpu as pltpu
from jax.sharding import PartitionSpec as P

C1, C2 = 16, 32
ROWS, COLS = 16, 128
HALO = 4
BF, F32 = jnp.bfloat16, jnp.float32
VMEM_LIMIT = 48 * 1024 * 1024


def lanes_of(shape):
    return lax.broadcasted_iota(jnp.int32, shape, len(shape) - 1)


def row(index, count=1):
    return slice(index * COLS, (index + count) * COLS)


def pair_sum(value):
    lane = lanes_of(value.shape)
    other = jnp.where(lane % 2 == 0, pltpu.roll(value, COLS - 1, 1), pltpu.roll(value, 1, 1))
    return value + other


def pooled(first, second):
    total = first + second
    return (pair_sum(total[0:16] + total[16:32]) * 0.125).astype(BF)


def dot(a, b):
    return jnp.dot(a, b, preferred_element_type=F32)


def dot_nt(a, b):
    return lax.dot_general(a, b, (((1,), (1,)), ((), ())), preferred_element_type=F32)


def params():
    return pltpu.CompilerParams(vmem_limit_bytes=VMEM_LIMIT)


SLOTS = 5


def pack_kernel(sides, in_ref, s_ref, strip_ref, odd_ref, even_ref, wide_ref, base_ref):
    lane = lanes_of((C1, COLS))
    place = lax.axis_index("narrow")
    odd = lax.axis_index("wide") % 2
    strips = [[jnp.zeros((C1, COLS), F32) for _ in range(sides)] for _ in range(2)]
    for a in range(2):
        wide_ref[...] = in_ref[a].astype(F32)
        for z in range(2):
            chans = slice(a * 32 + z * 16, a * 32 + z * 16 + 16)
            for y in range(ROWS):
                value = wide_ref[pl.ds(2 * y + z, C1, stride=2 * ROWS), :]
                s_ref[chans, row(y)] = value.astype(BF)
                start = 64 * a + HALO * y
                inside = (lane >= start) & (lane < start + HALO)
                for side in range(sides):
                    if sides == 2:
                        shift = (start + HALO * side) % COLS
                    else:
                        shift = lax.rem(start + HALO * (1 - place), COLS)
                    strips[z][side] = jnp.where(inside, pltpu.roll(value, shift, 1), strips[z][side])
    for z in range(2):
        for side in range(sides):
            strip_ref[z * 16 : z * 16 + 16, row(side)] = strips[z][side].astype(BF)
    for to, near, pairs, cot in ((0, ROWS - 1, (6, 7), ROWS - 3), (1, 0, (0, 1), 0)):
        base_ref[to, :, row(0)] = s_ref[0:32, row(near)]
        for i, pair in enumerate(pairs):
            first, second = (s_ref[0:32, row(2 * pair + j)].astype(F32) for j in range(2))
            base_ref[to, i * 16 : i * 16 + 16, row(1)] = pooled(first, second)
        base_ref[to, :, row(2, 3)] = s_ref[32:64, row(cot, 3)]
    even_ref[:, row(0, SLOTS)] = base_ref[odd]
    odd_ref[:, row(0, SLOTS)] = base_ref[1 - odd]
    even_ref[:, row(SLOTS, sides)] = jnp.zeros((32, sides * COLS), BF)
    odd_ref[:, row(SLOTS, sides)] = jnp.zeros((32, sides * COLS), BF)


def pack(features, cotangent, sides):
    flat = lambda a: a.reshape(C1 * ROWS * 2, COLS)
    message = jax.ShapeDtypeStruct((32, (SLOTS + sides) * COLS), BF)
    return pl.pallas_call(
        functools.partial(pack_kernel, sides),
        out_shape=(
            jax.ShapeDtypeStruct((64, ROWS * COLS), BF),
            jax.ShapeDtypeStruct((32, sides * COLS), BF),
            message,
            message,
        ),
        scratch_shapes=[
            pltpu.VMEM((C1 * ROWS * 2, COLS), F32),
            pltpu.VMEM((2, 32, SLOTS * COLS), BF),
        ],
        compiler_params=params(),
        cost_estimate=pl.CostEstimate(flops=10**6, bytes_accessed=10**6, transcendentals=0),
        name="pack",
    )(jnp.stack([flat(features), flat(cotangent)]))


def beside(columns, at):
    lane = lanes_of(columns[0].shape)
    if len(columns) == 1:
        place = lax.axis_index("narrow")
        first = (COLS - HALO) * place
        turned = pltpu.roll(columns[0], lax.rem(COLS - at + first, COLS), 1)
        return jnp.where((lane >= first) & (lane < first + HALO), turned, 0.0)
    right = pltpu.roll(columns[0], (-at) % COLS, 1)
    left = pltpu.roll(columns[1], (COLS - HALO - at) % COLS, 1)
    return jnp.where(lane < HALO, right, jnp.where(lane >= COLS - HALO, left, 0.0))


def turn(main, side, by):
    lane = lanes_of(main.shape)
    a, b = pltpu.roll(main, (-by) % COLS, 1), pltpu.roll(side, (-by) % COLS, 1)
    crossed = lane >= COLS - by if by > 0 else lane < -by
    return jnp.where(crossed, b, a), jnp.where(crossed, a, b)


def put_pooled(main, side, main_ref, side_ref, at, side_at):
    main, side = main.astype(F32), side.astype(F32)
    for d in range(3):
        a, b = (main, side) if d == 1 else turn(main, side, 2 * (d - 1))
        main_ref[d * 16 : d * 16 + 16, row(at)] = a.astype(BF)
        side_ref[d * 16 : d * 16 + 16, row(side_at)] = b.astype(BF)


def put_cotangent(main, side, main_ref, side_ref, at, side_at):
    for d in range(3):
        a, b = (main, side) if d == 1 else turn(main, side, d - 1)
        main_ref[d * 32 : d * 32 + 32, row(at)] = a.astype(BF)
        side_ref[d * 32 : d * 32 + 32, row(side_at)] = b.astype(BF)


def put_features(main, side, ref, step, at):
    for d in range(3):
        a = main if d == 1 else turn(main, side, d - 1)[0]
        ref[d * step : d * step + 32, row(at)] = a.astype(BF)


def coarse_part(wg_ref, stack):
    return jnp.concatenate(
        [dot(wg_ref[d * 64 + 32 : d * 64 + 64, :], stack) for d in range(3)], 0
    )


def own_kernel(
    sides,
    s_ref, columns_ref, wc_ref, wg_ref,
    pst_ref, jf_ref, gst_ref, pre_ref, prb_ref, rg_ref, rgb_ref,
    psb_ref, gsb_ref,
):
    columns = [columns_ref[:, row(side)].astype(F32) for side in range(sides)]
    last = None
    for y in range(ROWS):
        main, side = s_ref[0:32, row(y)].astype(F32), beside(columns, HALO * y)
        put_features(main, side, jf_ref, 32, y)
        if y % 2 == 1:
            means = [pooled(a, b) for a, b in zip(last, (main, side))]
            put_pooled(*means, pst_ref, psb_ref, y // 2, y // 2)
        last = (main, side)
        main, side = s_ref[32:64, row(y)].astype(F32), beside(columns, 64 + HALO * y)
        put_cotangent(main, side, gst_ref, gsb_ref, y, y)
    pre_ref[...] = dot(wc_ref[...], pst_ref[...])
    prb_ref[...] = dot(wc_ref[...], psb_ref[...])
    rg_ref[...] = dot(wg_ref[...], gst_ref[...])
    rgb_ref[...] = coarse_part(wg_ref, gsb_ref[...])


def own_rows(s, columns, wc, wg, sides):
    half = ROWS // 2
    shape = lambda rows_, lanes_, kind: jax.ShapeDtypeStruct((rows_, lanes_ * COLS), kind)
    return pl.pallas_call(
        functools.partial(own_kernel, sides),
        out_shape=(
            shape(48, half, BF), shape(96, ROWS, BF), shape(96, ROWS, BF),
            shape(96, half, F32), shape(96, half, F32),
            shape(192, ROWS, F32), shape(96, ROWS, F32),
        ),
        scratch_shapes=[
            pltpu.VMEM((48, half * COLS), BF),
            pltpu.VMEM((96, ROWS * COLS), BF),
        ],
        compiler_params=params(),
        cost_estimate=pl.CostEstimate(flops=10**9, bytes_accessed=4 * 10**6, transcendentals=0),
        name="own_rows",
    )(s, columns, wc, wg)


def rest_kernel(
    counts, sides,
    odd_ref, even_ref, pst_own, jf_own, gst_own, pre_own, prb_own, rg_own, rgb_own,
    wo_ref, wg_ref, wc_ref, wq_ref,
    out_ref, gf_ref, gw_ref,
    halo_ref, jst_ref, gst_ref, gsb_ref, pst_ref, psb_ref, qst_ref,
    pre_ref, prb_ref, rg_ref, rgb_ref, ro_ref, rq_ref, flat_ref, fa_ref, fb_ref, fc_ref,
):
    w, n = lax.axis_index("wide"), lax.axis_index("narrow")
    lane32 = lanes_of((C2, COLS))
    flag = lambda is_there: jnp.where(is_there, 1.0, 0.0)
    has_left, has_right = flag(n > 0), flag(n < counts[1] - 1)
    has_above, has_below = flag(w > 0), flag(w < counts[0] - 1)

    odd = w % 2
    halo_ref[1 - odd] = even_ref[...]
    halo_ref[odd] = odd_ref[...]

    pst_ref[:, row(2, 8)] = pst_own[...]
    gst_ref[:, row(3, ROWS)] = gst_own[...]
    for d in range(3):
        jst_ref[d * 64 : d * 64 + 32, row(1, ROWS)] = jf_own[d * 32 : d * 32 + 32, :]
    for i in range(2):
        columns = [halo_ref[i, :, row(SLOTS + side)].astype(F32) for side in range(sides)]
        lane = HALO * (ROWS - HALO) if i == 0 else 0
        sides_f = [beside(columns, lane + HALO * r) for r in range(HALO)]
        near = HALO - 1 if i == 0 else 0
        put_features(halo_ref[i, :, row(0)].astype(F32), sides_f[near], jst_ref, 64, 17 * i)
        for j in range(2):
            main = halo_ref[i, j * 16 : j * 16 + 16, row(1)]
            side = pooled(sides_f[2 * j], sides_f[2 * j + 1])
            put_pooled(main, side, pst_ref, psb_ref, 10 * i + j, 2 * i + j)
        for j in range(3):
            main = halo_ref[i, :, row(2 + j)].astype(F32)
            side = beside(columns, 64 + lane + HALO * (j + 1 - i))
            put_cotangent(main, side, gst_ref, gsb_ref, 19 * i + j, 3 * i + j)
        pre_ref[:, row(2 * i, 2)] = dot(wc_ref[...], pst_ref[:, row(10 * i, 2)])
        rg_ref[:, row(3 * i, 3)] = dot(wg_ref[...], gst_ref[:, row(19 * i, 3)])
    prb_ref[...] = dot(wc_ref[...], psb_ref[...])
    rgb_ref[...] = coarse_part(wg_ref, gsb_ref[...])

    def part(own, halo, lo, size, at, edge, length):
        if at < edge:
            return halo[lo : lo + size, row(at)]
        if at < edge + length:
            return own[lo : lo + size, row(at - edge)]
        return halo[lo : lo + size, row(at - length)]

    for at in range(10):
        keep = has_above if at == 0 else has_below if at == 9 else 1.0
        keep_side = keep * jnp.where(lane32 < 64, has_right, has_left)
        act, grad = [], []
        for pre, joined, base, size, kept in (
            ((pre_own, pre_ref), (rg_own, rg_ref), 32, 64, keep),
            ((prb_own, prb_ref), (rgb_own, rgb_ref), 0, 32, keep_side),
        ):
            value = sum(part(*pre, d * 32, 32, at + d, 2, 8) for d in range(3))
            sig = 1.0 / (1.0 + jnp.exp(-value))
            act.append((value * sig * kept).astype(BF).astype(F32))
            total = sum(
                part(*joined, d * size + base, 32, r + d, 3, ROWS)
                for r in (2 * at, 2 * at + 1)
                for d in range(3)
            )
            grad_act = pair_sum(total).astype(BF).astype(F32)
            grad_pre = grad_act * (sig * (1.0 + value * (1.0 - sig)))
            grad.append((grad_pre * kept).astype(BF).astype(F32))
        for d in range(3):
            a = act[0] if d == 1 else turn(act[0], act[1], d - 1)[0]
            a = a.astype(BF)
            for r in (2 * at - 1, 2 * at):
                if 0 <= r < 18:
                    jst_ref[d * 64 + 32 : d * 64 + 64, row(r)] = a
            q = grad[0] if d == 1 else turn(grad[0], grad[1], 2 * (d - 1))[0]
            qst_ref[d * 32 : d * 32 + 32, row(at)] = q.astype(BF)

    ro_ref[...] = dot(wo_ref[...], jst_ref[...])
    for y in range(ROWS):
        value = ro_ref[0:32, row(y)] + ro_ref[32:64, row(y + 1)] + ro_ref[64:96, row(y + 2)]
        for z in range(2):
            flat_ref[pl.ds(2 * y + z, C1, stride=2 * ROWS), :] = value[z * 16 : z * 16 + 16]
    out_ref[...] = flat_ref[...].astype(BF)

    rq_ref[...] = dot(wq_ref[...], qst_ref[...])
    for at in range(ROWS // 2):
        coarse = rq_ref[0:16, row(at)] + rq_ref[16:32, row(at + 1)] + rq_ref[32:48, row(at + 2)]
        coarse = coarse.astype(BF).astype(F32) * 0.125
        for y in (2 * at, 2 * at + 1):
            for z in range(2):
                total = coarse
                for d in range(3):
                    total = total + part(rg_own, rg_ref, d * 64 + z * 16, 16, y + 2 + d, 3, ROWS)
                flat_ref[pl.ds(2 * y + z, C1, stride=2 * ROWS), :] = total
    gf_ref[...] = flat_ref[...].astype(BF)

    own = row(1, ROWS)
    fa_ref[0:16, :] = jst_ref[64:80, own]
    fa_ref[16:48, :] = jst_ref[96:128, own]
    fa_ref[48:64, :] = jst_ref[64:80, own]
    fa_ref[64:96, :] = jst_ref[96:128, own]
    fa_ref[96:128, :] = jnp.zeros((32, ROWS * COLS), BF)
    fb_ref[0:48, :] = jst_ref[80:128, own]
    fb_ref[48:96, :] = jst_ref[80:128, own]
    fb_ref[96:128, :] = jnp.zeros((32, ROWS * COLS), BF)
    fc_ref[0:96, :] = jnp.zeros((96, 8 * COLS), BF)
    fc_ref[96:128, :] = qst_ref[32:64, row(1, 8)]
    fine, coarse = {}, {}
    for ky in range(3):
        shifted = gst_ref[:, row(4 - ky, ROWS)]
        ra, rb = dot_nt(shifted, fa_ref[...]), dot_nt(shifted, fb_ref[...])
        rc = dot_nt(pst_ref[:, row(1 + ky, 8)], fc_ref[...])
        for kx in range(3):
            lo = (2 - kx) * 32
            fine[ky, 0, kx] = ra[lo + 16 : lo + 32]
            fine[ky, 1, kx] = ra[lo : lo + 16] + rb[lo + 16 : lo + 32]
            fine[ky, 2, kx] = rb[lo : lo + 16]
            coarse[ky, kx] = rc[kx * 16 : kx * 16 + 16] * 0.5
    lane16 = lanes_of((16, COLS))
    order = [(ky, kz, kx) for ky in range(3) for kz in range(3) for kx in range(3)]
    for i in range(16):
        value = jnp.zeros((16, COLS), F32)
        if i < 14:
            value = jnp.where(lane16 < 48, fine[order[i]], value)
        if i < 13:
            value = jnp.where((lane16 >= 48) & (lane16 < 96), fine[order[14 + i]], value)
        if i < 9:
            value = jnp.where(lane16 >= 96, coarse[i // 3, i % 3], value)
        gw_ref[i * 16 : i * 16 + 16, :] = value.astype(BF)


def rest(messages, own, matrices, counts, sides):
    cells = (C1 * ROWS * 2, COLS)
    v = lambda rows_, lanes_, kind: pltpu.VMEM((rows_, lanes_ * COLS), kind)
    return pl.pallas_call(
        functools.partial(rest_kernel, counts, sides),
        out_shape=(
            jax.ShapeDtypeStruct(cells, BF),
            jax.ShapeDtypeStruct(cells, BF),
            jax.ShapeDtypeStruct((256, COLS), BF),
        ),
        scratch_shapes=[
            pltpu.VMEM((2, 32, (SLOTS + sides) * COLS), BF),
            v(192, 18, BF),
            v(96, 22, BF), v(96, 6, BF),
            v(48, 12, BF), v(48, 4, BF),
            v(96, 10, BF),
            v(96, 4, F32), v(96, 4, F32),
            v(192, 6, F32), v(96, 6, F32),
            v(96, 18, F32),
            v(48, 10, F32),
            pltpu.VMEM(cells, F32),
            v(128, ROWS, BF), v(128, ROWS, BF), v(128, 8, BF),
        ],
        compiler_params=params(),
        cost_estimate=pl.CostEstimate(flops=10**9, bytes_accessed=4 * 10**6, transcendentals=10**5),
        name="rest",
    )(*messages, *own, *matrices)


def add_kernel(parts_ref, copies_ref):
    total = parts_ref[0].astype(F32)
    for i in range(1, parts_ref.shape[0]):
        total = total + parts_ref[i].astype(F32)
    total = total.astype(BF)
    for i in range(parts_ref.shape[0]):
        copies_ref[i] = total


def add_up(parts):
    return pl.pallas_call(
        add_kernel,
        out_shape=jax.ShapeDtypeStruct(parts.shape, BF),
        compiler_params=pltpu.CompilerParams(vmem_limit_bytes=VMEM_LIMIT),
        name="add_up",
    )(parts)


def spread_kernel(fine_scale, coarse_scale, sum_ref, fine_ref, coarse_ref):
    for i in range(27):
        if i < 14:
            value = sum_ref[i * 16 : i * 16 + 16, :].astype(F32)
        else:
            at = (i - 14) * 16
            value = pltpu.roll(sum_ref[at : at + 16, :].astype(F32), 80, 1)
        fine_ref[i * 16 : i * 16 + 16, :] = value[:, 0:48] * fine_scale
        ky, kz, kx = i // 9, i // 3 % 3, i % 3
        if kz == 1:
            at = (ky * 3 + kx) * 16
            value = pltpu.roll(sum_ref[at : at + 16, :].astype(F32), 32, 1)[:, 0:32] * coarse_scale
        else:
            value = jnp.zeros((16, 32), F32)
        coarse_ref[i * 16 : i * 16 + 16, :] = value


def spread(total, fine_scale, coarse_scale):
    return pl.pallas_call(
        functools.partial(spread_kernel, fine_scale, coarse_scale),
        out_shape=(
            jax.ShapeDtypeStruct((432, 48), F32),
            jax.ShapeDtypeStruct((432, 32), F32),
        ),
        compiler_params=pltpu.CompilerParams(vmem_limit_bytes=VMEM_LIMIT),
        name="spread",
    )(total)


def weight_matrices(coarse_weight, fine_weight):
    fine = jnp.transpose(fine_weight, (2, 3, 4, 0, 1))
    planes = []
    for zo in range(2):
        first, second = fine[:, 1 - zo], fine[:, 2 - zo]
        both = (first[..., C1:].astype(F32) + second[..., C1:].astype(F32)).astype(BF)
        planes.append(jnp.concatenate([first[..., :C1], second[..., :C1], both], -1))
    stacked = jnp.stack(planes, 1)
    wo = jnp.transpose(stacked, (0, 1, 3, 2, 4)).reshape(96, 192)
    wg = jnp.transpose(stacked[::-1, :, ::-1], (0, 4, 2, 1, 3)).reshape(192, 96)
    middle = coarse_weight[:, :, :, 1, :]
    wc = jnp.transpose(middle, (2, 0, 3, 1)).reshape(96, 48)
    wq = jnp.transpose(middle[:, :, ::-1, ::-1], (2, 1, 3, 0)).reshape(48, 96)
    return wo, wg, wc, wq


def shards(features, cotangent, coarse_weight, fine_weight):
    wide, narrow = lax.axis_size("wide"), lax.axis_size("narrow")
    wo, wg, wc, wq = weight_matrices(coarse_weight, fine_weight)
    sides = 1 if narrow == 2 else 2
    own, strip, to_odd, to_even = pack(features, cotangent, sides)
    if sides == 1:
        columns = lax.ppermute(strip, "narrow", [(0, 1), (1, 0)])
    else:
        right = lax.ppermute(strip[:, :COLS], "narrow", [(i + 1, i) for i in range(narrow - 1)])
        left = lax.ppermute(strip[:, COLS:], "narrow", [(i, i + 1) for i in range(narrow - 1)])
        columns = jnp.concatenate([right, left], 1)
    swaps = lambda start: [
        pair for i in range(start, wide - 1, 2) for pair in ((i, i + 1), (i + 1, i))
    ]
    with_columns = lambda message: lax.dynamic_update_slice(message, columns, (0, SLOTS * COLS))
    odd = lax.ppermute(with_columns(to_odd), "wide", swaps(1))
    even = lax.ppermute(with_columns(to_even), "wide", swaps(0))
    stacks = own_rows(own, columns, wc, wg, sides)
    output, grad_features, grads = rest((odd, even), stacks, (wo, wg, wc, wq), (wide, narrow), sides)
    devices = wide * narrow
    share = -(-256 // devices)
    grads = jnp.pad(grads, ((0, share * devices - 256), (0, 0))).reshape(devices, share, COLS)
    both = ("wide", "narrow")
    parts = lax.all_to_all(grads, both, 0, 0, tiled=True)
    total = lax.all_to_all(add_up(parts), both, 0, 0, tiled=True)
    total = total.reshape(share * devices, COLS)[:256]
    all_cells = features.shape[1] * features.shape[2] * features.shape[3] * devices
    grad_fine, grad_coarse = spread(
        total, 1.0 / math.sqrt(all_cells), 1.0 / math.sqrt(all_cells // 8)
    )
    grad_fine = jnp.transpose(grad_fine.reshape(3, 3, 3, C1, C1 + C2), (3, 4, 0, 1, 2))
    grad_coarse = jnp.transpose(grad_coarse.reshape(3, 3, 3, C1, C2), (4, 3, 0, 1, 2))
    return (
        output.reshape(features.shape),
        grad_features.reshape(features.shape),
        grad_fine,
        grad_coarse,
    )


def solution(mesh):
    placed = P(None, "wide", None, "narrow")
    return jax.shard_map(
        shards,
        mesh=mesh,
        in_specs=(placed, placed, P(), P()),
        out_specs=(placed, placed, P(), P()),
        check_vma=False,
    )
```

time: 43 us -> 38.9 us (0.905)
  waiting for transfers between devices: 6.68 us -> 0.01 us
  blocking collectives: 23 us -> 25.4 us
  local copies, waits for them, and re-layouts: 1.59 us -> 2.4 us
  Pallas kernels: 5.72 us -> 5.07 us
    ppermute x4 -> x3, waiting for transfers between devices: 6.68 us -> 0.01 us  [the longest x1 0.01 us: shards(): odd = lax.ppermute(with_columns(to_odd), 'wide', swaps(1))]
    all_to_all x1, blocking collectives: 13.7 us -> 16.1 us  [shards(): parts = lax.all_to_all(grads, both, 0, 0, tiled=True)]
    squeeze x1, local copies, waits for them, and re-layouts: 0.01 us -> 0.82 us  [weight_matrices(): first, second = (fine[:, 1 - zo], fine[:, 2 - zo])]
    pallas_call x1 -> x2, Pallas kernels: 4.35 us -> 3.74 us  [the longest x1 2.49 us: rest(): pl.pallas_call(functools.partial(rest_kernel, counts, sides), out_shape=(...]
    ppermute x4 -> x3, starting transfers between devices: 3.79 us -> 3.73 us  [the longest x1 3 us: shards(): columns = lax.ppermute(strip, 'narrow', [(0, 1), (1, 0)])]
  transfers between devices with their start and end apart: 4 -> 3, of which waited for: 3 -> 0; matrix products, arithmetic and copies ran while one was open for 4% -> 7% of each run, Pallas kernels for 0% -> 3%
where the time goes in v8:
time: 38.9 us; the launch traced here: 38.6 us
  blocking collectives  25.4 us (65%)
  Pallas kernels  5.07 us (13%)
  starting transfers between devices  3.73 us (10%)
  local copies, waits for them, and re-layouts  2.4 us (6%)
  other arithmetic  1.23 us (3%)
  between operations  0.76 us (2%)
    all_to_all x1, blocking collectives, shards(): parts = lax.all_to_all(grads, both, 0, 0, tiled=True)  16.1 us
    all_to_all x1, blocking collectives, shards(): total = lax.all_to_all(add_up(parts), both, 0, 0, tiled=True)  9.3 us
    ppermute x1, starting transfers between devices, shards(): columns = lax.ppermute(strip, 'narrow', [(0, 1), (1, 0)])  3 us
    pallas_call x1, Pallas kernels, rest(): pl.pallas_call(functools.partial(rest_kernel, counts, sides), out_shape=(...  2.49 us
    pallas_call x1, Pallas kernels, own_rows(): pl.pallas_call(functools.partial(own_kernel, sides), out_shape=(shape(48,...  1.25 us
    another operation x1, other arithmetic, pack(): jnp.stack([flat(features), flat(cotangent)])  0.99 us
    pallas_call x1, Pallas kernels, spread(): pl.pallas_call(functools.partial(spread_kernel, fine_scale, coarse_scale)...  0.85 us
    squeeze x1, local copies, waits for them, and re-layouts, weight_matrices(): first, second = (fine[:, 1 - zo], fine[:, 2 - zo])  0.82 us
  transfers between devices with their start and end apart: 3, of which 0 were waited for; matrix products, arithmetic and copies ran while one was open for 7% of the time, Pallas kernels for 3%

profile of v8, /device:TPU:0, one launch (start us, length us, event | category | flops | bytes accessed | tf_op | source)
XLA Modules:
  0.0 38.6 jit_solution(3450367622039169198)
XLA Ops:
  0.6 1.0 %pad_maximum_fusion.in_ref = bf16[2,512,128]{2,1,0:T(8,128)(2,1)S(1)} fusion(bf16[1,512,128]{2,1,0:T(8,128)(2,1)} %bitcast.50, bf16[1,512,128]{2,1,0:T(8,128)(2,1)} %bitcast.51), kind=kLoop, calls=%fused_computation | loop fusion | flops 131072 | bytes 524288 | tf_op jit(solution)/shard_map/stack | solution.py:105
  1.6 0.4 %pack.1 = (bf16[64,2048]{1,0:T(8,128)(2,1)S(1)}, bf16[32,128]{1,0:T(8,128)(2,1)S(1)}, bf16[32,768]{1,0:T(8,128)(2,1)S(1)}, bf16[32,768]{1,0:T(8,128)(2,1)S(1)}) custom-call(bf16[2,512,128]{2,1,0:T(8,128)(2,1)S(1)} %pad_maximum_fusion.in_ref), custom_call_target="tpu_custom_call" | custom-call | flops 1000000 | bytes 1000000 | tf_op jit(solution)/shard_map/pack/pallas_call | solution.py:90
  2.1 3.0 %collective-permute-start = (bf16[32,128]{1,0:T(8,128)(2,1)S(1)}, bf16[32,128]{1,0:T(8,128)(2,1)S(1)}, u32[]{:S(2)}, u32[]{:S(2)}) collective-permute-start(bf16[32,128]{1,0:T(8,128)(2,1)S(1)} %get-tuple-element.21), channel_id=1, source_target_pairs={{0,1},{1,0},{2,3},{3,2},{4,5},{5,4},{6,7},{7,6},{8,9},{9,8},{10,11... | collective-permute-start | bytes 24584 | tf_op jit(solution)/shard_map/ppermute | solution.py:425
  5.1 0.8 %slice_bitcast_fusion.4 = (bf16[32,16,3,3]{0,1,3,2:T(8,128)(2,1)S(1)}, bf16[3,32,3,16]{1,3,2,0:T(8,128)(2,1)S(1)}) fusion(bf16[32,16,3,3,3]{0,1,4,3,2:T(8,128)(2,1)} %param.6), kind=kLoop, calls=%fused_computation.14 | loop fusion | bytes 27648 | tf_op jit(solution)/shard_map/squeeze | solution.py:413
  5.8 0.8 %slice_bitcast_fusion.1 = (bf16[3,3,16,48]{3,2,1,0:T(8,128)(2,1)S(1)}, bf16[3,3,16,48]{3,2,1,0:T(8,128)(2,1)S(1)}, bf16[3,3,16,48]{3,2,1,0:T(8,128)(2,1)S(1)}) fusion(bf16[3,3,3,16,48]{4,3,2,1,0:T(8,128)(2,1)} %bitcast.52), kind=kLoop, calls=%fused_computation.8 | loop fusion | bytes 82944 | tf_op jit(solution)/shard_map/squeeze | solution.py:407
  6.7 0.1 fusion
  6.8 0.1 maximum_bitcast_fusion
  7.0 0.1 reshape.41.wq_ref
  7.1 0.1 reshape.38
  7.2 0.1 copy.18.wc_ref
  7.4 0.1 reshape.40.wo_ref
  7.5 0.1 reshape.39
  7.6 0.1 copy.19.wg_ref
  7.8 0.0 collective-permute-done.columns_ref
  7.8 0.1 collective-permute-start.2
  7.9 0.7 %collective-permute-start.1 = (bf16[32,768]{1,0:T(8,128)(2,1)S(1)}, bf16[32,768]{1,0:T(8,128)(2,1)S(1)}, u32[]{:S(2)}, u32[]{:S(2)}) collective-permute-start(bf16[32,768]{1,0:T(8,128)(2,1)S(1)} %get-tuple-element.48), channel_id=1, source_target_pairs={{2,4},{4,2},{6,8},{8,6},{10,12},{12,10},{14,16},{16,14},{18,20},{2... | collective-permute-start | bytes 147464 | tf_op jit(solution)/shard_map/ppermute | solution.py:434
  8.5 1.2 %own_rows.1 = (bf16[48,1024]{1,0:T(8,128)(2,1)S(1)}, bf16[96,2048]{1,0:T(8,128)(2,1)S(1)}, bf16[96,2048]{1,0:T(8,128)(2,1)S(1)}, f32[96,1024]{1,0:T(8,128)S(1)},...) custom-call(bf16[64,2048]{1,0:T(8,128)(2,1)S(1)} %get-tuple-element.23.s_ref, ...), custom_call_target="tpu_custom_call" | custom-call | flops 1000000000 | bytes 4000000 | tf_op jit(solution)/shard_map/own_rows/pallas_call | solution.py:180
  9.8 0.0 collective-permute-done.2.even_ref
  9.8 0.0 collective-permute-done.1.odd_ref
  9.8 2.5 %rest.1 = (bf16[512,128]{1,0:T(8,128)(2,1)}, bf16[512,128]{1,0:T(8,128)(2,1)}, bf16[256,128]{1,0:T(8,128)(2,1)S(1)}) custom-call(bf16[32,768]{1,0:T(8,128)(2,1)S(1)} %collective-permute-done.1.odd_ref, bf16[32,768]{1,0:T(8,128)(2,1)S(1)} %collective-permute-done.2.even_ref, bf16[48,1024]{1,0:T(8,128)(2,1)S(1)} %get-tuple-element.24.pst_own, ...), custom_call_target="tpu_custom_call" | custom-call | flops 1000000000 | bytes 4000000 | tf_op jit(solution)/shard_map/rest/pallas_call | solution.py:330
  12.3 16.1 %all_to_all.10.parts_ref = bf16[32,8,128]{2,1,0:T(8,128)(2,1)S(1)} all-to-all(bf16[32,8,128]{2,1,0:T(8,128)(2,1)S(1)} %bitcast.46), channel_id=1, replica_groups=mesh['wide'=16,'narrow'=2] {'wide','narrow'}, dimensions={0} | all-to-all | bytes 131072 | tf_op jit(solution)/shard_map/all_to_all | solution.py:442
  28.5 9.3 %all_to_all.11 = bf16[32,8,128]{2,1,0:T(8,128)(2,1)S(1)} all-to-all(bf16[32,8,128]{2,1,0:T(8,128)(2,1)S(1)} %add_up.1), channel_id=1, replica_groups=mesh['wide'=16,'narrow'=2] {'wide','narrow'}, dimensions={0} | all-to-all | bytes 131072 | tf_op jit(solution)/shard_map/all_to_all | solution.py:443
  37.8 0.9 %spread.1 = (f32[432,48]{1,0:T(8,128)}, f32[432,32]{1,0:T(8,128)}) custom-call(bf16[256,128]{1,0:T(8,128)(2,1)S(1)} %bitcast.45), custom_call_target="tpu_custom_call" | custom-call | tf_op jit(solution)/shard_map/spread/pallas_call | solution.py:392
  (9 shorter events, 0.2 us)
Async XLA Ops:
  2.1 5.7 %collective-permute-start = (bf16[32,128]{1,0:T(8,128)(2,1)S(1)}, bf16[32,128]{1,0:T(8,128)(2,1)S(1)}, u32[]{:S(2)}, u32[]{:S(2)}) collective-permute-start(bf16[32,128]{1,0:T(8,128)(2,1)S(1)} %get-tuple-element.21), channel_id=1, source_target_pairs={{0,1},{1,0},{2,3},{3,2},{4,5},{5,4},{6,7},{7,6},{8,9},{9,8},{10,11... | collective-permute-start | bytes 24584 | tf_op jit(solution)/shard_map/ppermute | solution.py:425
  7.8 2.0 %collective-permute-start.2 = (bf16[32,768]{1,0:T(8,128)(2,1)S(1)}, bf16[32,768]{1,0:T(8,128)(2,1)S(1)}, u32[]{:S(2)}, u32[]{:S(2)}) collective-permute-start(bf16[32,768]{1,0:T(8,128)(2,1)S(1)} %get-tuple-element.47), channel_id=1, source_target_pairs={{0,2},{2,0},{4,6},{6,4},{8,10},{10,8},{12,14},{14,12},{16,18},{18,... | collective-permute-start | bytes 147464 | tf_op jit(solution)/shard_map/ppermute | solution.py:435
  7.9 1.9 %collective-permute-start.1 = (bf16[32,768]{1,0:T(8,128)(2,1)S(1)}, bf16[32,768]{1,0:T(8,128)(2,1)S(1)}, u32[]{:S(2)}, u32[]{:S(2)}) collective-permute-start(bf16[32,768]{1,0:T(8,128)(2,1)S(1)} %get-tuple-element.48), channel_id=1, source_target_pairs={{2,4},{4,2},{6,8},{8,6},{10,12},{12,10},{14,16},{16,14},{18,20},{2... | collective-permute-start | bytes 147464 | tf_op jit(solution)/shard_map/ppermute | solution.py:434

commit v9 on v8

--- a/solution.py
+++ b/solution.py
@@ -78,10 +78,13 @@
             first, second = (s_ref[0:32, row(2 * pair + j)].astype(F32) for j in range(2))
             base_ref[to, i * 16 : i * 16 + 16, row(1)] = pooled(first, second)
         base_ref[to, :, row(2, 3)] = s_ref[32:64, row(cot, 3)]
-    even_ref[:, row(0, SLOTS)] = base_ref[odd]
-    odd_ref[:, row(0, SLOTS)] = base_ref[1 - odd]
-    even_ref[:, row(SLOTS, sides)] = jnp.zeros((32, sides * COLS), BF)
-    odd_ref[:, row(SLOTS, sides)] = jnp.zeros((32, sides * COLS), BF)
+        for side in range(sides):
+            for z in range(2):
+                kept = lane % 64 >= 48 if to == 0 else lane % 64 < 16
+                value = jnp.where(kept, strips[z][side], 0.0).astype(BF)
+                base_ref[to, z * 16 : z * 16 + 16, row(SLOTS + side)] = value
+    even_ref[...] = base_ref[odd]
+    odd_ref[...] = base_ref[1 - odd]
 
 
 def pack(features, cotangent, sides):
@@ -97,7 +100,7 @@
         ),
         scratch_shapes=[
             pltpu.VMEM((C1 * ROWS * 2, COLS), F32),
-            pltpu.VMEM((2, 32, SLOTS * COLS), BF),
+            pltpu.VMEM((2, 32, (SLOTS + sides) * COLS), BF),
         ],
         compiler_params=params(),
         cost_estimate=pl.CostEstimate(flops=10**6, bytes_accessed=10**6, transcendentals=0),
@@ -196,7 +199,7 @@
 
 def rest_kernel(
     counts, sides,
-    odd_ref, even_ref, pst_own, jf_own, gst_own, pre_own, prb_own, rg_own, rgb_own,
+    odd_ref, even_ref, corners_ref, pst_own, jf_own, gst_own, pre_own, prb_own, rg_own, rgb_own,
     wo_ref, wg_ref, wc_ref, wq_ref,
     out_ref, gf_ref, gw_ref,
     halo_ref, jst_ref, gst_ref, gsb_ref, pst_ref, psb_ref, qst_ref,
@@ -209,15 +212,15 @@
     has_above, has_below = flag(w > 0), flag(w < counts[0] - 1)
 
     odd = w % 2
-    halo_ref[1 - odd] = even_ref[...]
-    halo_ref[odd] = odd_ref[...]
+    halo_ref[1 - odd] = even_ref[:, row(0, SLOTS)]
+    halo_ref[odd] = odd_ref[:, row(0, SLOTS)]
+    columns = [corners_ref[:, row(side)].astype(F32) for side in range(sides)]
 
     pst_ref[:, row(2, 8)] = pst_own[...]
     gst_ref[:, row(3, ROWS)] = gst_own[...]
     for d in range(3):
         jst_ref[d * 64 : d * 64 + 32, row(1, ROWS)] = jf_own[d * 32 : d * 32 + 32, :]
     for i in range(2):
-        columns = [halo_ref[i, :, row(SLOTS + side)].astype(F32) for side in range(sides)]
         lane = HALO * (ROWS - HALO) if i == 0 else 0
         sides_f = [beside(columns, lane + HALO * r) for r in range(HALO)]
         near = HALO - 1 if i == 0 else 0
@@ -335,7 +338,7 @@
             jax.ShapeDtypeStruct((256, COLS), BF),
         ),
         scratch_shapes=[
-            pltpu.VMEM((2, 32, (SLOTS + sides) * COLS), BF),
+            pltpu.VMEM((2, 32, SLOTS * COLS), BF),
             v(192, 18, BF),
             v(96, 22, BF), v(96, 6, BF),
             v(48, 12, BF), v(48, 4, BF),
@@ -400,41 +403,83 @@
     )(total)
 
 
+def matrices_kernel(
+    fine_ref, coarse_ref, wo_ref, wg_ref, wc_ref, wq_ref, wide_ref, pieces_ref, blocks_ref
+):
+    lane = lanes_of((C1, COLS))
+    wide_ref[:, 0:48] = fine_ref[...].astype(F32)
+    for ky in range(3):
+        for zo in range(2):
+            tiles = [jnp.zeros((C1, COLS), F32) for _ in range(2)]
+            for kx in range(3):
+                at = ((ky * 3 + 1 - zo) * 3 + kx) * 16
+                first, second = (wide_ref[at + i : at + i + 16, :] for i in (0, 48))
+                both = (first + second).astype(BF).astype(F32)
+                piece = jnp.where(lane < 32, pltpu.roll(second, 16, 1), pltpu.roll(both, 16, 1))
+                piece = jnp.where(lane < 16, first, jnp.where(lane < 64, piece, 0.0))
+                spot = (2 - kx) * 32 + zo * 16
+                pieces_ref[2 - ky, spot : spot + 16, :] = piece
+                tiles[kx // 2] = tiles[kx // 2] + (pltpu.roll(piece, 64, 1) if kx == 1 else piece)
+            spot = ky * 32 + zo * 16
+            wo_ref[spot : spot + 16, 0:128] = tiles[0].astype(BF)
+            wo_ref[spot : spot + 16, 128:192] = tiles[1][:, 0:64].astype(BF)
+    wide_ref[:, 0:32] = coarse_ref[...].astype(F32)
+    for ky in range(3):
+        total = jnp.zeros((C1, COLS), F32)
+        for kx in range(3):
+            at = ((ky * 3 + 1) * 3 + kx) * 16
+            value = jnp.where(lane < 32, wide_ref[at : at + 16, :], 0.0)
+            blocks_ref[ky, kx * 16 : kx * 16 + 16, :] = value
+            spot = (2 - kx) * 32
+            total = total + (pltpu.roll(value, spot, 1) if spot else value)
+        wq_ref[(2 - ky) * 16 : (2 - ky) * 16 + 16, :] = total[:, 0:96].astype(BF)
+    for d in range(3):
+        wg_ref[d * 64 : d * 64 + 64, :] = jnp.transpose(pieces_ref[d])[0:64, 0:96].astype(BF)
+        wc_ref[d * 32 : d * 32 + 32, :] = jnp.transpose(blocks_ref[d])[0:32, 0:48].astype(BF)
+
+
 def weight_matrices(coarse_weight, fine_weight):
-    fine = jnp.transpose(fine_weight, (2, 3, 4, 0, 1))
-    planes = []
-    for zo in range(2):
-        first, second = fine[:, 1 - zo], fine[:, 2 - zo]
-        both = (first[..., C1:].astype(F32) + second[..., C1:].astype(F32)).astype(BF)
-        planes.append(jnp.concatenate([first[..., :C1], second[..., :C1], both], -1))
-    stacked = jnp.stack(planes, 1)
-    wo = jnp.transpose(stacked, (0, 1, 3, 2, 4)).reshape(96, 192)
-    wg = jnp.transpose(stacked[::-1, :, ::-1], (0, 4, 2, 1, 3)).reshape(192, 96)
-    middle = coarse_weight[:, :, :, 1, :]
-    wc = jnp.transpose(middle, (2, 0, 3, 1)).reshape(96, 48)
-    wq = jnp.transpose(middle[:, :, ::-1, ::-1], (2, 1, 3, 0)).reshape(48, 96)
-    return wo, wg, wc, wq
+    fine = jnp.transpose(fine_weight, (2, 3, 4, 0, 1)).reshape(432, 48)
+    coarse = jnp.transpose(coarse_weight, (2, 3, 4, 1, 0)).reshape(432, 32)
+    shape = lambda *dims: jax.ShapeDtypeStruct(dims, BF)
+    return pl.pallas_call(
+        matrices_kernel,
+        out_shape=(shape(96, 192), shape(192, 96), shape(96, 48), shape(48, 96)),
+        scratch_shapes=[
+            pltpu.VMEM((432, COLS), F32),
+            pltpu.VMEM((3, COLS, COLS), F32),
+            pltpu.VMEM((3, COLS, COLS), F32),
+        ],
+        compiler_params=params(),
+        cost_estimate=pl.CostEstimate(flops=10**6, bytes_accessed=10**6, transcendentals=0),
+        name="matrices",
+    )(fine, coarse)
+
+
+def beside_blocks(outer, narrow):
+    if outer.shape[1] == COLS:
+        return lax.ppermute(outer, "narrow", [(0, 1), (1, 0)])
+    right = lax.ppermute(outer[:, :COLS], "narrow", [(i + 1, i) for i in range(narrow - 1)])
+    left = lax.ppermute(outer[:, COLS:], "narrow", [(i, i + 1) for i in range(narrow - 1)])
+    return jnp.concatenate([right, left], 1)
 
 
 def shards(features, cotangent, coarse_weight, fine_weight):
     wide, narrow = lax.axis_size("wide"), lax.axis_size("narrow")
-    wo, wg, wc, wq = weight_matrices(coarse_weight, fine_weight)
     sides = 1 if narrow == 2 else 2
     own, strip, to_odd, to_even = pack(features, cotangent, sides)
-    if sides == 1:
-        columns = lax.ppermute(strip, "narrow", [(0, 1), (1, 0)])
-    else:
-        right = lax.ppermute(strip[:, :COLS], "narrow", [(i + 1, i) for i in range(narrow - 1)])
-        left = lax.ppermute(strip[:, COLS:], "narrow", [(i, i + 1) for i in range(narrow - 1)])
-        columns = jnp.concatenate([right, left], 1)
     swaps = lambda start: [
         pair for i in range(start, wide - 1, 2) for pair in ((i, i + 1), (i + 1, i))
     ]
-    with_columns = lambda message: lax.dynamic_update_slice(message, columns, (0, SLOTS * COLS))
-    odd = lax.ppermute(with_columns(to_odd), "wide", swaps(1))
-    even = lax.ppermute(with_columns(to_even), "wide", swaps(0))
+    odd = lax.ppermute(to_odd, "wide", swaps(1))
+    even = lax.ppermute(to_even, "wide", swaps(0))
+    columns = beside_blocks(strip, narrow)
+    wo, wg, wc, wq = weight_matrices(coarse_weight, fine_weight)
+    corners = odd[:, SLOTS * COLS :] + even[:, SLOTS * COLS :]
+    corners, columns = lax.optimization_barrier((corners, columns))
+    corners = beside_blocks(corners, narrow)
     stacks = own_rows(own, columns, wc, wg, sides)
-    output, grad_features, grads = rest((odd, even), stacks, (wo, wg, wc, wq), (wide, narrow), sides)
+    output, grad_features, grads = rest((odd, even, corners), stacks, (wo, wg, wc, wq), (wide, narrow), sides)
     devices = wide * narrow
     share = -(-256 // devices)
     grads = jnp.pad(grads, ((0, share * devices - 256), (0, 0))).reshape(devices, share, COLS)

time: 38.9 us -> 39.7 us (1.021)
  starting transfers between devices: 3.73 us -> 8.04 us
  blocking collectives: 25.4 us -> 21.6 us
  waiting for transfers between devices: 0.01 us -> 0.99 us
  local copies, waits for them, and re-layouts: 2.4 us -> 1.79 us
    ppermute x3 -> x4, starting transfers between devices: 3.73 us -> 8.04 us  [the longest x1 4.39 us: shards(): even = lax.ppermute(to_even, 'wide', swaps(0))]
    all_to_all x1, blocking collectives: 16.1 us -> 12.3 us  [shards(): parts = lax.all_to_all(grads, both, 0, 0, tiled=True)]
    unnamed x0 -> x4, local copies, waits for them, and re-layouts: none -> 1.79 us
    squeeze x2 -> x0, local copies, waits for them, and re-layouts: 1.6 us -> none  [the longest x1 0.82 us: weight_matrices(): first, second = (fine[:, 1 - zo], fine[:, 2 - zo])]
    ppermute x3 -> x4, waiting for transfers between devices: 0.01 us -> 0.99 us  [the longest x2 0.99 us: beside_blocks(): return lax.ppermute(outer, 'narrow', [(0, 1), (1, 0)])]
    reshape x6 -> x0, local copies, waits for them, and re-layouts: 0.65 us -> none  [the longest x2 0.23 us: weight_matrices(): wg = jnp.transpose(stacked[::-1, :, ::-1], (0, 4, 2, 1, 3)).reshape(192, 96)]
  transfers between devices with their start and end apart: 3 -> 4, of which waited for: 0 -> 1; matrix products, arithmetic and copies ran while one was open for 7% -> 0% of each run, Pallas kernels for 3% -> 4%
where the time goes in v9:
time: 39.7 us; the launch traced here: 39.4 us
  blocking collectives  21.6 us (54%)
  starting transfers between devices  8.04 us (20%)
  Pallas kernels  5.32 us (13%)
  local copies, waits for them, and re-layouts  1.79 us (5%)
  other arithmetic  1 us (3%)
  waiting for transfers between devices  0.99 us (2%)
  between operations  0.69 us (2%)
    all_to_all x1, blocking collectives, shards(): parts = lax.all_to_all(grads, both, 0, 0, tiled=True)  12.3 us
    all_to_all x1, blocking collectives, shards(): total = lax.all_to_all(add_up(parts), both, 0, 0, tiled=True)  9.3 us
    ppermute x1, starting transfers between devices, shards(): even = lax.ppermute(to_even, 'wide', swaps(0))  4.39 us
    ppermute x2, starting transfers between devices, beside_blocks(): return lax.ppermute(outer, 'narrow', [(0, 1), (1, 0)])  2.98 us
    pallas_call x1, Pallas kernels, rest(): pl.pallas_call(functools.partial(rest_kernel, counts, sides), out_shape=(...  2.47 us
    unnamed x4, local copies, waits for them, and re-layouts  1.79 us
    pallas_call x1, Pallas kernels, own_rows(): pl.pallas_call(functools.partial(own_kernel, sides), out_shape=(shape(48,...  1.24 us
    another operation x1, other arithmetic, pack(): jnp.stack([flat(features), flat(cotangent)])  0.99 us
  transfers between devices with their start and end apart: 4, of which 1 were waited for; matrix products, arithmetic and copies ran while one was open for 0% of the time, Pallas kernels for 4%

profile of v9, /device:TPU:0, one launch (start us, length us, event | category | flops | bytes accessed | tf_op | source)
XLA Modules:
  0.0 39.4 jit_solution(4964545287810520409)
XLA Ops:
  0.6 1.0 %pad_maximum_fusion.in_ref = bf16[2,512,128]{2,1,0:T(8,128)(2,1)S(1)} fusion(bf16[1,512,128]{2,1,0:T(8,128)(2,1)} %bitcast.22, bf16[1,512,128]{2,1,0:T(8,128)(2,1)} %bitcast.23), kind=kLoop, calls=%fused_computation | loop fusion | flops 131072 | bytes 524288 | tf_op jit(solution)/shard_map/stack | solution.py:108
  1.6 0.5 %pack.1 = (bf16[64,2048]{1,0:T(8,128)(2,1)S(1)}, bf16[32,128]{1,0:T(8,128)(2,1)S(1)}, bf16[32,768]{1,0:T(8,128)(2,1)S(1)}, bf16[32,768]{1,0:T(8,128)(2,1)S(1)}) custom-call(bf16[2,512,128]{2,1,0:T(8,128)(2,1)S(1)} %pad_maximum_fusion.in_ref), custom_call_target="tpu_custom_call" | custom-call | flops 1000000 | bytes 1000000 | tf_op jit(solution)/shard_map/pack/pallas_call | solution.py:93
  2.1 0.7 %collective-permute-start = (bf16[32,768]{1,0:T(8,128)(2,1)S(1)}, bf16[32,768]{1,0:T(8,128)(2,1)S(1)}, u32[]{:S(2)}, u32[]{:S(2)}) collective-permute-start(bf16[32,768]{1,0:T(8,128)(2,1)S(1)} %get-tuple-element.26), channel_id=1, source_target_pairs={{2,4},{4,2},{6,8},{8,6},{10,12},{12,10},{14,16},{16,14},{18,20},{2... | collective-permute-start | bytes 147464 | tf_op jit(solution)/shard_map/ppermute | solution.py:474
  2.8 4.4 %collective-permute-start.1 = (bf16[32,768]{1,0:T(8,128)(2,1)S(1)}, bf16[32,768]{1,0:T(8,128)(2,1)S(1)}, u32[]{:S(2)}, u32[]{:S(2)}) collective-permute-start(bf16[32,768]{1,0:T(8,128)(2,1)S(1)} %get-tuple-element.27), channel_id=1, source_target_pairs={{0,2},{2,0},{4,6},{6,4},{8,10},{10,8},{12,14},{14,12},{16,18},{18,... | collective-permute-start | bytes 147464 | tf_op jit(solution)/shard_map/ppermute | solution.py:475
  7.1 1.5 %collective-permute-start.2 = (bf16[32,128]{1,0:T(8,128)(2,1)S(1)}, bf16[32,128]{1,0:T(8,128)(2,1)S(1)}, u32[]{:S(2)}, u32[]{:S(2)}) collective-permute-start(bf16[32,128]{1,0:T(8,128)(2,1)S(1)} %get-tuple-element.28), channel_id=1, source_target_pairs={{0,1},{1,0},{2,3},{3,2},{4,5},{5,4},{6,7},{7,6},{8,9},{9,8},{10,11... | collective-permute-start | bytes 24584 | tf_op jit(solution)/shard_map/ppermute | solution.py:461
  8.6 0.0 copy-start
  8.6 0.9 %copy-done = bf16[16,48,3,3,3]{1,0,4,3,2:T(8,128)(2,1)S(1)} copy-done((bf16[16,48,3,3,3]{1,0,4,3,2:T(8,128)(2,1)S(1)}, bf16[16,48,3,3,3]{1,0,4,3,2:T(8,128)(2,1)}, u32[]{:S(2)}) %copy-start) | copy-done | bytes 41496
  9.5 0.0 copy-start.1
  9.5 0.9 %copy-done.1 = bf16[32,16,3,3,3]{0,1,4,3,2:T(8,128)(2,1)S(1)} copy-done((bf16[32,16,3,3,3]{0,1,4,3,2:T(8,128)(2,1)S(1)}, bf16[32,16,3,3,3]{0,1,4,3,2:T(8,128)(2,1)}, u32[]{:S(2)}) %copy-start.1) | copy-done | bytes 27672
  10.4 0.3 matrices.1
  10.7 0.0 collective-permute-done.odd_ref
  10.7 0.0 collective-permute-done.1.even_ref
  10.7 0.0 collective-permute-done.2.columns_ref
  10.8 1.5 %collective-permute-start.3 = (bf16[32,128]{1,0:T(8,128)(2,1)S(1)}, bf16[32,128]{1,0:T(8,128)(2,1)S(1)}, u32[]{:S(2)}, u32[]{:S(2)}) collective-permute-start(bf16[32,128]{1,0:T(8,128)(2,1)S(1)} %slice_add_fusion), channel_id=1, source_target_pairs={{0,1},{1,0},{2,3},{3,2},{4,5},{5,4},{6,7},{7,6},{8,9},{9,8},{10,11... | collective-permute-start | bytes 24584 | tf_op jit(solution)/shard_map/ppermute | solution.py:461
  12.3 1.2 %own_rows.1 = (bf16[48,1024]{1,0:T(8,128)(2,1)S(1)}, bf16[96,2048]{1,0:T(8,128)(2,1)S(1)}, bf16[96,2048]{1,0:T(8,128)(2,1)S(1)}, f32[96,1024]{1,0:T(8,128)S(1)},...) custom-call(bf16[64,2048]{1,0:T(8,128)(2,1)S(1)} %get-tuple-element.30.s_ref, ...), custom_call_target="tpu_custom_call" | custom-call | flops 1000000000 | bytes 4000000 | tf_op jit(solution)/shard_map/own_rows/pallas_call | solution.py:183
  13.5 0.9 %collective-permute-done.3.corners_ref = bf16[32,128]{1,0:T(8,128)(2,1)S(1)} collective-permute-done((bf16[32,128]{1,0:T(8,128)(2,1)S(1)}, bf16[32,128]{1,0:T(8,128)(2,1)S(1)}, u32[]{:S(2)}, u32[]{:S(2)}) %collective-permute-start.3) | collective-permute-done | bytes 8224 | tf_op jit(solution)/shard_map/ppermute | solution.py:461
  14.5 2.5 %rest.1 = (bf16[512,128]{1,0:T(8,128)(2,1)}, bf16[512,128]{1,0:T(8,128)(2,1)}, bf16[256,128]{1,0:T(8,128)(2,1)S(1)}) custom-call(bf16[32,768]{1,0:T(8,128)(2,1)S(1)} %collective-permute-done.odd_ref, bf16[32,768]{1,0:T(8,128)(2,1)S(1)} %collective-permute-done.1.even_ref, bf16[32,128]{1,0:T(8,128)(2,1)S(1)} %collective-permute-done.3.corners_ref, ...), custom_call_target="tpu_custom_call" | custom-call | flops 1000000000 | bytes 4000000 | tf_op jit(solution)/shard_map/rest/pallas_call | solution.py:333
  16.9 12.3 %all_to_all.10.parts_ref = bf16[32,8,128]{2,1,0:T(8,128)(2,1)S(1)} all-to-all(bf16[32,8,128]{2,1,0:T(8,128)(2,1)S(1)} %bitcast.21), channel_id=1, replica_groups=mesh['wide'=16,'narrow'=2] {'wide','narrow'}, dimensions={0} | all-to-all | bytes 131072 | tf_op jit(solution)/shard_map/all_to_all | solution.py:487
  29.3 9.3 %all_to_all.11 = bf16[32,8,128]{2,1,0:T(8,128)(2,1)S(1)} all-to-all(bf16[32,8,128]{2,1,0:T(8,128)(2,1)S(1)} %add_up.1), channel_id=1, replica_groups=mesh['wide'=16,'narrow'=2] {'wide','narrow'}, dimensions={0} | all-to-all | bytes 131072 | tf_op jit(solution)/shard_map/all_to_all | solution.py:488
  38.6 0.9 %spread.1 = (f32[432,48]{1,0:T(8,128)}, f32[432,32]{1,0:T(8,128)}) custom-call(bf16[256,128]{1,0:T(8,128)(2,1)S(1)} %bitcast.18), custom_call_target="tpu_custom_call" | custom-call | tf_op jit(solution)/shard_map/spread/pallas_call | solution.py:395
  (2 shorter events, 0.0 us)
Async XLA Ops:
  2.1 8.6 %collective-permute-start = (bf16[32,768]{1,0:T(8,128)(2,1)S(1)}, bf16[32,768]{1,0:T(8,128)(2,1)S(1)}, u32[]{:S(2)}, u32[]{:S(2)}) collective-permute-start(bf16[32,768]{1,0:T(8,128)(2,1)S(1)} %get-tuple-element.26), channel_id=1, source_target_pairs={{2,4},{4,2},{6,8},{8,6},{10,12},{12,10},{14,16},{16,14},{18,20},{2... | collective-permute-start | bytes 147464 | tf_op jit(solution)/shard_map/ppermute | solution.py:474
  2.8 8.0 %collective-permute-start.1 = (bf16[32,768]{1,0:T(8,128)(2,1)S(1)}, bf16[32,768]{1,0:T(8,128)(2,1)S(1)}, u32[]{:S(2)}, u32[]{:S(2)}) collective-permute-start(bf16[32,768]{1,0:T(8,128)(2,1)S(1)} %get-tuple-element.27), channel_id=1, source_target_pairs={{0,2},{2,0},{4,6},{6,4},{8,10},{10,8},{12,14},{14,12},{16,18},{18,... | collective-permute-start | bytes 147464 | tf_op jit(solution)/shard_map/ppermute | solution.py:475
  7.1 3.7 %collective-permute-start.2 = (bf16[32,128]{1,0:T(8,128)(2,1)S(1)}, bf16[32,128]{1,0:T(8,128)(2,1)S(1)}, u32[]{:S(2)}, u32[]{:S(2)}) collective-permute-start(bf16[32,128]{1,0:T(8,128)(2,1)S(1)} %get-tuple-element.28), channel_id=1, source_target_pairs={{0,1},{1,0},{2,3},{3,2},{4,5},{5,4},{6,7},{7,6},{8,9},{9,8},{10,11... | collective-permute-start | bytes 24584 | tf_op jit(solution)/shard_map/ppermute | solution.py:461
  8.6 0.9 %copy-start = (bf16[16,48,3,3,3]{1,0,4,3,2:T(8,128)(2,1)S(1)}, bf16[16,48,3,3,3]{1,0,4,3,2:T(8,128)(2,1)}, u32[]{:S(2)}) copy-start(bf16[16,48,3,3,3]{1,0,4,3,2:T(8,128)(2,1)} %param.7) | copy-start | bytes 124420
  9.5 0.9 %copy-start.1 = (bf16[32,16,3,3,3]{0,1,4,3,2:T(8,128)(2,1)S(1)}, bf16[32,16,3,3,3]{0,1,4,3,2:T(8,128)(2,1)}, u32[]{:S(2)}) copy-start(bf16[32,16,3,3,3]{0,1,4,3,2:T(8,128)(2,1)} %param.6) | copy-start | bytes 82948
  10.8 3.7 %collective-permute-start.3 = (bf16[32,128]{1,0:T(8,128)(2,1)S(1)}, bf16[32,128]{1,0:T(8,128)(2,1)S(1)}, u32[]{:S(2)}, u32[]{:S(2)}) collective-permute-start(bf16[32,128]{1,0:T(8,128)(2,1)S(1)} %slice_add_fusion), channel_id=1, source_target_pairs={{0,1},{1,0},{2,3},{3,2},{4,5},{5,4},{6,7},{7,6},{8,9},{9,8},{10,11... | collective-permute-start | bytes 24584 | tf_op jit(solution)/shard_map/ppermute | solution.py:461

commit v10 on v9

--- a/solution.py
+++ b/solution.py
@@ -47,6 +47,8 @@
 
 
 SLOTS = 5
+CELLS = C1 * ROWS * 2
+TAPS = 27 * C1
 
 
 def pack_kernel(sides, in_ref, s_ref, strip_ref, odd_ref, even_ref, wide_ref, base_ref):
@@ -55,7 +57,7 @@
     odd = lax.axis_index("wide") % 2
     strips = [[jnp.zeros((C1, COLS), F32) for _ in range(sides)] for _ in range(2)]
     for a in range(2):
-        wide_ref[...] = in_ref[a].astype(F32)
+        wide_ref[...] = in_ref[a * CELLS : (a + 1) * CELLS, :].astype(F32)
         for z in range(2):
             chans = slice(a * 32 + z * 16, a * 32 + z * 16 + 16)
             for y in range(ROWS):
@@ -87,8 +89,15 @@
     odd_ref[...] = base_ref[1 - odd]
 
 
-def pack(features, cotangent, sides):
-    flat = lambda a: a.reshape(C1 * ROWS * 2, COLS)
+def stack(features, cotangent, coarse_weight, fine_weight):
+    flat = lambda a: a.reshape(CELLS, COLS)
+    fine = jnp.transpose(fine_weight, (2, 3, 4, 0, 1)).reshape(TAPS, 48)
+    coarse = jnp.transpose(coarse_weight, (2, 3, 4, 1, 0)).reshape(TAPS, 32)
+    weights = jnp.concatenate([fine, coarse, jnp.zeros((TAPS, 48), BF)], 1)
+    return jnp.concatenate([flat(features), flat(cotangent), weights], 0)
+
+
+def pack(stacked, sides):
     message = jax.ShapeDtypeStruct((32, (SLOTS + sides) * COLS), BF)
     return pl.pallas_call(
         functools.partial(pack_kernel, sides),
@@ -105,7 +114,7 @@
         compiler_params=params(),
         cost_estimate=pl.CostEstimate(flops=10**6, bytes_accessed=10**6, transcendentals=0),
         name="pack",
-    )(jnp.stack([flat(features), flat(cotangent)]))
+    )(stacked)
 
 
 def beside(columns, at):
@@ -404,10 +413,10 @@
 
 
 def matrices_kernel(
-    fine_ref, coarse_ref, wo_ref, wg_ref, wc_ref, wq_ref, wide_ref, pieces_ref, blocks_ref
+    in_ref, wo_ref, wg_ref, wc_ref, wq_ref, wide_ref, pieces_ref, blocks_ref
 ):
     lane = lanes_of((C1, COLS))
-    wide_ref[:, 0:48] = fine_ref[...].astype(F32)
+    wide_ref[...] = in_ref[2 * CELLS : 2 * CELLS + TAPS, :].astype(F32)
     for ky in range(3):
         for zo in range(2):
             tiles = [jnp.zeros((C1, COLS), F32) for _ in range(2)]
@@ -423,12 +432,12 @@
             spot = ky * 32 + zo * 16
             wo_ref[spot : spot + 16, 0:128] = tiles[0].astype(BF)
             wo_ref[spot : spot + 16, 128:192] = tiles[1][:, 0:64].astype(BF)
-    wide_ref[:, 0:32] = coarse_ref[...].astype(F32)
     for ky in range(3):
         total = jnp.zeros((C1, COLS), F32)
         for kx in range(3):
             at = ((ky * 3 + 1) * 3 + kx) * 16
-            value = jnp.where(lane < 32, wide_ref[at : at + 16, :], 0.0)
+            value = pltpu.roll(wide_ref[at : at + 16, :], 80, 1)
+            value = jnp.where(lane < 32, value, 0.0)
             blocks_ref[ky, kx * 16 : kx * 16 + 16, :] = value
             spot = (2 - kx) * 32
             total = total + (pltpu.roll(value, spot, 1) if spot else value)
@@ -438,22 +447,20 @@
         wc_ref[d * 32 : d * 32 + 32, :] = jnp.transpose(blocks_ref[d])[0:32, 0:48].astype(BF)
 
 
-def weight_matrices(coarse_weight, fine_weight):
-    fine = jnp.transpose(fine_weight, (2, 3, 4, 0, 1)).reshape(432, 48)
-    coarse = jnp.transpose(coarse_weight, (2, 3, 4, 1, 0)).reshape(432, 32)
+def weight_matrices(stacked):
     shape = lambda *dims: jax.ShapeDtypeStruct(dims, BF)
     return pl.pallas_call(
         matrices_kernel,
         out_shape=(shape(96, 192), shape(192, 96), shape(96, 48), shape(48, 96)),
         scratch_shapes=[
-            pltpu.VMEM((432, COLS), F32),
+            pltpu.VMEM((TAPS, COLS), F32),
             pltpu.VMEM((3, COLS, COLS), F32),
             pltpu.VMEM((3, COLS, COLS), F32),
         ],
         compiler_params=params(),
         cost_estimate=pl.CostEstimate(flops=10**6, bytes_accessed=10**6, transcendentals=0),
         name="matrices",
-    )(fine, coarse)
+    )(stacked)
 
 
 def beside_blocks(outer, narrow):
@@ -467,14 +474,15 @@
 def shards(features, cotangent, coarse_weight, fine_weight):
     wide, narrow = lax.axis_size("wide"), lax.axis_size("narrow")
     sides = 1 if narrow == 2 else 2
-    own, strip, to_odd, to_even = pack(features, cotangent, sides)
+    stacked = stack(features, cotangent, coarse_weight, fine_weight)
+    own, strip, to_odd, to_even = pack(stacked, sides)
     swaps = lambda start: [
         pair for i in range(start, wide - 1, 2) for pair in ((i, i + 1), (i + 1, i))
     ]
     odd = lax.ppermute(to_odd, "wide", swaps(1))
     even = lax.ppermute(to_even, "wide", swaps(0))
     columns = beside_blocks(strip, narrow)
-    wo, wg, wc, wq = weight_matrices(coarse_weight, fine_weight)
+    wo, wg, wc, wq = weight_matrices(stacked)
     corners = odd[:, SLOTS * COLS :] + even[:, SLOTS * COLS :]
     corners, columns = lax.optimization_barrier((corners, columns))
     corners = beside_blocks(corners, narrow)

time: 39.7 us -> 39.9 us (level)
  waiting for transfers between devices: 0.99 us -> 2.79 us
  local copies, waits for them, and re-layouts: 1.79 us -> 0.02 us
    ppermute x2, waiting for transfers between devices: 0.99 us -> 2.78 us  [beside_blocks(): return lax.ppermute(outer, 'narrow', [(0, 1), (1, 0)])]
    unnamed x4 -> x0, local copies, waits for them, and re-layouts: 1.79 us -> none
    concatenate x0 -> x1, other arithmetic: none -> 1.21 us  [stack(): return jnp.concatenate([flat(features), flat(cotangent), weights], 0)]
    another operation x1 -> x0, other arithmetic: 0.99 us -> none  [pack(): jnp.stack([flat(features), flat(cotangent)])]
  transfers between devices with their start and end apart: 4 -> 4, of which waited for: 1 -> 2; matrix products, arithmetic and copies ran while one was open for 0% -> 0% of each run, Pallas kernels for 4% -> 4%
where the time goes in v10:
time: 39.9 us; the launch traced here: 39.7 us
  blocking collectives  21.6 us (54%)
  starting transfers between devices  8.04 us (20%)
  Pallas kernels  5.31 us (13%)
  waiting for transfers between devices  2.79 us (7%)
  other arithmetic  1.21 us (3%)
  between operations  0.69 us (2%)
    all_to_all x1, blocking collectives, shards(): parts = lax.all_to_all(grads, both, 0, 0, tiled=True)  12.3 us
    all_to_all x1, blocking collectives, shards(): total = lax.all_to_all(add_up(parts), both, 0, 0, tiled=True)  9.3 us
    ppermute x1, starting transfers between devices, shards(): even = lax.ppermute(to_even, 'wide', swaps(0))  4.39 us
    ppermute x2, starting transfers between devices, beside_blocks(): return lax.ppermute(outer, 'narrow', [(0, 1), (1, 0)])  2.98 us
    ppermute x2, waiting for transfers between devices, beside_blocks(): return lax.ppermute(outer, 'narrow', [(0, 1), (1, 0)])  2.78 us
    pallas_call x1, Pallas kernels, rest(): pl.pallas_call(functools.partial(rest_kernel, counts, sides), out_shape=(...  2.46 us
    pallas_call x1, Pallas kernels, own_rows(): pl.pallas_call(functools.partial(own_kernel, sides), out_shape=(shape(48,...  1.24 us
    concatenate x1, other arithmetic, stack(): return jnp.concatenate([flat(features), flat(cotangent), weights], 0)  1.21 us
  transfers between devices with their start and end apart: 4, of which 2 were waited for; matrix products, arithmetic and copies ran while one was open for 0% of the time, Pallas kernels for 4%

profile of v10, /device:TPU:0, one launch (start us, length us, event | category | flops | bytes accessed | tf_op | source)
XLA Modules:
  0.0 39.7 jit_solution(15175484087138652720)
XLA Ops:
  0.7 1.2 %maximum_maximum_fusion.in_ref = bf16[1456,128]{1,0:T(8,128)(2,1)S(1)} fusion(bf16[432,48]{1,0:T(8,128)(2,1)S(1)} %broadcast_in_dim.3, bf16[432,32]{1,0:T(8,128)(2,1)} %bitcast.22, bf16[432,48]{1,0:T(8,128)(2,1)} %bitcast.23, bf16[512,128]{1,0:T(8,128)(2,1)} %bitcast.20, bf16[512,128]{1,0:T(8,128)(2,1)} %bitcast.21), kind=kLoop, calls=%fused_computation | loop fusion | flops 1863680 | bytes 745472 | tf_op jit(solution)/shard_map/concatenate | solution.py:97
  1.9 0.5 %pack.1 = (bf16[64,2048]{1,0:T(8,128)(2,1)S(1)}, bf16[32,128]{1,0:T(8,128)(2,1)S(1)}, bf16[32,768]{1,0:T(8,128)(2,1)S(1)}, bf16[32,768]{1,0:T(8,128)(2,1)S(1)}) custom-call(bf16[1456,128]{1,0:T(8,128)(2,1)S(1)} %maximum_maximum_fusion.in_ref), custom_call_target="tpu_custom_call" | custom-call | flops 1000000 | bytes 1000000 | tf_op jit(solution)/shard_map/pack/pallas_call | solution.py:102
  2.3 0.7 %collective-permute-start = (bf16[32,768]{1,0:T(8,128)(2,1)S(1)}, bf16[32,768]{1,0:T(8,128)(2,1)S(1)}, u32[]{:S(2)}, u32[]{:S(2)}) collective-permute-start(bf16[32,768]{1,0:T(8,128)(2,1)S(1)} %get-tuple-element.26), channel_id=1, source_target_pairs={{2,4},{4,2},{6,8},{8,6},{10,12},{12,10},{14,16},{16,14},{18,20},{2... | collective-permute-start | bytes 147464 | tf_op jit(solution)/shard_map/ppermute | solution.py:482
  3.0 4.4 %collective-permute-start.1 = (bf16[32,768]{1,0:T(8,128)(2,1)S(1)}, bf16[32,768]{1,0:T(8,128)(2,1)S(1)}, u32[]{:S(2)}, u32[]{:S(2)}) collective-permute-start(bf16[32,768]{1,0:T(8,128)(2,1)S(1)} %get-tuple-element.27), channel_id=1, source_target_pairs={{0,2},{2,0},{4,6},{6,4},{8,10},{10,8},{12,14},{14,12},{16,18},{18,... | collective-permute-start | bytes 147464 | tf_op jit(solution)/shard_map/ppermute | solution.py:483
  7.4 1.5 %collective-permute-start.2 = (bf16[32,128]{1,0:T(8,128)(2,1)S(1)}, bf16[32,128]{1,0:T(8,128)(2,1)S(1)}, u32[]{:S(2)}, u32[]{:S(2)}) collective-permute-start(bf16[32,128]{1,0:T(8,128)(2,1)S(1)} %get-tuple-element.28), channel_id=1, source_target_pairs={{0,1},{1,0},{2,3},{3,2},{4,5},{5,4},{6,7},{7,6},{8,9},{9,8},{10,11... | collective-permute-start | bytes 24584 | tf_op jit(solution)/shard_map/ppermute | solution.py:468
  8.9 0.2 matrices.1
  9.1 0.0 collective-permute-done.odd_ref
  9.1 0.0 collective-permute-done.1.even_ref
  9.2 1.9 %collective-permute-done.2.columns_ref = bf16[32,128]{1,0:T(8,128)(2,1)S(1)} collective-permute-done((bf16[32,128]{1,0:T(8,128)(2,1)S(1)}, bf16[32,128]{1,0:T(8,128)(2,1)S(1)}, u32[]{:S(2)}, u32[]{:S(2)}) %collective-permute-start.2) | collective-permute-done | bytes 8224 | tf_op jit(solution)/shard_map/ppermute | solution.py:468
  11.0 1.5 %collective-permute-start.3 = (bf16[32,128]{1,0:T(8,128)(2,1)S(1)}, bf16[32,128]{1,0:T(8,128)(2,1)S(1)}, u32[]{:S(2)}, u32[]{:S(2)}) collective-permute-start(bf16[32,128]{1,0:T(8,128)(2,1)S(1)} %slice_add_fusion), channel_id=1, source_target_pairs={{0,1},{1,0},{2,3},{3,2},{4,5},{5,4},{6,7},{7,6},{8,9},{9,8},{10,11... | collective-permute-start | bytes 24584 | tf_op jit(solution)/shard_map/ppermute | solution.py:468
  12.5 1.2 %own_rows.1 = (bf16[48,1024]{1,0:T(8,128)(2,1)S(1)}, bf16[96,2048]{1,0:T(8,128)(2,1)S(1)}, bf16[96,2048]{1,0:T(8,128)(2,1)S(1)}, f32[96,1024]{1,0:T(8,128)S(1)},...) custom-call(bf16[64,2048]{1,0:T(8,128)(2,1)S(1)} %get-tuple-element.30.s_ref, ...), custom_call_target="tpu_custom_call" | custom-call | flops 1000000000 | bytes 4000000 | tf_op jit(solution)/shard_map/own_rows/pallas_call | solution.py:192
  13.8 0.9 %collective-permute-done.3.corners_ref = bf16[32,128]{1,0:T(8,128)(2,1)S(1)} collective-permute-done((bf16[32,128]{1,0:T(8,128)(2,1)S(1)}, bf16[32,128]{1,0:T(8,128)(2,1)S(1)}, u32[]{:S(2)}, u32[]{:S(2)}) %collective-permute-start.3) | collective-permute-done | bytes 8224 | tf_op jit(solution)/shard_map/ppermute | solution.py:468
  14.7 2.5 %rest.1 = (bf16[512,128]{1,0:T(8,128)(2,1)}, bf16[512,128]{1,0:T(8,128)(2,1)}, bf16[256,128]{1,0:T(8,128)(2,1)S(1)}) custom-call(bf16[32,768]{1,0:T(8,128)(2,1)S(1)} %collective-permute-done.odd_ref, bf16[32,768]{1,0:T(8,128)(2,1)S(1)} %collective-permute-done.1.even_ref, bf16[32,128]{1,0:T(8,128)(2,1)S(1)} %collective-permute-done.3.corners_ref, ...), custom_call_target="tpu_custom_call" | custom-call | flops 1000000000 | bytes 4000000 | tf_op jit(solution)/shard_map/rest/pallas_call | solution.py:342
  17.2 12.3 %all_to_all.10.parts_ref = bf16[32,8,128]{2,1,0:T(8,128)(2,1)S(1)} all-to-all(bf16[32,8,128]{2,1,0:T(8,128)(2,1)S(1)} %bitcast.19), channel_id=1, replica_groups=mesh['wide'=16,'narrow'=2] {'wide','narrow'}, dimensions={0} | all-to-all | bytes 131072 | tf_op jit(solution)/shard_map/all_to_all | solution.py:495
  29.5 9.3 %all_to_all.11 = bf16[32,8,128]{2,1,0:T(8,128)(2,1)S(1)} all-to-all(bf16[32,8,128]{2,1,0:T(8,128)(2,1)S(1)} %add_up.1), channel_id=1, replica_groups=mesh['wide'=16,'narrow'=2] {'wide','narrow'}, dimensions={0} | all-to-all | bytes 131072 | tf_op jit(solution)/shard_map/all_to_all | solution.py:496
  38.8 0.9 %spread.1 = (f32[432,48]{1,0:T(8,128)}, f32[432,32]{1,0:T(8,128)}) custom-call(bf16[256,128]{1,0:T(8,128)(2,1)S(1)} %bitcast.18), custom_call_target="tpu_custom_call" | custom-call | tf_op jit(solution)/shard_map/spread/pallas_call | solution.py:404
  (3 shorter events, 0.1 us)
Async XLA Ops:
  2.3 6.8 %collective-permute-start = (bf16[32,768]{1,0:T(8,128)(2,1)S(1)}, bf16[32,768]{1,0:T(8,128)(2,1)S(1)}, u32[]{:S(2)}, u32[]{:S(2)}) collective-permute-start(bf16[32,768]{1,0:T(8,128)(2,1)S(1)} %get-tuple-element.26), channel_id=1, source_target_pairs={{2,4},{4,2},{6,8},{8,6},{10,12},{12,10},{14,16},{16,14},{18,20},{2... | collective-permute-start | bytes 147464 | tf_op jit(solution)/shard_map/ppermute | solution.py:482
  3.0 6.2 %collective-permute-start.1 = (bf16[32,768]{1,0:T(8,128)(2,1)S(1)}, bf16[32,768]{1,0:T(8,128)(2,1)S(1)}, u32[]{:S(2)}, u32[]{:S(2)}) collective-permute-start(bf16[32,768]{1,0:T(8,128)(2,1)S(1)} %get-tuple-element.27), channel_id=1, source_target_pairs={{0,2},{2,0},{4,6},{6,4},{8,10},{10,8},{12,14},{14,12},{16,18},{18,... | collective-permute-start | bytes 147464 | tf_op jit(solution)/shard_map/ppermute | solution.py:483
  7.4 3.7 %collective-permute-start.2 = (bf16[32,128]{1,0:T(8,128)(2,1)S(1)}, bf16[32,128]{1,0:T(8,128)(2,1)S(1)}, u32[]{:S(2)}, u32[]{:S(2)}) collective-permute-start(bf16[32,128]{1,0:T(8,128)(2,1)S(1)} %get-tuple-element.28), channel_id=1, source_target_pairs={{0,1},{1,0},{2,3},{3,2},{4,5},{5,4},{6,7},{7,6},{8,9},{9,8},{10,11... | collective-permute-start | bytes 24584 | tf_op jit(solution)/shard_map/ppermute | solution.py:468
  11.0 3.7 %collective-permute-start.3 = (bf16[32,128]{1,0:T(8,128)(2,1)S(1)}, bf16[32,128]{1,0:T(8,128)(2,1)S(1)}, u32[]{:S(2)}, u32[]{:S(2)}) collective-permute-start(bf16[32,128]{1,0:T(8,128)(2,1)S(1)} %slice_add_fusion), channel_id=1, source_target_pairs={{0,1},{1,0},{2,3},{3,2},{4,5},{5,4},{6,7},{7,6},{8,9},{9,8},{10,11... | collective-permute-start | bytes 24584 | tf_op jit(solution)/shard_map/ppermute | solution.py:468

commit v11 on v10

--- a/solution.py
+++ b/solution.py
@@ -157,23 +157,39 @@
         ref[d * step : d * step + 32, row(at)] = a.astype(BF)
 
 
-def coarse_part(wg_ref, stack):
-    return jnp.concatenate(
-        [dot(wg_ref[d * 64 + 32 : d * 64 + 64, :], stack) for d in range(3)], 0
-    )
+def coarse_row(values, totals, keeps):
+    act, grad = [], []
+    for value, total, kept in zip(values, totals, keeps):
+        sig = 1.0 / (1.0 + jnp.exp(-value))
+        act.append((value * sig * kept).astype(BF).astype(F32))
+        grad_act = pair_sum(total).astype(BF).astype(F32)
+        grad_pre = grad_act * (sig * (1.0 + value * (1.0 - sig)))
+        grad.append((grad_pre * kept).astype(BF).astype(F32))
+    acts = [act[0] if d == 1 else turn(act[0], act[1], d - 1)[0] for d in range(3)]
+    grads = [grad[0] if d == 1 else turn(grad[0], grad[1], 2 * (d - 1))[0] for d in range(3)]
+    return [a.astype(BF) for a in acts], [g.astype(BF) for g in grads]
+
+
+def column_masks(count):
+    n = lax.axis_index("narrow")
+    flag = lambda is_there: jnp.where(is_there, 1.0, 0.0)
+    return jnp.where(lanes_of((C2, COLS)) < 64, flag(n < count - 1), flag(n > 0))
+
+
+INNER = range(1, ROWS // 2 - 1)
 
 
 def own_kernel(
-    sides,
-    s_ref, columns_ref, wc_ref, wg_ref,
-    pst_ref, jf_ref, gst_ref, pre_ref, prb_ref, rg_ref, rgb_ref,
+    counts, sides,
+    s_ref, columns_ref, wo_ref, wc_ref, wg_ref,
+    pst_ref, jst_ref, gst_ref, qst_ref, pre_ref, prb_ref, rg_ref, rgb_ref, ro_ref,
     psb_ref, gsb_ref,
 ):
     columns = [columns_ref[:, row(side)].astype(F32) for side in range(sides)]
     last = None
     for y in range(ROWS):
         main, side = s_ref[0:32, row(y)].astype(F32), beside(columns, HALO * y)
-        put_features(main, side, jf_ref, 32, y)
+        put_features(main, side, jst_ref, 64, y)
         if y % 2 == 1:
             means = [pooled(a, b) for a, b in zip(last, (main, side))]
             put_pooled(*means, pst_ref, psb_ref, y // 2, y // 2)
@@ -183,18 +199,40 @@
     pre_ref[...] = dot(wc_ref[...], pst_ref[...])
     prb_ref[...] = dot(wc_ref[...], psb_ref[...])
     rg_ref[...] = dot(wg_ref[...], gst_ref[...])
-    rgb_ref[...] = coarse_part(wg_ref, gsb_ref[...])
-
-
-def own_rows(s, columns, wc, wg, sides):
+    rgb_ref[...] = dot(wg_ref[96:192, :], gsb_ref[...])
+    there = column_masks(counts[1])
+    for at in INNER:
+        values = [
+            sum(ref[d * 32 : d * 32 + 32, row(at + d - 1)] for d in range(3)) for ref in (pre_ref, prb_ref)
+        ]
+        totals = [
+            sum(
+                ref[lo + d * 32 : lo + d * 32 + 32, row(r + d - 1)]
+                for r in (2 * at, 2 * at + 1)
+                for d in range(3)
+            )
+            for ref, lo in ((rg_ref, 96), (rgb_ref, 0))
+        ]
+        acts, grads = coarse_row(values, totals, (1.0, there))
+        for d in range(3):
+            for r in (2 * at, 2 * at + 1):
+                jst_ref[d * 64 + 32 : d * 64 + 64, row(r)] = acts[d]
+            qst_ref[d * 32 : d * 32 + 32, row(at - 1)] = grads[d]
+    for r in (0, 1, ROWS - 2, ROWS - 1):
+        for d in range(3):
+            jst_ref[d * 64 + 32 : d * 64 + 64, row(r)] = jnp.zeros((C2, COLS), BF)
+    ro_ref[...] = dot(wo_ref[...], jst_ref[:, row(2, ROWS - 4)])
+
+
+def own_rows(s, columns, wo, wc, wg, counts, sides):
     half = ROWS // 2
     shape = lambda rows_, lanes_, kind: jax.ShapeDtypeStruct((rows_, lanes_ * COLS), kind)
     return pl.pallas_call(
-        functools.partial(own_kernel, sides),
+        functools.partial(own_kernel, counts, sides),
         out_shape=(
-            shape(48, half, BF), shape(96, ROWS, BF), shape(96, ROWS, BF),
+            shape(48, half, BF), shape(192, ROWS, BF), shape(96, ROWS, BF), shape(96, len(INNER), BF),
             shape(96, half, F32), shape(96, half, F32),
-            shape(192, ROWS, F32), shape(96, ROWS, F32),
+            shape(192, ROWS, F32), shape(96, ROWS, F32), shape(96, ROWS - 4, F32),
         ),
         scratch_shapes=[
             pltpu.VMEM((48, half * COLS), BF),
@@ -203,21 +241,20 @@
         compiler_params=params(),
         cost_estimate=pl.CostEstimate(flops=10**9, bytes_accessed=4 * 10**6, transcendentals=0),
         name="own_rows",
-    )(s, columns, wc, wg)
+    )(s, columns, wo, wc, wg)
 
 
 def rest_kernel(
     counts, sides,
-    odd_ref, even_ref, corners_ref, pst_own, jf_own, gst_own, pre_own, prb_own, rg_own, rgb_own,
+    odd_ref, even_ref, corners_ref, pst_own, jst_own, gst_own, qst_own, pre_own, prb_own, rg_own, rgb_own, ro_own,
     wo_ref, wg_ref, wc_ref, wq_ref,
     out_ref, gf_ref, gw_ref,
     halo_ref, jst_ref, gst_ref, gsb_ref, pst_ref, psb_ref, qst_ref,
-    pre_ref, prb_ref, rg_ref, rgb_ref, ro_ref, rq_ref, flat_ref, fa_ref, fb_ref, fc_ref,
+    pre_ref, prb_ref, rg_ref, rgb_ref, ro_ref, rq_ref, flat_ref, gl_ref, jl_ref, pl_ref, ql_ref,
 ):
-    w, n = lax.axis_index("wide"), lax.axis_index("narrow")
-    lane32 = lanes_of((C2, COLS))
+    w = lax.axis_index("wide")
+    there = column_masks(counts[1])
     flag = lambda is_there: jnp.where(is_there, 1.0, 0.0)
-    has_left, has_right = flag(n > 0), flag(n < counts[1] - 1)
     has_above, has_below = flag(w > 0), flag(w < counts[0] - 1)
 
     odd = w % 2
@@ -227,8 +264,8 @@
 
     pst_ref[:, row(2, 8)] = pst_own[...]
     gst_ref[:, row(3, ROWS)] = gst_own[...]
-    for d in range(3):
-        jst_ref[d * 64 : d * 64 + 32, row(1, ROWS)] = jf_own[d * 32 : d * 32 + 32, :]
+    jst_ref[:, row(1, ROWS)] = jst_own[...]
+    qst_ref[:, row(2, len(INNER))] = qst_own[...]
     for i in range(2):
         lane = HALO * (ROWS - HALO) if i == 0 else 0
         sides_f = [beside(columns, lane + HALO * r) for r in range(HALO)]
@@ -245,7 +282,7 @@
         pre_ref[:, row(2 * i, 2)] = dot(wc_ref[...], pst_ref[:, row(10 * i, 2)])
         rg_ref[:, row(3 * i, 3)] = dot(wg_ref[...], gst_ref[:, row(19 * i, 3)])
     prb_ref[...] = dot(wc_ref[...], psb_ref[...])
-    rgb_ref[...] = coarse_part(wg_ref, gsb_ref[...])
+    rgb_ref[...] = dot(wg_ref[96:192, :], gsb_ref[...])
 
     def part(own, halo, lo, size, at, edge, length):
         if at < edge:
@@ -254,37 +291,31 @@
             return own[lo : lo + size, row(at - edge)]
         return halo[lo : lo + size, row(at - length)]
 
-    for at in range(10):
+    for at in (0, 1, 8, 9):
         keep = has_above if at == 0 else has_below if at == 9 else 1.0
-        keep_side = keep * jnp.where(lane32 < 64, has_right, has_left)
-        act, grad = [], []
-        for pre, joined, base, size, kept in (
-            ((pre_own, pre_ref), (rg_own, rg_ref), 32, 64, keep),
-            ((prb_own, prb_ref), (rgb_own, rgb_ref), 0, 32, keep_side),
-        ):
-            value = sum(part(*pre, d * 32, 32, at + d, 2, 8) for d in range(3))
-            sig = 1.0 / (1.0 + jnp.exp(-value))
-            act.append((value * sig * kept).astype(BF).astype(F32))
-            total = sum(
-                part(*joined, d * size + base, 32, r + d, 3, ROWS)
+        values = [
+            sum(part(own, halo, d * 32, 32, at + d, 2, 8) for d in range(3))
+            for own, halo in ((pre_own, pre_ref), (prb_own, prb_ref))
+        ]
+        totals = [
+            sum(
+                part(own, halo, lo + d * 32, 32, r + d, 3, ROWS)
                 for r in (2 * at, 2 * at + 1)
                 for d in range(3)
             )
-            grad_act = pair_sum(total).astype(BF).astype(F32)
-            grad_pre = grad_act * (sig * (1.0 + value * (1.0 - sig)))
-            grad.append((grad_pre * kept).astype(BF).astype(F32))
+            for own, halo, lo in ((rg_own, rg_ref, 96), (rgb_own, rgb_ref, 0))
+        ]
+        acts, grads = coarse_row(values, totals, (keep, keep * there))
         for d in range(3):
-            a = act[0] if d == 1 else turn(act[0], act[1], d - 1)[0]
-            a = a.astype(BF)
             for r in (2 * at - 1, 2 * at):
                 if 0 <= r < 18:
-                    jst_ref[d * 64 + 32 : d * 64 + 64, row(r)] = a
-            q = grad[0] if d == 1 else turn(grad[0], grad[1], 2 * (d - 1))[0]
-            qst_ref[d * 32 : d * 32 + 32, row(at)] = q.astype(BF)
-
-    ro_ref[...] = dot(wo_ref[...], jst_ref[...])
+                    jst_ref[d * 64 + 32 : d * 64 + 64, row(r)] = acts[d]
+            qst_ref[d * 32 : d * 32 + 32, row(at)] = grads[d]
+
+    for i in range(2):
+        ro_ref[:, row(3 * i, 3)] = dot(wo_ref[...], jst_ref[:, row(15 * i, 3)])
     for y in range(ROWS):
-        value = ro_ref[0:32, row(y)] + ro_ref[32:64, row(y + 1)] + ro_ref[64:96, row(y + 2)]
+        value = sum(part(ro_own, ro_ref, d * 32, 32, y + d, 3, ROWS - 4) for d in range(3))
         for z in range(2):
             flat_ref[pl.ds(2 * y + z, C1, stride=2 * ROWS), :] = value[z * 16 : z * 16 + 16]
     out_ref[...] = flat_ref[...].astype(BF)
@@ -297,32 +328,32 @@
             for z in range(2):
                 total = coarse
                 for d in range(3):
-                    total = total + part(rg_own, rg_ref, d * 64 + z * 16, 16, y + 2 + d, 3, ROWS)
+                    total = total + part(rg_own, rg_ref, d * 32 + z * 16, 16, y + 2 + d, 3, ROWS)
                 flat_ref[pl.ds(2 * y + z, C1, stride=2 * ROWS), :] = total
     gf_ref[...] = flat_ref[...].astype(BF)
 
     own = row(1, ROWS)
-    fa_ref[0:16, :] = jst_ref[64:80, own]
-    fa_ref[16:48, :] = jst_ref[96:128, own]
-    fa_ref[48:64, :] = jst_ref[64:80, own]
-    fa_ref[64:96, :] = jst_ref[96:128, own]
-    fa_ref[96:128, :] = jnp.zeros((32, ROWS * COLS), BF)
-    fb_ref[0:48, :] = jst_ref[80:128, own]
-    fb_ref[48:96, :] = jst_ref[80:128, own]
-    fb_ref[96:128, :] = jnp.zeros((32, ROWS * COLS), BF)
-    fc_ref[0:96, :] = jnp.zeros((96, 8 * COLS), BF)
-    fc_ref[96:128, :] = qst_ref[32:64, row(1, 8)]
+    for lo in (0, 48):
+        jl_ref[lo : lo + 16, :] = jst_ref[64:80, own]
+        jl_ref[lo + 16 : lo + 48, :] = jst_ref[96:128, own]
+        jl_ref[128 + lo : 128 + lo + 48, :] = jst_ref[80:128, own]
+    for lo in (96, 224):
+        jl_ref[lo : lo + 32, :] = jnp.zeros((32, ROWS * COLS), BF)
+    ql_ref[0:96, :] = jnp.zeros((96, 8 * COLS), BF)
+    ql_ref[96:128, :] = qst_ref[32:64, row(1, 8)]
+    for ky in range(3):
+        gl_ref[ky * 96 : ky * 96 + 96, :] = gst_ref[:, row(4 - ky, ROWS)]
+        pl_ref[ky * 48 : ky * 48 + 48, :] = pst_ref[:, row(1 + ky, 8)]
+    rf = dot_nt(gl_ref[...], jl_ref[...])
+    rc = dot_nt(pl_ref[...], ql_ref[...])
     fine, coarse = {}, {}
     for ky in range(3):
-        shifted = gst_ref[:, row(4 - ky, ROWS)]
-        ra, rb = dot_nt(shifted, fa_ref[...]), dot_nt(shifted, fb_ref[...])
-        rc = dot_nt(pst_ref[:, row(1 + ky, 8)], fc_ref[...])
         for kx in range(3):
-            lo = (2 - kx) * 32
-            fine[ky, 0, kx] = ra[lo + 16 : lo + 32]
-            fine[ky, 1, kx] = ra[lo : lo + 16] + rb[lo + 16 : lo + 32]
-            fine[ky, 2, kx] = rb[lo : lo + 16]
-            coarse[ky, kx] = rc[kx * 16 : kx * 16 + 16] * 0.5
+            lo = ky * 96 + (2 - kx) * 32
+            fine[ky, 0, kx] = rf[lo + 16 : lo + 32, 0:128]
+            fine[ky, 1, kx] = rf[lo : lo + 16, 0:128] + rf[lo + 16 : lo + 32, 128:256]
+            fine[ky, 2, kx] = rf[lo : lo + 16, 128:256]
+            coarse[ky, kx] = rc[ky * 48 + kx * 16 : ky * 48 + kx * 16 + 16] * 0.5
     lane16 = lanes_of((16, COLS))
     order = [(ky, kz, kx) for ky in range(3) for kz in range(3) for kx in range(3)]
     for i in range(16):
@@ -354,10 +385,10 @@
             v(96, 10, BF),
             v(96, 4, F32), v(96, 4, F32),
             v(192, 6, F32), v(96, 6, F32),
-            v(96, 18, F32),
+            v(96, 6, F32),
             v(48, 10, F32),
             pltpu.VMEM(cells, F32),
-            v(128, ROWS, BF), v(128, ROWS, BF), v(128, 8, BF),
+            v(288, ROWS, BF), v(256, ROWS, BF), v(144, 8, BF), v(128, 8, BF),
         ],
         compiler_params=params(),
         cost_estimate=pl.CostEstimate(flops=10**9, bytes_accessed=4 * 10**6, transcendentals=10**5),
@@ -443,7 +474,9 @@
             total = total + (pltpu.roll(value, spot, 1) if spot else value)
         wq_ref[(2 - ky) * 16 : (2 - ky) * 16 + 16, :] = total[:, 0:96].astype(BF)
     for d in range(3):
-        wg_ref[d * 64 : d * 64 + 64, :] = jnp.transpose(pieces_ref[d])[0:64, 0:96].astype(BF)
+        turned = jnp.transpose(pieces_ref[d])[0:64, 0:96].astype(BF)
+        wg_ref[d * 32 : d * 32 + 32, :] = turned[0:32]
+        wg_ref[96 + d * 32 : 96 + d * 32 + 32, :] = turned[32:64]
         wc_ref[d * 32 : d * 32 + 32, :] = jnp.transpose(blocks_ref[d])[0:32, 0:48].astype(BF)
 
 
@@ -484,9 +517,9 @@
     columns = beside_blocks(strip, narrow)
     wo, wg, wc, wq = weight_matrices(stacked)
     corners = odd[:, SLOTS * COLS :] + even[:, SLOTS * COLS :]
-    corners, columns = lax.optimization_barrier((corners, columns))
+    columns, _ = lax.optimization_barrier((columns, corners))
     corners = beside_blocks(corners, narrow)
-    stacks = own_rows(own, columns, wc, wg, sides)
+    stacks = own_rows(own, columns, wo, wc, wg, (wide, narrow), sides)
     output, grad_features, grads = rest((odd, even, corners), stacks, (wo, wg, wc, wq), (wide, narrow), sides)
     devices = wide * narrow
     share = -(-256 // devices)

time: 39.9 us -> 38.7 us (0.970)
  waiting for transfers between devices: 2.79 us -> 1.28 us
  Pallas kernels: 5.31 us -> 6.28 us
  starting transfers between devices: 8.04 us -> 7.15 us
    ppermute x2, waiting for transfers between devices: 2.78 us -> 1.27 us  [beside_blocks(): return lax.ppermute(outer, 'narrow', [(0, 1), (1, 0)])]
    pallas_call x1, Pallas kernels: 1.24 us -> 2.39 us  [own_rows(): pl.pallas_call(functools.partial(own_kernel, counts, sides), out_shape=(s...]
    ppermute x2, starting transfers between devices: 2.98 us -> 2.09 us  [beside_blocks(): return lax.ppermute(outer, 'narrow', [(0, 1), (1, 0)])]
  transfers between devices with their start and end apart: 4 -> 4, of which waited for: 2 -> 1; matrix products, arithmetic and copies ran while one was open for 0% -> 0% of each run, Pallas kernels for 4% -> 7%
where the time goes in v11:
time: 38.7 us; the launch traced here: 38.6 us
  blocking collectives  21.9 us (57%)
  starting transfers between devices  7.15 us (18%)
  Pallas kernels  6.28 us (16%)
  waiting for transfers between devices  1.28 us (3%)
  other arithmetic  1.21 us (3%)
  between operations  0.7 us (2%)
    all_to_all x1, blocking collectives, shards(): parts = lax.all_to_all(grads, both, 0, 0, tiled=True)  12.6 us
    all_to_all x1, blocking collectives, shards(): total = lax.all_to_all(add_up(parts), both, 0, 0, tiled=True)  9.3 us
    ppermute x1, starting transfers between devices, shards(): even = lax.ppermute(to_even, 'wide', swaps(0))  4.39 us
    pallas_call x1, Pallas kernels, own_rows(): pl.pallas_call(functools.partial(own_kernel, counts, sides), out_shape=(s...  2.39 us
    pallas_call x1, Pallas kernels, rest(): pl.pallas_call(functools.partial(rest_kernel, counts, sides), out_shape=(...  2.29 us
    ppermute x2, starting transfers between devices, beside_blocks(): return lax.ppermute(outer, 'narrow', [(0, 1), (1, 0)])  2.09 us
    ppermute x2, waiting for transfers between devices, beside_blocks(): return lax.ppermute(outer, 'narrow', [(0, 1), (1, 0)])  1.27 us
    concatenate x1, other arithmetic, stack(): return jnp.concatenate([flat(features), flat(cotangent), weights], 0)  1.21 us
  transfers between devices with their start and end apart: 4, of which 1 were waited for; matrix products, arithmetic and copies ran while one was open for 0% of the time, Pallas kernels for 7%

profile of v11, /device:TPU:0, one launch (start us, length us, event | category | flops | bytes accessed | tf_op | source)
XLA Modules:
  0.0 38.6 jit_solution(16582588213863273442)
XLA Ops:
  0.7 1.2 %maximum_maximum_fusion.in_ref = bf16[1456,128]{1,0:T(8,128)(2,1)S(1)} fusion(bf16[432,48]{1,0:T(8,128)(2,1)S(1)} %broadcast_in_dim.3, bf16[432,32]{1,0:T(8,128)(2,1)} %bitcast.22, bf16[432,48]{1,0:T(8,128)(2,1)} %bitcast.23, bf16[512,128]{1,0:T(8,128)(2,1)} %bitcast.20, bf16[512,128]{1,0:T(8,128)(2,1)} %bitcast.21), kind=kLoop, calls=%fused_computation | loop fusion | flops 1863680 | bytes 745472 | tf_op jit(solution)/shard_map/concatenate | solution.py:97
  1.9 0.5 %pack.1 = (bf16[64,2048]{1,0:T(8,128)(2,1)S(1)}, bf16[32,128]{1,0:T(8,128)(2,1)S(1)}, bf16[32,768]{1,0:T(8,128)(2,1)S(1)}, bf16[32,768]{1,0:T(8,128)(2,1)S(1)}) custom-call(bf16[1456,128]{1,0:T(8,128)(2,1)S(1)} %maximum_maximum_fusion.in_ref), custom_call_target="tpu_custom_call" | custom-call | flops 1000000 | bytes 1000000 | tf_op jit(solution)/shard_map/pack/pallas_call | solution.py:102
  2.3 0.7 %collective-permute-start = (bf16[32,768]{1,0:T(8,128)(2,1)S(1)}, bf16[32,768]{1,0:T(8,128)(2,1)S(1)}, u32[]{:S(2)}, u32[]{:S(2)}) collective-permute-start(bf16[32,768]{1,0:T(8,128)(2,1)S(1)} %get-tuple-element.27), channel_id=1, source_target_pairs={{2,4},{4,2},{6,8},{8,6},{10,12},{12,10},{14,16},{16,14},{18,20},{2... | collective-permute-start | bytes 147464 | tf_op jit(solution)/shard_map/ppermute | solution.py:515
  3.0 4.4 %collective-permute-start.1 = (bf16[32,768]{1,0:T(8,128)(2,1)S(1)}, bf16[32,768]{1,0:T(8,128)(2,1)S(1)}, u32[]{:S(2)}, u32[]{:S(2)}) collective-permute-start(bf16[32,768]{1,0:T(8,128)(2,1)S(1)} %get-tuple-element.28), channel_id=1, source_target_pairs={{0,2},{2,0},{4,6},{6,4},{8,10},{10,8},{12,14},{14,12},{16,18},{18,... | collective-permute-start | bytes 147464 | tf_op jit(solution)/shard_map/ppermute | solution.py:516
  7.4 1.5 %collective-permute-start.3 = (bf16[32,128]{1,0:T(8,128)(2,1)S(1)}, bf16[32,128]{1,0:T(8,128)(2,1)S(1)}, u32[]{:S(2)}, u32[]{:S(2)}) collective-permute-start(bf16[32,128]{1,0:T(8,128)(2,1)S(1)} %get-tuple-element.30), channel_id=1, source_target_pairs={{0,1},{1,0},{2,3},{3,2},{4,5},{5,4},{6,7},{7,6},{8,9},{9,8},{10,11... | collective-permute-start | bytes 24584 | tf_op jit(solution)/shard_map/ppermute | solution.py:501
  8.9 0.2 matrices.1
  9.1 0.0 collective-permute-done.odd_ref
  9.1 0.0 collective-permute-done.1.even_ref
  9.2 0.6 %collective-permute-start.2 = (bf16[32,128]{1,0:T(8,128)(2,1)S(1)}, bf16[32,128]{1,0:T(8,128)(2,1)S(1)}, u32[]{:S(2)}, u32[]{:S(2)}) collective-permute-start(bf16[32,128]{1,0:T(8,128)(2,1)S(1)} %slice_add_fusion), channel_id=1, source_target_pairs={{0,1},{1,0},{2,3},{3,2},{4,5},{5,4},{6,7},{7,6},{8,9},{9,8},{10,11... | collective-permute-start | bytes 24584 | tf_op jit(solution)/shard_map/ppermute | solution.py:501
  9.8 1.3 %collective-permute-done.3.columns_ref = bf16[32,128]{1,0:T(8,128)(2,1)S(1)} collective-permute-done((bf16[32,128]{1,0:T(8,128)(2,1)S(1)}, bf16[32,128]{1,0:T(8,128)(2,1)S(1)}, u32[]{:S(2)}, u32[]{:S(2)}) %collective-permute-start.3) | collective-permute-done | bytes 8224 | tf_op jit(solution)/shard_map/ppermute | solution.py:501
  11.0 2.4 %own_rows.1 = (bf16[48,1024]{1,0:T(8,128)(2,1)S(1)}, bf16[192,2048]{1,0:T(8,128)(2,1)S(1)}, bf16[96,2048]{1,0:T(8,128)(2,1)S(1)}, bf16[96,768]{1,0:T(8,128)(2,1)...) custom-call(bf16[64,2048]{1,0:T(8,128)(2,1)S(1)} %get-tuple-element., ...), custom_call_target="tpu_custom_call" | custom-call | flops 1000000000 | bytes 4000000 | tf_op jit(solution)/shard_map/own_rows/pallas_call | solution.py:230
  13.4 0.0 collective-permute-done.2.corners_ref
  13.4 2.3 %rest.1 = (bf16[512,128]{1,0:T(8,128)(2,1)}, bf16[512,128]{1,0:T(8,128)(2,1)}, bf16[256,128]{1,0:T(8,128)(2,1)S(1)}) custom-call(bf16[32,768]{1,0:T(8,128)(2,1)S(1)} %collective-permute-done.odd_ref, bf16[32,768]{1,0:T(8,128)(2,1)S(1)} %collective-permute-done.1.even_ref, bf16[32,128]{1,0:T(8,128)(2,1)S(1)} %collective-permute-done.2.corners_ref, ...), custom_call_target="tpu_custom_call" | custom-call | flops 1000000000 | bytes 4000000 | tf_op jit(solution)/shard_map/rest/pallas_call | solution.py:373
  15.7 12.6 %all_to_all.10.parts_ref = bf16[32,8,128]{2,1,0:T(8,128)(2,1)S(1)} all-to-all(bf16[32,8,128]{2,1,0:T(8,128)(2,1)S(1)} %bitcast.19), channel_id=1, replica_groups=mesh['wide'=16,'narrow'=2] {'wide','narrow'}, dimensions={0} | all-to-all | bytes 131072 | tf_op jit(solution)/shard_map/all_to_all | solution.py:528
  28.4 9.3 %all_to_all.11 = bf16[32,8,128]{2,1,0:T(8,128)(2,1)S(1)} all-to-all(bf16[32,8,128]{2,1,0:T(8,128)(2,1)S(1)} %add_up.1), channel_id=1, replica_groups=mesh['wide'=16,'narrow'=2] {'wide','narrow'}, dimensions={0} | all-to-all | bytes 131072 | tf_op jit(solution)/shard_map/all_to_all | solution.py:529
  37.7 0.9 %spread.1 = (f32[432,48]{1,0:T(8,128)}, f32[432,32]{1,0:T(8,128)}) custom-call(bf16[256,128]{1,0:T(8,128)(2,1)S(1)} %bitcast.18), custom_call_target="tpu_custom_call" | custom-call | tf_op jit(solution)/shard_map/spread/pallas_call | solution.py:435
  (3 shorter events, 0.1 us)
Async XLA Ops:
  2.3 6.8 %collective-permute-start = (bf16[32,768]{1,0:T(8,128)(2,1)S(1)}, bf16[32,768]{1,0:T(8,128)(2,1)S(1)}, u32[]{:S(2)}, u32[]{:S(2)}) collective-permute-start(bf16[32,768]{1,0:T(8,128)(2,1)S(1)} %get-tuple-element.27), channel_id=1, source_target_pairs={{2,4},{4,2},{6,8},{8,6},{10,12},{12,10},{14,16},{16,14},{18,20},{2... | collective-permute-start | bytes 147464 | tf_op jit(solution)/shard_map/ppermute | solution.py:515
  3.0 6.2 %collective-permute-start.1 = (bf16[32,768]{1,0:T(8,128)(2,1)S(1)}, bf16[32,768]{1,0:T(8,128)(2,1)S(1)}, u32[]{:S(2)}, u32[]{:S(2)}) collective-permute-start(bf16[32,768]{1,0:T(8,128)(2,1)S(1)} %get-tuple-element.28), channel_id=1, source_target_pairs={{0,2},{2,0},{4,6},{6,4},{8,10},{10,8},{12,14},{14,12},{16,18},{18,... | collective-permute-start | bytes 147464 | tf_op jit(solution)/shard_map/ppermute | solution.py:516
  7.4 3.7 %collective-permute-start.3 = (bf16[32,128]{1,0:T(8,128)(2,1)S(1)}, bf16[32,128]{1,0:T(8,128)(2,1)S(1)}, u32[]{:S(2)}, u32[]{:S(2)}) collective-permute-start(bf16[32,128]{1,0:T(8,128)(2,1)S(1)} %get-tuple-element.30), channel_id=1, source_target_pairs={{0,1},{1,0},{2,3},{3,2},{4,5},{5,4},{6,7},{7,6},{8,9},{9,8},{10,11... | collective-permute-start | bytes 24584 | tf_op jit(solution)/shard_map/ppermute | solution.py:501
  9.2 4.3 %collective-permute-start.2 = (bf16[32,128]{1,0:T(8,128)(2,1)S(1)}, bf16[32,128]{1,0:T(8,128)(2,1)S(1)}, u32[]{:S(2)}, u32[]{:S(2)}) collective-permute-start(bf16[32,128]{1,0:T(8,128)(2,1)S(1)} %slice_add_fusion), channel_id=1, source_target_pairs={{0,1},{1,0},{2,3},{3,2},{4,5},{5,4},{6,7},{7,6},{8,9},{9,8},{10,11... | collective-permute-start | bytes 24584 | tf_op jit(solution)/shard_map/ppermute | solution.py:501

commit v12 on v11

--- a/solution.py
+++ b/solution.py
@@ -244,12 +244,50 @@
     )(s, columns, wo, wc, wg)
 
 
+def put_joined(jst_ref, at, jl_ref, to):
+    for lo in (0, 48):
+        jl_ref[lo : lo + 16, to] = jst_ref[64:80, at]
+        jl_ref[lo + 16 : lo + 48, to] = jst_ref[96:128, at]
+        jl_ref[128 + lo : 128 + lo + 48, to] = jst_ref[80:128, at]
+    for lo in (96, 224):
+        jl_ref[lo : lo + 32, to] = jnp.zeros((32, to.stop - to.start), BF)
+
+
+def inner_kernel(pst_ref, jst_ref, gst_ref, qst_ref, rf_ref, rc_ref, gl_ref, jl_ref, pl_ref, ql_ref):
+    rows, coarse_rows = ROWS - 4, len(INNER)
+    put_joined(jst_ref, row(2, rows), jl_ref, row(0, rows))
+    ql_ref[0:96, :] = jnp.zeros((96, coarse_rows * COLS), BF)
+    ql_ref[96:128, :] = qst_ref[32:64, :]
+    for ky in range(3):
+        gl_ref[ky * 96 : ky * 96 + 96, :] = gst_ref[:, row(3 - ky, rows)]
+        pl_ref[ky * 48 : ky * 48 + 48, :] = pst_ref[:, row(ky, coarse_rows)]
+    rf_ref[...] = dot_nt(gl_ref[...], jl_ref[...])
+    rc_ref[...] = dot_nt(pl_ref[...], ql_ref[...])
+
+
+def inner_sums(pst, jst, gst, qst):
+    rows, coarse_rows = (ROWS - 4) * COLS, len(INNER) * COLS
+    return pl.pallas_call(
+        inner_kernel,
+        out_shape=(jax.ShapeDtypeStruct((288, 256), F32), jax.ShapeDtypeStruct((144, COLS), F32)),
+        scratch_shapes=[
+            pltpu.VMEM((288, rows), BF),
+            pltpu.VMEM((256, rows), BF),
+            pltpu.VMEM((144, coarse_rows), BF),
+            pltpu.VMEM((128, coarse_rows), BF),
+        ],
+        compiler_params=params(),
+        cost_estimate=pl.CostEstimate(flops=10**9, bytes_accessed=4 * 10**6, transcendentals=0),
+        name="inner_sums",
+    )(pst, jst, gst, qst)
+
+
 def rest_kernel(
     counts, sides,
     odd_ref, even_ref, corners_ref, pst_own, jst_own, gst_own, qst_own, pre_own, prb_own, rg_own, rgb_own, ro_own,
-    wo_ref, wg_ref, wc_ref, wq_ref,
-    out_ref, gf_ref, gw_ref,
-    halo_ref, jst_ref, gst_ref, gsb_ref, pst_ref, psb_ref, qst_ref,
+    rf_inner, rc_inner, wo_ref, wg_ref, wc_ref, wq_ref,
+    out_hbm, gf_hbm, gw_ref,
+    out_ref, gf_ref, sems, halo_ref, jst_ref, gst_ref, gsb_ref, pst_ref, psb_ref, qst_ref,
     pre_ref, prb_ref, rg_ref, rgb_ref, ro_ref, rq_ref, flat_ref, gl_ref, jl_ref, pl_ref, ql_ref,
 ):
     w = lax.axis_index("wide")
@@ -319,6 +357,8 @@
         for z in range(2):
             flat_ref[pl.ds(2 * y + z, C1, stride=2 * ROWS), :] = value[z * 16 : z * 16 + 16]
     out_ref[...] = flat_ref[...].astype(BF)
+    out_copy = pltpu.make_async_copy(out_ref, out_hbm, sems.at[0])
+    out_copy.start()
 
     rq_ref[...] = dot(wq_ref[...], qst_ref[...])
     for at in range(ROWS // 2):
@@ -331,21 +371,19 @@
                     total = total + part(rg_own, rg_ref, d * 32 + z * 16, 16, y + 2 + d, 3, ROWS)
                 flat_ref[pl.ds(2 * y + z, C1, stride=2 * ROWS), :] = total
     gf_ref[...] = flat_ref[...].astype(BF)
-
-    own = row(1, ROWS)
-    for lo in (0, 48):
-        jl_ref[lo : lo + 16, :] = jst_ref[64:80, own]
-        jl_ref[lo + 16 : lo + 48, :] = jst_ref[96:128, own]
-        jl_ref[128 + lo : 128 + lo + 48, :] = jst_ref[80:128, own]
-    for lo in (96, 224):
-        jl_ref[lo : lo + 32, :] = jnp.zeros((32, ROWS * COLS), BF)
-    ql_ref[0:96, :] = jnp.zeros((96, 8 * COLS), BF)
-    ql_ref[96:128, :] = qst_ref[32:64, row(1, 8)]
-    for ky in range(3):
-        gl_ref[ky * 96 : ky * 96 + 96, :] = gst_ref[:, row(4 - ky, ROWS)]
-        pl_ref[ky * 48 : ky * 48 + 48, :] = pst_ref[:, row(1 + ky, 8)]
-    rf = dot_nt(gl_ref[...], jl_ref[...])
-    rc = dot_nt(pl_ref[...], ql_ref[...])
+    gf_copy = pltpu.make_async_copy(gf_ref, gf_hbm, sems.at[1])
+    gf_copy.start()
+
+    for i in range(2):
+        at = row(1 + 14 * i, 2)
+        put_joined(jst_ref, at, jl_ref, row(2 * i, 2))
+        ql_ref[96:128, row(i)] = qst_ref[32:64, row(1 + 7 * i)]
+        for ky in range(3):
+            gl_ref[ky * 96 : ky * 96 + 96, row(2 * i, 2)] = gst_ref[:, row(14 * i + 4 - ky, 2)]
+            pl_ref[ky * 48 : ky * 48 + 48, row(i)] = pst_ref[:, row(7 * i + 1 + ky)]
+    ql_ref[0:96, :] = jnp.zeros((96, 2 * COLS), BF)
+    rf = rf_inner[...] + dot_nt(gl_ref[...], jl_ref[...])
+    rc = rc_inner[...] + dot_nt(pl_ref[...], ql_ref[...])
     fine, coarse = {}, {}
     for ky in range(3):
         for kx in range(3):
@@ -365,9 +403,11 @@
         if i < 9:
             value = jnp.where(lane16 >= 96, coarse[i // 3, i % 3], value)
         gw_ref[i * 16 : i * 16 + 16, :] = value.astype(BF)
-
-
-def rest(messages, own, matrices, counts, sides):
+    out_copy.wait()
+    gf_copy.wait()
+
+
+def rest(messages, own, inner, matrices, counts, sides):
     cells = (C1 * ROWS * 2, COLS)
     v = lambda rows_, lanes_, kind: pltpu.VMEM((rows_, lanes_ * COLS), kind)
     return pl.pallas_call(
@@ -377,7 +417,13 @@
             jax.ShapeDtypeStruct(cells, BF),
             jax.ShapeDtypeStruct((256, COLS), BF),
         ),
+        out_specs=(
+            pl.BlockSpec(memory_space=pl.ANY),
+            pl.BlockSpec(memory_space=pl.ANY),
+            pl.BlockSpec(memory_space=pltpu.VMEM),
+        ),
         scratch_shapes=[
+            pltpu.VMEM(cells, BF), pltpu.VMEM(cells, BF), pltpu.SemaphoreType.DMA((2,)),
             pltpu.VMEM((2, 32, SLOTS * COLS), BF),
             v(192, 18, BF),
             v(96, 22, BF), v(96, 6, BF),
@@ -388,12 +434,12 @@
             v(96, 6, F32),
             v(48, 10, F32),
             pltpu.VMEM(cells, F32),
-            v(288, ROWS, BF), v(256, ROWS, BF), v(144, 8, BF), v(128, 8, BF),
+            v(288, 4, BF), v(256, 4, BF), v(144, 2, BF), v(128, 2, BF),
         ],
         compiler_params=params(),
         cost_estimate=pl.CostEstimate(flops=10**9, bytes_accessed=4 * 10**6, transcendentals=10**5),
         name="rest",
-    )(*messages, *own, *matrices)
+    )(*messages, *own, *inner, *matrices)
 
 
 def add_kernel(parts_ref, copies_ref):
@@ -517,10 +563,13 @@
     columns = beside_blocks(strip, narrow)
     wo, wg, wc, wq = weight_matrices(stacked)
     corners = odd[:, SLOTS * COLS :] + even[:, SLOTS * COLS :]
-    columns, _ = lax.optimization_barrier((columns, corners))
+    stacks = own_rows(own, columns, wo, wc, wg, (wide, narrow), sides)
+    inner, _ = lax.optimization_barrier((stacks[:4], corners))
+    inner = inner_sums(*inner)
     corners = beside_blocks(corners, narrow)
-    stacks = own_rows(own, columns, wo, wc, wg, (wide, narrow), sides)
-    output, grad_features, grads = rest((odd, even, corners), stacks, (wo, wg, wc, wq), (wide, narrow), sides)
+    output, grad_features, grads = rest(
+        (odd, even, corners), stacks, inner, (wo, wg, wc, wq), (wide, narrow), sides
+    )
     devices = wide * narrow
     share = -(-256 // devices)
     grads = jnp.pad(grads, ((0, share * devices - 256), (0, 0))).reshape(devices, share, COLS)

time: 38.7 us -> 39.5 us (1.021)
  waiting for transfers between devices: 1.28 us -> 2.63 us
  blocking collectives: 21.9 us -> 20.8 us
  Pallas kernels: 6.28 us -> 6.69 us
    ppermute x2, starting transfers between devices: 2.09 us -> 3.59 us  [beside_blocks(): return lax.ppermute(outer, 'narrow', [(0, 1), (1, 0)])]
    ppermute x1, starting transfers between devices: 4.39 us -> 2.94 us  [shards(): even = lax.ppermute(to_even, 'wide', swaps(0))]
    ppermute x2, waiting for transfers between devices: 1.27 us -> 2.62 us  [beside_blocks(): return lax.ppermute(outer, 'narrow', [(0, 1), (1, 0)])]
    all_to_all x1, blocking collectives: 12.6 us -> 11.5 us  [shards(): parts = lax.all_to_all(grads, both, 0, 0, tiled=True)]
    pallas_call x0 -> x1, Pallas kernels: none -> 0.5 us  [inner_sums(): pl.pallas_call(inner_kernel, out_shape=(jax.ShapeDtypeStruct((288, 256),...]
  transfers between devices with their start and end apart: 4 -> 4, of which waited for: 1 -> 1; matrix products, arithmetic and copies ran while one was open for 0% -> 0% of each run, Pallas kernels for 7% -> 8%
where the time goes in v12:
time: 39.5 us; the launch traced here: 39.3 us
  blocking collectives  20.8 us (53%)
  starting transfers between devices  7.19 us (18%)
  Pallas kernels  6.69 us (17%)
  waiting for transfers between devices  2.63 us (7%)
  other arithmetic  1.21 us (3%)
  between operations  0.72 us (2%)
    all_to_all x1, blocking collectives, shards(): parts = lax.all_to_all(grads, both, 0, 0, tiled=True)  11.5 us
    all_to_all x1, blocking collectives, shards(): total = lax.all_to_all(add_up(parts), both, 0, 0, tiled=True)  9.3 us
    ppermute x2, starting transfers between devices, beside_blocks(): return lax.ppermute(outer, 'narrow', [(0, 1), (1, 0)])  3.59 us
    ppermute x1, starting transfers between devices, shards(): even = lax.ppermute(to_even, 'wide', swaps(0))  2.94 us
    ppermute x2, waiting for transfers between devices, beside_blocks(): return lax.ppermute(outer, 'narrow', [(0, 1), (1, 0)])  2.62 us
    pallas_call x1, Pallas kernels, own_rows(): pl.pallas_call(functools.partial(own_kernel, counts, sides), out_shape=(s...  2.4 us
    pallas_call x1, Pallas kernels, rest(): pl.pallas_call(functools.partial(rest_kernel, counts, sides), out_shape=(...  2.2 us
    concatenate x1, other arithmetic, stack(): return jnp.concatenate([flat(features), flat(cotangent), weights], 0)  1.21 us
  transfers between devices with their start and end apart: 4, of which 1 were waited for; matrix products, arithmetic and copies ran while one was open for 0% of the time, Pallas kernels for 8%

profile of v12, /device:TPU:0, one launch (start us, length us, event | category | flops | bytes accessed | tf_op | source)
XLA Modules:
  0.0 39.3 jit_solution(1198600391281146400)
XLA Ops:
  0.7 1.2 %maximum_maximum_fusion.in_ref = bf16[1456,128]{1,0:T(8,128)(2,1)S(1)} fusion(bf16[432,48]{1,0:T(8,128)(2,1)S(1)} %broadcast_in_dim.3, bf16[432,32]{1,0:T(8,128)(2,1)} %bitcast.22, bf16[432,48]{1,0:T(8,128)(2,1)} %bitcast.23, bf16[512,128]{1,0:T(8,128)(2,1)} %bitcast.20, bf16[512,128]{1,0:T(8,128)(2,1)} %bitcast.21), kind=kLoop, calls=%fused_computation | loop fusion | flops 1863680 | bytes 745472 | tf_op jit(solution)/shard_map/concatenate | solution.py:97
  1.9 0.5 %pack.1 = (bf16[64,2048]{1,0:T(8,128)(2,1)S(1)}, bf16[32,128]{1,0:T(8,128)(2,1)S(1)}, bf16[32,768]{1,0:T(8,128)(2,1)S(1)}, bf16[32,768]{1,0:T(8,128)(2,1)S(1)}) custom-call(bf16[1456,128]{1,0:T(8,128)(2,1)S(1)} %maximum_maximum_fusion.in_ref), custom_call_target="tpu_custom_call" | custom-call | flops 1000000 | bytes 1000000 | tf_op jit(solution)/shard_map/pack/pallas_call | solution.py:102
  2.3 3.0 %collective-permute-start.3 = (bf16[32,128]{1,0:T(8,128)(2,1)S(1)}, bf16[32,128]{1,0:T(8,128)(2,1)S(1)}, u32[]{:S(2)}, u32[]{:S(2)}) collective-permute-start(bf16[32,128]{1,0:T(8,128)(2,1)S(1)} %get-tuple-element.35), channel_id=1, source_target_pairs={{0,1},{1,0},{2,3},{3,2},{4,5},{5,4},{6,7},{7,6},{8,9},{9,8},{10,11... | collective-permute-start | bytes 24584 | tf_op jit(solution)/shard_map/ppermute | solution.py:547
  5.3 0.7 %collective-permute-start = (bf16[32,768]{1,0:T(8,128)(2,1)S(1)}, bf16[32,768]{1,0:T(8,128)(2,1)S(1)}, u32[]{:S(2)}, u32[]{:S(2)}) collective-permute-start(bf16[32,768]{1,0:T(8,128)(2,1)S(1)} %get-tuple-element.32), channel_id=1, source_target_pairs={{2,4},{4,2},{6,8},{8,6},{10,12},{12,10},{14,16},{16,14},{18,20},{2... | collective-permute-start | bytes 147464 | tf_op jit(solution)/shard_map/ppermute | solution.py:561
  6.0 2.9 %collective-permute-start.1 = (bf16[32,768]{1,0:T(8,128)(2,1)S(1)}, bf16[32,768]{1,0:T(8,128)(2,1)S(1)}, u32[]{:S(2)}, u32[]{:S(2)}) collective-permute-start(bf16[32,768]{1,0:T(8,128)(2,1)S(1)} %get-tuple-element.33), channel_id=1, source_target_pairs={{0,2},{2,0},{4,6},{6,4},{8,10},{10,8},{12,14},{14,12},{16,18},{18,... | collective-permute-start | bytes 147464 | tf_op jit(solution)/shard_map/ppermute | solution.py:562
  8.9 0.2 matrices.1
  9.2 0.0 collective-permute-done.3.columns_ref
  9.2 2.4 %own_rows.1 = (bf16[48,1024]{1,0:T(8,128)(2,1)S(1)}, bf16[192,2048]{1,0:T(8,128)(2,1)S(1)}, bf16[96,2048]{1,0:T(8,128)(2,1)S(1)}, bf16[96,768]{1,0:T(8,128)(2,1)...) custom-call(bf16[64,2048]{1,0:T(8,128)(2,1)S(1)} %get-tuple-element., ...), custom_call_target="tpu_custom_call" | custom-call | flops 1000000000 | bytes 4000000 | tf_op jit(solution)/shard_map/own_rows/pallas_call | solution.py:230
  11.6 0.0 collective-permute-done.odd_ref
  11.6 0.0 collective-permute-done.1.even_ref
  11.6 0.6 %collective-permute-start.2 = (bf16[32,128]{1,0:T(8,128)(2,1)S(1)}, bf16[32,128]{1,0:T(8,128)(2,1)S(1)}, u32[]{:S(2)}, u32[]{:S(2)}) collective-permute-start(bf16[32,128]{1,0:T(8,128)(2,1)S(1)} %slice_add_fusion), channel_id=1, source_target_pairs={{0,1},{1,0},{2,3},{3,2},{4,5},{5,4},{6,7},{7,6},{8,9},{9,8},{10,11... | collective-permute-start | bytes 24584 | tf_op jit(solution)/shard_map/ppermute | solution.py:547
  12.2 0.5 %inner_sums.1 = (f32[288,256]{1,0:T(8,128)S(1)}, f32[144,128]{1,0:T(8,128)S(1)}) custom-call(bf16[48,1024]{1,0:T(8,128)(2,1)S(1)} %get-tuple-element.48.pst_ref.pst_own, bf16[192,2048]{1,0:T(8,128)(2,1)S(1)} %get-tuple-element.49.jst_ref.jst_own, bf16[96,2048]{1,0:T(8,128)(2,1)S(1)} %get-tuple-element.50.gst_ref.gst_own, ...), custom_call_target="tpu_custom_call" | custom-call | flops 1000000000 | bytes 4000000 | tf_op jit(solution)/shard_map/inner_sums/pallas_call | solution.py:270
  12.7 2.6 %collective-permute-done.2.corners_ref = bf16[32,128]{1,0:T(8,128)(2,1)S(1)} collective-permute-done((bf16[32,128]{1,0:T(8,128)(2,1)S(1)}, bf16[32,128]{1,0:T(8,128)(2,1)S(1)}, u32[]{:S(2)}, u32[]{:S(2)}) %collective-permute-start.2) | collective-permute-done | bytes 8224 | tf_op jit(solution)/shard_map/ppermute | solution.py:547
  15.4 2.2 %rest.1 = (bf16[512,128]{1,0:T(8,128)(2,1)}, bf16[512,128]{1,0:T(8,128)(2,1)}, bf16[256,128]{1,0:T(8,128)(2,1)S(1)}) custom-call(bf16[32,768]{1,0:T(8,128)(2,1)S(1)} %collective-permute-done.odd_ref, bf16[32,768]{1,0:T(8,128)(2,1)S(1)} %collective-permute-done.1.even_ref, bf16[32,128]{1,0:T(8,128)(2,1)S(1)} %collective-permute-done.2.corners_ref, ...), custom_call_target="tpu_custom_call" | custom-call | flops 1000000000 | bytes 4000000 | tf_op jit(solution)/shard_map/rest/pallas_call | solution.py:413
  17.6 11.5 %all_to_all.10.parts_ref = bf16[32,8,128]{2,1,0:T(8,128)(2,1)S(1)} all-to-all(bf16[32,8,128]{2,1,0:T(8,128)(2,1)S(1)} %bitcast.19), channel_id=1, replica_groups=mesh['wide'=16,'narrow'=2] {'wide','narrow'}, dimensions={0} | all-to-all | bytes 131072 | tf_op jit(solution)/shard_map/all_to_all | solution.py:577
  29.1 9.3 %all_to_all.11 = bf16[32,8,128]{2,1,0:T(8,128)(2,1)S(1)} all-to-all(bf16[32,8,128]{2,1,0:T(8,128)(2,1)S(1)} %add_up.1), channel_id=1, replica_groups=mesh['wide'=16,'narrow'=2] {'wide','narrow'}, dimensions={0} | all-to-all | bytes 131072 | tf_op jit(solution)/shard_map/all_to_all | solution.py:578
  38.4 0.9 %spread.1 = (f32[432,48]{1,0:T(8,128)}, f32[432,32]{1,0:T(8,128)}) custom-call(bf16[256,128]{1,0:T(8,128)(2,1)S(1)} %bitcast.18), custom_call_target="tpu_custom_call" | custom-call | tf_op jit(solution)/shard_map/spread/pallas_call | solution.py:481
  (3 shorter events, 0.1 us)
Async XLA Ops:
  2.3 6.9 %collective-permute-start.3 = (bf16[32,128]{1,0:T(8,128)(2,1)S(1)}, bf16[32,128]{1,0:T(8,128)(2,1)S(1)}, u32[]{:S(2)}, u32[]{:S(2)}) collective-permute-start(bf16[32,128]{1,0:T(8,128)(2,1)S(1)} %get-tuple-element.35), channel_id=1, source_target_pairs={{0,1},{1,0},{2,3},{3,2},{4,5},{5,4},{6,7},{7,6},{8,9},{9,8},{10,11... | collective-permute-start | bytes 24584 | tf_op jit(solution)/shard_map/ppermute | solution.py:547
  5.3 6.3 %collective-permute-start = (bf16[32,768]{1,0:T(8,128)(2,1)S(1)}, bf16[32,768]{1,0:T(8,128)(2,1)S(1)}, u32[]{:S(2)}, u32[]{:S(2)}) collective-permute-start(bf16[32,768]{1,0:T(8,128)(2,1)S(1)} %get-tuple-element.32), channel_id=1, source_target_pairs={{2,4},{4,2},{6,8},{8,6},{10,12},{12,10},{14,16},{16,14},{18,20},{2... | collective-permute-start | bytes 147464 | tf_op jit(solution)/shard_map/ppermute | solution.py:561
  6.0 5.6 %collective-permute-start.1 = (bf16[32,768]{1,0:T(8,128)(2,1)S(1)}, bf16[32,768]{1,0:T(8,128)(2,1)S(1)}, u32[]{:S(2)}, u32[]{:S(2)}) collective-permute-start(bf16[32,768]{1,0:T(8,128)(2,1)S(1)} %get-tuple-element.33), channel_id=1, source_target_pairs={{0,2},{2,0},{4,6},{6,4},{8,10},{10,8},{12,14},{14,12},{16,18},{18,... | collective-permute-start | bytes 147464 | tf_op jit(solution)/shard_map/ppermute | solution.py:562
  11.6 3.7 %collective-permute-start.2 = (bf16[32,128]{1,0:T(8,128)(2,1)S(1)}, bf16[32,128]{1,0:T(8,128)(2,1)S(1)}, u32[]{:S(2)}, u32[]{:S(2)}) collective-permute-start(bf16[32,128]{1,0:T(8,128)(2,1)S(1)} %slice_add_fusion), channel_id=1, source_target_pairs={{0,1},{1,0},{2,3},{3,2},{4,5},{5,4},{6,7},{7,6},{8,9},{9,8},{10,11... | collective-permute-start | bytes 24584 | tf_op jit(solution)/shard_map/ppermute | solution.py:547

commit v13 on v11

--- a/solution.py
+++ b/solution.py
@@ -12,7 +12,7 @@
 ROWS, COLS = 16, 128
 HALO = 4
 BF, F32 = jnp.bfloat16, jnp.float32
-VMEM_LIMIT = 48 * 1024 * 1024
+VMEM_LIMIT = 20 * 1024 * 1024
 
 
 def lanes_of(shape):
@@ -180,16 +180,16 @@
 
 
 def own_kernel(
-    counts, sides,
-    s_ref, columns_ref, wo_ref, wc_ref, wg_ref,
-    pst_ref, jst_ref, gst_ref, qst_ref, pre_ref, prb_ref, rg_ref, rgb_ref, ro_ref,
+    sides,
+    s_ref, columns_ref, wc_ref, wg_ref,
+    pst_ref, jf_ref, gst_ref, pre_ref, prb_ref, rg_ref, rgb_ref,
     psb_ref, gsb_ref,
 ):
     columns = [columns_ref[:, row(side)].astype(F32) for side in range(sides)]
     last = None
     for y in range(ROWS):
         main, side = s_ref[0:32, row(y)].astype(F32), beside(columns, HALO * y)
-        put_features(main, side, jst_ref, 64, y)
+        put_features(main, side, jf_ref, 32, y)
         if y % 2 == 1:
             means = [pooled(a, b) for a, b in zip(last, (main, side))]
             put_pooled(*means, pst_ref, psb_ref, y // 2, y // 2)
@@ -200,7 +200,58 @@
     prb_ref[...] = dot(wc_ref[...], psb_ref[...])
     rg_ref[...] = dot(wg_ref[...], gst_ref[...])
     rgb_ref[...] = dot(wg_ref[96:192, :], gsb_ref[...])
-    there = column_masks(counts[1])
+
+
+def shaped(rows_, lanes_, kind):
+    return jax.ShapeDtypeStruct((rows_, lanes_ * COLS), kind)
+
+
+def scratch(rows_, lanes_, kind):
+    return pltpu.VMEM((rows_, lanes_ * COLS), kind)
+
+
+def own_rows(s, columns, wc, wg, sides):
+    half = ROWS // 2
+    return pl.pallas_call(
+        functools.partial(own_kernel, sides),
+        out_shape=(
+            shaped(48, half, BF), shaped(96, ROWS, BF), shaped(96, ROWS, BF),
+            shaped(96, half, F32), shaped(96, half, F32),
+            shaped(192, ROWS, F32), shaped(96, ROWS, F32),
+        ),
+        scratch_shapes=[scratch(48, half, BF), scratch(96, ROWS, BF)],
+        compiler_params=params(),
+        cost_estimate=pl.CostEstimate(flops=10**9, bytes_accessed=4 * 10**6, transcendentals=0),
+        name="own_rows",
+    )(s, columns, wc, wg)
+
+
+def put_joined(jst_ref, at, jl_ref, to):
+    for lo in (0, 48):
+        jl_ref[lo : lo + 16, to] = jst_ref[64:80, at]
+        jl_ref[lo + 16 : lo + 48, to] = jst_ref[96:128, at]
+        jl_ref[128 + lo : 128 + lo + 48, to] = jst_ref[80:128, at]
+    for lo in (96, 224):
+        jl_ref[lo : lo + 32, to] = jnp.zeros((32, to.stop - to.start), BF)
+
+
+def put_field(flat_ref, y, plane, value):
+    flat_ref[pl.ds(2 * y + plane, C1, stride=2 * ROWS), :] = value
+
+
+FINE = range(2 * INNER.start, 2 * INNER.stop)
+
+
+def inner_kernel(
+    count,
+    pst_ref, jf_ref, gst_ref, pre_ref, prb_ref, rg_ref, rgb_ref, wo_ref, wq_ref,
+    out_ref, gf_ref, ro_ref, rq_ref, rf_ref, rc_ref,
+    jst_ref, qst_ref, gl_ref, jl_ref, pl_ref, ql_ref,
+):
+    rows, coarse_rows = len(FINE), len(INNER)
+    there = column_masks(count)
+    for d in range(3):
+        jst_ref[d * 64 : d * 64 + 32, :] = jf_ref[d * 32 : d * 32 + 32, row(FINE.start, rows)]
     for at in INNER:
         values = [
             sum(ref[d * 32 : d * 32 + 32, row(at + d - 1)] for d in range(3)) for ref in (pre_ref, prb_ref)
@@ -216,41 +267,63 @@
         acts, grads = coarse_row(values, totals, (1.0, there))
         for d in range(3):
             for r in (2 * at, 2 * at + 1):
-                jst_ref[d * 64 + 32 : d * 64 + 64, row(r)] = acts[d]
-            qst_ref[d * 32 : d * 32 + 32, row(at - 1)] = grads[d]
-    for r in (0, 1, ROWS - 2, ROWS - 1):
-        for d in range(3):
-            jst_ref[d * 64 + 32 : d * 64 + 64, row(r)] = jnp.zeros((C2, COLS), BF)
-    ro_ref[...] = dot(wo_ref[...], jst_ref[:, row(2, ROWS - 4)])
-
-
-def own_rows(s, columns, wo, wc, wg, counts, sides):
-    half = ROWS // 2
-    shape = lambda rows_, lanes_, kind: jax.ShapeDtypeStruct((rows_, lanes_ * COLS), kind)
+                jst_ref[d * 64 + 32 : d * 64 + 64, row(r - FINE.start)] = acts[d]
+            qst_ref[d * 32 : d * 32 + 32, row(at - INNER.start)] = grads[d]
+    ro_ref[...] = dot(wo_ref[...], jst_ref[...])
+    rq_ref[...] = dot(wq_ref[...], qst_ref[...])
+
+    put_joined(jst_ref, row(0, rows), jl_ref, row(0, rows))
+    ql_ref[0:96, :] = jnp.zeros((96, coarse_rows * COLS), BF)
+    ql_ref[96:128, :] = qst_ref[32:64, :]
+    for ky in range(3):
+        gl_ref[ky * 96 : ky * 96 + 96, :] = gst_ref[:, row(FINE.start + 1 - ky, rows)]
+        pl_ref[ky * 48 : ky * 48 + 48, :] = pst_ref[:, row(INNER.start + ky - 1, coarse_rows)]
+    rf_ref[...] = dot_nt(gl_ref[...], jl_ref[...])
+    rc_ref[...] = dot_nt(pl_ref[...], ql_ref[...])
+
+    for y in range(FINE.start + 1, FINE.stop - 1):
+        value = sum(ro_ref[d * 32 : d * 32 + 32, row(y - 1 + d - FINE.start)] for d in range(3))
+        for z in range(2):
+            put_field(out_ref, y, z, value[z * 16 : z * 16 + 16])
+    for at in range(INNER.start + 1, INNER.stop - 1):
+        coarse = sum(rq_ref[d * 16 : d * 16 + 16, row(at - 1 + d - INNER.start)] for d in range(3))
+        coarse = coarse.astype(BF).astype(F32) * 0.125
+        for y in (2 * at, 2 * at + 1):
+            for z in range(2):
+                lo = z * 16
+                value = sum(rg_ref[lo + d * 32 : lo + d * 32 + 16, row(y - 1 + d)] for d in range(3))
+                put_field(gf_ref, y, z, value + coarse)
+
+
+def inner_rows(own, wo, wq, count):
+    rows, coarse_rows = len(FINE), len(INNER)
     return pl.pallas_call(
-        functools.partial(own_kernel, counts, sides),
+        functools.partial(inner_kernel, count),
         out_shape=(
-            shape(48, half, BF), shape(192, ROWS, BF), shape(96, ROWS, BF), shape(96, len(INNER), BF),
-            shape(96, half, F32), shape(96, half, F32),
-            shape(192, ROWS, F32), shape(96, ROWS, F32), shape(96, ROWS - 4, F32),
+            shaped(CELLS, 1, F32), shaped(CELLS, 1, F32),
+            shaped(96, rows, F32), shaped(48, coarse_rows, F32),
+            shaped(288, 2, F32), shaped(144, 1, F32),
         ),
         scratch_shapes=[
-            pltpu.VMEM((48, half * COLS), BF),
-            pltpu.VMEM((96, ROWS * COLS), BF),
+            scratch(192, rows, BF), scratch(96, coarse_rows, BF),
+            scratch(288, rows, BF), scratch(256, rows, BF),
+            scratch(144, coarse_rows, BF), scratch(128, coarse_rows, BF),
         ],
         compiler_params=params(),
-        cost_estimate=pl.CostEstimate(flops=10**9, bytes_accessed=4 * 10**6, transcendentals=0),
-        name="own_rows",
-    )(s, columns, wo, wc, wg)
+        cost_estimate=pl.CostEstimate(flops=10**9, bytes_accessed=4 * 10**6, transcendentals=10**5),
+        name="inner_rows",
+    )(*own, wo, wq)
 
 
 def rest_kernel(
     counts, sides,
-    odd_ref, even_ref, corners_ref, pst_own, jst_own, gst_own, qst_own, pre_own, prb_own, rg_own, rgb_own, ro_own,
+    odd_ref, even_ref, corners_ref,
+    pst_own, jf_own, gst_own, pre_own, prb_own, rg_own, rgb_own,
+    out_inner, gf_inner, ro_inner, rq_inner, rf_inner, rc_inner,
     wo_ref, wg_ref, wc_ref, wq_ref,
     out_ref, gf_ref, gw_ref,
     halo_ref, jst_ref, gst_ref, gsb_ref, pst_ref, psb_ref, qst_ref,
-    pre_ref, prb_ref, rg_ref, rgb_ref, ro_ref, rq_ref, flat_ref, gl_ref, jl_ref, pl_ref, ql_ref,
+    pre_ref, prb_ref, rg_ref, rgb_ref, ro_ref, rq_ref, gl_ref, jl_ref, pl_ref, ql_ref, flat_ref,
 ):
     w = lax.axis_index("wide")
     there = column_masks(counts[1])
@@ -262,27 +335,29 @@
     halo_ref[odd] = odd_ref[:, row(0, SLOTS)]
     columns = [corners_ref[:, row(side)].astype(F32) for side in range(sides)]
 
-    pst_ref[:, row(2, 8)] = pst_own[...]
-    gst_ref[:, row(3, ROWS)] = gst_own[...]
-    jst_ref[:, row(1, ROWS)] = jst_own[...]
-    qst_ref[:, row(2, len(INNER))] = qst_own[...]
+    for i in range(2):
+        lane = HALO * (ROWS - HALO) if i == 0 else 0
+        for j in range(3):
+            main = halo_ref[i, :, row(2 + j)].astype(F32)
+            side = beside(columns, 64 + lane + HALO * (j + 1 - i))
+            put_cotangent(main, side, gst_ref, gsb_ref, 9 * i + j, 3 * i + j)
+        gst_ref[:, row(3 + 3 * i, 3)] = gst_own[:, row(13 * i, 3)]
+        rg_ref[:, row(3 * i, 3)] = dot(wg_ref[...], gst_ref[:, row(9 * i, 3)])
+    rgb_ref[...] = dot(wg_ref[96:192, :], gsb_ref[...])
     for i in range(2):
         lane = HALO * (ROWS - HALO) if i == 0 else 0
         sides_f = [beside(columns, lane + HALO * r) for r in range(HALO)]
         near = HALO - 1 if i == 0 else 0
-        put_features(halo_ref[i, :, row(0)].astype(F32), sides_f[near], jst_ref, 64, 17 * i)
         for j in range(2):
             main = halo_ref[i, j * 16 : j * 16 + 16, row(1)]
             side = pooled(sides_f[2 * j], sides_f[2 * j + 1])
-            put_pooled(main, side, pst_ref, psb_ref, 10 * i + j, 2 * i + j)
-        for j in range(3):
-            main = halo_ref[i, :, row(2 + j)].astype(F32)
-            side = beside(columns, 64 + lane + HALO * (j + 1 - i))
-            put_cotangent(main, side, gst_ref, gsb_ref, 19 * i + j, 3 * i + j)
-        pre_ref[:, row(2 * i, 2)] = dot(wc_ref[...], pst_ref[:, row(10 * i, 2)])
-        rg_ref[:, row(3 * i, 3)] = dot(wg_ref[...], gst_ref[:, row(19 * i, 3)])
+            put_pooled(main, side, pst_ref, psb_ref, 6 * i + j, 2 * i + j)
+        pst_ref[:, row(2 + 2 * i, 2)] = pst_own[:, row(6 * i, 2)]
+        pre_ref[:, row(2 * i, 2)] = dot(wc_ref[...], pst_ref[:, row(6 * i, 2)])
+        put_features(halo_ref[i, :, row(0)].astype(F32), sides_f[near], jst_ref, 64, 5 * i)
+        for d in range(3):
+            jst_ref[d * 64 : d * 64 + 32, row(1 + 2 * i, 2)] = jf_own[d * 32 : d * 32 + 32, row(14 * i, 2)]
     prb_ref[...] = dot(wc_ref[...], psb_ref[...])
-    rgb_ref[...] = dot(wg_ref[96:192, :], gsb_ref[...])
 
     def part(own, halo, lo, size, at, edge, length):
         if at < edge:
@@ -291,7 +366,7 @@
             return own[lo : lo + size, row(at - edge)]
         return halo[lo : lo + size, row(at - length)]
 
-    for at in (0, 1, 8, 9):
+    for k, at in enumerate((0, 1, 8, 9)):
         keep = has_above if at == 0 else has_below if at == 9 else 1.0
         values = [
             sum(part(own, halo, d * 32, 32, at + d, 2, 8) for d in range(3))
@@ -307,45 +382,21 @@
         ]
         acts, grads = coarse_row(values, totals, (keep, keep * there))
         for d in range(3):
-            for r in (2 * at - 1, 2 * at):
-                if 0 <= r < 18:
-                    jst_ref[d * 64 + 32 : d * 64 + 64, row(r)] = acts[d]
-            qst_ref[d * 32 : d * 32 + 32, row(at)] = grads[d]
-
+            for r in ((0,), (1, 2), (3, 4), (5,))[k]:
+                jst_ref[d * 64 + 32 : d * 64 + 64, row(r)] = acts[d]
+            qst_ref[d * 32 : d * 32 + 32, row(k)] = grads[d]
+
+    put_joined(jst_ref, row(1, 4), jl_ref, row(0, 4))
+    ql_ref[0:96, :] = jnp.zeros((96, 2 * COLS), BF)
+    ql_ref[96:128, :] = qst_ref[32:64, row(1, 2)]
     for i in range(2):
-        ro_ref[:, row(3 * i, 3)] = dot(wo_ref[...], jst_ref[:, row(15 * i, 3)])
-    for y in range(ROWS):
-        value = sum(part(ro_own, ro_ref, d * 32, 32, y + d, 3, ROWS - 4) for d in range(3))
-        for z in range(2):
-            flat_ref[pl.ds(2 * y + z, C1, stride=2 * ROWS), :] = value[z * 16 : z * 16 + 16]
-    out_ref[...] = flat_ref[...].astype(BF)
-
+        for ky in range(3):
+            gl_ref[ky * 96 : ky * 96 + 96, row(2 * i, 2)] = gst_ref[:, row(4 + 4 * i - ky, 2)]
+            pl_ref[ky * 48 : ky * 48 + 48, row(i)] = pst_ref[:, row(1 + 3 * i + ky)]
+    rf = rf_inner[...] + dot_nt(gl_ref[...], jl_ref[...])
+    rc = rc_inner[...] + dot_nt(pl_ref[...], ql_ref[...])
+    ro_ref[...] = dot(wo_ref[...], jst_ref[...])
     rq_ref[...] = dot(wq_ref[...], qst_ref[...])
-    for at in range(ROWS // 2):
-        coarse = rq_ref[0:16, row(at)] + rq_ref[16:32, row(at + 1)] + rq_ref[32:48, row(at + 2)]
-        coarse = coarse.astype(BF).astype(F32) * 0.125
-        for y in (2 * at, 2 * at + 1):
-            for z in range(2):
-                total = coarse
-                for d in range(3):
-                    total = total + part(rg_own, rg_ref, d * 32 + z * 16, 16, y + 2 + d, 3, ROWS)
-                flat_ref[pl.ds(2 * y + z, C1, stride=2 * ROWS), :] = total
-    gf_ref[...] = flat_ref[...].astype(BF)
-
-    own = row(1, ROWS)
-    for lo in (0, 48):
-        jl_ref[lo : lo + 16, :] = jst_ref[64:80, own]
-        jl_ref[lo + 16 : lo + 48, :] = jst_ref[96:128, own]
-        jl_ref[128 + lo : 128 + lo + 48, :] = jst_ref[80:128, own]
-    for lo in (96, 224):
-        jl_ref[lo : lo + 32, :] = jnp.zeros((32, ROWS * COLS), BF)
-    ql_ref[0:96, :] = jnp.zeros((96, 8 * COLS), BF)
-    ql_ref[96:128, :] = qst_ref[32:64, row(1, 8)]
-    for ky in range(3):
-        gl_ref[ky * 96 : ky * 96 + 96, :] = gst_ref[:, row(4 - ky, ROWS)]
-        pl_ref[ky * 48 : ky * 48 + 48, :] = pst_ref[:, row(1 + ky, 8)]
-    rf = dot_nt(gl_ref[...], jl_ref[...])
-    rc = dot_nt(pl_ref[...], ql_ref[...])
     fine, coarse = {}, {}
     for ky in range(3):
         for kx in range(3):
@@ -366,34 +417,50 @@
             value = jnp.where(lane16 >= 96, coarse[i // 3, i % 3], value)
         gw_ref[i * 16 : i * 16 + 16, :] = value.astype(BF)
 
-
-def rest(messages, own, matrices, counts, sides):
-    cells = (C1 * ROWS * 2, COLS)
-    v = lambda rows_, lanes_, kind: pltpu.VMEM((rows_, lanes_ * COLS), kind)
+    flat_ref[0] = out_inner[...]
+    flat_ref[1] = gf_inner[...]
+    for y in (0, 1, 2, 13, 14, 15):
+        value = sum(part(ro_inner, ro_ref, d * 32, 32, y + d, 3, len(FINE)) for d in range(3))
+        for z in range(2):
+            put_field(flat_ref.at[0], y, z, value[z * 16 : z * 16 + 16])
+    out_ref[...] = flat_ref[0].astype(BF)
+
+    for at in (0, 1, 6, 7):
+        coarse = sum(part(rq_inner, rq_ref, d * 16, 16, at + d, 2, len(INNER)) for d in range(3))
+        coarse = coarse.astype(BF).astype(F32) * 0.125
+        for y in (2 * at, 2 * at + 1):
+            for z in range(2):
+                lo = z * 16
+                value = sum(part(rg_own, rg_ref, lo + d * 32, 16, y + 2 + d, 3, ROWS) for d in range(3))
+                put_field(flat_ref.at[1], y, z, value + coarse)
+    gf_ref[...] = flat_ref[1].astype(BF)
+
+
+def rest(messages, own, inner, matrices, counts, sides):
     return pl.pallas_call(
         functools.partial(rest_kernel, counts, sides),
         out_shape=(
-            jax.ShapeDtypeStruct(cells, BF),
-            jax.ShapeDtypeStruct(cells, BF),
+            pltpu.VMEM((CELLS, COLS), BF),
+            pltpu.VMEM((CELLS, COLS), BF),
             jax.ShapeDtypeStruct((256, COLS), BF),
         ),
         scratch_shapes=[
             pltpu.VMEM((2, 32, SLOTS * COLS), BF),
-            v(192, 18, BF),
-            v(96, 22, BF), v(96, 6, BF),
-            v(48, 12, BF), v(48, 4, BF),
-            v(96, 10, BF),
-            v(96, 4, F32), v(96, 4, F32),
-            v(192, 6, F32), v(96, 6, F32),
-            v(96, 6, F32),
-            v(48, 10, F32),
-            pltpu.VMEM(cells, F32),
-            v(288, ROWS, BF), v(256, ROWS, BF), v(144, 8, BF), v(128, 8, BF),
+            scratch(192, 6, BF),
+            scratch(96, 12, BF), scratch(96, 6, BF),
+            scratch(48, 8, BF), scratch(48, 4, BF),
+            scratch(96, 4, BF),
+            scratch(96, 4, F32), scratch(96, 4, F32),
+            scratch(192, 6, F32), scratch(96, 6, F32),
+            scratch(96, 6, F32),
+            scratch(48, 4, F32),
+            scratch(288, 4, BF), scratch(256, 4, BF), scratch(144, 2, BF), scratch(128, 2, BF),
+            pltpu.VMEM((2, CELLS, COLS), F32),
         ],
         compiler_params=params(),
         cost_estimate=pl.CostEstimate(flops=10**9, bytes_accessed=4 * 10**6, transcendentals=10**5),
         name="rest",
-    )(*messages, *own, *matrices)
+    )(*messages, *own, *inner, *matrices)
 
 
 def add_kernel(parts_ref, copies_ref):
@@ -414,7 +481,15 @@
     )(parts)
 
 
-def spread_kernel(fine_scale, coarse_scale, sum_ref, fine_ref, coarse_ref):
+def spread_kernel(
+    fine_scale, coarse_scale, sum_ref, out_ref, gf_ref, out_hbm, gf_hbm, fine_ref, coarse_ref, sems
+):
+    copies = [
+        pltpu.make_async_copy(ref, hbm, sems.at[i])
+        for i, (ref, hbm) in enumerate(((out_ref, out_hbm), (gf_ref, gf_hbm)))
+    ]
+    for copy in copies:
+        copy.start()
     for i in range(27):
         if i < 14:
             value = sum_ref[i * 16 : i * 16 + 16, :].astype(F32)
@@ -429,18 +504,26 @@
         else:
             value = jnp.zeros((16, 32), F32)
         coarse_ref[i * 16 : i * 16 + 16, :] = value
-
-
-def spread(total, fine_scale, coarse_scale):
+    for copy in copies:
+        copy.wait()
+
+
+def spread(total, output, grad_features, fine_scale, coarse_scale):
+    vmem, anywhere = pl.BlockSpec(memory_space=pltpu.VMEM), pl.BlockSpec(memory_space=pl.ANY)
     return pl.pallas_call(
         functools.partial(spread_kernel, fine_scale, coarse_scale),
+        in_specs=[vmem] * 3,
+        out_specs=(anywhere, anywhere, vmem, vmem),
         out_shape=(
-            jax.ShapeDtypeStruct((432, 48), F32),
-            jax.ShapeDtypeStruct((432, 32), F32),
+            jax.ShapeDtypeStruct((CELLS, COLS), BF),
+            jax.ShapeDtypeStruct((CELLS, COLS), BF),
+            jax.ShapeDtypeStruct((TAPS, 48), F32),
+            jax.ShapeDtypeStruct((TAPS, 32), F32),
         ),
-        compiler_params=pltpu.CompilerParams(vmem_limit_bytes=VMEM_LIMIT),
+        scratch_shapes=[pltpu.SemaphoreType.DMA((2,))],
+        compiler_params=params(),
         name="spread",
-    )(total)
+    )(total, output, grad_features)
 
 
 def matrices_kernel(
@@ -517,10 +600,13 @@
     columns = beside_blocks(strip, narrow)
     wo, wg, wc, wq = weight_matrices(stacked)
     corners = odd[:, SLOTS * COLS :] + even[:, SLOTS * COLS :]
-    columns, _ = lax.optimization_barrier((columns, corners))
+    stacks = own_rows(own, columns, wc, wg, sides)
+    stacks, _ = lax.optimization_barrier((stacks, corners))
+    inner = inner_rows(stacks, wo, wq, narrow)
     corners = beside_blocks(corners, narrow)
-    stacks = own_rows(own, columns, wo, wc, wg, (wide, narrow), sides)
-    output, grad_features, grads = rest((odd, even, corners), stacks, (wo, wg, wc, wq), (wide, narrow), sides)
+    output, grad_features, grads = rest(
+        (odd, even, corners), stacks, inner, (wo, wg, wc, wq), (wide, narrow), sides
+    )
     devices = wide * narrow
     share = -(-256 // devices)
     grads = jnp.pad(grads, ((0, share * devices - 256), (0, 0))).reshape(devices, share, COLS)
@@ -529,8 +615,8 @@
     total = lax.all_to_all(add_up(parts), both, 0, 0, tiled=True)
     total = total.reshape(share * devices, COLS)[:256]
     all_cells = features.shape[1] * features.shape[2] * features.shape[3] * devices
-    grad_fine, grad_coarse = spread(
-        total, 1.0 / math.sqrt(all_cells), 1.0 / math.sqrt(all_cells // 8)
+    output, grad_features, grad_fine, grad_coarse = spread(
+        total, output, grad_features, 1.0 / math.sqrt(all_cells), 1.0 / math.sqrt(all_cells // 8)
     )
     grad_fine = jnp.transpose(grad_fine.reshape(3, 3, 3, C1, C1 + C2), (3, 4, 0, 1, 2))
     grad_coarse = jnp.transpose(grad_coarse.reshape(3, 3, 3, C1, C2), (4, 3, 0, 1, 2))

time: 38.7 us -> 38.8 us (level)
  waiting for transfers between devices: 1.28 us -> 2.09 us
  Pallas kernels: 6.28 us -> 5.65 us
    ppermute x2, starting transfers between devices: 2.09 us -> 3.61 us  [beside_blocks(): return lax.ppermute(outer, 'narrow', [(0, 1), (1, 0)])]
    ppermute x1, starting transfers between devices: 4.39 us -> 2.94 us  [shards(): even = lax.ppermute(to_even, 'wide', swaps(0))]
    pallas_call x1, Pallas kernels: 2.29 us -> 1.11 us  [rest(): pl.pallas_call(functools.partial(rest_kernel, counts, sides), out_shape=(...]
    ppermute x2, waiting for transfers between devices: 1.27 us -> 2.09 us  [beside_blocks(): return lax.ppermute(outer, 'narrow', [(0, 1), (1, 0)])]
    pallas_call x1, Pallas kernels: 0.85 us -> 1.47 us  [spread(): pl.pallas_call(functools.partial(spread_kernel, fine_scale, coarse_scale)...]
    pallas_call x1 -> x2, Pallas kernels: 2.39 us -> 2.32 us  [the longest x1 1.3 us: own_rows(): pl.pallas_call(functools.partial(own_kernel, sides), out_shape=(shaped(48...]
where the time goes in v13:
time: 38.8 us; the launch traced here: 38.7 us
  blocking collectives  21.8 us (56%)
  starting transfers between devices  7.2 us (19%)
  Pallas kernels  5.65 us (15%)
  waiting for transfers between devices  2.09 us (5%)
  other arithmetic  1.21 us (3%)
  between operations  0.71 us (2%)
    all_to_all x1, blocking collectives, shards(): parts = lax.all_to_all(grads, both, 0, 0, tiled=True)  12.5 us
    all_to_all x1, blocking collectives, shards(): total = lax.all_to_all(add_up(parts), both, 0, 0, tiled=True)  9.3 us
    ppermute x2, starting transfers between devices, beside_blocks(): return lax.ppermute(outer, 'narrow', [(0, 1), (1, 0)])  3.61 us
    ppermute x1, starting transfers between devices, shards(): even = lax.ppermute(to_even, 'wide', swaps(0))  2.94 us
    ppermute x2, waiting for transfers between devices, beside_blocks(): return lax.ppermute(outer, 'narrow', [(0, 1), (1, 0)])  2.09 us
    pallas_call x1, Pallas kernels, spread(): pl.pallas_call(functools.partial(spread_kernel, fine_scale, coarse_scale)...  1.47 us
    pallas_call x1, Pallas kernels, own_rows(): pl.pallas_call(functools.partial(own_kernel, sides), out_shape=(shaped(48...  1.3 us
    concatenate x1, other arithmetic, stack(): return jnp.concatenate([flat(features), flat(cotangent), weights], 0)  1.21 us
  transfers between devices with their start and end apart: 4, of which 1 were waited for; matrix products, arithmetic and copies ran while one was open for 0% of the time, Pallas kernels for 7%

profile of v13, /device:TPU:0, one launch (start us, length us, event | category | flops | bytes accessed | tf_op | source)
XLA Modules:
  0.0 38.7 jit_solution(1594020873810630184)
XLA Ops:
  0.7 1.2 %maximum_maximum_fusion.in_ref = bf16[1456,128]{1,0:T(8,128)(2,1)S(1)} fusion(bf16[432,48]{1,0:T(8,128)(2,1)S(1)} %broadcast_in_dim.3, bf16[432,32]{1,0:T(8,128)(2,1)} %bitcast.22, bf16[432,48]{1,0:T(8,128)(2,1)} %bitcast.23, bf16[512,128]{1,0:T(8,128)(2,1)} %bitcast.20, bf16[512,128]{1,0:T(8,128)(2,1)} %bitcast.21), kind=kLoop, calls=%fused_computation | loop fusion | flops 1863680 | bytes 745472 | tf_op jit(solution)/shard_map/concatenate | solution.py:97
  1.9 0.5 %pack.1 = (bf16[64,2048]{1,0:T(8,128)(2,1)S(1)}, bf16[32,128]{1,0:T(8,128)(2,1)S(1)}, bf16[32,768]{1,0:T(8,128)(2,1)S(1)}, bf16[32,768]{1,0:T(8,128)(2,1)S(1)}) custom-call(bf16[1456,128]{1,0:T(8,128)(2,1)S(1)} %maximum_maximum_fusion.in_ref), custom_call_target="tpu_custom_call" | custom-call | flops 1000000 | bytes 1000000 | tf_op jit(solution)/shard_map/pack/pallas_call | solution.py:102
  2.3 3.0 %collective-permute-start.3 = (bf16[32,128]{1,0:T(8,128)(2,1)S(1)}, bf16[32,128]{1,0:T(8,128)(2,1)S(1)}, u32[]{:S(2)}, u32[]{:S(2)}) collective-permute-start(bf16[32,128]{1,0:T(8,128)(2,1)S(1)} %get-tuple-element.42), channel_id=1, source_target_pairs={{0,1},{1,0},{2,3},{3,2},{4,5},{5,4},{6,7},{7,6},{8,9},{9,8},{10,11... | collective-permute-start | bytes 24584 | tf_op jit(solution)/shard_map/ppermute | solution.py:584
  5.3 0.7 %collective-permute-start = (bf16[32,768]{1,0:T(8,128)(2,1)S(1)}, bf16[32,768]{1,0:T(8,128)(2,1)S(1)}, u32[]{:S(2)}, u32[]{:S(2)}) collective-permute-start(bf16[32,768]{1,0:T(8,128)(2,1)S(1)} %get-tuple-element.39), channel_id=1, source_target_pairs={{2,4},{4,2},{6,8},{8,6},{10,12},{12,10},{14,16},{16,14},{18,20},{2... | collective-permute-start | bytes 147464 | tf_op jit(solution)/shard_map/ppermute | solution.py:598
  6.0 2.9 %collective-permute-start.1 = (bf16[32,768]{1,0:T(8,128)(2,1)S(1)}, bf16[32,768]{1,0:T(8,128)(2,1)S(1)}, u32[]{:S(2)}, u32[]{:S(2)}) collective-permute-start(bf16[32,768]{1,0:T(8,128)(2,1)S(1)} %get-tuple-element.40), channel_id=1, source_target_pairs={{0,2},{2,0},{4,6},{6,4},{8,10},{10,8},{12,14},{14,12},{16,18},{18,... | collective-permute-start | bytes 147464 | tf_op jit(solution)/shard_map/ppermute | solution.py:599
  8.9 0.2 matrices.1
  9.2 0.0 collective-permute-done.3.columns_ref
  9.2 1.3 %own_rows.1 = (bf16[48,1024]{1,0:T(8,128)(2,1)S(1)}, bf16[96,2048]{1,0:T(8,128)(2,1)S(1)}, bf16[96,2048]{1,0:T(8,128)(2,1)S(1)}, f32[96,1024]{1,0:T(8,128)S(1)},...) custom-call(bf16[64,2048]{1,0:T(8,128)(2,1)S(1)} %get-tuple-element.41.s_ref, ...), custom_call_target="tpu_custom_call" | custom-call | flops 1000000000 | bytes 4000000 | tf_op jit(solution)/shard_map/own_rows/pallas_call | solution.py:215
  10.5 0.0 collective-permute-done.odd_ref
  10.5 0.0 collective-permute-done.1.even_ref
  10.5 0.6 %collective-permute-start.2 = (bf16[32,128]{1,0:T(8,128)(2,1)S(1)}, bf16[32,128]{1,0:T(8,128)(2,1)S(1)}, u32[]{:S(2)}, u32[]{:S(2)}) collective-permute-start(bf16[32,128]{1,0:T(8,128)(2,1)S(1)} %slice_add_fusion), channel_id=1, source_target_pairs={{0,1},{1,0},{2,3},{3,2},{4,5},{5,4},{6,7},{7,6},{8,9},{9,8},{10,11... | collective-permute-start | bytes 24584 | tf_op jit(solution)/shard_map/ppermute | solution.py:584
  11.1 1.0 %inner_rows.1 = (f32[512,128]{1,0:T(8,128)S(1)}, f32[512,128]{1,0:T(8,128)S(1)}, f32[96,1536]{1,0:T(8,128)S(1)}, f32[48,768]{1,0:T(8,128)S(1)}, f32[288,256]{1,0:T(8,128)S(1)}, /*index=5*/f32[144,128]{1,0:T(8,128)S(1)}) custom-call(bf16[48,1024]{1,0:T(8,128)(2,1)S(1)} %get-tuple-element.52.pst_ref.pst_own, ...), custom_call_target="tpu_custom_call" | custom-call | flops 1000000000 | bytes 4000000 | tf_op jit(solution)/shard_map/inner_rows/pallas_call | solution.py:300
  12.2 2.1 %collective-permute-done.2.corners_ref = bf16[32,128]{1,0:T(8,128)(2,1)S(1)} collective-permute-done((bf16[32,128]{1,0:T(8,128)(2,1)S(1)}, bf16[32,128]{1,0:T(8,128)(2,1)S(1)}, u32[]{:S(2)}, u32[]{:S(2)}) %collective-permute-start.2) | collective-permute-done | bytes 8224 | tf_op jit(solution)/shard_map/ppermute | solution.py:584
  14.3 1.1 %rest.1 = (bf16[512,128]{1,0:T(8,128)(2,1)S(1)}, bf16[512,128]{1,0:T(8,128)(2,1)S(1)}, bf16[256,128]{1,0:T(8,128)(2,1)S(1)}) custom-call(bf16[32,768]{1,0:T(8,128)(2,1)S(1)} %collective-permute-done.odd_ref, bf16[32,768]{1,0:T(8,128)(2,1)S(1)} %collective-permute-done.1.even_ref, bf16[32,128]{1,0:T(8,128)(2,1)S(1)} %collective-permute-done.2.corners_ref, ...), custom_call_target="tpu_custom_call" | custom-call | flops 1000000000 | bytes 4000000 | tf_op jit(solution)/shard_map/rest/pallas_call | solution.py:440
  15.4 12.5 %all_to_all.10.parts_ref = bf16[32,8,128]{2,1,0:T(8,128)(2,1)S(1)} all-to-all(bf16[32,8,128]{2,1,0:T(8,128)(2,1)S(1)} %bitcast.19), channel_id=1, replica_groups=mesh['wide'=16,'narrow'=2] {'wide','narrow'}, dimensions={0} | all-to-all | bytes 131072 | tf_op jit(solution)/shard_map/all_to_all | solution.py:614
  27.9 9.3 %all_to_all.11 = bf16[32,8,128]{2,1,0:T(8,128)(2,1)S(1)} all-to-all(bf16[32,8,128]{2,1,0:T(8,128)(2,1)S(1)} %add_up.1), channel_id=1, replica_groups=mesh['wide'=16,'narrow'=2] {'wide','narrow'}, dimensions={0} | all-to-all | bytes 131072 | tf_op jit(solution)/shard_map/all_to_all | solution.py:615
  37.2 1.5 %spread.1 = (bf16[512,128]{1,0:T(8,128)(2,1)}, bf16[512,128]{1,0:T(8,128)(2,1)}, f32[432,48]{1,0:T(8,128)}, f32[432,32]{1,0:T(8,128)}) custom-call(bf16[256,128]{1,0:T(8,128)(2,1)S(1)} %bitcast.18, bf16[512,128]{1,0:T(8,128)(2,1)S(1)} %get-tuple-element.68.out_ref, bf16[512,128]{1,0:T(8,128)(2,1)S(1)} %get-tuple-element.69.gf_ref), custom_call_target="tpu_custom_call" | custom-call | tf_op jit(solution)/shard_map/spread/pallas_call | solution.py:513
  (3 shorter events, 0.1 us)
Async XLA Ops:
  2.3 6.9 %collective-permute-start.3 = (bf16[32,128]{1,0:T(8,128)(2,1)S(1)}, bf16[32,128]{1,0:T(8,128)(2,1)S(1)}, u32[]{:S(2)}, u32[]{:S(2)}) collective-permute-start(bf16[32,128]{1,0:T(8,128)(2,1)S(1)} %get-tuple-element.42), channel_id=1, source_target_pairs={{0,1},{1,0},{2,3},{3,2},{4,5},{5,4},{6,7},{7,6},{8,9},{9,8},{10,11... | collective-permute-start | bytes 24584 | tf_op jit(solution)/shard_map/ppermute | solution.py:584
  5.3 5.2 %collective-permute-start = (bf16[32,768]{1,0:T(8,128)(2,1)S(1)}, bf16[32,768]{1,0:T(8,128)(2,1)S(1)}, u32[]{:S(2)}, u32[]{:S(2)}) collective-permute-start(bf16[32,768]{1,0:T(8,128)(2,1)S(1)} %get-tuple-element.39), channel_id=1, source_target_pairs={{2,4},{4,2},{6,8},{8,6},{10,12},{12,10},{14,16},{16,14},{18,20},{2... | collective-permute-start | bytes 147464 | tf_op jit(solution)/shard_map/ppermute | solution.py:598
  6.0 4.5 %collective-permute-start.1 = (bf16[32,768]{1,0:T(8,128)(2,1)S(1)}, bf16[32,768]{1,0:T(8,128)(2,1)S(1)}, u32[]{:S(2)}, u32[]{:S(2)}) collective-permute-start(bf16[32,768]{1,0:T(8,128)(2,1)S(1)} %get-tuple-element.40), channel_id=1, source_target_pairs={{0,2},{2,0},{4,6},{6,4},{8,10},{10,8},{12,14},{14,12},{16,18},{18,... | collective-permute-start | bytes 147464 | tf_op jit(solution)/shard_map/ppermute | solution.py:599
  10.5 3.7 %collective-permute-start.2 = (bf16[32,128]{1,0:T(8,128)(2,1)S(1)}, bf16[32,128]{1,0:T(8,128)(2,1)S(1)}, u32[]{:S(2)}, u32[]{:S(2)}) collective-permute-start(bf16[32,128]{1,0:T(8,128)(2,1)S(1)} %slice_add_fusion), channel_id=1, source_target_pairs={{0,1},{1,0},{2,3},{3,2},{4,5},{5,4},{6,7},{7,6},{8,9},{9,8},{10,11... | collective-permute-start | bytes 24584 | tf_op jit(solution)/shard_map/ppermute | solution.py:584

commit v14 on v13

--- a/solution.py
+++ b/solution.py
@@ -51,25 +51,54 @@
 TAPS = 27 * C1
 
 
-def pack_kernel(sides, in_ref, s_ref, strip_ref, odd_ref, even_ref, wide_ref, base_ref):
+def chunks(pairs, sems, pieces):
+    copies = []
+    for i, (source, target) in enumerate(pairs):
+        rows = source.shape[0] // pieces
+        copies.append([
+            pltpu.make_async_copy(
+                source.at[pl.ds(j * rows, rows)], target.at[pl.ds(j * rows, rows)], sems.at[i, j]
+            )
+            for j in range(pieces)
+        ])
+    return copies
+
+
+def start(copies):
+    for copy in copies:
+        copy.start()
+
+
+def wait(copies):
+    for copy in copies:
+        copy.wait()
+
+
+def pack_kernel(
+    sides, f_hbm, g_hbm, s_ref, strip_ref, odd_ref, even_ref, f_ref, g_ref, wide_ref, base_ref, sems
+):
+    arrivals = chunks(((f_hbm, f_ref), (g_hbm, g_ref)), sems, 4)
+    for copies in arrivals:
+        start(copies)
     lane = lanes_of((C1, COLS))
     place = lax.axis_index("narrow")
     odd = lax.axis_index("wide") % 2
     strips = [[jnp.zeros((C1, COLS), F32) for _ in range(sides)] for _ in range(2)]
     for a in range(2):
-        wide_ref[...] = in_ref[a * CELLS : (a + 1) * CELLS, :].astype(F32)
+        wait(arrivals[a])
+        wide_ref[...] = (f_ref, g_ref)[a][...].astype(F32)
         for z in range(2):
             chans = slice(a * 32 + z * 16, a * 32 + z * 16 + 16)
             for y in range(ROWS):
                 value = wide_ref[pl.ds(2 * y + z, C1, stride=2 * ROWS), :]
                 s_ref[chans, row(y)] = value.astype(BF)
-                start = 64 * a + HALO * y
-                inside = (lane >= start) & (lane < start + HALO)
+                first = 64 * a + HALO * y
+                inside = (lane >= first) & (lane < first + HALO)
                 for side in range(sides):
                     if sides == 2:
-                        shift = (start + HALO * side) % COLS
+                        shift = (first + HALO * side) % COLS
                     else:
-                        shift = lax.rem(start + HALO * (1 - place), COLS)
+                        shift = lax.rem(first + HALO * (1 - place), COLS)
                     strips[z][side] = jnp.where(inside, pltpu.roll(value, shift, 1), strips[z][side])
     for z in range(2):
         for side in range(sides):
@@ -89,18 +118,16 @@
     odd_ref[...] = base_ref[1 - odd]
 
 
-def stack(features, cotangent, coarse_weight, fine_weight):
-    flat = lambda a: a.reshape(CELLS, COLS)
-    fine = jnp.transpose(fine_weight, (2, 3, 4, 0, 1)).reshape(TAPS, 48)
-    coarse = jnp.transpose(coarse_weight, (2, 3, 4, 1, 0)).reshape(TAPS, 32)
-    weights = jnp.concatenate([fine, coarse, jnp.zeros((TAPS, 48), BF)], 1)
-    return jnp.concatenate([flat(features), flat(cotangent), weights], 0)
-
-
-def pack(stacked, sides):
+def kept_in_hbm(array):
+    return pltpu.with_memory_space_constraint(array, pltpu.HBM)
+
+
+def pack(features, cotangent, sides):
+    flat = lambda a: kept_in_hbm(a.reshape(CELLS, COLS))
     message = jax.ShapeDtypeStruct((32, (SLOTS + sides) * COLS), BF)
     return pl.pallas_call(
         functools.partial(pack_kernel, sides),
+        in_specs=[pl.BlockSpec(memory_space=pltpu.HBM)] * 2,
         out_shape=(
             jax.ShapeDtypeStruct((64, ROWS * COLS), BF),
             jax.ShapeDtypeStruct((32, sides * COLS), BF),
@@ -108,13 +135,16 @@
             message,
         ),
         scratch_shapes=[
-            pltpu.VMEM((C1 * ROWS * 2, COLS), F32),
+            pltpu.VMEM((CELLS, COLS), BF),
+            pltpu.VMEM((CELLS, COLS), BF),
+            pltpu.VMEM((CELLS, COLS), F32),
             pltpu.VMEM((2, 32, (SLOTS + sides) * COLS), BF),
+            pltpu.SemaphoreType.DMA((2, 4)),
         ],
         compiler_params=params(),
         cost_estimate=pl.CostEstimate(flops=10**6, bytes_accessed=10**6, transcendentals=0),
         name="pack",
-    )(stacked)
+    )(flat(features), flat(cotangent))
 
 
 def beside(columns, at):
@@ -482,20 +512,20 @@
 
 
 def spread_kernel(
-    fine_scale, coarse_scale, sum_ref, out_ref, gf_ref, out_hbm, gf_hbm, fine_ref, coarse_ref, sems
+    fine_scale, coarse_scale,
+    sum_ref, out_ref, gf_ref,
+    out_hbm, gf_hbm, fine_hbm, coarse_hbm,
+    fine_ref, coarse_ref, field_sems, weight_sems,
 ):
-    copies = [
-        pltpu.make_async_copy(ref, hbm, sems.at[i])
-        for i, (ref, hbm) in enumerate(((out_ref, out_hbm), (gf_ref, gf_hbm)))
-    ]
-    for copy in copies:
-        copy.start()
+    fields = chunks(((out_ref, out_hbm), (gf_ref, gf_hbm)), field_sems, 4)
+    weights = chunks(((fine_ref, fine_hbm), (coarse_ref, coarse_hbm)), weight_sems, 3)
+    for copies in fields:
+        start(copies)
     for i in range(27):
-        if i < 14:
-            value = sum_ref[i * 16 : i * 16 + 16, :].astype(F32)
-        else:
-            at = (i - 14) * 16
-            value = pltpu.roll(sum_ref[at : at + 16, :].astype(F32), 80, 1)
+        at = (i if i < 14 else i - 14) * 16
+        value = sum_ref[at : at + 16, :].astype(F32)
+        if i >= 14:
+            value = pltpu.roll(value, 80, 1)
         fine_ref[i * 16 : i * 16 + 16, :] = value[:, 0:48] * fine_scale
         ky, kz, kx = i // 9, i // 3 % 3, i % 3
         if kz == 1:
@@ -504,33 +534,45 @@
         else:
             value = jnp.zeros((16, 32), F32)
         coarse_ref[i * 16 : i * 16 + 16, :] = value
-    for copy in copies:
-        copy.wait()
+        if i % 9 == 8:
+            weights[0][ky].start()
+            weights[1][ky].start()
+    for copies in fields + weights:
+        wait(copies)
 
 
 def spread(total, output, grad_features, fine_scale, coarse_scale):
-    vmem, anywhere = pl.BlockSpec(memory_space=pltpu.VMEM), pl.BlockSpec(memory_space=pl.ANY)
     return pl.pallas_call(
         functools.partial(spread_kernel, fine_scale, coarse_scale),
-        in_specs=[vmem] * 3,
-        out_specs=(anywhere, anywhere, vmem, vmem),
+        in_specs=[pl.BlockSpec(memory_space=pltpu.VMEM)] * 3,
+        out_specs=(pl.BlockSpec(memory_space=pl.ANY),) * 4,
         out_shape=(
             jax.ShapeDtypeStruct((CELLS, COLS), BF),
             jax.ShapeDtypeStruct((CELLS, COLS), BF),
             jax.ShapeDtypeStruct((TAPS, 48), F32),
             jax.ShapeDtypeStruct((TAPS, 32), F32),
         ),
-        scratch_shapes=[pltpu.SemaphoreType.DMA((2,))],
+        scratch_shapes=[
+            pltpu.VMEM((TAPS, 48), F32),
+            pltpu.VMEM((TAPS, 32), F32),
+            pltpu.SemaphoreType.DMA((2, 4)),
+            pltpu.SemaphoreType.DMA((2, 3)),
+        ],
         compiler_params=params(),
         name="spread",
     )(total, output, grad_features)
 
 
 def matrices_kernel(
-    in_ref, wo_ref, wg_ref, wc_ref, wq_ref, wide_ref, pieces_ref, blocks_ref
+    fine_hbm, coarse_hbm, wo_ref, wg_ref, wc_ref, wq_ref,
+    fine_ref, coarse_ref, wide_ref, pieces_ref, blocks_ref, sems,
 ):
+    fine_copies, coarse_copies = chunks(((fine_hbm, fine_ref), (coarse_hbm, coarse_ref)), sems, 3)
+    start(fine_copies)
+    start(coarse_copies)
     lane = lanes_of((C1, COLS))
-    wide_ref[...] = in_ref[2 * CELLS : 2 * CELLS + TAPS, :].astype(F32)
+    wait(fine_copies)
+    wide_ref[:, 0:48] = fine_ref[...].astype(F32)
     for ky in range(3):
         for zo in range(2):
             tiles = [jnp.zeros((C1, COLS), F32) for _ in range(2)]
@@ -546,12 +588,13 @@
             spot = ky * 32 + zo * 16
             wo_ref[spot : spot + 16, 0:128] = tiles[0].astype(BF)
             wo_ref[spot : spot + 16, 128:192] = tiles[1][:, 0:64].astype(BF)
+    wait(coarse_copies)
+    wide_ref[:, 0:32] = coarse_ref[...].astype(F32)
     for ky in range(3):
         total = jnp.zeros((C1, COLS), F32)
         for kx in range(3):
             at = ((ky * 3 + 1) * 3 + kx) * 16
-            value = pltpu.roll(wide_ref[at : at + 16, :], 80, 1)
-            value = jnp.where(lane < 32, value, 0.0)
+            value = jnp.where(lane < 32, wide_ref[at : at + 16, :], 0.0)
             blocks_ref[ky, kx * 16 : kx * 16 + 16, :] = value
             spot = (2 - kx) * 32
             total = total + (pltpu.roll(value, spot, 1) if spot else value)
@@ -563,20 +606,26 @@
         wc_ref[d * 32 : d * 32 + 32, :] = jnp.transpose(blocks_ref[d])[0:32, 0:48].astype(BF)
 
 
-def weight_matrices(stacked):
+def weight_matrices(coarse_weight, fine_weight):
+    fine = jnp.transpose(fine_weight, (2, 3, 4, 0, 1)).reshape(TAPS, 48)
+    coarse = jnp.transpose(coarse_weight, (2, 3, 4, 1, 0)).reshape(TAPS, 32)
     shape = lambda *dims: jax.ShapeDtypeStruct(dims, BF)
     return pl.pallas_call(
         matrices_kernel,
+        in_specs=[pl.BlockSpec(memory_space=pltpu.HBM)] * 2,
         out_shape=(shape(96, 192), shape(192, 96), shape(96, 48), shape(48, 96)),
         scratch_shapes=[
+            pltpu.VMEM((TAPS, 48), BF),
+            pltpu.VMEM((TAPS, 32), BF),
             pltpu.VMEM((TAPS, COLS), F32),
             pltpu.VMEM((3, COLS, COLS), F32),
             pltpu.VMEM((3, COLS, COLS), F32),
+            pltpu.SemaphoreType.DMA((2, 3)),
         ],
         compiler_params=params(),
         cost_estimate=pl.CostEstimate(flops=10**6, bytes_accessed=10**6, transcendentals=0),
         name="matrices",
-    )(stacked)
+    )(kept_in_hbm(fine), kept_in_hbm(coarse))
 
 
 def beside_blocks(outer, narrow):
@@ -590,15 +639,14 @@
 def shards(features, cotangent, coarse_weight, fine_weight):
     wide, narrow = lax.axis_size("wide"), lax.axis_size("narrow")
     sides = 1 if narrow == 2 else 2
-    stacked = stack(features, cotangent, coarse_weight, fine_weight)
-    own, strip, to_odd, to_even = pack(stacked, sides)
+    own, strip, to_odd, to_even = pack(features, cotangent, sides)
     swaps = lambda start: [
         pair for i in range(start, wide - 1, 2) for pair in ((i, i + 1), (i + 1, i))
     ]
     odd = lax.ppermute(to_odd, "wide", swaps(1))
     even = lax.ppermute(to_even, "wide", swaps(0))
     columns = beside_blocks(strip, narrow)
-    wo, wg, wc, wq = weight_matrices(stacked)
+    wo, wg, wc, wq = weight_matrices(coarse_weight, fine_weight)
     corners = odd[:, SLOTS * COLS :] + even[:, SLOTS * COLS :]
     stacks = own_rows(own, columns, wc, wg, sides)
     stacks, _ = lax.optimization_barrier((stacks, corners))

time: 38.8 us -> 38.2 us (0.985)
  Pallas kernels: 5.65 us -> 7.04 us
  other arithmetic: 1.21 us -> 0.01 us
  blocking collectives: 21.8 us -> 20.8 us
    pallas_call x2, Pallas kernels: 0.71 us -> 2.6 us  [the longest x1 1.4 us: pack(): pl.pallas_call(functools.partial(pack_kernel, sides), in_specs=[pl.BlockS...]
    concatenate x1 -> x0, other arithmetic: 1.21 us -> none  [stack(): return jnp.concatenate([flat(features), flat(cotangent), weights], 0)]
    all_to_all x1, blocking collectives: 12.5 us -> 11.5 us  [shards(): parts = lax.all_to_all(grads, both, 0, 0, tiled=True)]
    pallas_call x1, Pallas kernels: 1.47 us -> 0.96 us  [spread(): pl.pallas_call(functools.partial(spread_kernel, fine_scale, coarse_scale)...]
  transfers between devices with their start and end apart: 4 -> 4, of which waited for: 1 -> 1; matrix products, arithmetic and copies ran while one was open for 0% -> 0% of each run, Pallas kernels for 7% -> 9%
where the time goes in v14:
time: 38.2 us; the launch traced here: 37.9 us
  blocking collectives  20.8 us (54%)
  starting transfers between devices  7.2 us (19%)
  Pallas kernels  7.04 us (18%)
  waiting for transfers between devices  2.1 us (5%)
  between operations  0.7 us (2%)
    all_to_all x1, blocking collectives, shards(): parts = lax.all_to_all(grads, both, 0, 0, tiled=True)  11.5 us
    all_to_all x1, blocking collectives, shards(): total = lax.all_to_all(add_up(parts), both, 0, 0, tiled=True)  9.3 us
    ppermute x2, starting transfers between devices, beside_blocks(): return lax.ppermute(outer, 'narrow', [(0, 1), (1, 0)])  3.6 us
    ppermute x1, starting transfers between devices, shards(): even = lax.ppermute(to_even, 'wide', swaps(0))  2.94 us
    ppermute x2, waiting for transfers between devices, beside_blocks(): return lax.ppermute(outer, 'narrow', [(0, 1), (1, 0)])  2.09 us
    pallas_call x1, Pallas kernels, pack(): pl.pallas_call(functools.partial(pack_kernel, sides), in_specs=[pl.BlockS...  1.4 us
    pallas_call x1, Pallas kernels, own_rows(): pl.pallas_call(functools.partial(own_kernel, sides), out_shape=(shaped(48...  1.3 us
    pallas_call x1, Pallas kernels, weight_matrices(): pl.pallas_call(matrices_kernel, in_specs=[pl.BlockSpec(memory_space=pltpu...  1.2 us
  transfers between devices with their start and end apart: 4, of which 1 were waited for; matrix products, arithmetic and copies ran while one was open for 0% of the time, Pallas kernels for 9%

profile of v14, /device:TPU:0, one launch (start us, length us, event | category | flops | bytes accessed | tf_op | source)
XLA Modules:
  0.0 37.9 jit_solution(14353293875699821747)
XLA Ops:
  0.6 1.4 %pack.1 = (bf16[64,2048]{1,0:T(8,128)(2,1)S(1)}, bf16[32,128]{1,0:T(8,128)(2,1)S(1)}, bf16[32,768]{1,0:T(8,128)(2,1)S(1)}, bf16[32,768]{1,0:T(8,128)(2,1)S(1)}) custom-call(bf16[512,128]{1,0:T(8,128)(2,1)} %bitcast.20, bf16[512,128]{1,0:T(8,128)(2,1)} %bitcast.21), custom_call_target="tpu_custom_call" | custom-call | flops 1000000 | bytes 1000000 | tf_op jit(solution)/shard_map/pack/pallas_call | solution.py:128
  2.0 3.0 %collective-permute-start.3 = (bf16[32,128]{1,0:T(8,128)(2,1)S(1)}, bf16[32,128]{1,0:T(8,128)(2,1)S(1)}, u32[]{:S(2)}, u32[]{:S(2)}) collective-permute-start(bf16[32,128]{1,0:T(8,128)(2,1)S(1)} %get-tuple-element.42), channel_id=1, source_target_pairs={{0,1},{1,0},{2,3},{3,2},{4,5},{5,4},{6,7},{7,6},{8,9},{9,8},{10,11... | collective-permute-start | bytes 24584 | tf_op jit(solution)/shard_map/ppermute | solution.py:633
  5.0 0.7 %collective-permute-start = (bf16[32,768]{1,0:T(8,128)(2,1)S(1)}, bf16[32,768]{1,0:T(8,128)(2,1)S(1)}, u32[]{:S(2)}, u32[]{:S(2)}) collective-permute-start(bf16[32,768]{1,0:T(8,128)(2,1)S(1)} %get-tuple-element.39), channel_id=1, source_target_pairs={{2,4},{4,2},{6,8},{8,6},{10,12},{12,10},{14,16},{16,14},{18,20},{2... | collective-permute-start | bytes 147464 | tf_op jit(solution)/shard_map/ppermute | solution.py:646
  5.7 2.9 %collective-permute-start.1 = (bf16[32,768]{1,0:T(8,128)(2,1)S(1)}, bf16[32,768]{1,0:T(8,128)(2,1)S(1)}, u32[]{:S(2)}, u32[]{:S(2)}) collective-permute-start(bf16[32,768]{1,0:T(8,128)(2,1)S(1)} %get-tuple-element.40), channel_id=1, source_target_pairs={{0,2},{2,0},{4,6},{6,4},{8,10},{10,8},{12,14},{14,12},{16,18},{18,... | collective-permute-start | bytes 147464 | tf_op jit(solution)/shard_map/ppermute | solution.py:647
  8.6 1.2 %matrices.1 = (bf16[96,192]{1,0:T(8,128)(2,1)S(1)}, bf16[192,96]{1,0:T(8,128)(2,1)S(1)}, bf16[96,48]{1,0:T(8,128)(2,1)S(1)}, bf16[48,96]{1,0:T(8,128)(2,1)S(1)}) custom-call(bf16[432,48]{1,0:T(8,128)(2,1)} %bitcast.22, bf16[432,32]{1,0:T(8,128)(2,1)} %bitcast.23), custom_call_target="tpu_custom_call" | custom-call | flops 1000000 | bytes 1000000 | tf_op jit(solution)/shard_map/matrices/pallas_call | solution.py:613
  9.9 0.0 collective-permute-done.3.columns_ref
  9.9 1.3 %own_rows.1 = (bf16[48,1024]{1,0:T(8,128)(2,1)S(1)}, bf16[96,2048]{1,0:T(8,128)(2,1)S(1)}, bf16[96,2048]{1,0:T(8,128)(2,1)S(1)}, f32[96,1024]{1,0:T(8,128)S(1)},...) custom-call(bf16[64,2048]{1,0:T(8,128)(2,1)S(1)} %get-tuple-element.41.s_ref, ...), custom_call_target="tpu_custom_call" | custom-call | flops 1000000000 | bytes 4000000 | tf_op jit(solution)/shard_map/own_rows/pallas_call | solution.py:245
  11.2 0.0 collective-permute-done.odd_ref
  11.2 0.0 collective-permute-done.1.even_ref
  11.2 0.6 %collective-permute-start.2 = (bf16[32,128]{1,0:T(8,128)(2,1)S(1)}, bf16[32,128]{1,0:T(8,128)(2,1)S(1)}, u32[]{:S(2)}, u32[]{:S(2)}) collective-permute-start(bf16[32,128]{1,0:T(8,128)(2,1)S(1)} %slice_add_fusion), channel_id=1, source_target_pairs={{0,1},{1,0},{2,3},{3,2},{4,5},{5,4},{6,7},{7,6},{8,9},{9,8},{10,11... | collective-permute-start | bytes 24584 | tf_op jit(solution)/shard_map/ppermute | solution.py:633
  11.8 1.0 %inner_rows.1 = (f32[512,128]{1,0:T(8,128)S(1)}, f32[512,128]{1,0:T(8,128)S(1)}, f32[96,1536]{1,0:T(8,128)S(1)}, f32[48,768]{1,0:T(8,128)S(1)}, f32[288,256]{1,0:T(8,128)S(1)}, /*index=5*/f32[144,128]{1,0:T(8,128)S(1)}) custom-call(bf16[48,1024]{1,0:T(8,128)(2,1)S(1)} %get-tuple-element.52.pst_ref.pst_own, ...), custom_call_target="tpu_custom_call" | custom-call | flops 1000000000 | bytes 4000000 | tf_op jit(solution)/shard_map/inner_rows/pallas_call | solution.py:330
  12.8 2.1 %collective-permute-done.2.corners_ref = bf16[32,128]{1,0:T(8,128)(2,1)S(1)} collective-permute-done((bf16[32,128]{1,0:T(8,128)(2,1)S(1)}, bf16[32,128]{1,0:T(8,128)(2,1)S(1)}, u32[]{:S(2)}, u32[]{:S(2)}) %collective-permute-start.2) | collective-permute-done | bytes 8224 | tf_op jit(solution)/shard_map/ppermute | solution.py:633
  14.9 1.1 %rest.1 = (bf16[512,128]{1,0:T(8,128)(2,1)S(1)}, bf16[512,128]{1,0:T(8,128)(2,1)S(1)}, bf16[256,128]{1,0:T(8,128)(2,1)S(1)}) custom-call(bf16[32,768]{1,0:T(8,128)(2,1)S(1)} %collective-permute-done.odd_ref, bf16[32,768]{1,0:T(8,128)(2,1)S(1)} %collective-permute-done.1.even_ref, bf16[32,128]{1,0:T(8,128)(2,1)S(1)} %collective-permute-done.2.corners_ref, ...), custom_call_target="tpu_custom_call" | custom-call | flops 1000000000 | bytes 4000000 | tf_op jit(solution)/shard_map/rest/pallas_call | solution.py:470
  16.0 11.5 %all_to_all.10.parts_ref = bf16[32,8,128]{2,1,0:T(8,128)(2,1)S(1)} all-to-all(bf16[32,8,128]{2,1,0:T(8,128)(2,1)S(1)} %bitcast.19), channel_id=1, replica_groups=mesh['wide'=16,'narrow'=2] {'wide','narrow'}, dimensions={0} | all-to-all | bytes 131072 | tf_op jit(solution)/shard_map/all_to_all | solution.py:662
  27.6 9.3 %all_to_all.11 = bf16[32,8,128]{2,1,0:T(8,128)(2,1)S(1)} all-to-all(bf16[32,8,128]{2,1,0:T(8,128)(2,1)S(1)} %add_up.1), channel_id=1, replica_groups=mesh['wide'=16,'narrow'=2] {'wide','narrow'}, dimensions={0} | all-to-all | bytes 131072 | tf_op jit(solution)/shard_map/all_to_all | solution.py:663
  36.9 1.0 %spread.1 = (bf16[512,128]{1,0:T(8,128)(2,1)}, bf16[512,128]{1,0:T(8,128)(2,1)}, f32[432,48]{1,0:T(8,128)}, f32[432,32]{1,0:T(8,128)}) custom-call(bf16[256,128]{1,0:T(8,128)(2,1)S(1)} %bitcast.18, bf16[512,128]{1,0:T(8,128)(2,1)S(1)} %get-tuple-element.68.out_ref, bf16[512,128]{1,0:T(8,128)(2,1)S(1)} %get-tuple-element.69.gf_ref), custom_call_target="tpu_custom_call" | custom-call | tf_op jit(solution)/shard_map/spread/pallas_call | solution.py:545
  (2 shorter events, 0.0 us)
Async XLA Ops:
  2.0 7.8 %collective-permute-start.3 = (bf16[32,128]{1,0:T(8,128)(2,1)S(1)}, bf16[32,128]{1,0:T(8,128)(2,1)S(1)}, u32[]{:S(2)}, u32[]{:S(2)}) collective-permute-start(bf16[32,128]{1,0:T(8,128)(2,1)S(1)} %get-tuple-element.42), channel_id=1, source_target_pairs={{0,1},{1,0},{2,3},{3,2},{4,5},{5,4},{6,7},{7,6},{8,9},{9,8},{10,11... | collective-permute-start | bytes 24584 | tf_op jit(solution)/shard_map/ppermute | solution.py:633
  5.0 6.1 %collective-permute-start = (bf16[32,768]{1,0:T(8,128)(2,1)S(1)}, bf16[32,768]{1,0:T(8,128)(2,1)S(1)}, u32[]{:S(2)}, u32[]{:S(2)}) collective-permute-start(bf16[32,768]{1,0:T(8,128)(2,1)S(1)} %get-tuple-element.39), channel_id=1, source_target_pairs={{2,4},{4,2},{6,8},{8,6},{10,12},{12,10},{14,16},{16,14},{18,20},{2... | collective-permute-start | bytes 147464 | tf_op jit(solution)/shard_map/ppermute | solution.py:646
  5.7 5.5 %collective-permute-start.1 = (bf16[32,768]{1,0:T(8,128)(2,1)S(1)}, bf16[32,768]{1,0:T(8,128)(2,1)S(1)}, u32[]{:S(2)}, u32[]{:S(2)}) collective-permute-start(bf16[32,768]{1,0:T(8,128)(2,1)S(1)} %get-tuple-element.40), channel_id=1, source_target_pairs={{0,2},{2,0},{4,6},{6,4},{8,10},{10,8},{12,14},{14,12},{16,18},{18,... | collective-permute-start | bytes 147464 | tf_op jit(solution)/shard_map/ppermute | solution.py:647
  11.2 3.7 %collective-permute-start.2 = (bf16[32,128]{1,0:T(8,128)(2,1)S(1)}, bf16[32,128]{1,0:T(8,128)(2,1)S(1)}, u32[]{:S(2)}, u32[]{:S(2)}) collective-permute-start(bf16[32,128]{1,0:T(8,128)(2,1)S(1)} %slice_add_fusion), channel_id=1, source_target_pairs={{0,1},{1,0},{2,3},{3,2},{4,5},{5,4},{6,7},{7,6},{8,9},{9,8},{10,11... | collective-permute-start | bytes 24584 | tf_op jit(solution)/shard_map/ppermute | solution.py:633

commit v15 on v14

--- a/solution.py
+++ b/solution.py
@@ -648,8 +648,8 @@
     columns = beside_blocks(strip, narrow)
     wo, wg, wc, wq = weight_matrices(coarse_weight, fine_weight)
     corners = odd[:, SLOTS * COLS :] + even[:, SLOTS * COLS :]
+    columns, _ = lax.optimization_barrier((columns, corners))
     stacks = own_rows(own, columns, wc, wg, sides)
-    stacks, _ = lax.optimization_barrier((stacks, corners))
     inner = inner_rows(stacks, wo, wq, narrow)
     corners = beside_blocks(corners, narrow)
     output, grad_features, grads = rest(

time: 38.2 us -> 37.5 us (0.982)
  waiting for transfers between devices: 2.1 us -> 0.79 us
  blocking collectives: 20.8 us -> 21.6 us
    ppermute x2, starting transfers between devices: 3.6 us -> 2.09 us  [beside_blocks(): return lax.ppermute(outer, 'narrow', [(0, 1), (1, 0)])]
    ppermute x1, starting transfers between devices: 2.94 us -> 4.39 us  [shards(): even = lax.ppermute(to_even, 'wide', swaps(0))]
    ppermute x2, waiting for transfers between devices: 2.09 us -> 0.78 us  [beside_blocks(): return lax.ppermute(outer, 'narrow', [(0, 1), (1, 0)])]
    all_to_all x1, blocking collectives: 11.5 us -> 12.3 us  [shards(): parts = lax.all_to_all(grads, both, 0, 0, tiled=True)]
  transfers between devices with their start and end apart: 4 -> 4, of which waited for: 1 -> 2; matrix products, arithmetic and copies ran while one was open for 0% -> 0% of each run, Pallas kernels for 9% -> 9%
where the time goes in v15:
time: 37.5 us; the launch traced here: 37.2 us
  blocking collectives  21.6 us (58%)
  starting transfers between devices  7.15 us (19%)
  Pallas kernels  7.04 us (19%)
  waiting for transfers between devices  0.79 us (2%)
  between operations  0.7 us (2%)
    all_to_all x1, blocking collectives, shards(): parts = lax.all_to_all(grads, both, 0, 0, tiled=True)  12.3 us
    all_to_all x1, blocking collectives, shards(): total = lax.all_to_all(add_up(parts), both, 0, 0, tiled=True)  9.3 us
    ppermute x1, starting transfers between devices, shards(): even = lax.ppermute(to_even, 'wide', swaps(0))  4.39 us
    ppermute x2, starting transfers between devices, beside_blocks(): return lax.ppermute(outer, 'narrow', [(0, 1), (1, 0)])  2.09 us
    pallas_call x1, Pallas kernels, pack(): pl.pallas_call(functools.partial(pack_kernel, sides), in_specs=[pl.BlockS...  1.4 us
    pallas_call x1, Pallas kernels, own_rows(): pl.pallas_call(functools.partial(own_kernel, sides), out_shape=(shaped(48...  1.3 us
    pallas_call x1, Pallas kernels, weight_matrices(): pl.pallas_call(matrices_kernel, in_specs=[pl.BlockSpec(memory_space=pltpu...  1.2 us
    pallas_call x1, Pallas kernels, rest(): pl.pallas_call(functools.partial(rest_kernel, counts, sides), out_shape=(...  1.11 us
  transfers between devices with their start and end apart: 4, of which 2 were waited for; matrix products, arithmetic and copies ran while one was open for 0% of the time, Pallas kernels for 9%

profile of v15, /device:TPU:0, one launch (start us, length us, event | category | flops | bytes accessed | tf_op | source)
XLA Modules:
  0.0 37.2 jit_solution(8642170201712609281)
XLA Ops:
  0.6 1.4 %pack.1 = (bf16[64,2048]{1,0:T(8,128)(2,1)S(1)}, bf16[32,128]{1,0:T(8,128)(2,1)S(1)}, bf16[32,768]{1,0:T(8,128)(2,1)S(1)}, bf16[32,768]{1,0:T(8,128)(2,1)S(1)}) custom-call(bf16[512,128]{1,0:T(8,128)(2,1)} %bitcast.20, bf16[512,128]{1,0:T(8,128)(2,1)} %bitcast.21), custom_call_target="tpu_custom_call" | custom-call | flops 1000000 | bytes 1000000 | tf_op jit(solution)/shard_map/pack/pallas_call | solution.py:128
  2.0 0.7 %collective-permute-start = (bf16[32,768]{1,0:T(8,128)(2,1)S(1)}, bf16[32,768]{1,0:T(8,128)(2,1)S(1)}, u32[]{:S(2)}, u32[]{:S(2)}) collective-permute-start(bf16[32,768]{1,0:T(8,128)(2,1)S(1)} %get-tuple-element.33), channel_id=1, source_target_pairs={{2,4},{4,2},{6,8},{8,6},{10,12},{12,10},{14,16},{16,14},{18,20},{2... | collective-permute-start | bytes 147464 | tf_op jit(solution)/shard_map/ppermute | solution.py:646
  2.7 4.4 %collective-permute-start.1 = (bf16[32,768]{1,0:T(8,128)(2,1)S(1)}, bf16[32,768]{1,0:T(8,128)(2,1)S(1)}, u32[]{:S(2)}, u32[]{:S(2)}) collective-permute-start(bf16[32,768]{1,0:T(8,128)(2,1)S(1)} %get-tuple-element.34), channel_id=1, source_target_pairs={{0,2},{2,0},{4,6},{6,4},{8,10},{10,8},{12,14},{14,12},{16,18},{18,... | collective-permute-start | bytes 147464 | tf_op jit(solution)/shard_map/ppermute | solution.py:647
  7.1 1.5 %collective-permute-start.3 = (bf16[32,128]{1,0:T(8,128)(2,1)S(1)}, bf16[32,128]{1,0:T(8,128)(2,1)S(1)}, u32[]{:S(2)}, u32[]{:S(2)}) collective-permute-start(bf16[32,128]{1,0:T(8,128)(2,1)S(1)} %get-tuple-element.36), channel_id=1, source_target_pairs={{0,1},{1,0},{2,3},{3,2},{4,5},{5,4},{6,7},{7,6},{8,9},{9,8},{10,11... | collective-permute-start | bytes 24584 | tf_op jit(solution)/shard_map/ppermute | solution.py:633
  8.6 1.2 %matrices.1 = (bf16[96,192]{1,0:T(8,128)(2,1)S(1)}, bf16[192,96]{1,0:T(8,128)(2,1)S(1)}, bf16[96,48]{1,0:T(8,128)(2,1)S(1)}, bf16[48,96]{1,0:T(8,128)(2,1)S(1)}) custom-call(bf16[432,48]{1,0:T(8,128)(2,1)} %bitcast.22, bf16[432,32]{1,0:T(8,128)(2,1)} %bitcast.23), custom_call_target="tpu_custom_call" | custom-call | flops 1000000 | bytes 1000000 | tf_op jit(solution)/shard_map/matrices/pallas_call | solution.py:613
  9.8 0.0 collective-permute-done.odd_ref
  9.8 0.0 collective-permute-done.1.even_ref
  9.8 0.6 %collective-permute-start.2 = (bf16[32,128]{1,0:T(8,128)(2,1)S(1)}, bf16[32,128]{1,0:T(8,128)(2,1)S(1)}, u32[]{:S(2)}, u32[]{:S(2)}) collective-permute-start(bf16[32,128]{1,0:T(8,128)(2,1)S(1)} %slice_add_fusion), channel_id=1, source_target_pairs={{0,1},{1,0},{2,3},{3,2},{4,5},{5,4},{6,7},{7,6},{8,9},{9,8},{10,11... | collective-permute-start | bytes 24584 | tf_op jit(solution)/shard_map/ppermute | solution.py:633
  10.4 0.3 collective-permute-done.3.columns_ref
  10.8 1.3 %own_rows.1 = (bf16[48,1024]{1,0:T(8,128)(2,1)S(1)}, bf16[96,2048]{1,0:T(8,128)(2,1)S(1)}, bf16[96,2048]{1,0:T(8,128)(2,1)S(1)}, f32[96,1024]{1,0:T(8,128)S(1)},...) custom-call(bf16[64,2048]{1,0:T(8,128)(2,1)S(1)} %get-tuple-element.35.s_ref, ...), custom_call_target="tpu_custom_call" | custom-call | flops 1000000000 | bytes 4000000 | tf_op jit(solution)/shard_map/own_rows/pallas_call | solution.py:245
  12.1 1.0 %inner_rows.1 = (f32[512,128]{1,0:T(8,128)S(1)}, f32[512,128]{1,0:T(8,128)S(1)}, f32[96,1536]{1,0:T(8,128)S(1)}, f32[48,768]{1,0:T(8,128)S(1)}, f32[288,256]{1,0:T(8,128)S(1)}, /*index=5*/f32[144,128]{1,0:T(8,128)S(1)}) custom-call(bf16[48,1024]{1,0:T(8,128)(2,1)S(1)} %get-tuple-element.40.pst_ref.pst_own, ...), custom_call_target="tpu_custom_call" | custom-call | flops 1000000000 | bytes 4000000 | tf_op jit(solution)/shard_map/inner_rows/pallas_call | solution.py:330
  13.1 0.5 %collective-permute-done.2.corners_ref = bf16[32,128]{1,0:T(8,128)(2,1)S(1)} collective-permute-done((bf16[32,128]{1,0:T(8,128)(2,1)S(1)}, bf16[32,128]{1,0:T(8,128)(2,1)S(1)}, u32[]{:S(2)}, u32[]{:S(2)}) %collective-permute-start.2) | collective-permute-done | bytes 8224 | tf_op jit(solution)/shard_map/ppermute | solution.py:633
  13.6 1.1 %rest.1 = (bf16[512,128]{1,0:T(8,128)(2,1)S(1)}, bf16[512,128]{1,0:T(8,128)(2,1)S(1)}, bf16[256,128]{1,0:T(8,128)(2,1)S(1)}) custom-call(bf16[32,768]{1,0:T(8,128)(2,1)S(1)} %collective-permute-done.odd_ref, bf16[32,768]{1,0:T(8,128)(2,1)S(1)} %collective-permute-done.1.even_ref, bf16[32,128]{1,0:T(8,128)(2,1)S(1)} %collective-permute-done.2.corners_ref, ...), custom_call_target="tpu_custom_call" | custom-call | flops 1000000000 | bytes 4000000 | tf_op jit(solution)/shard_map/rest/pallas_call | solution.py:470
  14.7 12.3 %all_to_all.10.parts_ref = bf16[32,8,128]{2,1,0:T(8,128)(2,1)S(1)} all-to-all(bf16[32,8,128]{2,1,0:T(8,128)(2,1)S(1)} %bitcast.19), channel_id=1, replica_groups=mesh['wide'=16,'narrow'=2] {'wide','narrow'}, dimensions={0} | all-to-all | bytes 131072 | tf_op jit(solution)/shard_map/all_to_all | solution.py:662
  27.0 9.3 %all_to_all.11 = bf16[32,8,128]{2,1,0:T(8,128)(2,1)S(1)} all-to-all(bf16[32,8,128]{2,1,0:T(8,128)(2,1)S(1)} %add_up.1), channel_id=1, replica_groups=mesh['wide'=16,'narrow'=2] {'wide','narrow'}, dimensions={0} | all-to-all | bytes 131072 | tf_op jit(solution)/shard_map/all_to_all | solution.py:663
  36.3 1.0 %spread.1 = (bf16[512,128]{1,0:T(8,128)(2,1)}, bf16[512,128]{1,0:T(8,128)(2,1)}, f32[432,48]{1,0:T(8,128)}, f32[432,32]{1,0:T(8,128)}) custom-call(bf16[256,128]{1,0:T(8,128)(2,1)S(1)} %bitcast.18, bf16[512,128]{1,0:T(8,128)(2,1)S(1)} %get-tuple-element.56.out_ref, bf16[512,128]{1,0:T(8,128)(2,1)S(1)} %get-tuple-element.57.gf_ref), custom_call_target="tpu_custom_call" | custom-call | tf_op jit(solution)/shard_map/spread/pallas_call | solution.py:545
  (2 shorter events, 0.0 us)
Async XLA Ops:
  2.0 7.8 %collective-permute-start = (bf16[32,768]{1,0:T(8,128)(2,1)S(1)}, bf16[32,768]{1,0:T(8,128)(2,1)S(1)}, u32[]{:S(2)}, u32[]{:S(2)}) collective-permute-start(bf16[32,768]{1,0:T(8,128)(2,1)S(1)} %get-tuple-element.33), channel_id=1, source_target_pairs={{2,4},{4,2},{6,8},{8,6},{10,12},{12,10},{14,16},{16,14},{18,20},{2... | collective-permute-start | bytes 147464 | tf_op jit(solution)/shard_map/ppermute | solution.py:646
  2.7 7.1 %collective-permute-start.1 = (bf16[32,768]{1,0:T(8,128)(2,1)S(1)}, bf16[32,768]{1,0:T(8,128)(2,1)S(1)}, u32[]{:S(2)}, u32[]{:S(2)}) collective-permute-start(bf16[32,768]{1,0:T(8,128)(2,1)S(1)} %get-tuple-element.34), channel_id=1, source_target_pairs={{0,2},{2,0},{4,6},{6,4},{8,10},{10,8},{12,14},{14,12},{16,18},{18,... | collective-permute-start | bytes 147464 | tf_op jit(solution)/shard_map/ppermute | solution.py:647
  7.1 3.7 %collective-permute-start.3 = (bf16[32,128]{1,0:T(8,128)(2,1)S(1)}, bf16[32,128]{1,0:T(8,128)(2,1)S(1)}, u32[]{:S(2)}, u32[]{:S(2)}) collective-permute-start(bf16[32,128]{1,0:T(8,128)(2,1)S(1)} %get-tuple-element.36), channel_id=1, source_target_pairs={{0,1},{1,0},{2,3},{3,2},{4,5},{5,4},{6,7},{7,6},{8,9},{9,8},{10,11... | collective-permute-start | bytes 24584 | tf_op jit(solution)/shard_map/ppermute | solution.py:633
  9.8 3.7 %collective-permute-start.2 = (bf16[32,128]{1,0:T(8,128)(2,1)S(1)}, bf16[32,128]{1,0:T(8,128)(2,1)S(1)}, u32[]{:S(2)}, u32[]{:S(2)}) collective-permute-start(bf16[32,128]{1,0:T(8,128)(2,1)S(1)} %slice_add_fusion), channel_id=1, source_target_pairs={{0,1},{1,0},{2,3},{3,2},{4,5},{5,4},{6,7},{7,6},{8,9},{9,8},{10,11... | collective-permute-start | bytes 24584 | tf_op jit(solution)/shard_map/ppermute | solution.py:633

commit v16 on v15

--- a/solution.py
+++ b/solution.py
@@ -493,19 +493,17 @@
     )(*messages, *own, *inner, *matrices)
 
 
-def add_kernel(parts_ref, copies_ref):
+def add_kernel(parts_ref, total_ref):
     total = parts_ref[0].astype(F32)
     for i in range(1, parts_ref.shape[0]):
         total = total + parts_ref[i].astype(F32)
-    total = total.astype(BF)
-    for i in range(parts_ref.shape[0]):
-        copies_ref[i] = total
+    total_ref[...] = total.astype(BF)
 
 
 def add_up(parts):
     return pl.pallas_call(
         add_kernel,
-        out_shape=jax.ShapeDtypeStruct(parts.shape, BF),
+        out_shape=jax.ShapeDtypeStruct(parts.shape[1:], BF),
         compiler_params=pltpu.CompilerParams(vmem_limit_bytes=VMEM_LIMIT),
         name="add_up",
     )(parts)
@@ -660,7 +658,7 @@
     grads = jnp.pad(grads, ((0, share * devices - 256), (0, 0))).reshape(devices, share, COLS)
     both = ("wide", "narrow")
     parts = lax.all_to_all(grads, both, 0, 0, tiled=True)
-    total = lax.all_to_all(add_up(parts), both, 0, 0, tiled=True)
+    total = lax.all_gather(add_up(parts), both, axis=0, tiled=True)
     total = total.reshape(share * devices, COLS)[:256]
     all_cells = features.shape[1] * features.shape[2] * features.shape[3] * devices
     output, grad_features, grad_fine, grad_coarse = spread(

time: 37.5 us -> 92.3 us (2.46)
  blocking collectives: 21.6 us -> 76.3 us
    all_gather x0 -> x1, blocking collectives: none -> 64.1 us  [shards(): total = lax.all_gather(add_up(parts), both, axis=0, tiled=True)]
    all_to_all x1 -> x0, blocking collectives: 9.3 us -> none  [shards(): total = lax.all_to_all(add_up(parts), both, 0, 0, tiled=True)]
  transfers between devices with their start and end apart: 4 -> 4, of which waited for: 2 -> 2; matrix products, arithmetic and copies ran while one was open for 0% -> 0% of each run, Pallas kernels for 9% -> 4%
where the time goes in v16:
time: 92.3 us; the launch traced here: 92 us
  blocking collectives  76.3 us (83%)
  starting transfers between devices  7.15 us (8%)
  Pallas kernels  7.04 us (8%)
    all_gather x1, blocking collectives, shards(): total = lax.all_gather(add_up(parts), both, axis=0, tiled=True)  64.1 us
    all_to_all x1, blocking collectives, shards(): parts = lax.all_to_all(grads, both, 0, 0, tiled=True)  12.3 us
    ppermute x1, starting transfers between devices, shards(): even = lax.ppermute(to_even, 'wide', swaps(0))  4.39 us
    ppermute x2, starting transfers between devices, beside_blocks(): return lax.ppermute(outer, 'narrow', [(0, 1), (1, 0)])  2.09 us
  transfers between devices with their start and end apart: 4, of which 2 were waited for; matrix products, arithmetic and copies ran while one was open for 0% of the time, Pallas kernels for 4%

profile of v16, /device:TPU:0, one launch (start us, length us, event | category | flops | bytes accessed | tf_op | source)
XLA Modules:
  0.0 92.0 jit_solution(9338765763196283595)
XLA Ops:
  0.6 1.4 %pack.1 = (bf16[64,2048]{1,0:T(8,128)(2,1)S(1)}, bf16[32,128]{1,0:T(8,128)(2,1)S(1)}, bf16[32,768]{1,0:T(8,128)(2,1)S(1)}, bf16[32,768]{1,0:T(8,128)(2,1)S(1)}) custom-call(bf16[512,128]{1,0:T(8,128)(2,1)} %bitcast.18, bf16[512,128]{1,0:T(8,128)(2,1)} %bitcast.19), custom_call_target="tpu_custom_call" | custom-call | flops 1000000 | bytes 1000000 | tf_op jit(solution)/shard_map/pack/pallas_call | solution.py:128
  2.0 0.7 collective-permute-start
  2.7 4.4 %collective-permute-start.1 = (bf16[32,768]{1,0:T(8,128)(2,1)S(1)}, bf16[32,768]{1,0:T(8,128)(2,1)S(1)}, u32[]{:S(2)}, u32[]{:S(2)}) collective-permute-start(bf16[32,768]{1,0:T(8,128)(2,1)S(1)} %get-tuple-element.34), channel_id=1, source_target_pairs={{0,2},{2,0},{4,6},{6,4},{8,10},{10,8},{12,14},{14,12},{16,18},{18,... | collective-permute-start | bytes 147464 | tf_op jit(solution)/shard_map/ppermute | solution.py:645
  7.1 1.5 %collective-permute-start.3 = (bf16[32,128]{1,0:T(8,128)(2,1)S(1)}, bf16[32,128]{1,0:T(8,128)(2,1)S(1)}, u32[]{:S(2)}, u32[]{:S(2)}) collective-permute-start(bf16[32,128]{1,0:T(8,128)(2,1)S(1)} %get-tuple-element.36), channel_id=1, source_target_pairs={{0,1},{1,0},{2,3},{3,2},{4,5},{5,4},{6,7},{7,6},{8,9},{9,8},{10,11... | collective-permute-start | bytes 24584 | tf_op jit(solution)/shard_map/ppermute | solution.py:631
  8.6 1.2 %matrices.1 = (bf16[96,192]{1,0:T(8,128)(2,1)S(1)}, bf16[192,96]{1,0:T(8,128)(2,1)S(1)}, bf16[96,48]{1,0:T(8,128)(2,1)S(1)}, bf16[48,96]{1,0:T(8,128)(2,1)S(1)}) custom-call(bf16[432,48]{1,0:T(8,128)(2,1)} %bitcast.20, bf16[432,32]{1,0:T(8,128)(2,1)} %bitcast.21), custom_call_target="tpu_custom_call" | custom-call | flops 1000000 | bytes 1000000 | tf_op jit(solution)/shard_map/matrices/pallas_call | solution.py:611
  9.8 0.0 collective-permute-done.odd_ref
  9.8 0.0 collective-permute-done.1.even_ref
  9.8 0.6 collective-permute-start.2
  10.4 0.3 collective-permute-done.3.columns_ref
  10.8 1.3 %own_rows.1 = (bf16[48,1024]{1,0:T(8,128)(2,1)S(1)}, bf16[96,2048]{1,0:T(8,128)(2,1)S(1)}, bf16[96,2048]{1,0:T(8,128)(2,1)S(1)}, f32[96,1024]{1,0:T(8,128)S(1)},...) custom-call(bf16[64,2048]{1,0:T(8,128)(2,1)S(1)} %get-tuple-element.35.s_ref, ...), custom_call_target="tpu_custom_call" | custom-call | flops 1000000000 | bytes 4000000 | tf_op jit(solution)/shard_map/own_rows/pallas_call | solution.py:245
  12.1 1.0 %inner_rows.1 = (f32[512,128]{1,0:T(8,128)S(1)}, f32[512,128]{1,0:T(8,128)S(1)}, f32[96,1536]{1,0:T(8,128)S(1)}, f32[48,768]{1,0:T(8,128)S(1)}, f32[288,256]{1,0:T(8,128)S(1)}, /*index=5*/f32[144,128]{1,0:T(8,128)S(1)}) custom-call(bf16[48,1024]{1,0:T(8,128)(2,1)S(1)} %get-tuple-element.40.pst_ref.pst_own, ...), custom_call_target="tpu_custom_call" | custom-call | flops 1000000000 | bytes 4000000 | tf_op jit(solution)/shard_map/inner_rows/pallas_call | solution.py:330
  13.1 0.5 collective-permute-done.2.corners_ref
  13.6 1.1 %rest.1 = (bf16[512,128]{1,0:T(8,128)(2,1)S(1)}, bf16[512,128]{1,0:T(8,128)(2,1)S(1)}, bf16[256,128]{1,0:T(8,128)(2,1)S(1)}) custom-call(bf16[32,768]{1,0:T(8,128)(2,1)S(1)} %collective-permute-done.odd_ref, bf16[32,768]{1,0:T(8,128)(2,1)S(1)} %collective-permute-done.1.even_ref, bf16[32,128]{1,0:T(8,128)(2,1)S(1)} %collective-permute-done.2.corners_ref, ...), custom_call_target="tpu_custom_call" | custom-call | flops 1000000000 | bytes 4000000 | tf_op jit(solution)/shard_map/rest/pallas_call | solution.py:470
  14.7 12.3 %all_to_all.5.parts_ref = bf16[32,8,128]{2,1,0:T(8,128)(2,1)S(1)} all-to-all(bf16[32,8,128]{2,1,0:T(8,128)(2,1)S(1)} %bitcast.17), channel_id=1, replica_groups=mesh['wide'=16,'narrow'=2] {'wide','narrow'}, dimensions={0} | all-to-all | bytes 131072 | tf_op jit(solution)/shard_map/all_to_all | solution.py:660
  27.0 64.1 %all_gather.3.sum_ref = bf16[256,128]{1,0:T(8,128)(2,1)S(1)} all-gather(bf16[8,128]{1,0:T(8,128)(2,1)S(1)} %add_up.1), channel_id=1, replica_groups=mesh['wide'=16,'narrow'=2] {'wide','narrow'}, dimensions={0}, use_global_device_ids=true | all-gather | bytes 67584 | tf_op jit(solution)/shard_map/all_gather | solution.py:661
  91.1 1.0 %spread.1 = (bf16[512,128]{1,0:T(8,128)(2,1)}, bf16[512,128]{1,0:T(8,128)(2,1)}, f32[432,48]{1,0:T(8,128)}, f32[432,32]{1,0:T(8,128)}) custom-call(bf16[256,128]{1,0:T(8,128)(2,1)S(1)} %all_gather.3.sum_ref, bf16[512,128]{1,0:T(8,128)(2,1)S(1)} %get-tuple-element.56.out_ref, bf16[512,128]{1,0:T(8,128)(2,1)S(1)} %get-tuple-element.57.gf_ref), custom_call_target="tpu_custom_call" | custom-call | tf_op jit(solution)/shard_map/spread/pallas_call | solution.py:543
  (2 shorter events, 0.0 us)
Async XLA Ops:
  2.0 7.8 %collective-permute-start = (bf16[32,768]{1,0:T(8,128)(2,1)S(1)}, bf16[32,768]{1,0:T(8,128)(2,1)S(1)}, u32[]{:S(2)}, u32[]{:S(2)}) collective-permute-start(bf16[32,768]{1,0:T(8,128)(2,1)S(1)} %get-tuple-element.33), channel_id=1, source_target_pairs={{2,4},{4,2},{6,8},{8,6},{10,12},{12,10},{14,16},{16,14},{18,20},{2... | collective-permute-start | bytes 147464 | tf_op jit(solution)/shard_map/ppermute | solution.py:644
  2.7 7.1 %collective-permute-start.1 = (bf16[32,768]{1,0:T(8,128)(2,1)S(1)}, bf16[32,768]{1,0:T(8,128)(2,1)S(1)}, u32[]{:S(2)}, u32[]{:S(2)}) collective-permute-start(bf16[32,768]{1,0:T(8,128)(2,1)S(1)} %get-tuple-element.34), channel_id=1, source_target_pairs={{0,2},{2,0},{4,6},{6,4},{8,10},{10,8},{12,14},{14,12},{16,18},{18,... | collective-permute-start | bytes 147464 | tf_op jit(solution)/shard_map/ppermute | solution.py:645
  7.1 3.7 %collective-permute-start.3 = (bf16[32,128]{1,0:T(8,128)(2,1)S(1)}, bf16[32,128]{1,0:T(8,128)(2,1)S(1)}, u32[]{:S(2)}, u32[]{:S(2)}) collective-permute-start(bf16[32,128]{1,0:T(8,128)(2,1)S(1)} %get-tuple-element.36), channel_id=1, source_target_pairs={{0,1},{1,0},{2,3},{3,2},{4,5},{5,4},{6,7},{7,6},{8,9},{9,8},{10,11... | collective-permute-start | bytes 24584 | tf_op jit(solution)/shard_map/ppermute | solution.py:631
  9.8 3.7 %collective-permute-start.2 = (bf16[32,128]{1,0:T(8,128)(2,1)S(1)}, bf16[32,128]{1,0:T(8,128)(2,1)S(1)}, u32[]{:S(2)}, u32[]{:S(2)}) collective-permute-start(bf16[32,128]{1,0:T(8,128)(2,1)S(1)} %slice_add_fusion), channel_id=1, source_target_pairs={{0,1},{1,0},{2,3},{3,2},{4,5},{5,4},{6,7},{7,6},{8,9},{9,8},{10,11... | collective-permute-start | bytes 24584 | tf_op jit(solution)/shard_map/ppermute | solution.py:631

commit v17 on v15

--- a/solution.py
+++ b/solution.py
@@ -109,13 +109,10 @@
             first, second = (s_ref[0:32, row(2 * pair + j)].astype(F32) for j in range(2))
             base_ref[to, i * 16 : i * 16 + 16, row(1)] = pooled(first, second)
         base_ref[to, :, row(2, 3)] = s_ref[32:64, row(cot, 3)]
-        for side in range(sides):
-            for z in range(2):
-                kept = lane % 64 >= 48 if to == 0 else lane % 64 < 16
-                value = jnp.where(kept, strips[z][side], 0.0).astype(BF)
-                base_ref[to, z * 16 : z * 16 + 16, row(SLOTS + side)] = value
-    even_ref[...] = base_ref[odd]
-    odd_ref[...] = base_ref[1 - odd]
+    even_ref[:, row(0, SLOTS)] = base_ref[odd]
+    odd_ref[:, row(0, SLOTS)] = base_ref[1 - odd]
+    even_ref[:, row(SLOTS, sides)] = jnp.zeros((32, sides * COLS), BF)
+    odd_ref[:, row(SLOTS, sides)] = jnp.zeros((32, sides * COLS), BF)
 
 
 def kept_in_hbm(array):
@@ -138,7 +135,7 @@
             pltpu.VMEM((CELLS, COLS), BF),
             pltpu.VMEM((CELLS, COLS), BF),
             pltpu.VMEM((CELLS, COLS), F32),
-            pltpu.VMEM((2, 32, (SLOTS + sides) * COLS), BF),
+            pltpu.VMEM((2, 32, SLOTS * COLS), BF),
             pltpu.SemaphoreType.DMA((2, 4)),
         ],
         compiler_params=params(),
@@ -347,7 +344,7 @@
 
 def rest_kernel(
     counts, sides,
-    odd_ref, even_ref, corners_ref,
+    even_ref, odd_ref,
     pst_own, jf_own, gst_own, pre_own, prb_own, rg_own, rgb_own,
     out_inner, gf_inner, ro_inner, rq_inner, rf_inner, rc_inner,
     wo_ref, wg_ref, wc_ref, wq_ref,
@@ -361,22 +358,24 @@
     has_above, has_below = flag(w > 0), flag(w < counts[0] - 1)
 
     odd = w % 2
-    halo_ref[1 - odd] = even_ref[:, row(0, SLOTS)]
-    halo_ref[odd] = odd_ref[:, row(0, SLOTS)]
-    columns = [corners_ref[:, row(side)].astype(F32) for side in range(sides)]
+    halo_ref[1 - odd] = even_ref[...]
+    halo_ref[odd] = odd_ref[...]
+    columns = [
+        [halo_ref[i, :, row(SLOTS + side)].astype(F32) for side in range(sides)] for i in range(2)
+    ]
 
     for i in range(2):
         lane = HALO * (ROWS - HALO) if i == 0 else 0
         for j in range(3):
             main = halo_ref[i, :, row(2 + j)].astype(F32)
-            side = beside(columns, 64 + lane + HALO * (j + 1 - i))
+            side = beside(columns[i], 64 + lane + HALO * (j + 1 - i))
             put_cotangent(main, side, gst_ref, gsb_ref, 9 * i + j, 3 * i + j)
         gst_ref[:, row(3 + 3 * i, 3)] = gst_own[:, row(13 * i, 3)]
         rg_ref[:, row(3 * i, 3)] = dot(wg_ref[...], gst_ref[:, row(9 * i, 3)])
     rgb_ref[...] = dot(wg_ref[96:192, :], gsb_ref[...])
     for i in range(2):
         lane = HALO * (ROWS - HALO) if i == 0 else 0
-        sides_f = [beside(columns, lane + HALO * r) for r in range(HALO)]
+        sides_f = [beside(columns[i], lane + HALO * r) for r in range(HALO)]
         near = HALO - 1 if i == 0 else 0
         for j in range(2):
             main = halo_ref[i, j * 16 : j * 16 + 16, row(1)]
@@ -475,7 +474,7 @@
             jax.ShapeDtypeStruct((256, COLS), BF),
         ),
         scratch_shapes=[
-            pltpu.VMEM((2, 32, SLOTS * COLS), BF),
+            pltpu.VMEM((2, 32, (SLOTS + sides) * COLS), BF),
             scratch(192, 6, BF),
             scratch(96, 12, BF), scratch(96, 6, BF),
             scratch(48, 8, BF), scratch(48, 4, BF),
@@ -643,17 +642,15 @@
     swaps = lambda start: [
         pair for i in range(start, wide - 1, 2) for pair in ((i, i + 1), (i + 1, i))
     ]
-    odd = lax.ppermute(to_odd, "wide", swaps(1))
-    even = lax.ppermute(to_even, "wide", swaps(0))
     columns = beside_blocks(strip, narrow)
     wo, wg, wc, wq = weight_matrices(coarse_weight, fine_weight)
-    corners = odd[:, SLOTS * COLS :] + even[:, SLOTS * COLS :]
-    columns, _ = lax.optimization_barrier((columns, corners))
+    with_columns = lambda message: lax.dynamic_update_slice(message, columns, (0, SLOTS * COLS))
+    odd = lax.ppermute(with_columns(to_odd), "wide", swaps(1))
+    even = lax.ppermute(with_columns(to_even), "wide", swaps(0))
     stacks = own_rows(own, columns, wc, wg, sides)
     inner = inner_rows(stacks, wo, wq, narrow)
-    corners = beside_blocks(corners, narrow)
     output, grad_features, grads = rest(
-        (odd, even, corners), stacks, inner, (wo, wg, wc, wq), (wide, narrow), sides
+        (even, odd), stacks, inner, (wo, wg, wc, wq), (wide, narrow), sides
     )
     devices = wide * narrow
     share = -(-256 // devices)

time: 37.5 us -> 37.6 us (level)
  blocking collectives: 21.6 us -> 22 us
    ppermute x2, starting transfers between devices: 5.06 us -> 4.13 us  [the longest x1 3.47 us: shards(): even = lax.ppermute(with_columns(to_even), 'wide', swaps(0))]
    ppermute x2 -> x1, starting transfers between devices: 2.09 us -> 3 us  [beside_blocks(): return lax.ppermute(outer, 'narrow', [(0, 1), (1, 0)])]
    all_to_all x1, blocking collectives: 12.3 us -> 12.7 us  [shards(): parts = lax.all_to_all(grads, both, 0, 0, tiled=True)]
    ppermute x2 -> x1, waiting for transfers between devices: 0.78 us -> 0.42 us  [beside_blocks(): return lax.ppermute(outer, 'narrow', [(0, 1), (1, 0)])]
  transfers between devices with their start and end apart: 4 -> 3, of which waited for: 2 -> 1; matrix products, arithmetic and copies ran while one was open for 0% -> 0% of each run, Pallas kernels for 9% -> 9%
where the time goes in v17:
time: 37.6 us; the launch traced here: 37.3 us
  blocking collectives  22 us (59%)
  starting transfers between devices  7.13 us (19%)
  Pallas kernels  7.08 us (19%)
  between operations  0.69 us (2%)
  waiting for transfers between devices  0.42 us (1%)
    all_to_all x1, blocking collectives, shards(): parts = lax.all_to_all(grads, both, 0, 0, tiled=True)  12.7 us
    all_to_all x1, blocking collectives, shards(): total = lax.all_to_all(add_up(parts), both, 0, 0, tiled=True)  9.3 us
    ppermute x1, starting transfers between devices, shards(): even = lax.ppermute(with_columns(to_even), 'wide', swaps(0))  3.47 us
    ppermute x1, starting transfers between devices, beside_blocks(): return lax.ppermute(outer, 'narrow', [(0, 1), (1, 0)])  3 us
    pallas_call x1, Pallas kernels, pack(): pl.pallas_call(functools.partial(pack_kernel, sides), in_specs=[pl.BlockS...  1.39 us
    pallas_call x1, Pallas kernels, own_rows(): pl.pallas_call(functools.partial(own_kernel, sides), out_shape=(shaped(48...  1.3 us
    pallas_call x1, Pallas kernels, weight_matrices(): pl.pallas_call(matrices_kernel, in_specs=[pl.BlockSpec(memory_space=pltpu...  1.2 us
    pallas_call x1, Pallas kernels, rest(): pl.pallas_call(functools.partial(rest_kernel, counts, sides), out_shape=(...  1.15 us
  transfers between devices with their start and end apart: 3, of which 1 were waited for; matrix products, arithmetic and copies ran while one was open for 0% of the time, Pallas kernels for 9%

profile of v17, /device:TPU:0, one launch (start us, length us, event | category | flops | bytes accessed | tf_op | source)
XLA Modules:
  0.0 37.3 jit_solution(13622154819695263323)
XLA Ops:
  0.6 1.4 %pack.1 = (bf16[64,2048]{1,0:T(8,128)(2,1)S(1)}, bf16[32,128]{1,0:T(8,128)(2,1)S(1)}, bf16[32,768]{1,0:T(8,128)(2,1)S(1)}, bf16[32,768]{1,0:T(8,128)(2,1)S(1)}) custom-call(bf16[512,128]{1,0:T(8,128)(2,1)} %bitcast.20, bf16[512,128]{1,0:T(8,128)(2,1)} %bitcast.21), custom_call_target="tpu_custom_call" | custom-call | flops 1000000 | bytes 1000000 | tf_op jit(solution)/shard_map/pack/pallas_call | solution.py:125
  2.0 3.0 %collective-permute-start = (bf16[32,128]{1,0:T(8,128)(2,1)S(1)}, bf16[32,128]{1,0:T(8,128)(2,1)S(1)}, u32[]{:S(2)}, u32[]{:S(2)}) collective-permute-start(bf16[32,128]{1,0:T(8,128)(2,1)S(1)} %get-tuple-element.33), channel_id=1, source_target_pairs={{0,1},{1,0},{2,3},{3,2},{4,5},{5,4},{6,7},{7,6},{8,9},{9,8},{10,11... | collective-permute-start | bytes 24584 | tf_op jit(solution)/shard_map/ppermute | solution.py:632
  5.0 1.2 %matrices.1 = (bf16[96,192]{1,0:T(8,128)(2,1)S(1)}, bf16[192,96]{1,0:T(8,128)(2,1)S(1)}, bf16[96,48]{1,0:T(8,128)(2,1)S(1)}, bf16[48,96]{1,0:T(8,128)(2,1)S(1)}) custom-call(bf16[432,48]{1,0:T(8,128)(2,1)} %bitcast.22, bf16[432,32]{1,0:T(8,128)(2,1)} %bitcast.23), custom_call_target="tpu_custom_call" | custom-call | flops 1000000 | bytes 1000000 | tf_op jit(solution)/shard_map/matrices/pallas_call | solution.py:612
  6.2 0.4 %collective-permute-done.columns_ref = bf16[32,128]{1,0:T(8,128)(2,1)S(1)} collective-permute-done((bf16[32,128]{1,0:T(8,128)(2,1)S(1)}, bf16[32,128]{1,0:T(8,128)(2,1)S(1)}, u32[]{:S(2)}, u32[]{:S(2)}) %collective-permute-start) | collective-permute-done | bytes 8224 | tf_op jit(solution)/shard_map/ppermute | solution.py:632
  6.7 0.7 %collective-permute-start.2 = (bf16[32,768]{1,0:T(8,128)(2,1)S(1)}, bf16[32,768]{1,0:T(8,128)(2,1)S(1)}, u32[]{:S(2)}, u32[]{:S(2)}) collective-permute-start(bf16[32,768]{1,0:T(8,128)(2,1)S(1)} %get-tuple-element.60), channel_id=1, source_target_pairs={{2,4},{4,2},{6,8},{8,6},{10,12},{12,10},{14,16},{16,14},{18,20},{2... | collective-permute-start | bytes 147464 | tf_op jit(solution)/shard_map/ppermute | solution.py:648
  7.3 3.5 %collective-permute-start.1 = (bf16[32,768]{1,0:T(8,128)(2,1)S(1)}, bf16[32,768]{1,0:T(8,128)(2,1)S(1)}, u32[]{:S(2)}, u32[]{:S(2)}) collective-permute-start(bf16[32,768]{1,0:T(8,128)(2,1)S(1)} %get-tuple-element.61), channel_id=1, source_target_pairs={{0,2},{2,0},{4,6},{6,4},{8,10},{10,8},{12,14},{14,12},{16,18},{18,... | collective-permute-start | bytes 147464 | tf_op jit(solution)/shard_map/ppermute | solution.py:649
  10.8 1.3 %own_rows.1 = (bf16[48,1024]{1,0:T(8,128)(2,1)S(1)}, bf16[96,2048]{1,0:T(8,128)(2,1)S(1)}, bf16[96,2048]{1,0:T(8,128)(2,1)S(1)}, f32[96,1024]{1,0:T(8,128)S(1)},...) custom-call(bf16[64,2048]{1,0:T(8,128)(2,1)S(1)} %get-tuple-element.35.s_ref, ...), custom_call_target="tpu_custom_call" | custom-call | flops 1000000000 | bytes 4000000 | tf_op jit(solution)/shard_map/own_rows/pallas_call | solution.py:242
  12.1 1.0 %inner_rows.1 = (f32[512,128]{1,0:T(8,128)S(1)}, f32[512,128]{1,0:T(8,128)S(1)}, f32[96,1536]{1,0:T(8,128)S(1)}, f32[48,768]{1,0:T(8,128)S(1)}, f32[288,256]{1,0:T(8,128)S(1)}, /*index=5*/f32[144,128]{1,0:T(8,128)S(1)}) custom-call(bf16[48,1024]{1,0:T(8,128)(2,1)S(1)} %get-tuple-element.38.pst_ref.pst_own, ...), custom_call_target="tpu_custom_call" | custom-call | flops 1000000000 | bytes 4000000 | tf_op jit(solution)/shard_map/inner_rows/pallas_call | solution.py:327
  13.1 0.0 collective-permute-done.2.odd_ref
  13.2 0.0 collective-permute-done.1.even_ref
  13.2 1.2 %rest.1 = (bf16[512,128]{1,0:T(8,128)(2,1)S(1)}, bf16[512,128]{1,0:T(8,128)(2,1)S(1)}, bf16[256,128]{1,0:T(8,128)(2,1)S(1)}) custom-call(bf16[32,768]{1,0:T(8,128)(2,1)S(1)} %collective-permute-done.1.even_ref, bf16[32,768]{1,0:T(8,128)(2,1)S(1)} %collective-permute-done.2.odd_ref, bf16[48,1024]{1,0:T(8,128)(2,1)S(1)} %get-tuple-element.38.pst_ref.pst_own, ...), custom_call_target="tpu_custom_call" | custom-call | flops 1000000000 | bytes 4000000 | tf_op jit(solution)/shard_map/rest/pallas_call | solution.py:469
  14.3 12.7 %all_to_all.10.parts_ref = bf16[32,8,128]{2,1,0:T(8,128)(2,1)S(1)} all-to-all(bf16[32,8,128]{2,1,0:T(8,128)(2,1)S(1)} %bitcast.19), channel_id=1, replica_groups=mesh['wide'=16,'narrow'=2] {'wide','narrow'}, dimensions={0} | all-to-all | bytes 131072 | tf_op jit(solution)/shard_map/all_to_all | solution.py:659
  27.0 9.3 %all_to_all.11 = bf16[32,8,128]{2,1,0:T(8,128)(2,1)S(1)} all-to-all(bf16[32,8,128]{2,1,0:T(8,128)(2,1)S(1)} %add_up.1), channel_id=1, replica_groups=mesh['wide'=16,'narrow'=2] {'wide','narrow'}, dimensions={0} | all-to-all | bytes 131072 | tf_op jit(solution)/shard_map/all_to_all | solution.py:660
  36.3 1.0 %spread.1 = (bf16[512,128]{1,0:T(8,128)(2,1)}, bf16[512,128]{1,0:T(8,128)(2,1)}, f32[432,48]{1,0:T(8,128)}, f32[432,32]{1,0:T(8,128)}) custom-call(bf16[256,128]{1,0:T(8,128)(2,1)S(1)} %bitcast.18, bf16[512,128]{1,0:T(8,128)(2,1)S(1)} %get-tuple-element.54.out_ref, bf16[512,128]{1,0:T(8,128)(2,1)S(1)} %get-tuple-element.55.gf_ref), custom_call_target="tpu_custom_call" | custom-call | tf_op jit(solution)/shard_map/spread/pallas_call | solution.py:544
  (2 shorter events, 0.0 us)
Async XLA Ops:
  2.0 4.6 %collective-permute-start = (bf16[32,128]{1,0:T(8,128)(2,1)S(1)}, bf16[32,128]{1,0:T(8,128)(2,1)S(1)}, u32[]{:S(2)}, u32[]{:S(2)}) collective-permute-start(bf16[32,128]{1,0:T(8,128)(2,1)S(1)} %get-tuple-element.33), channel_id=1, source_target_pairs={{0,1},{1,0},{2,3},{3,2},{4,5},{5,4},{6,7},{7,6},{8,9},{9,8},{10,11... | collective-permute-start | bytes 24584 | tf_op jit(solution)/shard_map/ppermute | solution.py:632
  6.7 6.5 %collective-permute-start.2 = (bf16[32,768]{1,0:T(8,128)(2,1)S(1)}, bf16[32,768]{1,0:T(8,128)(2,1)S(1)}, u32[]{:S(2)}, u32[]{:S(2)}) collective-permute-start(bf16[32,768]{1,0:T(8,128)(2,1)S(1)} %get-tuple-element.60), channel_id=1, source_target_pairs={{2,4},{4,2},{6,8},{8,6},{10,12},{12,10},{14,16},{16,14},{18,20},{2... | collective-permute-start | bytes 147464 | tf_op jit(solution)/shard_map/ppermute | solution.py:648
  7.3 5.8 %collective-permute-start.1 = (bf16[32,768]{1,0:T(8,128)(2,1)S(1)}, bf16[32,768]{1,0:T(8,128)(2,1)S(1)}, u32[]{:S(2)}, u32[]{:S(2)}) collective-permute-start(bf16[32,768]{1,0:T(8,128)(2,1)S(1)} %get-tuple-element.61), channel_id=1, source_target_pairs={{0,2},{2,0},{4,6},{6,4},{8,10},{10,8},{12,14},{14,12},{16,18},{18,... | collective-permute-start | bytes 147464 | tf_op jit(solution)/shard_map/ppermute | solution.py:649

commit v18 on v17

--- a/solution.py
+++ b/solution.py
@@ -359,7 +359,8 @@
 
     odd = w % 2
     halo_ref[1 - odd] = even_ref[...]
-    halo_ref[odd] = odd_ref[...]
+    inside = flag((w > 0) & (w < counts[0] - 1))
+    halo_ref[odd] = (odd_ref[...].astype(F32) * inside).astype(BF)
     columns = [
         [halo_ref[i, :, row(SLOTS + side)].astype(F32) for side in range(sides)] for i in range(2)
     ]
@@ -640,7 +641,9 @@
     sides = 1 if narrow == 2 else 2
     own, strip, to_odd, to_even = pack(features, cotangent, sides)
     swaps = lambda start: [
-        pair for i in range(start, wide - 1, 2) for pair in ((i, i + 1), (i + 1, i))
+        pair
+        for i in range(start, wide, 2)
+        for pair in ((i, (i + 1) % wide), ((i + 1) % wide, i))
     ]
     columns = beside_blocks(strip, narrow)
     wo, wg, wc, wq = weight_matrices(coarse_weight, fine_weight)

time: 37.6 us -> 36.7 us (0.976)
  starting transfers between devices: 7.13 us -> 6.41 us
  blocking collectives: 22 us -> 21.4 us
  waiting for transfers between devices: 0.42 us -> 0.89 us
    ppermute x1, starting transfers between devices: 3.47 us -> 0.01 us  [shards(): even = lax.ppermute(with_columns(to_even), 'wide', swaps(0))]
    ppermute x1, starting transfers between devices: 0.65 us -> 3.4 us  [shards(): odd = lax.ppermute(with_columns(to_odd), 'wide', swaps(1))]
    all_to_all x1, blocking collectives: 12.7 us -> 12.1 us  [shards(): parts = lax.all_to_all(grads, both, 0, 0, tiled=True)]
    ppermute x1, waiting for transfers between devices: 0.01 us -> 0.47 us  [shards(): odd = lax.ppermute(with_columns(to_odd), 'wide', swaps(1))]
  transfers between devices with their start and end apart: 3 -> 3, of which waited for: 1 -> 2; matrix products, arithmetic and copies ran while one was open for 0% -> 0% of each run, Pallas kernels for 9% -> 10%
where the time goes in v18:
time: 36.7 us; the launch traced here: 36.4 us
  blocking collectives  21.4 us (58%)
  Pallas kernels  7.06 us (19%)
  starting transfers between devices  6.41 us (17%)
  waiting for transfers between devices  0.89 us (2%)
  between operations  0.67 us (2%)
    all_to_all x1, blocking collectives, shards(): parts = lax.all_to_all(grads, both, 0, 0, tiled=True)  12.1 us
    all_to_all x1, blocking collectives, shards(): total = lax.all_to_all(add_up(parts), both, 0, 0, tiled=True)  9.3 us
    ppermute x1, starting transfers between devices, shards(): odd = lax.ppermute(with_columns(to_odd), 'wide', swaps(1))  3.4 us
    ppermute x1, starting transfers between devices, beside_blocks(): return lax.ppermute(outer, 'narrow', [(0, 1), (1, 0)])  3 us
    pallas_call x1, Pallas kernels, pack(): pl.pallas_call(functools.partial(pack_kernel, sides), in_specs=[pl.BlockS...  1.39 us
    pallas_call x1, Pallas kernels, own_rows(): pl.pallas_call(functools.partial(own_kernel, sides), out_shape=(shaped(48...  1.3 us
    pallas_call x1, Pallas kernels, weight_matrices(): pl.pallas_call(matrices_kernel, in_specs=[pl.BlockSpec(memory_space=pltpu...  1.2 us
    pallas_call x1, Pallas kernels, rest(): pl.pallas_call(functools.partial(rest_kernel, counts, sides), out_shape=(...  1.14 us
  transfers between devices with their start and end apart: 3, of which 2 were waited for; matrix products, arithmetic and copies ran while one was open for 0% of the time, Pallas kernels for 10%

profile of v18, /device:TPU:0, one launch (start us, length us, event | category | flops | bytes accessed | tf_op | source)
XLA Modules:
  0.0 36.4 jit_solution(8759927457180776487)
XLA Ops:
  0.6 1.4 %pack.1 = (bf16[64,2048]{1,0:T(8,128)(2,1)S(1)}, bf16[32,128]{1,0:T(8,128)(2,1)S(1)}, bf16[32,768]{1,0:T(8,128)(2,1)S(1)}, bf16[32,768]{1,0:T(8,128)(2,1)S(1)}) custom-call(bf16[512,128]{1,0:T(8,128)(2,1)} %bitcast.20, bf16[512,128]{1,0:T(8,128)(2,1)} %bitcast.21), custom_call_target="tpu_custom_call" | custom-call | flops 1000000 | bytes 1000000 | tf_op jit(solution)/shard_map/pack/pallas_call | solution.py:125
  2.0 3.0 %collective-permute-start = (bf16[32,128]{1,0:T(8,128)(2,1)S(1)}, bf16[32,128]{1,0:T(8,128)(2,1)S(1)}, u32[]{:S(2)}, u32[]{:S(2)}) collective-permute-start(bf16[32,128]{1,0:T(8,128)(2,1)S(1)} %get-tuple-element.33), channel_id=1, source_target_pairs={{0,1},{1,0},{2,3},{3,2},{4,5},{5,4},{6,7},{7,6},{8,9},{9,8},{10,11... | collective-permute-start | bytes 24584 | tf_op jit(solution)/shard_map/ppermute | solution.py:633
  5.0 1.2 %matrices.1 = (bf16[96,192]{1,0:T(8,128)(2,1)S(1)}, bf16[192,96]{1,0:T(8,128)(2,1)S(1)}, bf16[96,48]{1,0:T(8,128)(2,1)S(1)}, bf16[48,96]{1,0:T(8,128)(2,1)S(1)}) custom-call(bf16[432,48]{1,0:T(8,128)(2,1)} %bitcast.22, bf16[432,32]{1,0:T(8,128)(2,1)} %bitcast.23), custom_call_target="tpu_custom_call" | custom-call | flops 1000000 | bytes 1000000 | tf_op jit(solution)/shard_map/matrices/pallas_call | solution.py:613
  6.2 0.4 %collective-permute-done.columns_ref = bf16[32,128]{1,0:T(8,128)(2,1)S(1)} collective-permute-done((bf16[32,128]{1,0:T(8,128)(2,1)S(1)}, bf16[32,128]{1,0:T(8,128)(2,1)S(1)}, u32[]{:S(2)}, u32[]{:S(2)}) %collective-permute-start) | collective-permute-done | bytes 8224 | tf_op jit(solution)/shard_map/ppermute | solution.py:633
  6.7 3.4 %collective-permute-start.2 = (bf16[32,768]{1,0:T(8,128)(2,1)S(1)}, bf16[32,768]{1,0:T(8,128)(2,1)S(1)}, u32[]{:S(2)}, u32[]{:S(2)}) collective-permute-start(bf16[32,768]{1,0:T(8,128)(2,1)S(1)} %get-tuple-element.60), channel_id=1, source_target_pairs={{2,4},{4,2},{6,8},{8,6},{10,12},{12,10},{14,16},{16,14},{18,20},{2... | collective-permute-start | bytes 147464 | tf_op jit(solution)/shard_map/ppermute | solution.py:651
  10.1 0.0 collective-permute-start.1
  10.1 1.3 %own_rows.1 = (bf16[48,1024]{1,0:T(8,128)(2,1)S(1)}, bf16[96,2048]{1,0:T(8,128)(2,1)S(1)}, bf16[96,2048]{1,0:T(8,128)(2,1)S(1)}, f32[96,1024]{1,0:T(8,128)S(1)},...) custom-call(bf16[64,2048]{1,0:T(8,128)(2,1)S(1)} %get-tuple-element.35.s_ref, ...), custom_call_target="tpu_custom_call" | custom-call | flops 1000000000 | bytes 4000000 | tf_op jit(solution)/shard_map/own_rows/pallas_call | solution.py:242
  11.4 1.0 %inner_rows.1 = (f32[512,128]{1,0:T(8,128)S(1)}, f32[512,128]{1,0:T(8,128)S(1)}, f32[96,1536]{1,0:T(8,128)S(1)}, f32[48,768]{1,0:T(8,128)S(1)}, f32[288,256]{1,0:T(8,128)S(1)}, /*index=5*/f32[144,128]{1,0:T(8,128)S(1)}) custom-call(bf16[48,1024]{1,0:T(8,128)(2,1)S(1)} %get-tuple-element.38.pst_ref.pst_own, ...), custom_call_target="tpu_custom_call" | custom-call | flops 1000000000 | bytes 4000000 | tf_op jit(solution)/shard_map/inner_rows/pallas_call | solution.py:327
  12.4 0.5 %collective-permute-done.2.odd_ref = bf16[32,768]{1,0:T(8,128)(2,1)S(1)} collective-permute-done((bf16[32,768]{1,0:T(8,128)(2,1)S(1)}, bf16[32,768]{1,0:T(8,128)(2,1)S(1)}, u32[]{:S(2)}, u32[]{:S(2)}) %collective-permute-start.2) | collective-permute-done | bytes 49184 | tf_op jit(solution)/shard_map/ppermute | solution.py:651
  12.9 0.0 collective-permute-done.1.even_ref
  12.9 1.1 %rest.1 = (bf16[512,128]{1,0:T(8,128)(2,1)S(1)}, bf16[512,128]{1,0:T(8,128)(2,1)S(1)}, bf16[256,128]{1,0:T(8,128)(2,1)S(1)}) custom-call(bf16[32,768]{1,0:T(8,128)(2,1)S(1)} %collective-permute-done.1.even_ref, bf16[32,768]{1,0:T(8,128)(2,1)S(1)} %collective-permute-done.2.odd_ref, bf16[48,1024]{1,0:T(8,128)(2,1)S(1)} %get-tuple-element.38.pst_ref.pst_own, ...), custom_call_target="tpu_custom_call" | custom-call | flops 1000000000 | bytes 4000000 | tf_op jit(solution)/shard_map/rest/pallas_call | solution.py:470
  14.0 12.1 %all_to_all.10.parts_ref = bf16[32,8,128]{2,1,0:T(8,128)(2,1)S(1)} all-to-all(bf16[32,8,128]{2,1,0:T(8,128)(2,1)S(1)} %bitcast.19), channel_id=1, replica_groups=mesh['wide'=16,'narrow'=2] {'wide','narrow'}, dimensions={0} | all-to-all | bytes 131072 | tf_op jit(solution)/shard_map/all_to_all | solution.py:662
  26.2 9.3 %all_to_all.11 = bf16[32,8,128]{2,1,0:T(8,128)(2,1)S(1)} all-to-all(bf16[32,8,128]{2,1,0:T(8,128)(2,1)S(1)} %add_up.1), channel_id=1, replica_groups=mesh['wide'=16,'narrow'=2] {'wide','narrow'}, dimensions={0} | all-to-all | bytes 131072 | tf_op jit(solution)/shard_map/all_to_all | solution.py:663
  35.5 1.0 %spread.1 = (bf16[512,128]{1,0:T(8,128)(2,1)}, bf16[512,128]{1,0:T(8,128)(2,1)}, f32[432,48]{1,0:T(8,128)}, f32[432,32]{1,0:T(8,128)}) custom-call(bf16[256,128]{1,0:T(8,128)(2,1)S(1)} %bitcast.18, bf16[512,128]{1,0:T(8,128)(2,1)S(1)} %get-tuple-element.54.out_ref, bf16[512,128]{1,0:T(8,128)(2,1)S(1)} %get-tuple-element.55.gf_ref), custom_call_target="tpu_custom_call" | custom-call | tf_op jit(solution)/shard_map/spread/pallas_call | solution.py:545
  (2 shorter events, 0.0 us)
Async XLA Ops:
  2.0 4.6 %collective-permute-start = (bf16[32,128]{1,0:T(8,128)(2,1)S(1)}, bf16[32,128]{1,0:T(8,128)(2,1)S(1)}, u32[]{:S(2)}, u32[]{:S(2)}) collective-permute-start(bf16[32,128]{1,0:T(8,128)(2,1)S(1)} %get-tuple-element.33), channel_id=1, source_target_pairs={{0,1},{1,0},{2,3},{3,2},{4,5},{5,4},{6,7},{7,6},{8,9},{9,8},{10,11... | collective-permute-start | bytes 24584 | tf_op jit(solution)/shard_map/ppermute | solution.py:633
  6.7 6.2 %collective-permute-start.2 = (bf16[32,768]{1,0:T(8,128)(2,1)S(1)}, bf16[32,768]{1,0:T(8,128)(2,1)S(1)}, u32[]{:S(2)}, u32[]{:S(2)}) collective-permute-start(bf16[32,768]{1,0:T(8,128)(2,1)S(1)} %get-tuple-element.60), channel_id=1, source_target_pairs={{2,4},{4,2},{6,8},{8,6},{10,12},{12,10},{14,16},{16,14},{18,20},{2... | collective-permute-start | bytes 147464 | tf_op jit(solution)/shard_map/ppermute | solution.py:651
  10.1 2.8 %collective-permute-start.1 = (bf16[32,768]{1,0:T(8,128)(2,1)S(1)}, bf16[32,768]{1,0:T(8,128)(2,1)S(1)}, u32[]{:S(2)}, u32[]{:S(2)}) collective-permute-start(bf16[32,768]{1,0:T(8,128)(2,1)S(1)} %get-tuple-element.61), channel_id=1, source_target_pairs={{0,2},{2,0},{4,6},{6,4},{8,10},{10,8},{12,14},{14,12},{16,18},{18,... | collective-permute-start | bytes 147464 | tf_op jit(solution)/shard_map/ppermute | solution.py:652

commit v19 on v18

--- a/solution.py
+++ b/solution.py
@@ -640,16 +640,23 @@
     wide, narrow = lax.axis_size("wide"), lax.axis_size("narrow")
     sides = 1 if narrow == 2 else 2
     own, strip, to_odd, to_even = pack(features, cotangent, sides)
-    swaps = lambda start: [
-        pair
-        for i in range(start, wide, 2)
-        for pair in ((i, (i + 1) % wide), ((i + 1) % wide, i))
+    both = ("wide", "narrow")
+    even_pairs = [pair for i in range(0, wide, 2) for pair in ((i, i + 1), (i + 1, i))]
+    odd_pairs = [
+        (i * narrow + n, j * narrow + n)
+        for i in range(wide)
+        for j in (i + 1 if i % 2 else i - 1,)
+        if 0 <= j < wide
+        for n in range(narrow)
+    ]
+    odd_pairs += [
+        (i * narrow + n, i * narrow + (n ^ 1)) for i in (0, wide - 1) for n in range(narrow)
     ]
     columns = beside_blocks(strip, narrow)
     wo, wg, wc, wq = weight_matrices(coarse_weight, fine_weight)
     with_columns = lambda message: lax.dynamic_update_slice(message, columns, (0, SLOTS * COLS))
-    odd = lax.ppermute(with_columns(to_odd), "wide", swaps(1))
-    even = lax.ppermute(with_columns(to_even), "wide", swaps(0))
+    odd = lax.ppermute(with_columns(to_odd), both, odd_pairs)
+    even = lax.ppermute(with_columns(to_even), "wide", even_pairs)
     stacks = own_rows(own, columns, wc, wg, sides)
     inner = inner_rows(stacks, wo, wq, narrow)
     output, grad_features, grads = rest(
@@ -658,7 +665,6 @@
     devices = wide * narrow
     share = -(-256 // devices)
     grads = jnp.pad(grads, ((0, share * devices - 256), (0, 0))).reshape(devices, share, COLS)
-    both = ("wide", "narrow")
     parts = lax.all_to_all(grads, both, 0, 0, tiled=True)
     total = lax.all_to_all(add_up(parts), both, 0, 0, tiled=True)
     total = total.reshape(share * devices, COLS)[:256]

time: 36.7 us -> 35.7 us (0.973)
  starting transfers between devices: 6.41 us -> 5.17 us
  blocking collectives: 21.4 us -> 22.1 us
  waiting for transfers between devices: 0.89 us -> 0.42 us
    ppermute x2, starting transfers between devices: 3.41 us -> 2.16 us  [the longest x1 2.02 us: shards(): odd = lax.ppermute(with_columns(to_odd), both, odd_pairs)]
    all_to_all x1, blocking collectives: 12.1 us -> 12.8 us  [shards(): parts = lax.all_to_all(grads, both, 0, 0, tiled=True)]
    ppermute x2, waiting for transfers between devices: 0.47 us -> 0.01 us  [the longest x1 0.01 us: shards(): odd = lax.ppermute(with_columns(to_odd), both, odd_pairs)]
  transfers between devices with their start and end apart: 3 -> 3, of which waited for: 2 -> 1; matrix products, arithmetic and copies ran while one was open for 0% -> 0% of each run, Pallas kernels for 10% -> 10%
where the time goes in v19:
time: 35.7 us; the launch traced here: 35.4 us
  blocking collectives  22.1 us (62%)
  Pallas kernels  7.08 us (20%)
  starting transfers between devices  5.17 us (14%)
  between operations  0.68 us (2%)
  waiting for transfers between devices  0.42 us (1%)
    all_to_all x1, blocking collectives, shards(): parts = lax.all_to_all(grads, both, 0, 0, tiled=True)  12.8 us
    all_to_all x1, blocking collectives, shards(): total = lax.all_to_all(add_up(parts), both, 0, 0, tiled=True)  9.3 us
    ppermute x1, starting transfers between devices, beside_blocks(): return lax.ppermute(outer, 'narrow', [(0, 1), (1, 0)])  3 us
    ppermute x1, starting transfers between devices, shards(): odd = lax.ppermute(with_columns(to_odd), both, odd_pairs)  2.02 us
    pallas_call x1, Pallas kernels, pack(): pl.pallas_call(functools.partial(pack_kernel, sides), in_specs=[pl.BlockS...  1.39 us
    pallas_call x1, Pallas kernels, own_rows(): pl.pallas_call(functools.partial(own_kernel, sides), out_shape=(shaped(48...  1.29 us
    pallas_call x1, Pallas kernels, weight_matrices(): pl.pallas_call(matrices_kernel, in_specs=[pl.BlockSpec(memory_space=pltpu...  1.2 us
    pallas_call x1, Pallas kernels, rest(): pl.pallas_call(functools.partial(rest_kernel, counts, sides), out_shape=(...  1.16 us
  transfers between devices with their start and end apart: 3, of which 1 were waited for; matrix products, arithmetic and copies ran while one was open for 0% of the time, Pallas kernels for 10%

profile of v19, /device:TPU:0, one launch (start us, length us, event | category | flops | bytes accessed | tf_op | source)
XLA Modules:
  0.0 35.4 jit_solution(7032180481486681127)
XLA Ops:
  0.6 1.4 %pack.1 = (bf16[64,2048]{1,0:T(8,128)(2,1)S(1)}, bf16[32,128]{1,0:T(8,128)(2,1)S(1)}, bf16[32,768]{1,0:T(8,128)(2,1)S(1)}, bf16[32,768]{1,0:T(8,128)(2,1)S(1)}) custom-call(bf16[512,128]{1,0:T(8,128)(2,1)} %bitcast.20, bf16[512,128]{1,0:T(8,128)(2,1)} %bitcast.21), custom_call_target="tpu_custom_call" | custom-call | flops 1000000 | bytes 1000000 | tf_op jit(solution)/shard_map/pack/pallas_call | solution.py:125
  2.0 3.0 %collective-permute-start = (bf16[32,128]{1,0:T(8,128)(2,1)S(1)}, bf16[32,128]{1,0:T(8,128)(2,1)S(1)}, u32[]{:S(2)}, u32[]{:S(2)}) collective-permute-start(bf16[32,128]{1,0:T(8,128)(2,1)S(1)} %get-tuple-element.33), channel_id=1, source_target_pairs={{0,1},{1,0},{2,3},{3,2},{4,5},{5,4},{6,7},{7,6},{8,9},{9,8},{10,11... | collective-permute-start | bytes 24584 | tf_op jit(solution)/shard_map/ppermute | solution.py:633
  5.0 1.2 %matrices.1 = (bf16[96,192]{1,0:T(8,128)(2,1)S(1)}, bf16[192,96]{1,0:T(8,128)(2,1)S(1)}, bf16[96,48]{1,0:T(8,128)(2,1)S(1)}, bf16[48,96]{1,0:T(8,128)(2,1)S(1)}) custom-call(bf16[432,48]{1,0:T(8,128)(2,1)} %bitcast.22, bf16[432,32]{1,0:T(8,128)(2,1)} %bitcast.23), custom_call_target="tpu_custom_call" | custom-call | flops 1000000 | bytes 1000000 | tf_op jit(solution)/shard_map/matrices/pallas_call | solution.py:613
  6.2 0.4 %collective-permute-done.columns_ref = bf16[32,128]{1,0:T(8,128)(2,1)S(1)} collective-permute-done((bf16[32,128]{1,0:T(8,128)(2,1)S(1)}, bf16[32,128]{1,0:T(8,128)(2,1)S(1)}, u32[]{:S(2)}, u32[]{:S(2)}) %collective-permute-start) | collective-permute-done | bytes 8224 | tf_op jit(solution)/shard_map/ppermute | solution.py:633
  6.7 2.0 %collective-permute-start.2 = (bf16[32,768]{1,0:T(8,128)(2,1)S(1)}, bf16[32,768]{1,0:T(8,128)(2,1)S(1)}, u32[]{:S(2)}, u32[]{:S(2)}) collective-permute-start(bf16[32,768]{1,0:T(8,128)(2,1)S(1)} %get-tuple-element.60), channel_id=1, source_target_pairs={{2,4},{3,5},{4,2},{5,3},{6,8},{7,9},{8,6},{9,7},{10,12},{11,13},{1... | collective-permute-start | bytes 147464 | tf_op jit(solution)/shard_map/ppermute | solution.py:658
  8.7 0.1 collective-permute-start.1
  8.8 1.3 %own_rows.1 = (bf16[48,1024]{1,0:T(8,128)(2,1)S(1)}, bf16[96,2048]{1,0:T(8,128)(2,1)S(1)}, bf16[96,2048]{1,0:T(8,128)(2,1)S(1)}, f32[96,1024]{1,0:T(8,128)S(1)},...) custom-call(bf16[64,2048]{1,0:T(8,128)(2,1)S(1)} %get-tuple-element.35.s_ref, ...), custom_call_target="tpu_custom_call" | custom-call | flops 1000000000 | bytes 4000000 | tf_op jit(solution)/shard_map/own_rows/pallas_call | solution.py:242
  10.1 1.0 %inner_rows.1 = (f32[512,128]{1,0:T(8,128)S(1)}, f32[512,128]{1,0:T(8,128)S(1)}, f32[96,1536]{1,0:T(8,128)S(1)}, f32[48,768]{1,0:T(8,128)S(1)}, f32[288,256]{1,0:T(8,128)S(1)}, /*index=5*/f32[144,128]{1,0:T(8,128)S(1)}) custom-call(bf16[48,1024]{1,0:T(8,128)(2,1)S(1)} %get-tuple-element.38.pst_ref.pst_own, ...), custom_call_target="tpu_custom_call" | custom-call | flops 1000000000 | bytes 4000000 | tf_op jit(solution)/shard_map/inner_rows/pallas_call | solution.py:327
  11.2 0.0 collective-permute-done.2.odd_ref
  11.2 0.0 collective-permute-done.1.even_ref
  11.2 1.2 %rest.1 = (bf16[512,128]{1,0:T(8,128)(2,1)S(1)}, bf16[512,128]{1,0:T(8,128)(2,1)S(1)}, bf16[256,128]{1,0:T(8,128)(2,1)S(1)}) custom-call(bf16[32,768]{1,0:T(8,128)(2,1)S(1)} %collective-permute-done.1.even_ref, bf16[32,768]{1,0:T(8,128)(2,1)S(1)} %collective-permute-done.2.odd_ref, bf16[48,1024]{1,0:T(8,128)(2,1)S(1)} %get-tuple-element.38.pst_ref.pst_own, ...), custom_call_target="tpu_custom_call" | custom-call | flops 1000000000 | bytes 4000000 | tf_op jit(solution)/shard_map/rest/pallas_call | solution.py:470
  12.4 12.8 %all_to_all.10.parts_ref = bf16[32,8,128]{2,1,0:T(8,128)(2,1)S(1)} all-to-all(bf16[32,8,128]{2,1,0:T(8,128)(2,1)S(1)} %bitcast.19), channel_id=1, replica_groups=mesh['wide'=16,'narrow'=2] {'wide','narrow'}, dimensions={0} | all-to-all | bytes 131072 | tf_op jit(solution)/shard_map/all_to_all | solution.py:668
  25.2 9.3 %all_to_all.11 = bf16[32,8,128]{2,1,0:T(8,128)(2,1)S(1)} all-to-all(bf16[32,8,128]{2,1,0:T(8,128)(2,1)S(1)} %add_up.1), channel_id=1, replica_groups=mesh['wide'=16,'narrow'=2] {'wide','narrow'}, dimensions={0} | all-to-all | bytes 131072 | tf_op jit(solution)/shard_map/all_to_all | solution.py:669
  34.5 1.0 %spread.1 = (bf16[512,128]{1,0:T(8,128)(2,1)}, bf16[512,128]{1,0:T(8,128)(2,1)}, f32[432,48]{1,0:T(8,128)}, f32[432,32]{1,0:T(8,128)}) custom-call(bf16[256,128]{1,0:T(8,128)(2,1)S(1)} %bitcast.18, bf16[512,128]{1,0:T(8,128)(2,1)S(1)} %get-tuple-element.54.out_ref, bf16[512,128]{1,0:T(8,128)(2,1)S(1)} %get-tuple-element.55.gf_ref), custom_call_target="tpu_custom_call" | custom-call | tf_op jit(solution)/shard_map/spread/pallas_call | solution.py:545
  (2 shorter events, 0.0 us)
Async XLA Ops:
  2.0 4.6 %collective-permute-start = (bf16[32,128]{1,0:T(8,128)(2,1)S(1)}, bf16[32,128]{1,0:T(8,128)(2,1)S(1)}, u32[]{:S(2)}, u32[]{:S(2)}) collective-permute-start(bf16[32,128]{1,0:T(8,128)(2,1)S(1)} %get-tuple-element.33), channel_id=1, source_target_pairs={{0,1},{1,0},{2,3},{3,2},{4,5},{5,4},{6,7},{7,6},{8,9},{9,8},{10,11... | collective-permute-start | bytes 24584 | tf_op jit(solution)/shard_map/ppermute | solution.py:633
  6.7 4.5 %collective-permute-start.2 = (bf16[32,768]{1,0:T(8,128)(2,1)S(1)}, bf16[32,768]{1,0:T(8,128)(2,1)S(1)}, u32[]{:S(2)}, u32[]{:S(2)}) collective-permute-start(bf16[32,768]{1,0:T(8,128)(2,1)S(1)} %get-tuple-element.60), channel_id=1, source_target_pairs={{2,4},{3,5},{4,2},{5,3},{6,8},{7,9},{8,6},{9,7},{10,12},{11,13},{1... | collective-permute-start | bytes 147464 | tf_op jit(solution)/shard_map/ppermute | solution.py:658
  8.7 2.5 %collective-permute-start.1 = (bf16[32,768]{1,0:T(8,128)(2,1)S(1)}, bf16[32,768]{1,0:T(8,128)(2,1)S(1)}, u32[]{:S(2)}, u32[]{:S(2)}) collective-permute-start(bf16[32,768]{1,0:T(8,128)(2,1)S(1)} %get-tuple-element.61), channel_id=1, source_target_pairs={{0,2},{2,0},{4,6},{6,4},{8,10},{10,8},{12,14},{14,12},{16,18},{18,... | collective-permute-start | bytes 147464 | tf_op jit(solution)/shard_map/ppermute | solution.py:659

commit v20 on v15

--- a/solution.py
+++ b/solution.py
@@ -362,7 +362,8 @@
 
     odd = w % 2
     halo_ref[1 - odd] = even_ref[:, row(0, SLOTS)]
-    halo_ref[odd] = odd_ref[:, row(0, SLOTS)]
+    inside = flag((w > 0) & (w < counts[0] - 1))
+    halo_ref[odd] = (odd_ref[:, row(0, SLOTS)].astype(F32) * inside).astype(BF)
     columns = [corners_ref[:, row(side)].astype(F32) for side in range(sides)]
 
     for i in range(2):
@@ -640,14 +641,25 @@
     wide, narrow = lax.axis_size("wide"), lax.axis_size("narrow")
     sides = 1 if narrow == 2 else 2
     own, strip, to_odd, to_even = pack(features, cotangent, sides)
-    swaps = lambda start: [
-        pair for i in range(start, wide - 1, 2) for pair in ((i, i + 1), (i + 1, i))
+    both = ("wide", "narrow")
+    even_pairs = [pair for i in range(0, wide, 2) for pair in ((i, i + 1), (i + 1, i))]
+    odd_pairs = [
+        (i * narrow + n, j * narrow + n)
+        for i in range(wide)
+        for j in (i + 1 if i % 2 else i - 1,)
+        if 0 <= j < wide
+        for n in range(narrow)
     ]
-    odd = lax.ppermute(to_odd, "wide", swaps(1))
-    even = lax.ppermute(to_even, "wide", swaps(0))
+    odd_pairs += [
+        (i * narrow + n, i * narrow + (n ^ 1)) for i in (0, wide - 1) for n in range(narrow)
+    ]
+    odd = lax.ppermute(to_odd, both, odd_pairs)
+    even = lax.ppermute(to_even, "wide", even_pairs)
     columns = beside_blocks(strip, narrow)
     wo, wg, wc, wq = weight_matrices(coarse_weight, fine_weight)
-    corners = odd[:, SLOTS * COLS :] + even[:, SLOTS * COLS :]
+    place = lax.axis_index("wide")
+    inside = jnp.where((place > 0) & (place < wide - 1), 1.0, 0.0).astype(BF)
+    corners = odd[:, SLOTS * COLS :] * inside + even[:, SLOTS * COLS :]
     columns, _ = lax.optimization_barrier((columns, corners))
     stacks = own_rows(own, columns, wc, wg, sides)
     inner = inner_rows(stacks, wo, wq, narrow)
@@ -658,7 +670,6 @@
     devices = wide * narrow
     share = -(-256 // devices)
     grads = jnp.pad(grads, ((0, share * devices - 256), (0, 0))).reshape(devices, share, COLS)
-    both = ("wide", "narrow")
     parts = lax.all_to_all(grads, both, 0, 0, tiled=True)
     total = lax.all_to_all(add_up(parts), both, 0, 0, tiled=True)
     total = total.reshape(share * devices, COLS)[:256]

time: 37.5 us -> 35.8 us (0.955)
  starting transfers between devices: 7.15 us -> 5.91 us
  waiting for transfers between devices: 0.79 us -> 0.11 us
    ppermute x2, starting transfers between devices: 5.06 us -> 3.15 us  [the longest x1 3 us: shards(): odd = lax.ppermute(to_odd, both, odd_pairs)]
    ppermute x2, waiting for transfers between devices: 0.78 us -> 0.11 us  [beside_blocks(): return lax.ppermute(outer, 'narrow', [(0, 1), (1, 0)])]
    ppermute x2, starting transfers between devices: 2.09 us -> 2.77 us  [beside_blocks(): return lax.ppermute(outer, 'narrow', [(0, 1), (1, 0)])]
  transfers between devices with their start and end apart: 4 -> 4, of which waited for: 2 -> 1; matrix products, arithmetic and copies ran while one was open for 0% -> 0% of each run, Pallas kernels for 9% -> 10%
where the time goes in v20:
time: 35.8 us; the launch traced here: 35.5 us
  blocking collectives  21.7 us (61%)
  Pallas kernels  7.05 us (20%)
  starting transfers between devices  5.91 us (17%)
  between operations  0.69 us (2%)
    all_to_all x1, blocking collectives, shards(): parts = lax.all_to_all(grads, both, 0, 0, tiled=True)  12.4 us
    all_to_all x1, blocking collectives, shards(): total = lax.all_to_all(add_up(parts), both, 0, 0, tiled=True)  9.3 us
    ppermute x1, starting transfers between devices, shards(): odd = lax.ppermute(to_odd, both, odd_pairs)  3 us
    ppermute x2, starting transfers between devices, beside_blocks(): return lax.ppermute(outer, 'narrow', [(0, 1), (1, 0)])  2.77 us
    pallas_call x1, Pallas kernels, pack(): pl.pallas_call(functools.partial(pack_kernel, sides), in_specs=[pl.BlockS...  1.4 us
    pallas_call x1, Pallas kernels, own_rows(): pl.pallas_call(functools.partial(own_kernel, sides), out_shape=(shaped(48...  1.3 us
    pallas_call x1, Pallas kernels, weight_matrices(): pl.pallas_call(matrices_kernel, in_specs=[pl.BlockSpec(memory_space=pltpu...  1.2 us
    pallas_call x1, Pallas kernels, rest(): pl.pallas_call(functools.partial(rest_kernel, counts, sides), out_shape=(...  1.11 us
  transfers between devices with their start and end apart: 4, of which 1 were waited for; matrix products, arithmetic and copies ran while one was open for 0% of the time, Pallas kernels for 10%

profile of v20, /device:TPU:0, one launch (start us, length us, event | category | flops | bytes accessed | tf_op | source)
XLA Modules:
  0.0 35.5 jit_solution(7754760446747279586)
XLA Ops:
  0.6 1.4 %pack.1 = (bf16[64,2048]{1,0:T(8,128)(2,1)S(1)}, bf16[32,128]{1,0:T(8,128)(2,1)S(1)}, bf16[32,768]{1,0:T(8,128)(2,1)S(1)}, bf16[32,768]{1,0:T(8,128)(2,1)S(1)}) custom-call(bf16[512,128]{1,0:T(8,128)(2,1)} %bitcast.20, bf16[512,128]{1,0:T(8,128)(2,1)} %bitcast.21), custom_call_target="tpu_custom_call" | custom-call | flops 1000000 | bytes 1000000 | tf_op jit(solution)/shard_map/pack/pallas_call | solution.py:128
  2.0 3.0 %collective-permute-start = (bf16[32,768]{1,0:T(8,128)(2,1)S(1)}, bf16[32,768]{1,0:T(8,128)(2,1)S(1)}, u32[]{:S(2)}, u32[]{:S(2)}) collective-permute-start(bf16[32,768]{1,0:T(8,128)(2,1)S(1)} %get-tuple-element.33), channel_id=1, source_target_pairs={{2,4},{3,5},{4,2},{5,3},{6,8},{7,9},{8,6},{9,7},{10,12},{11,13},{1... | collective-permute-start | bytes 147464 | tf_op jit(solution)/shard_map/ppermute | solution.py:656
  5.0 0.1 collective-permute-start.1
  5.2 1.5 %collective-permute-start.3 = (bf16[32,128]{1,0:T(8,128)(2,1)S(1)}, bf16[32,128]{1,0:T(8,128)(2,1)S(1)}, u32[]{:S(2)}, u32[]{:S(2)}) collective-permute-start(bf16[32,128]{1,0:T(8,128)(2,1)S(1)} %get-tuple-element.36), channel_id=1, source_target_pairs={{0,1},{1,0},{2,3},{3,2},{4,5},{5,4},{6,7},{7,6},{8,9},{9,8},{10,11... | collective-permute-start | bytes 24584 | tf_op jit(solution)/shard_map/ppermute | solution.py:634
  6.7 1.2 %matrices.1 = (bf16[96,192]{1,0:T(8,128)(2,1)S(1)}, bf16[192,96]{1,0:T(8,128)(2,1)S(1)}, bf16[96,48]{1,0:T(8,128)(2,1)S(1)}, bf16[48,96]{1,0:T(8,128)(2,1)S(1)}) custom-call(bf16[432,48]{1,0:T(8,128)(2,1)} %bitcast.22, bf16[432,32]{1,0:T(8,128)(2,1)} %bitcast.23), custom_call_target="tpu_custom_call" | custom-call | flops 1000000 | bytes 1000000 | tf_op jit(solution)/shard_map/matrices/pallas_call | solution.py:614
  7.9 0.0 collective-permute-done.odd_ref
  7.9 0.0 collective-permute-done.1.even_ref
  7.9 1.3 %collective-permute-start.2 = (bf16[32,128]{1,0:T(8,128)(2,1)S(1)}, bf16[32,128]{1,0:T(8,128)(2,1)S(1)}, u32[]{:S(2)}, u32[]{:S(2)}) collective-permute-start(bf16[32,128]{1,0:T(8,128)(2,1)S(1)} %slice_add_fusion), channel_id=1, source_target_pairs={{0,1},{1,0},{2,3},{3,2},{4,5},{5,4},{6,7},{7,6},{8,9},{9,8},{10,11... | collective-permute-start | bytes 24584 | tf_op jit(solution)/shard_map/ppermute | solution.py:634
  9.2 0.0 collective-permute-done.3.columns_ref
  9.2 1.3 %own_rows.1 = (bf16[48,1024]{1,0:T(8,128)(2,1)S(1)}, bf16[96,2048]{1,0:T(8,128)(2,1)S(1)}, bf16[96,2048]{1,0:T(8,128)(2,1)S(1)}, f32[96,1024]{1,0:T(8,128)S(1)},...) custom-call(bf16[64,2048]{1,0:T(8,128)(2,1)S(1)} %get-tuple-element.35.s_ref, ...), custom_call_target="tpu_custom_call" | custom-call | flops 1000000000 | bytes 4000000 | tf_op jit(solution)/shard_map/own_rows/pallas_call | solution.py:245
  10.5 1.0 %inner_rows.1 = (f32[512,128]{1,0:T(8,128)S(1)}, f32[512,128]{1,0:T(8,128)S(1)}, f32[96,1536]{1,0:T(8,128)S(1)}, f32[48,768]{1,0:T(8,128)S(1)}, f32[288,256]{1,0:T(8,128)S(1)}, /*index=5*/f32[144,128]{1,0:T(8,128)S(1)}) custom-call(bf16[48,1024]{1,0:T(8,128)(2,1)S(1)} %get-tuple-element.40.pst_ref.pst_own, ...), custom_call_target="tpu_custom_call" | custom-call | flops 1000000000 | bytes 4000000 | tf_op jit(solution)/shard_map/inner_rows/pallas_call | solution.py:330
  11.5 0.1 collective-permute-done.2.corners_ref
  11.6 1.1 %rest.1 = (bf16[512,128]{1,0:T(8,128)(2,1)S(1)}, bf16[512,128]{1,0:T(8,128)(2,1)S(1)}, bf16[256,128]{1,0:T(8,128)(2,1)S(1)}) custom-call(bf16[32,768]{1,0:T(8,128)(2,1)S(1)} %collective-permute-done.odd_ref, bf16[32,768]{1,0:T(8,128)(2,1)S(1)} %collective-permute-done.1.even_ref, bf16[32,128]{1,0:T(8,128)(2,1)S(1)} %collective-permute-done.2.corners_ref, ...), custom_call_target="tpu_custom_call" | custom-call | flops 1000000000 | bytes 4000000 | tf_op jit(solution)/shard_map/rest/pallas_call | solution.py:471
  12.8 12.4 %all_to_all.10.parts_ref = bf16[32,8,128]{2,1,0:T(8,128)(2,1)S(1)} all-to-all(bf16[32,8,128]{2,1,0:T(8,128)(2,1)S(1)} %bitcast.19), channel_id=1, replica_groups=mesh['wide'=16,'narrow'=2] {'wide','narrow'}, dimensions={0} | all-to-all | bytes 131072 | tf_op jit(solution)/shard_map/all_to_all | solution.py:673
  25.2 9.3 %all_to_all.11 = bf16[32,8,128]{2,1,0:T(8,128)(2,1)S(1)} all-to-all(bf16[32,8,128]{2,1,0:T(8,128)(2,1)S(1)} %add_up.1), channel_id=1, replica_groups=mesh['wide'=16,'narrow'=2] {'wide','narrow'}, dimensions={0} | all-to-all | bytes 131072 | tf_op jit(solution)/shard_map/all_to_all | solution.py:674
  34.5 1.0 %spread.1 = (bf16[512,128]{1,0:T(8,128)(2,1)}, bf16[512,128]{1,0:T(8,128)(2,1)}, f32[432,48]{1,0:T(8,128)}, f32[432,32]{1,0:T(8,128)}) custom-call(bf16[256,128]{1,0:T(8,128)(2,1)S(1)} %bitcast.18, bf16[512,128]{1,0:T(8,128)(2,1)S(1)} %get-tuple-element.56.out_ref, bf16[512,128]{1,0:T(8,128)(2,1)S(1)} %get-tuple-element.57.gf_ref), custom_call_target="tpu_custom_call" | custom-call | tf_op jit(solution)/shard_map/spread/pallas_call | solution.py:546
  (2 shorter events, 0.0 us)
Async XLA Ops:
  2.0 5.9 %collective-permute-start = (bf16[32,768]{1,0:T(8,128)(2,1)S(1)}, bf16[32,768]{1,0:T(8,128)(2,1)S(1)}, u32[]{:S(2)}, u32[]{:S(2)}) collective-permute-start(bf16[32,768]{1,0:T(8,128)(2,1)S(1)} %get-tuple-element.33), channel_id=1, source_target_pairs={{2,4},{3,5},{4,2},{5,3},{6,8},{7,9},{8,6},{9,7},{10,12},{11,13},{1... | collective-permute-start | bytes 147464 | tf_op jit(solution)/shard_map/ppermute | solution.py:656
  5.0 2.9 %collective-permute-start.1 = (bf16[32,768]{1,0:T(8,128)(2,1)S(1)}, bf16[32,768]{1,0:T(8,128)(2,1)S(1)}, u32[]{:S(2)}, u32[]{:S(2)}) collective-permute-start(bf16[32,768]{1,0:T(8,128)(2,1)S(1)} %get-tuple-element.34), channel_id=1, source_target_pairs={{0,2},{2,0},{4,6},{6,4},{8,10},{10,8},{12,14},{14,12},{16,18},{18,... | collective-permute-start | bytes 147464 | tf_op jit(solution)/shard_map/ppermute | solution.py:657
  5.2 4.0 %collective-permute-start.3 = (bf16[32,128]{1,0:T(8,128)(2,1)S(1)}, bf16[32,128]{1,0:T(8,128)(2,1)S(1)}, u32[]{:S(2)}, u32[]{:S(2)}) collective-permute-start(bf16[32,128]{1,0:T(8,128)(2,1)S(1)} %get-tuple-element.36), channel_id=1, source_target_pairs={{0,1},{1,0},{2,3},{3,2},{4,5},{5,4},{6,7},{7,6},{8,9},{9,8},{10,11... | collective-permute-start | bytes 24584 | tf_op jit(solution)/shard_map/ppermute | solution.py:634
  7.9 3.7 %collective-permute-start.2 = (bf16[32,128]{1,0:T(8,128)(2,1)S(1)}, bf16[32,128]{1,0:T(8,128)(2,1)S(1)}, u32[]{:S(2)}, u32[]{:S(2)}) collective-permute-start(bf16[32,128]{1,0:T(8,128)(2,1)S(1)} %slice_add_fusion), channel_id=1, source_target_pairs={{0,1},{1,0},{2,3},{3,2},{4,5},{5,4},{6,7},{7,6},{8,9},{9,8},{10,11... | collective-permute-start | bytes 24584 | tf_op jit(solution)/shard_map/ppermute | solution.py:634

commit v21 on v19

--- a/solution.py
+++ b/solution.py
@@ -77,7 +77,7 @@
 def pack_kernel(
     sides, f_hbm, g_hbm, s_ref, strip_ref, odd_ref, even_ref, f_ref, g_ref, wide_ref, base_ref, sems
 ):
-    arrivals = chunks(((f_hbm, f_ref), (g_hbm, g_ref)), sems, 4)
+    arrivals = chunks(((f_hbm, f_ref), (g_hbm, g_ref)), sems, 2)
     for copies in arrivals:
         start(copies)
     lane = lanes_of((C1, COLS))
@@ -136,7 +136,7 @@
             pltpu.VMEM((CELLS, COLS), BF),
             pltpu.VMEM((CELLS, COLS), F32),
             pltpu.VMEM((2, 32, SLOTS * COLS), BF),
-            pltpu.SemaphoreType.DMA((2, 4)),
+            pltpu.SemaphoreType.DMA((2, 2)),
         ],
         compiler_params=params(),
         cost_estimate=pl.CostEstimate(flops=10**6, bytes_accessed=10**6, transcendentals=0),

time: 35.7 us -> 35.7 us (level)
  no operation moved by 1% of the time
where the time goes in v21:
time: 35.7 us; the launch traced here: 35.5 us
  blocking collectives  22.1 us (62%)
  Pallas kernels  7.11 us (20%)
  starting transfers between devices  5.17 us (14%)
  between operations  0.68 us (2%)
  waiting for transfers between devices  0.42 us (1%)
    all_to_all x1, blocking collectives, shards(): parts = lax.all_to_all(grads, both, 0, 0, tiled=True)  12.8 us
    all_to_all x1, blocking collectives, shards(): total = lax.all_to_all(add_up(parts), both, 0, 0, tiled=True)  9.3 us
    ppermute x1, starting transfers between devices, beside_blocks(): return lax.ppermute(outer, 'narrow', [(0, 1), (1, 0)])  3 us
    ppermute x1, starting transfers between devices, shards(): odd = lax.ppermute(with_columns(to_odd), both, odd_pairs)  2.02 us
    pallas_call x1, Pallas kernels, pack(): pl.pallas_call(functools.partial(pack_kernel, sides), in_specs=[pl.BlockS...  1.42 us
    pallas_call x1, Pallas kernels, own_rows(): pl.pallas_call(functools.partial(own_kernel, sides), out_shape=(shaped(48...  1.3 us
    pallas_call x1, Pallas kernels, weight_matrices(): pl.pallas_call(matrices_kernel, in_specs=[pl.BlockSpec(memory_space=pltpu...  1.2 us
    pallas_call x1, Pallas kernels, rest(): pl.pallas_call(functools.partial(rest_kernel, counts, sides), out_shape=(...  1.16 us
  transfers between devices with their start and end apart: 3, of which 1 were waited for; matrix products, arithmetic and copies ran while one was open for 0% of the time, Pallas kernels for 10%

profile of v21, /device:TPU:0, one launch (start us, length us, event | category | flops | bytes accessed | tf_op | source)
XLA Modules:
  0.0 35.5 jit_solution(8949853793586387468)
XLA Ops:
  0.6 1.4 %pack.1 = (bf16[64,2048]{1,0:T(8,128)(2,1)S(1)}, bf16[32,128]{1,0:T(8,128)(2,1)S(1)}, bf16[32,768]{1,0:T(8,128)(2,1)S(1)}, bf16[32,768]{1,0:T(8,128)(2,1)S(1)}) custom-call(bf16[512,128]{1,0:T(8,128)(2,1)} %bitcast.20, bf16[512,128]{1,0:T(8,128)(2,1)} %bitcast.21), custom_call_target="tpu_custom_call" | custom-call | flops 1000000 | bytes 1000000 | tf_op jit(solution)/shard_map/pack/pallas_call | solution.py:125
  2.1 3.0 %collective-permute-start = (bf16[32,128]{1,0:T(8,128)(2,1)S(1)}, bf16[32,128]{1,0:T(8,128)(2,1)S(1)}, u32[]{:S(2)}, u32[]{:S(2)}) collective-permute-start(bf16[32,128]{1,0:T(8,128)(2,1)S(1)} %get-tuple-element.33), channel_id=1, source_target_pairs={{0,1},{1,0},{2,3},{3,2},{4,5},{5,4},{6,7},{7,6},{8,9},{9,8},{10,11... | collective-permute-start | bytes 24584 | tf_op jit(solution)/shard_map/ppermute | solution.py:633
  5.1 1.2 %matrices.1 = (bf16[96,192]{1,0:T(8,128)(2,1)S(1)}, bf16[192,96]{1,0:T(8,128)(2,1)S(1)}, bf16[96,48]{1,0:T(8,128)(2,1)S(1)}, bf16[48,96]{1,0:T(8,128)(2,1)S(1)}) custom-call(bf16[432,48]{1,0:T(8,128)(2,1)} %bitcast.22, bf16[432,32]{1,0:T(8,128)(2,1)} %bitcast.23), custom_call_target="tpu_custom_call" | custom-call | flops 1000000 | bytes 1000000 | tf_op jit(solution)/shard_map/matrices/pallas_call | solution.py:613
  6.3 0.4 %collective-permute-done.columns_ref = bf16[32,128]{1,0:T(8,128)(2,1)S(1)} collective-permute-done((bf16[32,128]{1,0:T(8,128)(2,1)S(1)}, bf16[32,128]{1,0:T(8,128)(2,1)S(1)}, u32[]{:S(2)}, u32[]{:S(2)}) %collective-permute-start) | collective-permute-done | bytes 8224 | tf_op jit(solution)/shard_map/ppermute | solution.py:633
  6.7 2.0 %collective-permute-start.2 = (bf16[32,768]{1,0:T(8,128)(2,1)S(1)}, bf16[32,768]{1,0:T(8,128)(2,1)S(1)}, u32[]{:S(2)}, u32[]{:S(2)}) collective-permute-start(bf16[32,768]{1,0:T(8,128)(2,1)S(1)} %get-tuple-element.60), channel_id=1, source_target_pairs={{2,4},{3,5},{4,2},{5,3},{6,8},{7,9},{8,6},{9,7},{10,12},{11,13},{1... | collective-permute-start | bytes 147464 | tf_op jit(solution)/shard_map/ppermute | solution.py:658
  8.7 0.1 collective-permute-start.1
  8.9 1.3 %own_rows.1 = (bf16[48,1024]{1,0:T(8,128)(2,1)S(1)}, bf16[96,2048]{1,0:T(8,128)(2,1)S(1)}, bf16[96,2048]{1,0:T(8,128)(2,1)S(1)}, f32[96,1024]{1,0:T(8,128)S(1)},...) custom-call(bf16[64,2048]{1,0:T(8,128)(2,1)S(1)} %get-tuple-element.35.s_ref, ...), custom_call_target="tpu_custom_call" | custom-call | flops 1000000000 | bytes 4000000 | tf_op jit(solution)/shard_map/own_rows/pallas_call | solution.py:242
  10.2 1.0 %inner_rows.1 = (f32[512,128]{1,0:T(8,128)S(1)}, f32[512,128]{1,0:T(8,128)S(1)}, f32[96,1536]{1,0:T(8,128)S(1)}, f32[48,768]{1,0:T(8,128)S(1)}, f32[288,256]{1,0:T(8,128)S(1)}, /*index=5*/f32[144,128]{1,0:T(8,128)S(1)}) custom-call(bf16[48,1024]{1,0:T(8,128)(2,1)S(1)} %get-tuple-element.38.pst_ref.pst_own, ...), custom_call_target="tpu_custom_call" | custom-call | flops 1000000000 | bytes 4000000 | tf_op jit(solution)/shard_map/inner_rows/pallas_call | solution.py:327
  11.2 0.0 collective-permute-done.2.odd_ref
  11.2 0.0 collective-permute-done.1.even_ref
  11.2 1.2 %rest.1 = (bf16[512,128]{1,0:T(8,128)(2,1)S(1)}, bf16[512,128]{1,0:T(8,128)(2,1)S(1)}, bf16[256,128]{1,0:T(8,128)(2,1)S(1)}) custom-call(bf16[32,768]{1,0:T(8,128)(2,1)S(1)} %collective-permute-done.1.even_ref, bf16[32,768]{1,0:T(8,128)(2,1)S(1)} %collective-permute-done.2.odd_ref, bf16[48,1024]{1,0:T(8,128)(2,1)S(1)} %get-tuple-element.38.pst_ref.pst_own, ...), custom_call_target="tpu_custom_call" | custom-call | flops 1000000000 | bytes 4000000 | tf_op jit(solution)/shard_map/rest/pallas_call | solution.py:470
  12.4 12.8 %all_to_all.10.parts_ref = bf16[32,8,128]{2,1,0:T(8,128)(2,1)S(1)} all-to-all(bf16[32,8,128]{2,1,0:T(8,128)(2,1)S(1)} %bitcast.19), channel_id=1, replica_groups=mesh['wide'=16,'narrow'=2] {'wide','narrow'}, dimensions={0} | all-to-all | bytes 131072 | tf_op jit(solution)/shard_map/all_to_all | solution.py:668
  25.2 9.3 %all_to_all.11 = bf16[32,8,128]{2,1,0:T(8,128)(2,1)S(1)} all-to-all(bf16[32,8,128]{2,1,0:T(8,128)(2,1)S(1)} %add_up.1), channel_id=1, replica_groups=mesh['wide'=16,'narrow'=2] {'wide','narrow'}, dimensions={0} | all-to-all | bytes 131072 | tf_op jit(solution)/shard_map/all_to_all | solution.py:669
  34.5 1.0 %spread.1 = (bf16[512,128]{1,0:T(8,128)(2,1)}, bf16[512,128]{1,0:T(8,128)(2,1)}, f32[432,48]{1,0:T(8,128)}, f32[432,32]{1,0:T(8,128)}) custom-call(bf16[256,128]{1,0:T(8,128)(2,1)S(1)} %bitcast.18, bf16[512,128]{1,0:T(8,128)(2,1)S(1)} %get-tuple-element.54.out_ref, bf16[512,128]{1,0:T(8,128)(2,1)S(1)} %get-tuple-element.55.gf_ref), custom_call_target="tpu_custom_call" | custom-call | tf_op jit(solution)/shard_map/spread/pallas_call | solution.py:545
  (2 shorter events, 0.0 us)
Async XLA Ops:
  2.1 4.6 %collective-permute-start = (bf16[32,128]{1,0:T(8,128)(2,1)S(1)}, bf16[32,128]{1,0:T(8,128)(2,1)S(1)}, u32[]{:S(2)}, u32[]{:S(2)}) collective-permute-start(bf16[32,128]{1,0:T(8,128)(2,1)S(1)} %get-tuple-element.33), channel_id=1, source_target_pairs={{0,1},{1,0},{2,3},{3,2},{4,5},{5,4},{6,7},{7,6},{8,9},{9,8},{10,11... | collective-permute-start | bytes 24584 | tf_op jit(solution)/shard_map/ppermute | solution.py:633
  6.7 4.5 %collective-permute-start.2 = (bf16[32,768]{1,0:T(8,128)(2,1)S(1)}, bf16[32,768]{1,0:T(8,128)(2,1)S(1)}, u32[]{:S(2)}, u32[]{:S(2)}) collective-permute-start(bf16[32,768]{1,0:T(8,128)(2,1)S(1)} %get-tuple-element.60), channel_id=1, source_target_pairs={{2,4},{3,5},{4,2},{5,3},{6,8},{7,9},{8,6},{9,7},{10,12},{11,13},{1... | collective-permute-start | bytes 147464 | tf_op jit(solution)/shard_map/ppermute | solution.py:658
  8.7 2.5 %collective-permute-start.1 = (bf16[32,768]{1,0:T(8,128)(2,1)S(1)}, bf16[32,768]{1,0:T(8,128)(2,1)S(1)}, u32[]{:S(2)}, u32[]{:S(2)}) collective-permute-start(bf16[32,768]{1,0:T(8,128)(2,1)S(1)} %get-tuple-element.61), channel_id=1, source_target_pairs={{0,2},{2,0},{4,6},{6,4},{8,10},{10,8},{12,14},{14,12},{16,18},{18,... | collective-permute-start | bytes 147464 | tf_op jit(solution)/shard_map/ppermute | solution.py:659
